TPU v7x, 32 devices: a whole 2x2x4 slice. The times are simulated.
32 devices in a mesh: groups: 2 (over y), span: 4 (over z), mp: 2 (over x), seq: 2 (over core).
Axes of the slice: x: 2, y: 2, z: 4, core: 2. Of those that a mesh axis runs over, the one named last changes fastest.
Arguments:
- query: bfloat16 [4, 8, 144, 3072], P(None, ('groups', 'span'), None, ('mp', 'seq')), parts along dimension 1, may hold values from -600 to 600
- noisy_kv: bfloat16 [4, 2, 8, 144, 3072], P(None, None, ('groups', 'span'), None, ('mp', 'seq')), parts along dimension 2, may hold values from -11 to 11
- clean_kv: bfloat16 [2, 8, 144, 3072], P(None, ('groups', 'span'), None, ('mp', 'seq')), parts along dimension 1, may hold values from -11 to 11
- causal_mask: int32 [8, 4], P('groups'), parts along dimension 0, may hold values from 0 to 1, as said below
- step_index: int32 [8, 4], P('groups'), parts along dimension 0, may hold values from 0 to 63, as said below
- finished: bfloat16 [8, 144, 3072], P(('groups', 'span'), None, ('mp', 'seq')), parts along dimension 0, may hold values from -6 to 6
- w_in: bfloat16 [3072, 512], P(('mp', 'seq')), may hold values from -0.109375 to 0.109375
- conv_w: bfloat16 [3, 512, 512], replicated, may hold values from -0.15625 to 0.15625
- fade_count: int32 [8], P(('groups', 'span')), parts along dimension 0, may hold values from 0 to 2, as said below
Outputs:
- attended: bfloat16 [4, 8, 144, 3072], P(None, ('groups', 'span'), None, ('mp', 'seq')), parts along dimension 1
- decoded: bfloat16 [8, 144, 512], P(('groups', 'span'), ('mp', 'seq')), parts along dimension 0
There are 2 independent parts, one for each index of `groups`. A program takes and returns all parts, laid end to end along the dimension named above; an argument that names none is the same for every part. Nothing has to cross between parts.
Inputs may be any that keep to these rules, and one draw needn't show every extreme that they name: `causal_mask`: zero on and above the diagonal. `step_index`: each row counts up by one from its first entry; some row starts at 0 and some at 60. `fade_count`: some segment other than the first has 2.
All inputs are finite; a program needn't handle non-finite values.
Results may differ from a plain program's by a relative error of at most 0.015.
Values may be sent and summed in bfloat16 or wider, within the bound.
No kernel may reach another device: no remote copies, remote signals or barrier semaphores. Data moves between devices by JAX's collectives and lax.ppermute only.
A program may use at most 64 MiB of HBM per device.

v0:
```python
import functools
import math

import jax
import jax.numpy as jnp
from jax import lax
from jax.experimental import pallas as pl
from jax.experimental.pallas import tpu as pltpu
from jax.sharding import PartitionSpec as P

FR = 6
HD = 128
KT = 3
FADE = 2
NSTEPS = 64
LOG2E = 1.4426950408889634
VMEM_LIMIT = 24 * 1024 * 1024
VMEM_ALL = 60 * 1024 * 1024

SMEM_SPEC = pl.BlockSpec(memory_space=pltpu.SMEM)
VMEM_SPEC = pl.BlockSpec(memory_space=pltpu.VMEM)
HBM_SPEC = pl.BlockSpec(memory_space=pltpu.HBM)


def cost(flops, nbytes):
    return pl.CostEstimate(flops=flops, bytes_accessed=nbytes, transcendentals=0)


def hop(value, axis, steps):
    count = lax.axis_size(axis)
    return lax.ppermute(value, axis, [(source, source + steps) for source in range(count - steps)])


def swap(value, axes, offset):
    count = lax.axis_size(axes)
    if count & (count - 1) == 0:
        pairs = [(source, source ^ offset) for source in range(count)]
    else:
        pairs = [(source, (source + offset) % count) for source in range(count)]
    return lax.ppermute(value, axes, pairs)


def target_of(axes, offset):
    count = lax.axis_size(axes)
    mine = lax.axis_index(axes)
    if count & (count - 1) == 0:
        return mine ^ offset
    return lax.rem(mine + offset, count)


def after(value, *earlier):
    return lax.optimization_barrier((value, *earlier))[0]


def nt_dot(left, right):
    return lax.dot_general(left, right, (((1,), (1,)), ((), ())), preferred_element_type=jnp.float32)


def tn_dot(left, right):
    return lax.dot_general(left, right, (((0,), (0,)), ((), ())), preferred_element_type=jnp.float32)


def nn_dot(left, right):
    return jnp.dot(left, right, preferred_element_type=jnp.float32)


def row_factors(step_ref, position, steps, rows):
    lane = lax.broadcasted_iota(jnp.int32, (1, steps * rows), 1)
    index = jnp.full(lane.shape, step_ref[position, 0], jnp.int32)
    for step in range(1, steps):
        index = jnp.where(lane >= step * rows, step_ref[position, step], index)
    fraction = 1.0 - index.astype(jnp.float32) / NSTEPS
    level = 3.0 * fraction / (1.0 + 2.0 * fraction)
    return (0.5 + level) * (LOG2E / math.sqrt(HD))


def lane_windows(steps, rows):
    total = steps * rows
    return [
        (step * rows // HD * HD, min(total, -(-(step + 1) * rows // HD) * HD))
        for step in range(steps)
    ]


def join_steps(pieces, windows, rows):
    total = windows[-1][1]
    tiles = []
    for first in range(0, total, HD):
        stop = min(first + HD, total)
        tile = None
        for step, (begin, end) in enumerate(windows):
            if begin <= first and stop <= end and step * rows < stop and first < (step + 1) * rows:
                part = pieces[step][:, first - begin : stop - begin]
                if tile is None:
                    tile = part
                else:
                    lane = lax.broadcasted_iota(jnp.int32, part.shape, 1) + first
                    tile = jnp.where(lane >= step * rows, part, tile)
        tiles.append(tile)
    return jnp.concatenate(tiles, 1)


def own_kernel(step_ref, q_ref, kv_ref, acc_ref, top_ref, total_ref):
    position = lax.axis_index("span")
    steps, _, rows, columns = q_ref.shape
    factors = row_factors(step_ref, position, steps, rows)
    windows = lane_windows(steps, rows)
    for head in range(columns // HD):
        cut = slice(head * HD, (head + 1) * HD)
        queries = q_ref[:, 0, :, cut].reshape(steps * rows, HD)
        scores = join_steps(
            [nt_dot(kv_ref[s, 0, 0, :, cut], queries[a:b]) for s, (a, b) in enumerate(windows)],
            windows,
            rows,
        )
        scores = scores * factors
        top = jnp.max(scores, axis=0, keepdims=True)
        weights = jnp.exp2(scores - top)
        rounded = weights.astype(jnp.bfloat16)
        acc_ref[head] = join_steps(
            [tn_dot(kv_ref[s, 1, 0, :, cut], rounded[:, a:b]) for s, (a, b) in enumerate(windows)],
            windows,
            rows,
        )
        top_ref[head : head + 1] = top
        total_ref[head : head + 1] = jnp.sum(weights, axis=0, keepdims=True)


def absorb(queries, keys, values, factors, acc, top, total):
    scores = nt_dot(keys, queries) * factors
    newest = jnp.maximum(top, jnp.max(scores, axis=0, keepdims=True))
    weights = jnp.exp2(scores - newest)
    shrink = jnp.exp2(top - newest)
    total = total * shrink + jnp.sum(weights, axis=0, keepdims=True)
    acc = acc * shrink + tn_dot(values, weights.astype(jnp.bfloat16))
    return acc, newest, total


def visible(mask_ref, position, blocks):
    seen = False
    for place, block in blocks.items():
        seen = seen | ((position == place) & (mask_ref[place, block] > 0))
    return seen


def half(ref, which, cut):
    return ref[which, 0, :, cut] if len(ref.shape) == 4 else ref[0, :, cut]


def mid_kernel(plan, step_ref, mask_ref, q_ref, *refs):
    block_refs, (acc_in, top_in, total_in, acc_ref, top_ref, total_ref) = refs[:-6], refs[-6:]
    position = lax.axis_index("span")
    steps, _, rows, columns = q_ref.shape
    seen = visible(mask_ref, position, plan)

    @pl.when(seen)
    def _():
        factors = row_factors(step_ref, position, steps, rows)
        for head in range(columns // HD):
            cut = slice(head * HD, (head + 1) * HD)
            queries = q_ref[:, 0, :, cut].reshape(steps * rows, HD)
            acc, top, total = absorb(
                queries,
                half(block_refs[0], 0, cut),
                half(block_refs[-1], 1, cut),
                factors,
                acc_in[head],
                top_in[head : head + 1],
                total_in[head : head + 1],
            )
            acc_ref[head] = acc
            top_ref[head : head + 1] = top
            total_ref[head : head + 1] = total

    @pl.when(jnp.logical_not(seen))
    def _():
        acc_ref[...] = acc_in[...]
        top_ref[...] = top_in[...]
        total_ref[...] = total_in[...]


def score_kernel(plans, step_ref, mask_ref, q_ref, *refs):
    key_refs, (acc_in, top_in, total_in, acc_ref, w_ref) = refs[:-5], refs[-5:]
    position = lax.axis_index("span")
    steps, _, rows, columns = q_ref.shape

    def finish(key_ref):
        factors = row_factors(step_ref, position, steps, rows)
        for head in range(columns // HD):
            cut = slice(head * HD, (head + 1) * HD)
            queries = q_ref[:, 0, :, cut].reshape(steps * rows, HD)
            scores = nt_dot(half(key_ref, 0, cut), queries) * factors
            top = top_in[head : head + 1]
            newest = jnp.maximum(top, jnp.max(scores, axis=0, keepdims=True))
            weights = jnp.exp2(scores - newest)
            shrink = jnp.exp2(top - newest)
            total = total_in[head : head + 1] * shrink + jnp.sum(weights, axis=0, keepdims=True)
            inverse = 1.0 / total
            w_ref[head] = (weights * inverse).astype(jnp.bfloat16)
            acc_ref[head] = acc_in[head] * (shrink * inverse)

    rest = True
    for plan, key_ref in zip(plans, key_refs):
        seen = visible(mask_ref, position, plan)
        rest = jnp.logical_and(rest, jnp.logical_not(seen))
        pl.when(seen)(functools.partial(finish, key_ref))

    @pl.when(rest)
    def _():
        w_ref[...] = jnp.zeros_like(w_ref)
        for head in range(columns // HD):
            acc_ref[head] = acc_in[head] * (1.0 / total_in[head : head + 1])


def average_kernel(plans, acc_ref, w_ref, *refs):
    value_refs, (average_ref, square_ref) = refs[:-2], refs[-2:]
    position = lax.axis_index("span")

    def finish(value_ref):
        squares = jnp.zeros(square_ref.shape, jnp.float32)
        for head in range(acc_ref.shape[0]):
            average = acc_ref[head]
            if value_ref is not None:
                values = half(value_ref, 1, slice(head * HD, (head + 1) * HD))
                average = average + tn_dot(values, w_ref[head])
            average_ref[head] = average
            squares = squares + jnp.sum(average * average, axis=0, keepdims=True)
        square_ref[...] = squares

    rest = True
    for plan, value_ref in zip(plans, value_refs):
        here = functools.reduce(jnp.logical_or, [position == place for place in plan])
        rest = jnp.logical_and(rest, jnp.logical_not(here))
        pl.when(here)(functools.partial(finish, value_ref))
    pl.when(rest)(functools.partial(finish, None))


def turn_kernel(in_ref, out_ref):
    heads = in_ref.shape[0]
    steps, rows, _ = out_ref.shape
    for head in range(heads):
        out_ref[:, :, head * HD : (head + 1) * HD] = in_ref[head].T.reshape(steps, rows, HD)


def scale_kernel(width, average_ref, *refs):
    part_refs, (out_hbm, out_ref, sem) = refs[:-3], refs[-3:]
    total = part_refs[0][...]
    for ref in part_refs[1:]:
        total = total + ref[...]
    inverse = lax.rsqrt(total / width + 1e-06)
    steps, rows, columns = average_ref.shape
    spread = jnp.broadcast_to(inverse, (HD, steps * rows)).T
    copies = []
    for step in range(steps):
        factor = spread[step * rows : (step + 1) * rows]
        for first in range(0, columns, HD):
            cut = slice(first, first + HD)
            out_ref[step, :, cut] = (average_ref[step, :, cut] * factor).astype(jnp.bfloat16)
        copies.append(pltpu.make_async_copy(out_ref.at[step], out_hbm.at[step, 0], sem.at[step]))
        copies[-1].start()
    for copy in copies:
        copy.wait()


def send(value, pairs):
    return lax.ppermute(value, "span", pairs)


def delivered(span, back):
    return {place: place - back for place in range(back, span)}


def plain_call(kernel, name, out_shape, flops, operands, in_specs=(), out_specs=None, scratch=(), limit=VMEM_LIMIT):
    nbytes = sum(math.prod(o.shape) * o.dtype.itemsize for o in operands)
    if out_specs is None:
        out_specs = [VMEM_SPEC] * len(out_shape)
    return pl.pallas_call(
        kernel,
        in_specs=list(in_specs) + [VMEM_SPEC] * (len(operands) - len(in_specs)),
        out_specs=out_specs,
        out_shape=out_shape,
        scratch_shapes=list(scratch),
        compiler_params=pltpu.CompilerParams(vmem_limit_bytes=limit),
        cost_estimate=cost(flops, nbytes),
        name=name,
    )(*operands)


def picker(shape, wanted):
    row = lax.broadcasted_iota(jnp.int32, shape, 0)
    column = lax.broadcasted_iota(jnp.int32, shape, 1)
    return jnp.where(column == wanted(row), 1.0, 0.0).astype(jnp.bfloat16)


def project_kernel(axes, x_hbm, w_hbm, *refs):
    out_refs, (x_ref, w_ref, x_sem, w_sem) = refs[:-4], refs[-4:]
    rows, depth = x_ref.shape
    share = out_refs[0].shape[0]
    x_copy = pltpu.make_async_copy(x_hbm.at[0], x_ref, x_sem)
    x_copy.start()
    copies = []
    for place, first in enumerate(range(0, depth, 2 * HD)):
        cut = slice(first, min(first + 2 * HD, depth))
        copies.append((cut, pltpu.make_async_copy(w_hbm.at[cut], w_ref.at[cut], w_sem.at[place])))
        copies[-1][1].start()
    total = jnp.zeros((rows, w_ref.shape[1]), jnp.float32)
    x_copy.wait()
    for cut, w_copy in copies:
        w_copy.wait()
        total = total + nn_dot(x_ref[:, cut], w_ref[cut])
    projected = total.astype(jnp.bfloat16)
    for offset, out_ref in enumerate(out_refs):
        first = target_of(axes, offset) * share
        chosen = picker((share, rows), lambda row: row + first)
        out_ref[...] = nn_dot(chosen, projected).astype(jnp.bfloat16)


def gather_kernel(*refs):
    hidden_ref, tail_ref = refs[-2:]
    total = refs[0][...].astype(jnp.float32)
    for ref in refs[1:-2]:
        total = total + ref[...].astype(jnp.float32)
    hidden = total.astype(jnp.bfloat16)
    hidden_ref[...] = hidden
    kept = KT - 1 + FADE
    shape = (tail_ref.shape[0], hidden.shape[0])
    chosen = picker(shape, lambda row: row // kept * FR + FR - kept + row % kept)
    tail_ref[...] = nn_dot(chosen, hidden).astype(jnp.bfloat16)


def decode_kernel(fade_ref, hidden_ref, tail_ref, conv_ref, out_ref):
    position = lax.axis_index("span")
    share = hidden_ref.shape[0]
    spatial = share // FR
    kept = KT - 1 + FADE
    wide = FADE + FR
    hidden, tail = hidden_ref[...], tail_ref[...]
    mixed = jnp.zeros((spatial * wide, out_ref.shape[2]), jnp.float32)
    for tap in range(KT):
        def from_tail(row):
            place = row % wide + KT - 1 - tap
            return jnp.where(place < kept, row // wide * kept + place, -1)

        def from_hidden(row):
            place = row % wide + KT - 1 - tap
            return jnp.where(place >= kept, row // wide * FR + place - kept, -1)

        window = nn_dot(picker((spatial * wide, tail.shape[0]), from_tail), tail)
        window = window + nn_dot(picker((spatial * wide, share), from_hidden), hidden)
        mixed = mixed + nn_dot(window.astype(jnp.bfloat16), conv_ref[tap])
    frames = (mixed * jax.nn.sigmoid(mixed)).astype(jnp.bfloat16)
    fade = fade_ref[0]
    shape = (share, spatial * wide)
    current = nn_dot(picker(shape, lambda row: row // FR * wide + FADE + row % FR), frames)

    def faded(row):
        return jnp.where(row % FR < fade, row // FR * wide + FADE - fade + row % FR, -1)

    previous = nn_dot(picker(shape, faded), frames)
    frame = lax.broadcasted_iota(jnp.int32, (share, out_ref.shape[2]), 0) % FR
    fade_float = jnp.full(frame.shape, fade, jnp.int32).astype(jnp.float32)
    weight = (frame.astype(jnp.float32) + 1.0) / (fade_float + 1.0)
    weight = jnp.where((frame < fade) & (position > 0), weight, 1.0)
    out_ref[0] = (weight * current + (1.0 - weight) * previous).astype(jnp.bfloat16)


def project(finished, w_in):
    axes = ("mp", "seq")
    parts = lax.axis_size(axes)
    _, rows, depth = finished.shape
    channels = w_in.shape[1]
    chunks = -(-depth // (2 * HD))
    return plain_call(
        functools.partial(project_kernel, axes),
        "project",
        [jax.ShapeDtypeStruct((rows // parts, channels), jnp.bfloat16)] * parts,
        2 * rows * depth * channels,
        (finished, w_in),
        [HBM_SPEC] * 2,
        scratch=[
            pltpu.VMEM((rows, depth), jnp.bfloat16),
            pltpu.VMEM((depth, channels), jnp.bfloat16),
            pltpu.SemaphoreType.DMA,
            pltpu.SemaphoreType.DMA((chunks,)),
        ],
        limit=VMEM_ALL,
    )


def gather(parts, rows):
    share, channels = parts[0].shape
    tail_rows = share // FR * (KT - 1 + FADE)
    return plain_call(
        gather_kernel,
        "gather",
        [jax.ShapeDtypeStruct((count, channels), jnp.bfloat16) for count in (share, tail_rows)],
        rows * channels,
        parts,
    )


def decode(hidden, tail, conv_w, fade_count):
    share, channels = hidden.shape
    return plain_call(
        decode_kernel,
        "decode",
        [jax.ShapeDtypeStruct((1, share, channels), jnp.bfloat16)],
        2 * share * KT * channels * channels,
        (fade_count, hidden, tail, conv_w),
        [SMEM_SPEC],
    )[0]


def per_device(
    query, noisy_kv, clean_kv, causal_mask, step_index, finished, w_in, conv_w, fade_count
):
    steps, _, rows, columns = query.shape
    heads = columns // HD
    row_count = steps * rows
    span = lax.axis_size("span")
    axes = ("mp", "seq")
    acc_shape = jax.ShapeDtypeStruct((heads, HD, row_count), jnp.float32)
    stat_shape = jax.ShapeDtypeStruct((heads, row_count), jnp.float32)
    pair_flops = 4 * row_count * rows * columns

    first_pairs = [(0, 2), (2, 3)] if span == 4 else [(c, c + 1) for c in range(span - 1)]
    near = send(clean_kv, first_pairs)
    pieces = project(finished, w_in)
    parts = [pieces[0]] + [swap(p, axes, offset + 1) for offset, p in enumerate(pieces[1:])]
    if span == 4:
        direct = send(after(clean_kv, pieces[0]), [(1, 3)])
    carry = plain_call(
        own_kernel,
        "own",
        [acc_shape, stat_shape, stat_shape],
        pair_flops,
        (step_index, query, noisy_kv),
        [SMEM_SPEC],
    )
    hidden, tail = gather(parts, rows)
    tail = hop(tail, "span", 1)
    if span == 4:
        near = after(near, carry[0], hidden)
        forwards = lax.axis_index("span") == 2
        passed = [jnp.where(forwards, near[which], clean_kv[which]) for which in range(2)]
        passed = [hop(block, "span", 1) for block in passed]
        early = [(near, {2: 0, 3: 2}), (direct, {3: 1})]
        keys, values = passed
        last_plan = {1: 0, 2: 1, 3: 0}
    else:
        ring = [near]
        for _ in range(2, span):
            ring.append(hop(ring[-1], "span", 1))
        early = [(block, delivered(span, back + 1)) for back, block in enumerate(ring[:-1])]
        keys = values = ring[-1]
        last_plan = delivered(span, span - 1)
    for block, plan in early:
        carry = plain_call(
            functools.partial(mid_kernel, plan),
            "middle",
            [acc_shape, stat_shape, stat_shape],
            pair_flops,
            (step_index, causal_mask, query, block, *carry),
            [SMEM_SPEC] * 2,
        )
    acc, weights = plain_call(
        functools.partial(score_kernel, [last_plan]),
        "score",
        [acc_shape, jax.ShapeDtypeStruct((heads, rows, row_count), jnp.bfloat16)],
        pair_flops // 2,
        (step_index, causal_mask, query, keys, *carry),
        [SMEM_SPEC] * 2,
    )
    decoded = decode(after(hidden, weights), tail, conv_w, fade_count)
    averaged, squares = plain_call(
        functools.partial(average_kernel, [last_plan]),
        "average",
        [acc_shape, jax.ShapeDtypeStruct((1, row_count), jnp.float32)],
        pair_flops // 2,
        (after(acc, decoded), weights, values),
    )
    others = [swap(squares, axes, offset) for offset in range(1, lax.axis_size(axes))]
    turned = plain_call(
        turn_kernel,
        "turn",
        [jax.ShapeDtypeStruct((steps, rows, columns), jnp.float32)],
        row_count * columns,
        (averaged,),
    )[0]
    attended = plain_call(
        functools.partial(scale_kernel, columns * lax.axis_size(axes)),
        "scale",
        jax.ShapeDtypeStruct(query.shape, jnp.bfloat16),
        row_count * columns,
        (turned, squares, *others),
        out_specs=HBM_SPEC,
        scratch=[
            pltpu.VMEM((steps, rows, columns), jnp.bfloat16),
            pltpu.SemaphoreType.DMA((steps,)),
        ],
    )
    return (attended, decoded)


def solution(mesh):
    placed = (
        P(None, ("groups", "span"), None, ("mp", "seq")),
        P(None, None, ("groups", "span"), None, ("mp", "seq")),
        P(None, ("groups", "span"), None, ("mp", "seq")),
        P("groups", None),
        P("groups", None),
        P(("groups", "span"), None, ("mp", "seq")),
        P(("mp", "seq"), None),
        P(),
        P(("groups", "span")),
    )
    return jax.shard_map(
        per_device,
        mesh=mesh,
        in_specs=placed,
        out_specs=(
            P(None, ("groups", "span"), None, ("mp", "seq")),
            P(("groups", "span"), ("mp", "seq"), None),
        ),
        check_vma=False,
    )
```

profile of v0, /device:TPU:20, one launch (start us, length us, event | category | flops | bytes accessed | tf_op | source)
XLA Modules:
  0.0 43.5 jit_solution(8612633196136669785)
XLA Ops:
  0.6 0.0 copy-start.7
  0.6 3.6 %collective-permute-start = (bf16[2,1,144,768]{3,2,1,0:T(8,128)(2,1)}, bf16[2,1,144,768]{3,2,1,0:T(8,128)(2,1)S(1)}, u32[]{:S(2)}, u32[]{:S(2)}) collective-permute-start(bf16[2,1,144,768]{3,2,1,0:T(8,128)(2,1)} %param.11), channel_id=1, source_target_pairs={{0,8},{8,12},{1,9},{9,13},{2,10},{10,14},{3,11},{11,15},{16,24},{2... | collective-permute-start | bytes 1327112 | tf_op jit(solution)/shard_map/ppermute | solution.py:266
  4.3 2.3 %project.1 = (bf16[36,512]{1,0:T(8,128)(2,1)}, bf16[36,512]{1,0:T(8,128)(2,1)}, bf16[36,512]{1,0:T(8,128)(2,1)}, bf16[36,512]{1,0:T(8,128)(2,1)}) custom-call(bf16[1,144,768]{2,1,0:T(8,128)(2,1)} %x_hbm.1, bf16[768,512]{1,0:T(8,128)(2,1)} %w_hbm.1), custom_call_target="tpu_custom_call" | custom-call | flops 113246208 | bytes 1007616 | tf_op jit(solution)/shard_map/project/pallas_call | solution.py:277
  6.6 0.1 collective-permute-start.1
  6.6 1.6 %collective-permute-start.2 = (bf16[36,512]{1,0:T(8,128)(2,1)}, bf16[36,512]{1,0:T(8,128)(2,1)S(1)}, u32[]{:S(2)}, u32[]{:S(2)}) collective-permute-start(bf16[36,512]{1,0:T(8,128)(2,1)} %get-tuple-element.28), channel_id=1, source_target_pairs={{0,2},{1,3},{2,0},{3,1},{4,6},{5,7},{6,4},{7,5},{8,10},{9,11},{10,... | collective-permute-start | bytes 110600 | tf_op jit(solution)/shard_map/ppermute | solution.py:40
  8.2 0.3 collective-permute-start.3
  8.5 0.7 %collective-permute-start.5 = (bf16[2,1,144,768]{3,2,1,0:T(8,128)(2,1)}, bf16[2,1,144,768]{3,2,1,0:T(8,128)(2,1)S(1)}, u32[]{:S(2)}, u32[]{:S(2)}) collective-permute-start(bf16[2,1,144,768]{3,2,1,0:T(8,128)(2,1)} %param.11), channel_id=1, source_target_pairs={{4,12},{5,13},{6,14},{7,15},{20,28},{21,29},{22,30},{23,31}} | collective-permute-start | bytes 1327112 | tf_op jit(solution)/shard_map/ppermute | solution.py:266
  9.2 0.0 copy-start
  9.2 1.2 %copy-done = bf16[4,1,144,768]{3,2,1,0:T(8,128)(2,1)S(1)} copy-done((bf16[4,1,144,768]{3,2,1,0:T(8,128)(2,1)S(1)}, bf16[4,1,144,768]{3,2,1,0:T(8,128)(2,1)}, u32[]{:S(2)}) %copy-start) | copy-done | bytes 884760
  10.4 0.0 copy-start.2
  10.4 1.5 %copy-done.2 = bf16[4,2,1,144,768]{4,3,2,1,0:T(8,128)(2,1)S(1)} copy-done((bf16[4,2,1,144,768]{4,3,2,1,0:T(8,128)(2,1)S(1)}, bf16[4,2,1,144,768]{4,3,2,1,0:T(8,128)(2,1)}, u32[]{:S(2)}) %copy-start.2) | copy-done | bytes 1769496
  11.8 0.0 copy-start.5
  11.8 0.7 %copy-done.5 = s32[4,4]{1,0:T(4,128)S(1)} copy-done((s32[4,4]{1,0:T(4,128)S(1)}, s32[4,4]{1,0:T(4,128)}, u32[]{:S(2)}) %copy-start.5) | copy-done | bytes 88
  12.5 0.0 copy-start.4
  12.5 0.0 copy-start.1
  12.5 2.5 %own.1 = (f32[6,128,576]{2,1,0:T(8,128)S(1)}, f32[6,576]{1,0:T(8,128)S(1)}, f32[6,576]{1,0:T(8,128)S(1)}) custom-call(s32[4,4]{1,0:T(4,128)S(1)} %copy-done.5, bf16[4,1,144,768]{3,2,1,0:T(8,128)(2,1)S(1)} %copy-done, bf16[4,2,1,144,768]{4,3,2,1,0:T(8,128)(2,1)S(1)} %copy-done.2), custom_call_target="tpu_custom_call" | custom-call | flops 254803968 | bytes 2654272 | tf_op jit(solution)/shard_map/own/pallas_call | solution.py:277
  15.1 0.0 collective-permute-done.1.refs_1_
  15.1 0.0 collective-permute-done.2.refs_2_
  15.1 0.0 collective-permute-done.3.refs_3_
  15.1 0.0 copy-done.4
  15.1 0.1 gather.1
  15.3 0.5 %collective-permute-done.refs_0_ = bf16[2,1,144,768]{3,2,1,0:T(8,128)(2,1)S(1)} collective-permute-done((bf16[2,1,144,768]{3,2,1,0:T(8,128)(2,1)}, bf16[2,1,144,768]{3,2,1,0:T(8,128)(2,1)S(1)}, u32[]{:S(2)}, u32[]{:S(2)}) %collective-permute-start) | collective-permute-done | bytes 442400 | tf_op jit(solution)/shard_map/ppermute | solution.py:266
  15.8 0.0 copy-done.7
  15.8 0.1 select_bitcast_fusion
  15.8 2.6 %collective-permute-start.4 = (bf16[1,144,768]{2,1,0:T(8,128)(2,1)S(1)}, bf16[1,144,768]{2,1,0:T(8,128)(2,1)S(1)}, u32[]{:S(2)}, u32[]{:S(2)}) collective-permute-start(bf16[1,144,768]{2,1,0:T(8,128)(2,1)S(1)} %get-tuple-element.49), channel_id=1, source_target_pairs={{0,4},{4,8},{8,12},{1,5},{5,9},{9,13},{2,6},{6,10},{10,14},{3,7},{... | collective-permute-start | bytes 663560 | tf_op jit(solution)/shard_map/ppermute | solution.py:31
  18.4 1.9 %collective-permute-start.7 = (bf16[1,144,768]{2,1,0:T(8,128)(2,1)S(1)}, bf16[1,144,768]{2,1,0:T(8,128)(2,1)S(1)}, u32[]{:S(2)}, u32[]{:S(2)}) collective-permute-start(bf16[1,144,768]{2,1,0:T(8,128)(2,1)S(1)} %get-tuple-element.48), channel_id=1, source_target_pairs={{0,4},{4,8},{8,12},{1,5},{5,9},{9,13},{2,6},{6,10},{10,14},{3,7},{... | collective-permute-start | bytes 663560 | tf_op jit(solution)/shard_map/ppermute | solution.py:31
  21.0 1.9 %collective-permute-start.6 = (bf16[24,512]{1,0:T(8,128)(2,1)S(1)}, bf16[24,512]{1,0:T(8,128)(2,1)S(1)}, u32[]{:S(2)}, u32[]{:S(2)}) collective-permute-start(bf16[24,512]{1,0:T(8,128)(2,1)S(1)} %get-tuple-element.44), channel_id=1, source_target_pairs={{0,4},{4,8},{8,12},{1,5},{5,9},{9,13},{2,6},{6,10},{10,14},{3,7},{... | collective-permute-start | bytes 73736 | tf_op jit(solution)/shard_map/ppermute | solution.py:31
  22.9 0.0 copy-done.1
  23.0 0.0 copy-done.6
  23.0 0.7 %middle.2 = (f32[6,128,576]{2,1,0:T(8,128)S(1)}, f32[6,576]{1,0:T(8,128)S(1)}, f32[6,576]{1,0:T(8,128)S(1)}) custom-call(s32[4,4]{1,0:T(4,128)S(1)} %copy-done.5, s32[4,4]{1,0:T(4,128)S(1)} %copy-done.6, bf16[4,1,144,768]{3,2,1,0:T(8,128)(2,1)S(1)} %copy-done.1, bf16[2,1,144,768]{3,2,1,0:T(8,128)(2,1)S(1)} %collective-permute-done.refs_0_, ...), custom_call_target="tpu_custom_call" | custom-call | flops 254803968 | bytes 3124352 | tf_op jit(solution)/shard_map/middle/pallas_call | solution.py:277
  23.7 0.0 collective-permute-done.5.refs_0_
  23.7 0.7 %middle.3 = (f32[6,128,576]{2,1,0:T(8,128)S(1)}, f32[6,576]{1,0:T(8,128)S(1)}, f32[6,576]{1,0:T(8,128)S(1)}) custom-call(s32[4,4]{1,0:T(4,128)S(1)} %copy-done.5, s32[4,4]{1,0:T(4,128)S(1)} %copy-done.6, bf16[4,1,144,768]{3,2,1,0:T(8,128)(2,1)S(1)} %copy-done.1, bf16[2,1,144,768]{3,2,1,0:T(8,128)(2,1)S(1)} %collective-permute-done.5.refs_0_, ...), custom_call_target="tpu_custom_call" | custom-call | flops 254803968 | bytes 3124352 | tf_op jit(solution)/shard_map/middle/pallas_call | solution.py:277
  24.5 0.0 copy-start.3
  24.5 5.5 %collective-permute-done.4.refs_0_ = bf16[1,144,768]{2,1,0:T(8,128)(2,1)S(1)} collective-permute-done((bf16[1,144,768]{2,1,0:T(8,128)(2,1)S(1)}, bf16[1,144,768]{2,1,0:T(8,128)(2,1)S(1)}, u32[]{:S(2)}, u32[]{:S(2)}) %collective-permute-start.4) | collective-permute-done | bytes 221216 | tf_op jit(solution)/shard_map/ppermute | solution.py:31
  30.0 1.8 %score.1 = (f32[6,128,576]{2,1,0:T(8,128)S(1)}, bf16[6,144,576]{2,1,0:T(8,128)(2,1)S(1)}) custom-call(s32[4,4]{1,0:T(4,128)S(1)} %copy-done.5, s32[4,4]{1,0:T(4,128)S(1)} %copy-done.6, bf16[4,1,144,768]{3,2,1,0:T(8,128)(2,1)S(1)} %copy-done.1, bf16[1,144,768]{2,1,0:T(8,128)(2,1)S(1)} %collective-permute-done.4.refs_0_, ...), custom_call_target="tpu_custom_call" | custom-call | flops 127401984 | bytes 2903168 | tf_op jit(solution)/shard_map/score/pallas_call | solution.py:277
  31.8 3.4 %collective-permute-done.6.tail_ref = bf16[24,512]{1,0:T(8,128)(2,1)S(1)} collective-permute-done((bf16[24,512]{1,0:T(8,128)(2,1)S(1)}, bf16[24,512]{1,0:T(8,128)(2,1)S(1)}, u32[]{:S(2)}, u32[]{:S(2)}) %collective-permute-start.6) | collective-permute-done | bytes 24608 | tf_op jit(solution)/shard_map/ppermute | solution.py:31
  35.2 0.0 copy-done.3
  35.2 1.4 %decode.1 = bf16[1,36,512]{2,1,0:T(8,128)(2,1)} custom-call(s32[1]{0:T(128)S(6)} %copy.11.fade_ref, bf16[36,512]{1,0:T(8,128)(2,1)S(1)} %get-tuple-element.43.hidden_ref, bf16[24,512]{1,0:T(8,128)(2,1)S(1)} %collective-permute-done.6.tail_ref, bf16[3,512,512]{2,1,0:T(8,128)(2,1)S(1)} %copy-done.3), custom_call_target="tpu_custom_call" | custom-call | flops 56623104 | bytes 1634308 | tf_op jit(solution)/shard_map/decode/pallas_call | solution.py:277
  36.6 0.0 collective-permute-done.7.refs_0_
  36.6 0.5 %average.1 = (f32[6,128,576]{2,1,0:T(8,128)S(1)}, f32[1,576]{1,0:T(1,128)S(1)}) custom-call(f32[6,128,576]{2,1,0:T(8,128)S(1)} %get-tuple-element.45.acc_ref, bf16[6,144,576]{2,1,0:T(8,128)(2,1)S(1)} %get-tuple-element.42.w_ref, bf16[1,144,768]{2,1,0:T(8,128)(2,1)S(1)} %collective-permute-done.7.refs_0_), custom_call_target="tpu_custom_call" | custom-call | flops 127401984 | bytes 2985984 | tf_op jit(solution)/shard_map/average/pallas_call | solution.py:277
  37.2 1.2 %collective-permute-start.10 = (f32[1,576]{1,0:T(1,128)S(1)}, f32[1,576]{1,0:T(1,128)S(1)}, u32[]{:S(2)}, u32[]{:S(2)}) collective-permute-start(f32[1,576]{1,0:T(1,128)S(1)} %get-tuple-element.47.refs_0_), channel_id=1, source_target_pairs={{0,3},{1,2},{2,1},{3,0},{4,7},{5,6},{6,5},{7,4},{8,11},{9,10},{10,... | collective-permute-start | bytes 6920 | tf_op jit(solution)/shard_map/ppermute | solution.py:40
  38.4 0.5 %collective-permute-start.8 = (f32[1,576]{1,0:T(1,128)S(1)}, f32[1,576]{1,0:T(1,128)S(1)}, u32[]{:S(2)}, u32[]{:S(2)}) collective-permute-start(f32[1,576]{1,0:T(1,128)S(1)} %get-tuple-element.47.refs_0_), channel_id=1, source_target_pairs={{0,1},{1,0},{2,3},{3,2},{4,5},{5,4},{6,7},{7,6},{8,9},{9,8},{10,11... | collective-permute-start | bytes 6920 | tf_op jit(solution)/shard_map/ppermute | solution.py:40
  38.9 0.5 %collective-permute-start.9 = (f32[1,576]{1,0:T(1,128)S(1)}, f32[1,576]{1,0:T(1,128)S(1)}, u32[]{:S(2)}, u32[]{:S(2)}) collective-permute-start(f32[1,576]{1,0:T(1,128)S(1)} %get-tuple-element.47.refs_0_), channel_id=1, source_target_pairs={{0,2},{1,3},{2,0},{3,1},{4,6},{5,7},{6,4},{7,5},{8,10},{9,11},{10,... | collective-permute-start | bytes 6920 | tf_op jit(solution)/shard_map/ppermute | solution.py:40
  39.4 0.6 %turn.1.average_ref = f32[4,144,768]{2,1,0:T(8,128)S(1)} custom-call(f32[6,128,576]{2,1,0:T(8,128)S(1)} %get-tuple-element.46.in_ref), custom_call_target="tpu_custom_call" | custom-call | flops 442368 | bytes 1769472 | tf_op jit(solution)/shard_map/turn/pallas_call | solution.py:277
  40.0 0.3 collective-permute-done.10.refs_3_
  40.3 0.0 collective-permute-done.8.refs_1_
  40.3 2.2 %collective-permute-done.9.refs_2_ = f32[1,576]{1,0:T(1,128)S(1)} collective-permute-done((f32[1,576]{1,0:T(1,128)S(1)}, f32[1,576]{1,0:T(1,128)S(1)}, u32[]{:S(2)}, u32[]{:S(2)}) %collective-permute-start.9) | collective-permute-done | bytes 2336 | tf_op jit(solution)/shard_map/ppermute | solution.py:40
  42.4 1.1 %scale.1 = bf16[4,1,144,768]{3,2,1,0:T(8,128)(2,1)} custom-call(f32[4,144,768]{2,1,0:T(8,128)S(1)} %turn.1.average_ref, f32[1,576]{1,0:T(1,128)S(1)} %get-tuple-element.47.refs_0_, f32[1,576]{1,0:T(1,128)S(1)} %collective-permute-done.8.refs_1_, f32[1,576]{1,0:T(1,128)S(1)} %collective-permute-done.9.refs_2_, f32[1,576]{1,0:T(1,128)S(1)} %collective-permute-done.10.refs_3_), custom_call_target="tpu_custom_call" | custom-call | flops 442368 | bytes 1778688 | tf_op jit(solution)/shard_map/scale/pallas_call | solution.py:277
  (1 shorter events, 0.0 us)
Async XLA Ops:
  0.6 15.2 %copy-start.7 = (bf16[2,1,144,768]{3,2,1,0:T(8,128)(2,1)S(1)}, bf16[2,1,144,768]{3,2,1,0:T(8,128)(2,1)}, u32[]{:S(2)}) copy-start(bf16[2,1,144,768]{3,2,1,0:T(8,128)(2,1)} %param.11) | copy-start | bytes 1327108
  0.6 15.1 %collective-permute-start = (bf16[2,1,144,768]{3,2,1,0:T(8,128)(2,1)}, bf16[2,1,144,768]{3,2,1,0:T(8,128)(2,1)S(1)}, u32[]{:S(2)}, u32[]{:S(2)}) collective-permute-start(bf16[2,1,144,768]{3,2,1,0:T(8,128)(2,1)} %param.11), channel_id=1, source_target_pairs={{0,8},{8,12},{1,9},{9,13},{2,10},{10,14},{3,11},{11,15},{16,24},{2... | collective-permute-start | bytes 1327112 | tf_op jit(solution)/shard_map/ppermute | solution.py:266
  6.6 8.5 %collective-permute-start.1 = (bf16[36,512]{1,0:T(8,128)(2,1)}, bf16[36,512]{1,0:T(8,128)(2,1)S(1)}, u32[]{:S(2)}, u32[]{:S(2)}) collective-permute-start(bf16[36,512]{1,0:T(8,128)(2,1)} %get-tuple-element.27), channel_id=1, source_target_pairs={{0,1},{1,0},{2,3},{3,2},{4,5},{5,4},{6,7},{7,6},{8,9},{9,8},{10,11... | collective-permute-start | bytes 110600 | tf_op jit(solution)/shard_map/ppermute | solution.py:40
  6.6 8.5 %collective-permute-start.2 = (bf16[36,512]{1,0:T(8,128)(2,1)}, bf16[36,512]{1,0:T(8,128)(2,1)S(1)}, u32[]{:S(2)}, u32[]{:S(2)}) collective-permute-start(bf16[36,512]{1,0:T(8,128)(2,1)} %get-tuple-element.28), channel_id=1, source_target_pairs={{0,2},{1,3},{2,0},{3,1},{4,6},{5,7},{6,4},{7,5},{8,10},{9,11},{10,... | collective-permute-start | bytes 110600 | tf_op jit(solution)/shard_map/ppermute | solution.py:40
  8.2 6.9 %collective-permute-start.3 = (bf16[36,512]{1,0:T(8,128)(2,1)}, bf16[36,512]{1,0:T(8,128)(2,1)S(1)}, u32[]{:S(2)}, u32[]{:S(2)}) collective-permute-start(bf16[36,512]{1,0:T(8,128)(2,1)} %get-tuple-element.29), channel_id=1, source_target_pairs={{0,3},{1,2},{2,1},{3,0},{4,7},{5,6},{6,5},{7,4},{8,11},{9,10},{10,... | collective-permute-start | bytes 110600 | tf_op jit(solution)/shard_map/ppermute | solution.py:40
  8.5 15.2 %collective-permute-start.5 = (bf16[2,1,144,768]{3,2,1,0:T(8,128)(2,1)}, bf16[2,1,144,768]{3,2,1,0:T(8,128)(2,1)S(1)}, u32[]{:S(2)}, u32[]{:S(2)}) collective-permute-start(bf16[2,1,144,768]{3,2,1,0:T(8,128)(2,1)} %param.11), channel_id=1, source_target_pairs={{4,12},{5,13},{6,14},{7,15},{20,28},{21,29},{22,30},{23,31}} | collective-permute-start | bytes 1327112 | tf_op jit(solution)/shard_map/ppermute | solution.py:266
  9.2 1.2 %copy-start = (bf16[4,1,144,768]{3,2,1,0:T(8,128)(2,1)S(1)}, bf16[4,1,144,768]{3,2,1,0:T(8,128)(2,1)}, u32[]{:S(2)}) copy-start(bf16[4,1,144,768]{3,2,1,0:T(8,128)(2,1)} %q_ref.7) | copy-start | bytes 2654212
  10.4 1.5 %copy-start.2 = (bf16[4,2,1,144,768]{4,3,2,1,0:T(8,128)(2,1)S(1)}, bf16[4,2,1,144,768]{4,3,2,1,0:T(8,128)(2,1)}, u32[]{:S(2)}) copy-start(bf16[4,2,1,144,768]{4,3,2,1,0:T(8,128)(2,1)} %kv_ref.1) | copy-start | bytes 5308420
  11.8 0.7 %copy-start.5 = (s32[4,4]{1,0:T(4,128)S(1)}, s32[4,4]{1,0:T(4,128)}, u32[]{:S(2)}) copy-start(s32[4,4]{1,0:T(4,128)} %step_ref.7) | copy-start | bytes 196
  12.5 2.6 %copy-start.4 = (bf16[36,512]{1,0:T(8,128)(2,1)S(1)}, bf16[36,512]{1,0:T(8,128)(2,1)}, u32[]{:S(2)}) copy-start(bf16[36,512]{1,0:T(8,128)(2,1)} %get-tuple-element.26.refs_0_) | copy-start | bytes 110596
  12.5 10.4 %copy-start.1 = (bf16[4,1,144,768]{3,2,1,0:T(8,128)(2,1)S(1)}, bf16[4,1,144,768]{3,2,1,0:T(8,128)(2,1)}, u32[]{:S(2)}) copy-start(bf16[4,1,144,768]{3,2,1,0:T(8,128)(2,1)} %q_ref.7) | copy-start | bytes 2654212
  12.5 10.4 %copy-start.6 = (s32[4,4]{1,0:T(4,128)S(1)}, s32[4,4]{1,0:T(4,128)}, u32[]{:S(2)}) copy-start(s32[4,4]{1,0:T(4,128)} %mask_ref.5) | copy-start | bytes 196
  15.8 14.2 %collective-permute-start.4 = (bf16[1,144,768]{2,1,0:T(8,128)(2,1)S(1)}, bf16[1,144,768]{2,1,0:T(8,128)(2,1)S(1)}, u32[]{:S(2)}, u32[]{:S(2)}) collective-permute-start(bf16[1,144,768]{2,1,0:T(8,128)(2,1)S(1)} %get-tuple-element.49), channel_id=1, source_target_pairs={{0,4},{4,8},{8,12},{1,5},{5,9},{9,13},{2,6},{6,10},{10,14},{3,7},{... | collective-permute-start | bytes 663560 | tf_op jit(solution)/shard_map/ppermute | solution.py:31
  18.4 18.2 %collective-permute-start.7 = (bf16[1,144,768]{2,1,0:T(8,128)(2,1)S(1)}, bf16[1,144,768]{2,1,0:T(8,128)(2,1)S(1)}, u32[]{:S(2)}, u32[]{:S(2)}) collective-permute-start(bf16[1,144,768]{2,1,0:T(8,128)(2,1)S(1)} %get-tuple-element.48), channel_id=1, source_target_pairs={{0,4},{4,8},{8,12},{1,5},{5,9},{9,13},{2,6},{6,10},{10,14},{3,7},{... | collective-permute-start | bytes 663560 | tf_op jit(solution)/shard_map/ppermute | solution.py:31
  21.0 14.2 %collective-permute-start.6 = (bf16[24,512]{1,0:T(8,128)(2,1)S(1)}, bf16[24,512]{1,0:T(8,128)(2,1)S(1)}, u32[]{:S(2)}, u32[]{:S(2)}) collective-permute-start(bf16[24,512]{1,0:T(8,128)(2,1)S(1)} %get-tuple-element.44), channel_id=1, source_target_pairs={{0,4},{4,8},{8,12},{1,5},{5,9},{9,13},{2,6},{6,10},{10,14},{3,7},{... | collective-permute-start | bytes 73736 | tf_op jit(solution)/shard_map/ppermute | solution.py:31
  24.5 10.7 %copy-start.3 = (bf16[3,512,512]{2,1,0:T(8,128)(2,1)S(1)}, bf16[3,512,512]{2,1,0:T(8,128)(2,1)}, u32[]{:S(2)}) copy-start(bf16[3,512,512]{2,1,0:T(8,128)(2,1)} %conv_ref.1) | copy-start | bytes 4718596
  37.2 3.1 %collective-permute-start.10 = (f32[1,576]{1,0:T(1,128)S(1)}, f32[1,576]{1,0:T(1,128)S(1)}, u32[]{:S(2)}, u32[]{:S(2)}) collective-permute-start(f32[1,576]{1,0:T(1,128)S(1)} %get-tuple-element.47.refs_0_), channel_id=1, source_target_pairs={{0,3},{1,2},{2,1},{3,0},{4,7},{5,6},{6,5},{7,4},{8,11},{9,10},{10,... | collective-permute-start | bytes 6920 | tf_op jit(solution)/shard_map/ppermute | solution.py:40
  38.4 1.9 %collective-permute-start.8 = (f32[1,576]{1,0:T(1,128)S(1)}, f32[1,576]{1,0:T(1,128)S(1)}, u32[]{:S(2)}, u32[]{:S(2)}) collective-permute-start(f32[1,576]{1,0:T(1,128)S(1)} %get-tuple-element.47.refs_0_), channel_id=1, source_target_pairs={{0,1},{1,0},{2,3},{3,2},{4,5},{5,4},{6,7},{7,6},{8,9},{9,8},{10,11... | collective-permute-start | bytes 6920 | tf_op jit(solution)/shard_map/ppermute | solution.py:40
  38.9 3.6 %collective-permute-start.9 = (f32[1,576]{1,0:T(1,128)S(1)}, f32[1,576]{1,0:T(1,128)S(1)}, u32[]{:S(2)}, u32[]{:S(2)}) collective-permute-start(f32[1,576]{1,0:T(1,128)S(1)} %get-tuple-element.47.refs_0_), channel_id=1, source_target_pairs={{0,2},{1,3},{2,0},{3,1},{4,6},{5,7},{6,4},{7,5},{8,10},{9,11},{10,... | collective-permute-start | bytes 6920 | tf_op jit(solution)/shard_map/ppermute | solution.py:40
where the time goes:
time: 43.8 us; the launch traced here: 43.5 us
  starting transfers between devices  14.9 us (34%)
  waiting for transfers between devices  12 us (27%)
  Pallas kernels  11.8 us (27%)
  local copies, waits for them, and re-layouts  3.34 us (8%)
  between operations  1.47 us (3%)
    pallas_call x10, Pallas kernels, plain_call(): pl.pallas_call(kernel, in_specs=list(in_specs) + [VMEM_SPEC] * (len(opera...  11.8 us
    ppermute x3, waiting for transfers between devices, hop(): lax.ppermute(value, axis, [(source, source + steps) for source in range(c...  8.94 us
    ppermute x3, starting transfers between devices, hop(): lax.ppermute(value, axis, [(source, source + steps) for source in range(c...  6.43 us
    ppermute x2, starting transfers between devices, send(): return lax.ppermute(value, 'span', pairs)  4.3 us
    ppermute x6, starting transfers between devices, swap(): return lax.ppermute(value, axes, pairs)  4.14 us
    unnamed x16, local copies, waits for them, and re-layouts  3.34 us
    ppermute x6, waiting for transfers between devices, swap(): return lax.ppermute(value, axes, pairs)  2.49 us
  transfers between devices with their start and end apart: 11, of which 5 were waited for; matrix products, arithmetic and copies ran while one was open for 0% of the time, Pallas kernels for 24%

commit v1 on v0

--- a/solution.py
+++ b/solution.py
@@ -471,14 +471,14 @@
         (step_index, causal_mask, query, keys, *carry),
         [SMEM_SPEC] * 2,
     )
-    decoded = decode(after(hidden, weights), tail, conv_w, fade_count)
     averaged, squares = plain_call(
         functools.partial(average_kernel, [last_plan]),
         "average",
         [acc_shape, jax.ShapeDtypeStruct((1, row_count), jnp.float32)],
         pair_flops // 2,
-        (after(acc, decoded), weights, values),
-    )
+        (acc, weights, values),
+    )
+    decoded = decode(after(hidden, squares), tail, conv_w, fade_count)
     others = [swap(squares, axes, offset) for offset in range(1, lax.axis_size(axes))]
     turned = plain_call(
         turn_kernel,

time: 43.8 us -> 41.7 us (0.952)
  waiting for transfers between devices: 12 us -> 10.6 us
  Pallas kernels: 11.8 us -> 10.9 us
    ppermute x6, waiting for transfers between devices: 2.49 us -> 0.7 us  [swap(): return lax.ppermute(value, axes, pairs)]
    pallas_call x10, Pallas kernels: 11.8 us -> 10.9 us  [plain_call(): pl.pallas_call(kernel, in_specs=list(in_specs) + [VMEM_SPEC] * (len(opera...]
    ppermute x3, waiting for transfers between devices: 8.94 us -> 9.43 us  [hop(): lax.ppermute(value, axis, [(source, source + steps) for source in range(c...]
  transfers between devices with their start and end apart: 11 -> 11, of which waited for: 5 -> 4; matrix products, arithmetic and copies ran while one was open for 0% -> 0% of each run, Pallas kernels for 24% -> 24%
where the time goes in v1:
time: 41.7 us; the launch traced here: 41 us
  starting transfers between devices  14.6 us (35%)
  Pallas kernels  10.9 us (26%)
  waiting for transfers between devices  10.6 us (25%)
  local copies, waits for them, and re-layouts  3.34 us (8%)
  between operations  1.49 us (4%)
    pallas_call x10, Pallas kernels, plain_call(): pl.pallas_call(kernel, in_specs=list(in_specs) + [VMEM_SPEC] * (len(opera...  10.9 us
    ppermute x3, waiting for transfers between devices, hop(): lax.ppermute(value, axis, [(source, source + steps) for source in range(c...  9.43 us
    ppermute x3, starting transfers between devices, hop(): lax.ppermute(value, axis, [(source, source + steps) for source in range(c...  6.43 us
    ppermute x2, starting transfers between devices, send(): return lax.ppermute(value, 'span', pairs)  4.3 us
    ppermute x6, starting transfers between devices, swap(): return lax.ppermute(value, axes, pairs)  3.87 us
    unnamed x16, local copies, waits for them, and re-layouts  3.34 us
  transfers between devices with their start and end apart: 11, of which 4 were waited for; matrix products, arithmetic and copies ran while one was open for 0% of the time, Pallas kernels for 24%

profile of v1, /device:TPU:20, one launch (start us, length us, event | category | flops | bytes accessed | tf_op | source)
XLA Modules:
  0.0 41.0 jit_solution(8513685606551550759)
XLA Ops:
  0.6 0.0 copy-start.7
  0.6 3.6 %collective-permute-start = (bf16[2,1,144,768]{3,2,1,0:T(8,128)(2,1)}, bf16[2,1,144,768]{3,2,1,0:T(8,128)(2,1)S(1)}, u32[]{:S(2)}, u32[]{:S(2)}) collective-permute-start(bf16[2,1,144,768]{3,2,1,0:T(8,128)(2,1)} %param.11), channel_id=1, source_target_pairs={{0,8},{8,12},{1,9},{9,13},{2,10},{10,14},{3,11},{11,15},{16,24},{2... | collective-permute-start | bytes 1327112 | tf_op jit(solution)/shard_map/ppermute | solution.py:266
  4.3 2.3 %project.1 = (bf16[36,512]{1,0:T(8,128)(2,1)}, bf16[36,512]{1,0:T(8,128)(2,1)}, bf16[36,512]{1,0:T(8,128)(2,1)}, bf16[36,512]{1,0:T(8,128)(2,1)}) custom-call(bf16[1,144,768]{2,1,0:T(8,128)(2,1)} %x_hbm.1, bf16[768,512]{1,0:T(8,128)(2,1)} %w_hbm.1), custom_call_target="tpu_custom_call" | custom-call | flops 113246208 | bytes 1007616 | tf_op jit(solution)/shard_map/project/pallas_call | solution.py:277
  6.6 0.1 collective-permute-start.1
  6.6 1.6 %collective-permute-start.2 = (bf16[36,512]{1,0:T(8,128)(2,1)}, bf16[36,512]{1,0:T(8,128)(2,1)S(1)}, u32[]{:S(2)}, u32[]{:S(2)}) collective-permute-start(bf16[36,512]{1,0:T(8,128)(2,1)} %get-tuple-element.27), channel_id=1, source_target_pairs={{0,2},{1,3},{2,0},{3,1},{4,6},{5,7},{6,4},{7,5},{8,10},{9,11},{10,... | collective-permute-start | bytes 110600 | tf_op jit(solution)/shard_map/ppermute | solution.py:40
  8.2 0.3 collective-permute-start.3
  8.5 0.7 %collective-permute-start.5 = (bf16[2,1,144,768]{3,2,1,0:T(8,128)(2,1)}, bf16[2,1,144,768]{3,2,1,0:T(8,128)(2,1)S(1)}, u32[]{:S(2)}, u32[]{:S(2)}) collective-permute-start(bf16[2,1,144,768]{3,2,1,0:T(8,128)(2,1)} %param.11), channel_id=1, source_target_pairs={{4,12},{5,13},{6,14},{7,15},{20,28},{21,29},{22,30},{23,31}} | collective-permute-start | bytes 1327112 | tf_op jit(solution)/shard_map/ppermute | solution.py:266
  9.2 0.0 copy-start
  9.2 1.2 %copy-done = bf16[4,1,144,768]{3,2,1,0:T(8,128)(2,1)S(1)} copy-done((bf16[4,1,144,768]{3,2,1,0:T(8,128)(2,1)S(1)}, bf16[4,1,144,768]{3,2,1,0:T(8,128)(2,1)}, u32[]{:S(2)}) %copy-start) | copy-done | bytes 884760
  10.4 0.0 copy-start.2
  10.4 1.5 %copy-done.2 = bf16[4,2,1,144,768]{4,3,2,1,0:T(8,128)(2,1)S(1)} copy-done((bf16[4,2,1,144,768]{4,3,2,1,0:T(8,128)(2,1)S(1)}, bf16[4,2,1,144,768]{4,3,2,1,0:T(8,128)(2,1)}, u32[]{:S(2)}) %copy-start.2) | copy-done | bytes 1769496
  11.8 0.0 copy-start.5
  11.8 0.7 %copy-done.5 = s32[4,4]{1,0:T(4,128)S(1)} copy-done((s32[4,4]{1,0:T(4,128)S(1)}, s32[4,4]{1,0:T(4,128)}, u32[]{:S(2)}) %copy-start.5) | copy-done | bytes 88
  12.5 0.0 copy-start.4
  12.5 0.0 copy-start.1
  12.5 2.5 %own.1 = (f32[6,128,576]{2,1,0:T(8,128)S(1)}, f32[6,576]{1,0:T(8,128)S(1)}, f32[6,576]{1,0:T(8,128)S(1)}) custom-call(s32[4,4]{1,0:T(4,128)S(1)} %copy-done.5, bf16[4,1,144,768]{3,2,1,0:T(8,128)(2,1)S(1)} %copy-done, bf16[4,2,1,144,768]{4,3,2,1,0:T(8,128)(2,1)S(1)} %copy-done.2), custom_call_target="tpu_custom_call" | custom-call | flops 254803968 | bytes 2654272 | tf_op jit(solution)/shard_map/own/pallas_call | solution.py:277
  15.1 0.0 collective-permute-done.1.refs_1_
  15.1 0.0 collective-permute-done.2.refs_2_
  15.1 0.0 collective-permute-done.3.refs_3_
  15.1 0.0 copy-done.4
  15.1 0.1 gather.1
  15.3 0.5 %collective-permute-done.refs_0_ = bf16[2,1,144,768]{3,2,1,0:T(8,128)(2,1)S(1)} collective-permute-done((bf16[2,1,144,768]{3,2,1,0:T(8,128)(2,1)}, bf16[2,1,144,768]{3,2,1,0:T(8,128)(2,1)S(1)}, u32[]{:S(2)}, u32[]{:S(2)}) %collective-permute-start) | collective-permute-done | bytes 442400 | tf_op jit(solution)/shard_map/ppermute | solution.py:266
  15.8 0.0 copy-done.7
  15.8 0.1 select_bitcast_fusion
  15.8 2.6 %collective-permute-start.4 = (bf16[1,144,768]{2,1,0:T(8,128)(2,1)S(1)}, bf16[1,144,768]{2,1,0:T(8,128)(2,1)S(1)}, u32[]{:S(2)}, u32[]{:S(2)}) collective-permute-start(bf16[1,144,768]{2,1,0:T(8,128)(2,1)S(1)} %get-tuple-element.47), channel_id=1, source_target_pairs={{0,4},{4,8},{8,12},{1,5},{5,9},{9,13},{2,6},{6,10},{10,14},{3,7},{... | collective-permute-start | bytes 663560 | tf_op jit(solution)/shard_map/ppermute | solution.py:31
  18.4 1.9 %collective-permute-start.6 = (bf16[1,144,768]{2,1,0:T(8,128)(2,1)S(1)}, bf16[1,144,768]{2,1,0:T(8,128)(2,1)S(1)}, u32[]{:S(2)}, u32[]{:S(2)}) collective-permute-start(bf16[1,144,768]{2,1,0:T(8,128)(2,1)S(1)} %get-tuple-element.46), channel_id=1, source_target_pairs={{0,4},{4,8},{8,12},{1,5},{5,9},{9,13},{2,6},{6,10},{10,14},{3,7},{... | collective-permute-start | bytes 663560 | tf_op jit(solution)/shard_map/ppermute | solution.py:31
  21.0 1.9 %collective-permute-start.10 = (bf16[24,512]{1,0:T(8,128)(2,1)S(1)}, bf16[24,512]{1,0:T(8,128)(2,1)S(1)}, u32[]{:S(2)}, u32[]{:S(2)}) collective-permute-start(bf16[24,512]{1,0:T(8,128)(2,1)S(1)} %get-tuple-element.45), channel_id=1, source_target_pairs={{0,4},{4,8},{8,12},{1,5},{5,9},{9,13},{2,6},{6,10},{10,14},{3,7},{... | collective-permute-start | bytes 73736 | tf_op jit(solution)/shard_map/ppermute | solution.py:31
  22.9 0.0 copy-done.1
  23.0 0.0 copy-done.6
  23.0 0.7 %middle.2 = (f32[6,128,576]{2,1,0:T(8,128)S(1)}, f32[6,576]{1,0:T(8,128)S(1)}, f32[6,576]{1,0:T(8,128)S(1)}) custom-call(s32[4,4]{1,0:T(4,128)S(1)} %copy-done.5, s32[4,4]{1,0:T(4,128)S(1)} %copy-done.6, bf16[4,1,144,768]{3,2,1,0:T(8,128)(2,1)S(1)} %copy-done.1, bf16[2,1,144,768]{3,2,1,0:T(8,128)(2,1)S(1)} %collective-permute-done.refs_0_, ...), custom_call_target="tpu_custom_call" | custom-call | flops 254803968 | bytes 3124352 | tf_op jit(solution)/shard_map/middle/pallas_call | solution.py:277
  23.7 0.0 collective-permute-done.5.refs_0_
  23.7 0.7 %middle.3 = (f32[6,128,576]{2,1,0:T(8,128)S(1)}, f32[6,576]{1,0:T(8,128)S(1)}, f32[6,576]{1,0:T(8,128)S(1)}) custom-call(s32[4,4]{1,0:T(4,128)S(1)} %copy-done.5, s32[4,4]{1,0:T(4,128)S(1)} %copy-done.6, bf16[4,1,144,768]{3,2,1,0:T(8,128)(2,1)S(1)} %copy-done.1, bf16[2,1,144,768]{3,2,1,0:T(8,128)(2,1)S(1)} %collective-permute-done.5.refs_0_, ...), custom_call_target="tpu_custom_call" | custom-call | flops 254803968 | bytes 3124352 | tf_op jit(solution)/shard_map/middle/pallas_call | solution.py:277
  24.5 5.5 %collective-permute-done.4.refs_0_ = bf16[1,144,768]{2,1,0:T(8,128)(2,1)S(1)} collective-permute-done((bf16[1,144,768]{2,1,0:T(8,128)(2,1)S(1)}, bf16[1,144,768]{2,1,0:T(8,128)(2,1)S(1)}, u32[]{:S(2)}, u32[]{:S(2)}) %collective-permute-start.4) | collective-permute-done | bytes 221216 | tf_op jit(solution)/shard_map/ppermute | solution.py:31
  30.0 0.8 %score.1 = (f32[6,128,576]{2,1,0:T(8,128)S(1)}, bf16[6,144,576]{2,1,0:T(8,128)(2,1)S(1)}) custom-call(s32[4,4]{1,0:T(4,128)S(1)} %copy-done.5, s32[4,4]{1,0:T(4,128)S(1)} %copy-done.6, bf16[4,1,144,768]{3,2,1,0:T(8,128)(2,1)S(1)} %copy-done.1, bf16[1,144,768]{2,1,0:T(8,128)(2,1)S(1)} %collective-permute-done.4.refs_0_, ...), custom_call_target="tpu_custom_call" | custom-call | flops 127401984 | bytes 2903168 | tf_op jit(solution)/shard_map/score/pallas_call | solution.py:277
  30.8 0.0 copy-start.3
  30.9 3.9 %collective-permute-done.6.refs_0_ = bf16[1,144,768]{2,1,0:T(8,128)(2,1)S(1)} collective-permute-done((bf16[1,144,768]{2,1,0:T(8,128)(2,1)S(1)}, bf16[1,144,768]{2,1,0:T(8,128)(2,1)S(1)}, u32[]{:S(2)}, u32[]{:S(2)}) %collective-permute-start.6) | collective-permute-done | bytes 221216 | tf_op jit(solution)/shard_map/ppermute | solution.py:31
  34.7 0.5 %average.1 = (f32[6,128,576]{2,1,0:T(8,128)S(1)}, f32[1,576]{1,0:T(1,128)S(1)}) custom-call(f32[6,128,576]{2,1,0:T(8,128)S(1)} %get-tuple-element.40.acc_ref, bf16[6,144,576]{2,1,0:T(8,128)(2,1)S(1)} %get-tuple-element.41.w_ref, bf16[1,144,768]{2,1,0:T(8,128)(2,1)S(1)} %collective-permute-done.6.refs_0_), custom_call_target="tpu_custom_call" | custom-call | flops 127401984 | bytes 2985984 | tf_op jit(solution)/shard_map/average/pallas_call | solution.py:277
  35.3 0.1 collective-permute-start.7
  35.4 1.6 %collective-permute-start.8 = (f32[1,576]{1,0:T(1,128)S(1)}, f32[1,576]{1,0:T(1,128)S(1)}, u32[]{:S(2)}, u32[]{:S(2)}) collective-permute-start(f32[1,576]{1,0:T(1,128)S(1)} %get-tuple-element.43.refs_0_), channel_id=1, source_target_pairs={{0,2},{1,3},{2,0},{3,1},{4,6},{5,7},{6,4},{7,5},{8,10},{9,11},{10,... | collective-permute-start | bytes 6920 | tf_op jit(solution)/shard_map/ppermute | solution.py:40
  36.9 0.3 collective-permute-start.9
  37.2 0.0 collective-permute-done.10.tail_ref
  37.2 0.0 copy-done.3
  37.2 1.4 %decode.1 = bf16[1,36,512]{2,1,0:T(8,128)(2,1)} custom-call(s32[1]{0:T(128)S(6)} %copy.11.fade_ref, bf16[36,512]{1,0:T(8,128)(2,1)S(1)} %get-tuple-element.44.hidden_ref, bf16[24,512]{1,0:T(8,128)(2,1)S(1)} %collective-permute-done.10.tail_ref, bf16[3,512,512]{2,1,0:T(8,128)(2,1)S(1)} %copy-done.3), custom_call_target="tpu_custom_call" | custom-call | flops 56623104 | bytes 1634308 | tf_op jit(solution)/shard_map/decode/pallas_call | solution.py:277
  38.7 0.6 %turn.1.average_ref = f32[4,144,768]{2,1,0:T(8,128)S(1)} custom-call(f32[6,128,576]{2,1,0:T(8,128)S(1)} %get-tuple-element.42.in_ref), custom_call_target="tpu_custom_call" | custom-call | flops 442368 | bytes 1769472 | tf_op jit(solution)/shard_map/turn/pallas_call | solution.py:277
  39.2 0.0 collective-permute-done.7.refs_1_
  39.3 0.0 collective-permute-done.8.refs_2_
  39.3 0.7 %collective-permute-done.9.refs_3_ = f32[1,576]{1,0:T(1,128)S(1)} collective-permute-done((f32[1,576]{1,0:T(1,128)S(1)}, f32[1,576]{1,0:T(1,128)S(1)}, u32[]{:S(2)}, u32[]{:S(2)}) %collective-permute-start.9) | collective-permute-done | bytes 2336 | tf_op jit(solution)/shard_map/ppermute | solution.py:40
  39.9 1.1 %scale.1 = bf16[4,1,144,768]{3,2,1,0:T(8,128)(2,1)} custom-call(f32[4,144,768]{2,1,0:T(8,128)S(1)} %turn.1.average_ref, f32[1,576]{1,0:T(1,128)S(1)} %get-tuple-element.43.refs_0_, f32[1,576]{1,0:T(1,128)S(1)} %collective-permute-done.7.refs_1_, f32[1,576]{1,0:T(1,128)S(1)} %collective-permute-done.8.refs_2_, f32[1,576]{1,0:T(1,128)S(1)} %collective-permute-done.9.refs_3_), custom_call_target="tpu_custom_call" | custom-call | flops 442368 | bytes 1778688 | tf_op jit(solution)/shard_map/scale/pallas_call | solution.py:277
  (1 shorter events, 0.0 us)
Async XLA Ops:
  0.6 15.2 %copy-start.7 = (bf16[2,1,144,768]{3,2,1,0:T(8,128)(2,1)S(1)}, bf16[2,1,144,768]{3,2,1,0:T(8,128)(2,1)}, u32[]{:S(2)}) copy-start(bf16[2,1,144,768]{3,2,1,0:T(8,128)(2,1)} %param.11) | copy-start | bytes 1327108
  0.6 15.1 %collective-permute-start = (bf16[2,1,144,768]{3,2,1,0:T(8,128)(2,1)}, bf16[2,1,144,768]{3,2,1,0:T(8,128)(2,1)S(1)}, u32[]{:S(2)}, u32[]{:S(2)}) collective-permute-start(bf16[2,1,144,768]{3,2,1,0:T(8,128)(2,1)} %param.11), channel_id=1, source_target_pairs={{0,8},{8,12},{1,9},{9,13},{2,10},{10,14},{3,11},{11,15},{16,24},{2... | collective-permute-start | bytes 1327112 | tf_op jit(solution)/shard_map/ppermute | solution.py:266
  6.6 8.5 %collective-permute-start.1 = (bf16[36,512]{1,0:T(8,128)(2,1)}, bf16[36,512]{1,0:T(8,128)(2,1)S(1)}, u32[]{:S(2)}, u32[]{:S(2)}) collective-permute-start(bf16[36,512]{1,0:T(8,128)(2,1)} %get-tuple-element.26), channel_id=1, source_target_pairs={{0,1},{1,0},{2,3},{3,2},{4,5},{5,4},{6,7},{7,6},{8,9},{9,8},{10,11... | collective-permute-start | bytes 110600 | tf_op jit(solution)/shard_map/ppermute | solution.py:40
  6.6 8.5 %collective-permute-start.2 = (bf16[36,512]{1,0:T(8,128)(2,1)}, bf16[36,512]{1,0:T(8,128)(2,1)S(1)}, u32[]{:S(2)}, u32[]{:S(2)}) collective-permute-start(bf16[36,512]{1,0:T(8,128)(2,1)} %get-tuple-element.27), channel_id=1, source_target_pairs={{0,2},{1,3},{2,0},{3,1},{4,6},{5,7},{6,4},{7,5},{8,10},{9,11},{10,... | collective-permute-start | bytes 110600 | tf_op jit(solution)/shard_map/ppermute | solution.py:40
  8.2 6.9 %collective-permute-start.3 = (bf16[36,512]{1,0:T(8,128)(2,1)}, bf16[36,512]{1,0:T(8,128)(2,1)S(1)}, u32[]{:S(2)}, u32[]{:S(2)}) collective-permute-start(bf16[36,512]{1,0:T(8,128)(2,1)} %get-tuple-element.28), channel_id=1, source_target_pairs={{0,3},{1,2},{2,1},{3,0},{4,7},{5,6},{6,5},{7,4},{8,11},{9,10},{10,... | collective-permute-start | bytes 110600 | tf_op jit(solution)/shard_map/ppermute | solution.py:40
  8.5 15.2 %collective-permute-start.5 = (bf16[2,1,144,768]{3,2,1,0:T(8,128)(2,1)}, bf16[2,1,144,768]{3,2,1,0:T(8,128)(2,1)S(1)}, u32[]{:S(2)}, u32[]{:S(2)}) collective-permute-start(bf16[2,1,144,768]{3,2,1,0:T(8,128)(2,1)} %param.11), channel_id=1, source_target_pairs={{4,12},{5,13},{6,14},{7,15},{20,28},{21,29},{22,30},{23,31}} | collective-permute-start | bytes 1327112 | tf_op jit(solution)/shard_map/ppermute | solution.py:266
  9.2 1.2 %copy-start = (bf16[4,1,144,768]{3,2,1,0:T(8,128)(2,1)S(1)}, bf16[4,1,144,768]{3,2,1,0:T(8,128)(2,1)}, u32[]{:S(2)}) copy-start(bf16[4,1,144,768]{3,2,1,0:T(8,128)(2,1)} %q_ref.7) | copy-start | bytes 2654212
  10.4 1.5 %copy-start.2 = (bf16[4,2,1,144,768]{4,3,2,1,0:T(8,128)(2,1)S(1)}, bf16[4,2,1,144,768]{4,3,2,1,0:T(8,128)(2,1)}, u32[]{:S(2)}) copy-start(bf16[4,2,1,144,768]{4,3,2,1,0:T(8,128)(2,1)} %kv_ref.1) | copy-start | bytes 5308420
  11.8 0.7 %copy-start.5 = (s32[4,4]{1,0:T(4,128)S(1)}, s32[4,4]{1,0:T(4,128)}, u32[]{:S(2)}) copy-start(s32[4,4]{1,0:T(4,128)} %step_ref.7) | copy-start | bytes 196
  12.5 2.6 %copy-start.4 = (bf16[36,512]{1,0:T(8,128)(2,1)S(1)}, bf16[36,512]{1,0:T(8,128)(2,1)}, u32[]{:S(2)}) copy-start(bf16[36,512]{1,0:T(8,128)(2,1)} %get-tuple-element.25.refs_0_) | copy-start | bytes 110596
  12.5 10.4 %copy-start.1 = (bf16[4,1,144,768]{3,2,1,0:T(8,128)(2,1)S(1)}, bf16[4,1,144,768]{3,2,1,0:T(8,128)(2,1)}, u32[]{:S(2)}) copy-start(bf16[4,1,144,768]{3,2,1,0:T(8,128)(2,1)} %q_ref.7) | copy-start | bytes 2654212
  12.5 10.4 %copy-start.6 = (s32[4,4]{1,0:T(4,128)S(1)}, s32[4,4]{1,0:T(4,128)}, u32[]{:S(2)}) copy-start(s32[4,4]{1,0:T(4,128)} %mask_ref.5) | copy-start | bytes 196
  15.8 14.2 %collective-permute-start.4 = (bf16[1,144,768]{2,1,0:T(8,128)(2,1)S(1)}, bf16[1,144,768]{2,1,0:T(8,128)(2,1)S(1)}, u32[]{:S(2)}, u32[]{:S(2)}) collective-permute-start(bf16[1,144,768]{2,1,0:T(8,128)(2,1)S(1)} %get-tuple-element.47), channel_id=1, source_target_pairs={{0,4},{4,8},{8,12},{1,5},{5,9},{9,13},{2,6},{6,10},{10,14},{3,7},{... | collective-permute-start | bytes 663560 | tf_op jit(solution)/shard_map/ppermute | solution.py:31
  18.4 16.3 %collective-permute-start.6 = (bf16[1,144,768]{2,1,0:T(8,128)(2,1)S(1)}, bf16[1,144,768]{2,1,0:T(8,128)(2,1)S(1)}, u32[]{:S(2)}, u32[]{:S(2)}) collective-permute-start(bf16[1,144,768]{2,1,0:T(8,128)(2,1)S(1)} %get-tuple-element.46), channel_id=1, source_target_pairs={{0,4},{4,8},{8,12},{1,5},{5,9},{9,13},{2,6},{6,10},{10,14},{3,7},{... | collective-permute-start | bytes 663560 | tf_op jit(solution)/shard_map/ppermute | solution.py:31
  21.0 16.2 %collective-permute-start.10 = (bf16[24,512]{1,0:T(8,128)(2,1)S(1)}, bf16[24,512]{1,0:T(8,128)(2,1)S(1)}, u32[]{:S(2)}, u32[]{:S(2)}) collective-permute-start(bf16[24,512]{1,0:T(8,128)(2,1)S(1)} %get-tuple-element.45), channel_id=1, source_target_pairs={{0,4},{4,8},{8,12},{1,5},{5,9},{9,13},{2,6},{6,10},{10,14},{3,7},{... | collective-permute-start | bytes 73736 | tf_op jit(solution)/shard_map/ppermute | solution.py:31
  30.8 6.4 %copy-start.3 = (bf16[3,512,512]{2,1,0:T(8,128)(2,1)S(1)}, bf16[3,512,512]{2,1,0:T(8,128)(2,1)}, u32[]{:S(2)}) copy-start(bf16[3,512,512]{2,1,0:T(8,128)(2,1)} %conv_ref.1) | copy-start | bytes 4718596
  35.3 3.9 %collective-permute-start.7 = (f32[1,576]{1,0:T(1,128)S(1)}, f32[1,576]{1,0:T(1,128)S(1)}, u32[]{:S(2)}, u32[]{:S(2)}) collective-permute-start(f32[1,576]{1,0:T(1,128)S(1)} %get-tuple-element.43.refs_0_), channel_id=1, source_target_pairs={{0,1},{1,0},{2,3},{3,2},{4,5},{5,4},{6,7},{7,6},{8,9},{9,8},{10,11... | collective-permute-start | bytes 6920 | tf_op jit(solution)/shard_map/ppermute | solution.py:40
  35.4 3.9 %collective-permute-start.8 = (f32[1,576]{1,0:T(1,128)S(1)}, f32[1,576]{1,0:T(1,128)S(1)}, u32[]{:S(2)}, u32[]{:S(2)}) collective-permute-start(f32[1,576]{1,0:T(1,128)S(1)} %get-tuple-element.43.refs_0_), channel_id=1, source_target_pairs={{0,2},{1,3},{2,0},{3,1},{4,6},{5,7},{6,4},{7,5},{8,10},{9,11},{10,... | collective-permute-start | bytes 6920 | tf_op jit(solution)/shard_map/ppermute | solution.py:40
  36.9 3.0 %collective-permute-start.9 = (f32[1,576]{1,0:T(1,128)S(1)}, f32[1,576]{1,0:T(1,128)S(1)}, u32[]{:S(2)}, u32[]{:S(2)}) collective-permute-start(f32[1,576]{1,0:T(1,128)S(1)} %get-tuple-element.43.refs_0_), channel_id=1, source_target_pairs={{0,3},{1,2},{2,1},{3,0},{4,7},{5,6},{6,5},{7,4},{8,11},{9,10},{10,... | collective-permute-start | bytes 6920 | tf_op jit(solution)/shard_map/ppermute | solution.py:40

commit v2 on v1

--- a/solution.py
+++ b/solution.py
@@ -212,50 +212,57 @@
             acc_ref[head] = acc_in[head] * (1.0 / total_in[head : head + 1])
 
 
-def average_kernel(plans, acc_ref, w_ref, *refs):
-    value_refs, (average_ref, square_ref) = refs[:-2], refs[-2:]
-    position = lax.axis_index("span")
-
-    def finish(value_ref):
-        squares = jnp.zeros(square_ref.shape, jnp.float32)
-        for head in range(acc_ref.shape[0]):
-            average = acc_ref[head]
-            if value_ref is not None:
-                values = half(value_ref, 1, slice(head * HD, (head + 1) * HD))
-                average = average + tn_dot(values, w_ref[head])
-            average_ref[head] = average
-            squares = squares + jnp.sum(average * average, axis=0, keepdims=True)
-        square_ref[...] = squares
-
-    rest = True
-    for plan, value_ref in zip(plans, value_refs):
-        here = functools.reduce(jnp.logical_or, [position == place for place in plan])
-        rest = jnp.logical_and(rest, jnp.logical_not(here))
-        pl.when(here)(functools.partial(finish, value_ref))
-    pl.when(rest)(functools.partial(finish, None))
-
-
-def turn_kernel(in_ref, out_ref):
-    heads = in_ref.shape[0]
+def average_head(head, acc_ref, w_ref, value_ref, first):
+    if value_ref.shape[-1] == acc_ref.shape[0] * HD:
+        first = 0
+    cut = slice((head - first) * HD, (head - first + 1) * HD)
+    return acc_ref[head] + tn_dot(half(value_ref, 1, cut), w_ref[head])
+
+
+def average_kernel(begin, end, acc_ref, w_ref, value_ref, average_ref, square_ref):
+    squares = jnp.zeros(square_ref.shape, jnp.float32)
+    for head in range(begin, end):
+        average = average_head(head, acc_ref, w_ref, value_ref, begin)
+        squares = squares + jnp.sum(average * average, axis=0, keepdims=True)
+        average_ref[:, :, (head - begin) * HD : (head - begin + 1) * HD] = average.T.reshape(
+            average_ref.shape[:2] + (HD,)
+        )
+    square_ref[...] = squares
+
+
+def rest_kernel(begin, end, acc_ref, w_ref, value_ref, before_ref, average_ref, square_ref):
+    squares = before_ref[...]
+    for head in range(begin, end):
+        average = average_head(head, acc_ref, w_ref, value_ref, begin)
+        squares = squares + jnp.sum(average * average, axis=0, keepdims=True)
+        average_ref[head - begin] = average
+    square_ref[...] = squares
+
+
+def turn_kernel(in_ref, square_in, out_ref, square_ref):
     steps, rows, _ = out_ref.shape
-    for head in range(heads):
+    for head in range(in_ref.shape[0]):
         out_ref[:, :, head * HD : (head + 1) * HD] = in_ref[head].T.reshape(steps, rows, HD)
-
-
-def scale_kernel(width, average_ref, *refs):
+    square_ref[...] = square_in[...]
+
+
+def scale_kernel(width, front_ref, back_ref, *refs):
     part_refs, (out_hbm, out_ref, sem) = refs[:-3], refs[-3:]
     total = part_refs[0][...]
     for ref in part_refs[1:]:
         total = total + ref[...]
     inverse = lax.rsqrt(total / width + 1e-06)
-    steps, rows, columns = average_ref.shape
+    steps, rows, columns = out_ref.shape
     spread = jnp.broadcast_to(inverse, (HD, steps * rows)).T
     copies = []
     for step in range(steps):
         factor = spread[step * rows : (step + 1) * rows]
-        for first in range(0, columns, HD):
-            cut = slice(first, first + HD)
-            out_ref[step, :, cut] = (average_ref[step, :, cut] * factor).astype(jnp.bfloat16)
+        place = 0
+        for ref in (front_ref, back_ref):
+            for first in range(0, ref.shape[2], HD):
+                average = ref[step, :, first : first + HD]
+                out_ref[step, :, place : place + HD] = (average * factor).astype(jnp.bfloat16)
+                place += HD
         copies.append(pltpu.make_async_copy(out_ref.at[step], out_hbm.at[step, 0], sem.at[step]))
         copies[-1].start()
     for copy in copies:
@@ -416,6 +423,7 @@
 ):
     steps, _, rows, columns = query.shape
     heads = columns // HD
+    middle = (heads + 1) // 2 * HD
     row_count = steps * rows
     span = lax.axis_size("span")
     axes = ("mp", "seq")
@@ -443,16 +451,17 @@
         near = after(near, carry[0], hidden)
         forwards = lax.axis_index("span") == 2
         passed = [jnp.where(forwards, near[which], clean_kv[which]) for which in range(2)]
+        passed = [passed[0], passed[1][:, :, :middle], passed[1][:, :, middle:]]
         passed = [hop(block, "span", 1) for block in passed]
         early = [(near, {2: 0, 3: 2}), (direct, {3: 1})]
-        keys, values = passed
+        keys, *values = passed
         last_plan = {1: 0, 2: 1, 3: 0}
     else:
         ring = [near]
         for _ in range(2, span):
             ring.append(hop(ring[-1], "span", 1))
         early = [(block, delivered(span, back + 1)) for back, block in enumerate(ring[:-1])]
-        keys = values = ring[-1]
+        keys, values = ring[-1], ring[-1:] * 2
         last_plan = delivered(span, span - 1)
     for block, plan in early:
         carry = plain_call(
@@ -471,28 +480,37 @@
         (step_index, causal_mask, query, keys, *carry),
         [SMEM_SPEC] * 2,
     )
+    square_shape = jax.ShapeDtypeStruct((1, row_count), jnp.float32)
+    front, squares = plain_call(
+        functools.partial(average_kernel, 0, middle // HD),
+        "average",
+        [jax.ShapeDtypeStruct((steps, rows, middle), jnp.float32), square_shape],
+        pair_flops // 4,
+        (acc, weights, values[0]),
+    )
     averaged, squares = plain_call(
-        functools.partial(average_kernel, [last_plan]),
-        "average",
-        [acc_shape, jax.ShapeDtypeStruct((1, row_count), jnp.float32)],
-        pair_flops // 2,
-        (acc, weights, values),
-    )
-    decoded = decode(after(hidden, squares), tail, conv_w, fade_count)
-    others = [swap(squares, axes, offset) for offset in range(1, lax.axis_size(axes))]
-    turned = plain_call(
+        functools.partial(rest_kernel, middle // HD, heads),
+        "rest",
+        [jax.ShapeDtypeStruct((heads - middle // HD, HD, row_count), jnp.float32), square_shape],
+        pair_flops // 4,
+        (acc, weights, values[1], squares),
+    )
+    others = [swap(squares, axes, offset) for offset in range(2, lax.axis_size(axes))]
+    back, squares = plain_call(
         turn_kernel,
         "turn",
-        [jax.ShapeDtypeStruct((steps, rows, columns), jnp.float32)],
+        [jax.ShapeDtypeStruct((steps, rows, columns - middle), jnp.float32), square_shape],
         row_count * columns,
-        (averaged,),
-    )[0]
+        (averaged, squares),
+    )
+    others.append(swap(squares, axes, 1))
+    decoded = decode(after(hidden, back), tail, conv_w, fade_count)
     attended = plain_call(
         functools.partial(scale_kernel, columns * lax.axis_size(axes)),
         "scale",
         jax.ShapeDtypeStruct(query.shape, jnp.bfloat16),
         row_count * columns,
-        (turned, squares, *others),
+        (front, back, squares, *others),
         out_specs=HBM_SPEC,
         scratch=[
             pltpu.VMEM((steps, rows, columns), jnp.bfloat16),

time: 41.7 us -> 41.1 us (0.986)
  waiting for transfers between devices: 10.6 us -> 8.03 us
  starting transfers between devices: 14.6 us -> 16.8 us
    ppermute x3 -> x4, waiting for transfers between devices: 9.43 us -> 6.97 us  [hop(): lax.ppermute(value, axis, [(source, source + steps) for source in range(c...]
    ppermute x3 -> x4, starting transfers between devices: 6.43 us -> 8.35 us  [hop(): lax.ppermute(value, axis, [(source, source + steps) for source in range(c...]
    pallas_call x10 -> x11, Pallas kernels: 10.9 us -> 11 us  [plain_call(): pl.pallas_call(kernel, in_specs=list(in_specs) + [VMEM_SPEC] * (len(opera...]
  transfers between devices with their start and end apart: 11 -> 12, of which waited for: 4 -> 5; matrix products, arithmetic and copies ran while one was open for 0% -> 0% of each run, Pallas kernels for 24% -> 24%
where the time goes in v2:
time: 41.1 us; the launch traced here: 40.8 us
  starting transfers between devices  16.8 us (41%)
  Pallas kernels  11 us (27%)
  waiting for transfers between devices  8.03 us (20%)
  local copies, waits for them, and re-layouts  3.37 us (8%)
  between operations  1.48 us (4%)
    pallas_call x11, Pallas kernels, plain_call(): pl.pallas_call(kernel, in_specs=list(in_specs) + [VMEM_SPEC] * (len(opera...  11 us
    ppermute x4, starting transfers between devices, hop(): lax.ppermute(value, axis, [(source, source + steps) for source in range(c...  8.35 us
    ppermute x4, waiting for transfers between devices, hop(): lax.ppermute(value, axis, [(source, source + steps) for source in range(c...  6.97 us
    ppermute x2, starting transfers between devices, send(): return lax.ppermute(value, 'span', pairs)  4.3 us
    ppermute x6, starting transfers between devices, swap(): return lax.ppermute(value, axes, pairs)  4.2 us
    unnamed x16, local copies, waits for them, and re-layouts  3.34 us
  transfers between devices with their start and end apart: 12, of which 5 were waited for; matrix products, arithmetic and copies ran while one was open for 0% of the time, Pallas kernels for 24%

profile of v2, /device:TPU:20, one launch (start us, length us, event | category | flops | bytes accessed | tf_op | source)
XLA Modules:
  0.0 40.8 jit_solution(5206165960898124879)
XLA Ops:
  0.6 0.0 copy-start.7
  0.6 3.6 %collective-permute-start = (bf16[2,1,144,768]{3,2,1,0:T(8,128)(2,1)}, bf16[2,1,144,768]{3,2,1,0:T(8,128)(2,1)S(1)}, u32[]{:S(2)}, u32[]{:S(2)}) collective-permute-start(bf16[2,1,144,768]{3,2,1,0:T(8,128)(2,1)} %param.11), channel_id=1, source_target_pairs={{0,8},{8,12},{1,9},{9,13},{2,10},{10,14},{3,11},{11,15},{16,24},{2... | collective-permute-start | bytes 1327112 | tf_op jit(solution)/shard_map/ppermute | solution.py:273
  4.3 2.3 %project.1 = (bf16[36,512]{1,0:T(8,128)(2,1)}, bf16[36,512]{1,0:T(8,128)(2,1)}, bf16[36,512]{1,0:T(8,128)(2,1)}, bf16[36,512]{1,0:T(8,128)(2,1)}) custom-call(bf16[1,144,768]{2,1,0:T(8,128)(2,1)} %x_hbm.1, bf16[768,512]{1,0:T(8,128)(2,1)} %w_hbm.1), custom_call_target="tpu_custom_call" | custom-call | flops 113246208 | bytes 1007616 | tf_op jit(solution)/shard_map/project/pallas_call | solution.py:284
  6.6 0.1 collective-permute-start.1
  6.6 1.6 %collective-permute-start.2 = (bf16[36,512]{1,0:T(8,128)(2,1)}, bf16[36,512]{1,0:T(8,128)(2,1)S(1)}, u32[]{:S(2)}, u32[]{:S(2)}) collective-permute-start(bf16[36,512]{1,0:T(8,128)(2,1)} %get-tuple-element.31), channel_id=1, source_target_pairs={{0,2},{1,3},{2,0},{3,1},{4,6},{5,7},{6,4},{7,5},{8,10},{9,11},{10,... | collective-permute-start | bytes 110600 | tf_op jit(solution)/shard_map/ppermute | solution.py:40
  8.2 0.3 collective-permute-start.3
  8.5 0.7 %collective-permute-start.5 = (bf16[2,1,144,768]{3,2,1,0:T(8,128)(2,1)}, bf16[2,1,144,768]{3,2,1,0:T(8,128)(2,1)S(1)}, u32[]{:S(2)}, u32[]{:S(2)}) collective-permute-start(bf16[2,1,144,768]{3,2,1,0:T(8,128)(2,1)} %param.11), channel_id=1, source_target_pairs={{4,12},{5,13},{6,14},{7,15},{20,28},{21,29},{22,30},{23,31}} | collective-permute-start | bytes 1327112 | tf_op jit(solution)/shard_map/ppermute | solution.py:273
  9.2 0.0 copy-start
  9.2 1.2 %copy-done = bf16[4,1,144,768]{3,2,1,0:T(8,128)(2,1)S(1)} copy-done((bf16[4,1,144,768]{3,2,1,0:T(8,128)(2,1)S(1)}, bf16[4,1,144,768]{3,2,1,0:T(8,128)(2,1)}, u32[]{:S(2)}) %copy-start) | copy-done | bytes 884760
  10.4 0.0 copy-start.2
  10.4 1.5 %copy-done.2 = bf16[4,2,1,144,768]{4,3,2,1,0:T(8,128)(2,1)S(1)} copy-done((bf16[4,2,1,144,768]{4,3,2,1,0:T(8,128)(2,1)S(1)}, bf16[4,2,1,144,768]{4,3,2,1,0:T(8,128)(2,1)}, u32[]{:S(2)}) %copy-start.2) | copy-done | bytes 1769496
  11.8 0.0 copy-start.5
  11.8 0.7 %copy-done.5 = s32[4,4]{1,0:T(4,128)S(1)} copy-done((s32[4,4]{1,0:T(4,128)S(1)}, s32[4,4]{1,0:T(4,128)}, u32[]{:S(2)}) %copy-start.5) | copy-done | bytes 88
  12.5 2.5 %own.1 = (f32[6,128,576]{2,1,0:T(8,128)S(1)}, f32[6,576]{1,0:T(8,128)S(1)}, f32[6,576]{1,0:T(8,128)S(1)}) custom-call(s32[4,4]{1,0:T(4,128)S(1)} %copy-done.5, bf16[4,1,144,768]{3,2,1,0:T(8,128)(2,1)S(1)} %copy-done, bf16[4,2,1,144,768]{4,3,2,1,0:T(8,128)(2,1)S(1)} %copy-done.2), custom_call_target="tpu_custom_call" | custom-call | flops 254803968 | bytes 2654272 | tf_op jit(solution)/shard_map/own/pallas_call | solution.py:284
  15.1 0.0 collective-permute-done.1.refs_1_
  15.1 0.0 collective-permute-done.2.refs_2_
  15.1 0.0 collective-permute-done.3.refs_3_
  15.1 0.0 copy-done.4
  15.1 0.1 gather.1
  15.3 0.5 %collective-permute-done.refs_0_ = bf16[2,1,144,768]{3,2,1,0:T(8,128)(2,1)S(1)} collective-permute-done((bf16[2,1,144,768]{3,2,1,0:T(8,128)(2,1)}, bf16[2,1,144,768]{3,2,1,0:T(8,128)(2,1)S(1)}, u32[]{:S(2)}, u32[]{:S(2)}) %collective-permute-start) | collective-permute-done | bytes 442400 | tf_op jit(solution)/shard_map/ppermute | solution.py:273
  15.8 0.0 copy-done.7
  15.8 0.1 select_bitcast_fusion
  15.8 2.6 %collective-permute-start.4 = (bf16[1,144,768]{2,1,0:T(8,128)(2,1)S(1)}, bf16[1,144,768]{2,1,0:T(8,128)(2,1)S(1)}, u32[]{:S(2)}, u32[]{:S(2)}) collective-permute-start(bf16[1,144,768]{2,1,0:T(8,128)(2,1)S(1)} %get-tuple-element.55), channel_id=1, source_target_pairs={{0,4},{4,8},{8,12},{1,5},{5,9},{9,13},{2,6},{6,10},{10,14},{3,7},{... | collective-permute-start | bytes 663560 | tf_op jit(solution)/shard_map/ppermute | solution.py:31
  18.5 1.9 %collective-permute-start.6 = (bf16[1,144,384]{2,1,0:T(8,128)(2,1)S(1)}, bf16[1,144,384]{2,1,0:T(8,128)(2,1)S(1)}, u32[]{:S(2)}, u32[]{:S(2)}) collective-permute-start(bf16[1,144,384]{2,1,0:T(8,128)(2,1)S(1)} %get-tuple-element.57), channel_id=1, source_target_pairs={{0,4},{4,8},{8,12},{1,5},{5,9},{9,13},{2,6},{6,10},{10,14},{3,7},{... | collective-permute-start | bytes 331784 | tf_op jit(solution)/shard_map/ppermute | solution.py:31
  20.4 1.9 %collective-permute-start.7 = (bf16[1,144,384]{2,1,0:T(8,128)(2,1)S(1)}, bf16[1,144,384]{2,1,0:T(8,128)(2,1)S(1)}, u32[]{:S(2)}, u32[]{:S(2)}) collective-permute-start(bf16[1,144,384]{2,1,0:T(8,128)(2,1)S(1)} %get-tuple-element.56), channel_id=1, source_target_pairs={{0,4},{4,8},{8,12},{1,5},{5,9},{9,13},{2,6},{6,10},{10,14},{3,7},{... | collective-permute-start | bytes 331784 | tf_op jit(solution)/shard_map/ppermute | solution.py:31
  23.0 1.9 %collective-permute-start.11 = (bf16[24,512]{1,0:T(8,128)(2,1)S(1)}, bf16[24,512]{1,0:T(8,128)(2,1)S(1)}, u32[]{:S(2)}, u32[]{:S(2)}) collective-permute-start(bf16[24,512]{1,0:T(8,128)(2,1)S(1)} %get-tuple-element.53), channel_id=1, source_target_pairs={{0,4},{4,8},{8,12},{1,5},{5,9},{9,13},{2,6},{6,10},{10,14},{3,7},{... | collective-permute-start | bytes 73736 | tf_op jit(solution)/shard_map/ppermute | solution.py:31
  24.9 0.0 copy-done.1
  24.9 0.0 copy-done.6
  24.9 0.7 %middle.2 = (f32[6,128,576]{2,1,0:T(8,128)S(1)}, f32[6,576]{1,0:T(8,128)S(1)}, f32[6,576]{1,0:T(8,128)S(1)}) custom-call(s32[4,4]{1,0:T(4,128)S(1)} %copy-done.5, s32[4,4]{1,0:T(4,128)S(1)} %copy-done.6, bf16[4,1,144,768]{3,2,1,0:T(8,128)(2,1)S(1)} %copy-done.1, bf16[2,1,144,768]{3,2,1,0:T(8,128)(2,1)S(1)} %collective-permute-done.refs_0_, ...), custom_call_target="tpu_custom_call" | custom-call | flops 254803968 | bytes 3124352 | tf_op jit(solution)/shard_map/middle/pallas_call | solution.py:284
  25.7 0.0 collective-permute-done.5.refs_0_
  25.7 0.7 %middle.3 = (f32[6,128,576]{2,1,0:T(8,128)S(1)}, f32[6,576]{1,0:T(8,128)S(1)}, f32[6,576]{1,0:T(8,128)S(1)}) custom-call(s32[4,4]{1,0:T(4,128)S(1)} %copy-done.5, s32[4,4]{1,0:T(4,128)S(1)} %copy-done.6, bf16[4,1,144,768]{3,2,1,0:T(8,128)(2,1)S(1)} %copy-done.1, bf16[2,1,144,768]{3,2,1,0:T(8,128)(2,1)S(1)} %collective-permute-done.5.refs_0_, ...), custom_call_target="tpu_custom_call" | custom-call | flops 254803968 | bytes 3124352 | tf_op jit(solution)/shard_map/middle/pallas_call | solution.py:284
  26.4 3.6 %collective-permute-done.4.refs_0_ = bf16[1,144,768]{2,1,0:T(8,128)(2,1)S(1)} collective-permute-done((bf16[1,144,768]{2,1,0:T(8,128)(2,1)S(1)}, bf16[1,144,768]{2,1,0:T(8,128)(2,1)S(1)}, u32[]{:S(2)}, u32[]{:S(2)}) %collective-permute-start.4) | collective-permute-done | bytes 221216 | tf_op jit(solution)/shard_map/ppermute | solution.py:31
  30.0 0.8 %score.1 = (f32[6,128,576]{2,1,0:T(8,128)S(1)}, bf16[6,144,576]{2,1,0:T(8,128)(2,1)S(1)}) custom-call(s32[4,4]{1,0:T(4,128)S(1)} %copy-done.5, s32[4,4]{1,0:T(4,128)S(1)} %copy-done.6, bf16[4,1,144,768]{3,2,1,0:T(8,128)(2,1)S(1)} %copy-done.1, bf16[1,144,768]{2,1,0:T(8,128)(2,1)S(1)} %collective-permute-done.4.refs_0_, ...), custom_call_target="tpu_custom_call" | custom-call | flops 127401984 | bytes 2903168 | tf_op jit(solution)/shard_map/score/pallas_call | solution.py:284
  30.8 1.5 %collective-permute-done.6.value_ref = bf16[1,144,384]{2,1,0:T(8,128)(2,1)S(1)} collective-permute-done((bf16[1,144,384]{2,1,0:T(8,128)(2,1)S(1)}, bf16[1,144,384]{2,1,0:T(8,128)(2,1)S(1)}, u32[]{:S(2)}, u32[]{:S(2)}) %collective-permute-start.6) | collective-permute-done | bytes 110624 | tf_op jit(solution)/shard_map/ppermute | solution.py:31
  32.4 0.5 %average.1 = (f32[4,144,384]{2,1,0:T(8,128)S(1)}, f32[1,576]{1,0:T(1,128)S(1)}) custom-call(f32[6,128,576]{2,1,0:T(8,128)S(1)} %get-tuple-element.44.acc_ref, bf16[6,144,576]{2,1,0:T(8,128)(2,1)S(1)} %get-tuple-element.45.w_ref, bf16[1,144,384]{2,1,0:T(8,128)(2,1)S(1)} %collective-permute-done.6.value_ref), custom_call_target="tpu_custom_call" | custom-call | flops 63700992 | bytes 2875392 | tf_op jit(solution)/shard_map/average/pallas_call | solution.py:284
  32.9 1.9 %collective-permute-done.7.value_ref = bf16[1,144,384]{2,1,0:T(8,128)(2,1)S(1)} collective-permute-done((bf16[1,144,384]{2,1,0:T(8,128)(2,1)S(1)}, bf16[1,144,384]{2,1,0:T(8,128)(2,1)S(1)}, u32[]{:S(2)}, u32[]{:S(2)}) %collective-permute-start.7) | collective-permute-done | bytes 110624 | tf_op jit(solution)/shard_map/ppermute | solution.py:31
  34.7 0.4 rest.1
  35.1 1.6 %collective-permute-start.8 = (f32[1,576]{1,0:T(1,128)S(1)}, f32[1,576]{1,0:T(1,128)S(1)}, u32[]{:S(2)}, u32[]{:S(2)}) collective-permute-start(f32[1,576]{1,0:T(1,128)S(1)} %get-tuple-element.49.square_in), channel_id=1, source_target_pairs={{0,2},{1,3},{2,0},{3,1},{4,6},{5,7},{6,4},{7,5},{8,10},{9,11},{10,... | collective-permute-start | bytes 6920 | tf_op jit(solution)/shard_map/ppermute | solution.py:40
  36.7 0.0 collective-permute-start.9
  36.7 0.3 turn.1
  37.0 0.7 %collective-permute-start.10 = (f32[1,576]{1,0:T(1,128)S(1)}, f32[1,576]{1,0:T(1,128)S(1)}, u32[]{:S(2)}, u32[]{:S(2)}) collective-permute-start(f32[1,576]{1,0:T(1,128)S(1)} %get-tuple-element.51.refs_0_), channel_id=1, source_target_pairs={{0,1},{1,0},{2,3},{3,2},{4,5},{5,4},{6,7},{7,6},{8,9},{9,8},{10,11... | collective-permute-start | bytes 6920 | tf_op jit(solution)/shard_map/ppermute | solution.py:40
  37.7 0.0 collective-permute-done.11.tail_ref
  37.7 0.0 copy-done.3
  37.7 1.4 %decode.1 = bf16[1,36,512]{2,1,0:T(8,128)(2,1)} custom-call(s32[1]{0:T(128)S(6)} %copy.11.fade_ref, bf16[36,512]{1,0:T(8,128)(2,1)S(1)} %get-tuple-element.52.hidden_ref, bf16[24,512]{1,0:T(8,128)(2,1)S(1)} %collective-permute-done.11.tail_ref, bf16[3,512,512]{2,1,0:T(8,128)(2,1)S(1)} %copy-done.3), custom_call_target="tpu_custom_call" | custom-call | flops 56623104 | bytes 1634308 | tf_op jit(solution)/shard_map/decode/pallas_call | solution.py:284
  39.1 0.0 collective-permute-done.10.refs_3_
  39.1 0.0 collective-permute-done.8.refs_1_
  39.2 0.5 %collective-permute-done.9.refs_2_ = f32[1,576]{1,0:T(1,128)S(1)} collective-permute-done((f32[1,576]{1,0:T(1,128)S(1)}, f32[1,576]{1,0:T(1,128)S(1)}, u32[]{:S(2)}, u32[]{:S(2)}) %collective-permute-start.9) | collective-permute-done | bytes 2336 | tf_op jit(solution)/shard_map/ppermute | solution.py:40
  39.7 1.1 %scale.1 = bf16[4,1,144,768]{3,2,1,0:T(8,128)(2,1)} custom-call(f32[4,144,384]{2,1,0:T(8,128)S(1)} %get-tuple-element.46.front_ref, f32[4,144,384]{2,1,0:T(8,128)S(1)} %get-tuple-element.50.back_ref, f32[1,576]{1,0:T(1,128)S(1)} %get-tuple-element.51.refs_0_, f32[1,576]{1,0:T(1,128)S(1)} %collective-permute-done.8.refs_1_, ...), custom_call_target="tpu_custom_call" | custom-call | flops 442368 | bytes 1778688 | tf_op jit(solution)/shard_map/scale/pallas_call | solution.py:284
  (5 shorter events, 0.0 us)
Async XLA Ops:
  0.6 15.2 %copy-start.7 = (bf16[2,1,144,768]{3,2,1,0:T(8,128)(2,1)S(1)}, bf16[2,1,144,768]{3,2,1,0:T(8,128)(2,1)}, u32[]{:S(2)}) copy-start(bf16[2,1,144,768]{3,2,1,0:T(8,128)(2,1)} %param.11) | copy-start | bytes 1327108
  0.6 15.1 %collective-permute-start = (bf16[2,1,144,768]{3,2,1,0:T(8,128)(2,1)}, bf16[2,1,144,768]{3,2,1,0:T(8,128)(2,1)S(1)}, u32[]{:S(2)}, u32[]{:S(2)}) collective-permute-start(bf16[2,1,144,768]{3,2,1,0:T(8,128)(2,1)} %param.11), channel_id=1, source_target_pairs={{0,8},{8,12},{1,9},{9,13},{2,10},{10,14},{3,11},{11,15},{16,24},{2... | collective-permute-start | bytes 1327112 | tf_op jit(solution)/shard_map/ppermute | solution.py:273
  6.6 8.5 %collective-permute-start.1 = (bf16[36,512]{1,0:T(8,128)(2,1)}, bf16[36,512]{1,0:T(8,128)(2,1)S(1)}, u32[]{:S(2)}, u32[]{:S(2)}) collective-permute-start(bf16[36,512]{1,0:T(8,128)(2,1)} %get-tuple-element.30), channel_id=1, source_target_pairs={{0,1},{1,0},{2,3},{3,2},{4,5},{5,4},{6,7},{7,6},{8,9},{9,8},{10,11... | collective-permute-start | bytes 110600 | tf_op jit(solution)/shard_map/ppermute | solution.py:40
  6.6 8.5 %collective-permute-start.2 = (bf16[36,512]{1,0:T(8,128)(2,1)}, bf16[36,512]{1,0:T(8,128)(2,1)S(1)}, u32[]{:S(2)}, u32[]{:S(2)}) collective-permute-start(bf16[36,512]{1,0:T(8,128)(2,1)} %get-tuple-element.31), channel_id=1, source_target_pairs={{0,2},{1,3},{2,0},{3,1},{4,6},{5,7},{6,4},{7,5},{8,10},{9,11},{10,... | collective-permute-start | bytes 110600 | tf_op jit(solution)/shard_map/ppermute | solution.py:40
  8.2 6.9 %collective-permute-start.3 = (bf16[36,512]{1,0:T(8,128)(2,1)}, bf16[36,512]{1,0:T(8,128)(2,1)S(1)}, u32[]{:S(2)}, u32[]{:S(2)}) collective-permute-start(bf16[36,512]{1,0:T(8,128)(2,1)} %get-tuple-element.32), channel_id=1, source_target_pairs={{0,3},{1,2},{2,1},{3,0},{4,7},{5,6},{6,5},{7,4},{8,11},{9,10},{10,... | collective-permute-start | bytes 110600 | tf_op jit(solution)/shard_map/ppermute | solution.py:40
  8.5 17.2 %collective-permute-start.5 = (bf16[2,1,144,768]{3,2,1,0:T(8,128)(2,1)}, bf16[2,1,144,768]{3,2,1,0:T(8,128)(2,1)S(1)}, u32[]{:S(2)}, u32[]{:S(2)}) collective-permute-start(bf16[2,1,144,768]{3,2,1,0:T(8,128)(2,1)} %param.11), channel_id=1, source_target_pairs={{4,12},{5,13},{6,14},{7,15},{20,28},{21,29},{22,30},{23,31}} | collective-permute-start | bytes 1327112 | tf_op jit(solution)/shard_map/ppermute | solution.py:273
  9.2 1.2 %copy-start = (bf16[4,1,144,768]{3,2,1,0:T(8,128)(2,1)S(1)}, bf16[4,1,144,768]{3,2,1,0:T(8,128)(2,1)}, u32[]{:S(2)}) copy-start(bf16[4,1,144,768]{3,2,1,0:T(8,128)(2,1)} %q_ref.7) | copy-start | bytes 2654212
  10.4 1.5 %copy-start.2 = (bf16[4,2,1,144,768]{4,3,2,1,0:T(8,128)(2,1)S(1)}, bf16[4,2,1,144,768]{4,3,2,1,0:T(8,128)(2,1)}, u32[]{:S(2)}) copy-start(bf16[4,2,1,144,768]{4,3,2,1,0:T(8,128)(2,1)} %kv_ref.1) | copy-start | bytes 5308420
  11.8 0.7 %copy-start.5 = (s32[4,4]{1,0:T(4,128)S(1)}, s32[4,4]{1,0:T(4,128)}, u32[]{:S(2)}) copy-start(s32[4,4]{1,0:T(4,128)} %step_ref.7) | copy-start | bytes 196
  12.5 2.6 %copy-start.4 = (bf16[36,512]{1,0:T(8,128)(2,1)S(1)}, bf16[36,512]{1,0:T(8,128)(2,1)}, u32[]{:S(2)}) copy-start(bf16[36,512]{1,0:T(8,128)(2,1)} %get-tuple-element.29.refs_0_) | copy-start | bytes 110596
  12.5 12.4 %copy-start.1 = (bf16[4,1,144,768]{3,2,1,0:T(8,128)(2,1)S(1)}, bf16[4,1,144,768]{3,2,1,0:T(8,128)(2,1)}, u32[]{:S(2)}) copy-start(bf16[4,1,144,768]{3,2,1,0:T(8,128)(2,1)} %q_ref.7) | copy-start | bytes 2654212
  12.5 12.4 %copy-start.6 = (s32[4,4]{1,0:T(4,128)S(1)}, s32[4,4]{1,0:T(4,128)}, u32[]{:S(2)}) copy-start(s32[4,4]{1,0:T(4,128)} %mask_ref.5) | copy-start | bytes 196
  15.8 14.2 %collective-permute-start.4 = (bf16[1,144,768]{2,1,0:T(8,128)(2,1)S(1)}, bf16[1,144,768]{2,1,0:T(8,128)(2,1)S(1)}, u32[]{:S(2)}, u32[]{:S(2)}) collective-permute-start(bf16[1,144,768]{2,1,0:T(8,128)(2,1)S(1)} %get-tuple-element.55), channel_id=1, source_target_pairs={{0,4},{4,8},{8,12},{1,5},{5,9},{9,13},{2,6},{6,10},{10,14},{3,7},{... | collective-permute-start | bytes 663560 | tf_op jit(solution)/shard_map/ppermute | solution.py:31
  18.5 13.9 %collective-permute-start.6 = (bf16[1,144,384]{2,1,0:T(8,128)(2,1)S(1)}, bf16[1,144,384]{2,1,0:T(8,128)(2,1)S(1)}, u32[]{:S(2)}, u32[]{:S(2)}) collective-permute-start(bf16[1,144,384]{2,1,0:T(8,128)(2,1)S(1)} %get-tuple-element.57), channel_id=1, source_target_pairs={{0,4},{4,8},{8,12},{1,5},{5,9},{9,13},{2,6},{6,10},{10,14},{3,7},{... | collective-permute-start | bytes 331784 | tf_op jit(solution)/shard_map/ppermute | solution.py:31
  20.4 14.3 %collective-permute-start.7 = (bf16[1,144,384]{2,1,0:T(8,128)(2,1)S(1)}, bf16[1,144,384]{2,1,0:T(8,128)(2,1)S(1)}, u32[]{:S(2)}, u32[]{:S(2)}) collective-permute-start(bf16[1,144,384]{2,1,0:T(8,128)(2,1)S(1)} %get-tuple-element.56), channel_id=1, source_target_pairs={{0,4},{4,8},{8,12},{1,5},{5,9},{9,13},{2,6},{6,10},{10,14},{3,7},{... | collective-permute-start | bytes 331784 | tf_op jit(solution)/shard_map/ppermute | solution.py:31
  23.0 14.7 %collective-permute-start.11 = (bf16[24,512]{1,0:T(8,128)(2,1)S(1)}, bf16[24,512]{1,0:T(8,128)(2,1)S(1)}, u32[]{:S(2)}, u32[]{:S(2)}) collective-permute-start(bf16[24,512]{1,0:T(8,128)(2,1)S(1)} %get-tuple-element.53), channel_id=1, source_target_pairs={{0,4},{4,8},{8,12},{1,5},{5,9},{9,13},{2,6},{6,10},{10,14},{3,7},{... | collective-permute-start | bytes 73736 | tf_op jit(solution)/shard_map/ppermute | solution.py:31
  34.7 3.0 %copy-start.3 = (bf16[3,512,512]{2,1,0:T(8,128)(2,1)S(1)}, bf16[3,512,512]{2,1,0:T(8,128)(2,1)}, u32[]{:S(2)}) copy-start(bf16[3,512,512]{2,1,0:T(8,128)(2,1)} %conv_ref.1) | copy-start | bytes 4718596
  35.1 4.0 %collective-permute-start.8 = (f32[1,576]{1,0:T(1,128)S(1)}, f32[1,576]{1,0:T(1,128)S(1)}, u32[]{:S(2)}, u32[]{:S(2)}) collective-permute-start(f32[1,576]{1,0:T(1,128)S(1)} %get-tuple-element.49.square_in), channel_id=1, source_target_pairs={{0,2},{1,3},{2,0},{3,1},{4,6},{5,7},{6,4},{7,5},{8,10},{9,11},{10,... | collective-permute-start | bytes 6920 | tf_op jit(solution)/shard_map/ppermute | solution.py:40
  36.7 3.0 %collective-permute-start.9 = (f32[1,576]{1,0:T(1,128)S(1)}, f32[1,576]{1,0:T(1,128)S(1)}, u32[]{:S(2)}, u32[]{:S(2)}) collective-permute-start(f32[1,576]{1,0:T(1,128)S(1)} %get-tuple-element.49.square_in), channel_id=1, source_target_pairs={{0,3},{1,2},{2,1},{3,0},{4,7},{5,6},{6,5},{7,4},{8,11},{9,10},{10,... | collective-permute-start | bytes 6920 | tf_op jit(solution)/shard_map/ppermute | solution.py:40
  37.0 2.2 %collective-permute-start.10 = (f32[1,576]{1,0:T(1,128)S(1)}, f32[1,576]{1,0:T(1,128)S(1)}, u32[]{:S(2)}, u32[]{:S(2)}) collective-permute-start(f32[1,576]{1,0:T(1,128)S(1)} %get-tuple-element.51.refs_0_), channel_id=1, source_target_pairs={{0,1},{1,0},{2,3},{3,2},{4,5},{5,4},{6,7},{7,6},{8,9},{9,8},{10,11... | collective-permute-start | bytes 6920 | tf_op jit(solution)/shard_map/ppermute | solution.py:40

commit v3 on v2

--- a/solution.py
+++ b/solution.py
@@ -436,7 +436,7 @@
     pieces = project(finished, w_in)
     parts = [pieces[0]] + [swap(p, axes, offset + 1) for offset, p in enumerate(pieces[1:])]
     if span == 4:
-        direct = send(after(clean_kv, pieces[0]), [(1, 3)])
+        direct = send(clean_kv, [(1, 3)])
     carry = plain_call(
         own_kernel,
         "own",

time: 41.1 us -> 41.1 us (level)
  no operation moved by 1% of the time
where the time goes in v3:
time: 41.1 us; the launch traced here: 40.8 us
  starting transfers between devices  16.8 us (41%)
  Pallas kernels  11 us (27%)
  waiting for transfers between devices  8.03 us (20%)
  local copies, waits for them, and re-layouts  3.37 us (8%)
  between operations  1.48 us (4%)
    pallas_call x11, Pallas kernels, plain_call(): pl.pallas_call(kernel, in_specs=list(in_specs) + [VMEM_SPEC] * (len(opera...  11 us
    ppermute x4, starting transfers between devices, hop(): lax.ppermute(value, axis, [(source, source + steps) for source in range(c...  8.35 us
    ppermute x4, waiting for transfers between devices, hop(): lax.ppermute(value, axis, [(source, source + steps) for source in range(c...  6.97 us
    ppermute x2, starting transfers between devices, send(): return lax.ppermute(value, 'span', pairs)  4.3 us
    ppermute x6, starting transfers between devices, swap(): return lax.ppermute(value, axes, pairs)  4.2 us
    unnamed x16, local copies, waits for them, and re-layouts  3.34 us
  transfers between devices with their start and end apart: 12, of which 5 were waited for; matrix products, arithmetic and copies ran while one was open for 0% of the time, Pallas kernels for 24%

profile of v3, /device:TPU:20, one launch (start us, length us, event | category | flops | bytes accessed | tf_op | source)
XLA Modules:
  0.0 40.8 jit_solution(5206165960898124879)
XLA Ops:
  0.6 0.0 copy-start.7
  0.6 3.6 %collective-permute-start = (bf16[2,1,144,768]{3,2,1,0:T(8,128)(2,1)}, bf16[2,1,144,768]{3,2,1,0:T(8,128)(2,1)S(1)}, u32[]{:S(2)}, u32[]{:S(2)}) collective-permute-start(bf16[2,1,144,768]{3,2,1,0:T(8,128)(2,1)} %param.11), channel_id=1, source_target_pairs={{0,8},{8,12},{1,9},{9,13},{2,10},{10,14},{3,11},{11,15},{16,24},{2... | collective-permute-start | bytes 1327112 | tf_op jit(solution)/shard_map/ppermute | solution.py:273
  4.3 2.3 %project.1 = (bf16[36,512]{1,0:T(8,128)(2,1)}, bf16[36,512]{1,0:T(8,128)(2,1)}, bf16[36,512]{1,0:T(8,128)(2,1)}, bf16[36,512]{1,0:T(8,128)(2,1)}) custom-call(bf16[1,144,768]{2,1,0:T(8,128)(2,1)} %x_hbm.1, bf16[768,512]{1,0:T(8,128)(2,1)} %w_hbm.1), custom_call_target="tpu_custom_call" | custom-call | flops 113246208 | bytes 1007616 | tf_op jit(solution)/shard_map/project/pallas_call | solution.py:284
  6.6 0.1 collective-permute-start.1
  6.6 1.6 %collective-permute-start.2 = (bf16[36,512]{1,0:T(8,128)(2,1)}, bf16[36,512]{1,0:T(8,128)(2,1)S(1)}, u32[]{:S(2)}, u32[]{:S(2)}) collective-permute-start(bf16[36,512]{1,0:T(8,128)(2,1)} %get-tuple-element.30), channel_id=1, source_target_pairs={{0,2},{1,3},{2,0},{3,1},{4,6},{5,7},{6,4},{7,5},{8,10},{9,11},{10,... | collective-permute-start | bytes 110600 | tf_op jit(solution)/shard_map/ppermute | solution.py:40
  8.2 0.3 collective-permute-start.3
  8.5 0.7 %collective-permute-start.5 = (bf16[2,1,144,768]{3,2,1,0:T(8,128)(2,1)}, bf16[2,1,144,768]{3,2,1,0:T(8,128)(2,1)S(1)}, u32[]{:S(2)}, u32[]{:S(2)}) collective-permute-start(bf16[2,1,144,768]{3,2,1,0:T(8,128)(2,1)} %param.11), channel_id=1, source_target_pairs={{4,12},{5,13},{6,14},{7,15},{20,28},{21,29},{22,30},{23,31}} | collective-permute-start | bytes 1327112 | tf_op jit(solution)/shard_map/ppermute | solution.py:273
  9.2 0.0 copy-start
  9.2 1.2 %copy-done = bf16[4,1,144,768]{3,2,1,0:T(8,128)(2,1)S(1)} copy-done((bf16[4,1,144,768]{3,2,1,0:T(8,128)(2,1)S(1)}, bf16[4,1,144,768]{3,2,1,0:T(8,128)(2,1)}, u32[]{:S(2)}) %copy-start) | copy-done | bytes 884760
  10.4 0.0 copy-start.2
  10.4 1.5 %copy-done.2 = bf16[4,2,1,144,768]{4,3,2,1,0:T(8,128)(2,1)S(1)} copy-done((bf16[4,2,1,144,768]{4,3,2,1,0:T(8,128)(2,1)S(1)}, bf16[4,2,1,144,768]{4,3,2,1,0:T(8,128)(2,1)}, u32[]{:S(2)}) %copy-start.2) | copy-done | bytes 1769496
  11.8 0.0 copy-start.5
  11.8 0.7 %copy-done.5 = s32[4,4]{1,0:T(4,128)S(1)} copy-done((s32[4,4]{1,0:T(4,128)S(1)}, s32[4,4]{1,0:T(4,128)}, u32[]{:S(2)}) %copy-start.5) | copy-done | bytes 88
  12.5 2.5 %own.1 = (f32[6,128,576]{2,1,0:T(8,128)S(1)}, f32[6,576]{1,0:T(8,128)S(1)}, f32[6,576]{1,0:T(8,128)S(1)}) custom-call(s32[4,4]{1,0:T(4,128)S(1)} %copy-done.5, bf16[4,1,144,768]{3,2,1,0:T(8,128)(2,1)S(1)} %copy-done, bf16[4,2,1,144,768]{4,3,2,1,0:T(8,128)(2,1)S(1)} %copy-done.2), custom_call_target="tpu_custom_call" | custom-call | flops 254803968 | bytes 2654272 | tf_op jit(solution)/shard_map/own/pallas_call | solution.py:284
  15.1 0.0 collective-permute-done.1.refs_1_
  15.1 0.0 collective-permute-done.2.refs_2_
  15.1 0.0 collective-permute-done.3.refs_3_
  15.1 0.0 copy-done.4
  15.1 0.1 gather.1
  15.3 0.5 %collective-permute-done.refs_0_ = bf16[2,1,144,768]{3,2,1,0:T(8,128)(2,1)S(1)} collective-permute-done((bf16[2,1,144,768]{3,2,1,0:T(8,128)(2,1)}, bf16[2,1,144,768]{3,2,1,0:T(8,128)(2,1)S(1)}, u32[]{:S(2)}, u32[]{:S(2)}) %collective-permute-start) | collective-permute-done | bytes 442400 | tf_op jit(solution)/shard_map/ppermute | solution.py:273
  15.8 0.0 copy-done.7
  15.8 0.1 select_bitcast_fusion
  15.8 2.6 %collective-permute-start.4 = (bf16[1,144,768]{2,1,0:T(8,128)(2,1)S(1)}, bf16[1,144,768]{2,1,0:T(8,128)(2,1)S(1)}, u32[]{:S(2)}, u32[]{:S(2)}) collective-permute-start(bf16[1,144,768]{2,1,0:T(8,128)(2,1)S(1)} %get-tuple-element.53), channel_id=1, source_target_pairs={{0,4},{4,8},{8,12},{1,5},{5,9},{9,13},{2,6},{6,10},{10,14},{3,7},{... | collective-permute-start | bytes 663560 | tf_op jit(solution)/shard_map/ppermute | solution.py:31
  18.5 1.9 %collective-permute-start.6 = (bf16[1,144,384]{2,1,0:T(8,128)(2,1)S(1)}, bf16[1,144,384]{2,1,0:T(8,128)(2,1)S(1)}, u32[]{:S(2)}, u32[]{:S(2)}) collective-permute-start(bf16[1,144,384]{2,1,0:T(8,128)(2,1)S(1)} %get-tuple-element.55), channel_id=1, source_target_pairs={{0,4},{4,8},{8,12},{1,5},{5,9},{9,13},{2,6},{6,10},{10,14},{3,7},{... | collective-permute-start | bytes 331784 | tf_op jit(solution)/shard_map/ppermute | solution.py:31
  20.4 1.9 %collective-permute-start.7 = (bf16[1,144,384]{2,1,0:T(8,128)(2,1)S(1)}, bf16[1,144,384]{2,1,0:T(8,128)(2,1)S(1)}, u32[]{:S(2)}, u32[]{:S(2)}) collective-permute-start(bf16[1,144,384]{2,1,0:T(8,128)(2,1)S(1)} %get-tuple-element.54), channel_id=1, source_target_pairs={{0,4},{4,8},{8,12},{1,5},{5,9},{9,13},{2,6},{6,10},{10,14},{3,7},{... | collective-permute-start | bytes 331784 | tf_op jit(solution)/shard_map/ppermute | solution.py:31
  23.0 1.9 %collective-permute-start.11 = (bf16[24,512]{1,0:T(8,128)(2,1)S(1)}, bf16[24,512]{1,0:T(8,128)(2,1)S(1)}, u32[]{:S(2)}, u32[]{:S(2)}) collective-permute-start(bf16[24,512]{1,0:T(8,128)(2,1)S(1)} %get-tuple-element.51), channel_id=1, source_target_pairs={{0,4},{4,8},{8,12},{1,5},{5,9},{9,13},{2,6},{6,10},{10,14},{3,7},{... | collective-permute-start | bytes 73736 | tf_op jit(solution)/shard_map/ppermute | solution.py:31
  24.9 0.0 copy-done.1
  24.9 0.0 copy-done.6
  24.9 0.7 %middle.2 = (f32[6,128,576]{2,1,0:T(8,128)S(1)}, f32[6,576]{1,0:T(8,128)S(1)}, f32[6,576]{1,0:T(8,128)S(1)}) custom-call(s32[4,4]{1,0:T(4,128)S(1)} %copy-done.5, s32[4,4]{1,0:T(4,128)S(1)} %copy-done.6, bf16[4,1,144,768]{3,2,1,0:T(8,128)(2,1)S(1)} %copy-done.1, bf16[2,1,144,768]{3,2,1,0:T(8,128)(2,1)S(1)} %collective-permute-done.refs_0_, ...), custom_call_target="tpu_custom_call" | custom-call | flops 254803968 | bytes 3124352 | tf_op jit(solution)/shard_map/middle/pallas_call | solution.py:284
  25.7 0.0 collective-permute-done.5.refs_0_
  25.7 0.7 %middle.3 = (f32[6,128,576]{2,1,0:T(8,128)S(1)}, f32[6,576]{1,0:T(8,128)S(1)}, f32[6,576]{1,0:T(8,128)S(1)}) custom-call(s32[4,4]{1,0:T(4,128)S(1)} %copy-done.5, s32[4,4]{1,0:T(4,128)S(1)} %copy-done.6, bf16[4,1,144,768]{3,2,1,0:T(8,128)(2,1)S(1)} %copy-done.1, bf16[2,1,144,768]{3,2,1,0:T(8,128)(2,1)S(1)} %collective-permute-done.5.refs_0_, ...), custom_call_target="tpu_custom_call" | custom-call | flops 254803968 | bytes 3124352 | tf_op jit(solution)/shard_map/middle/pallas_call | solution.py:284
  26.4 3.6 %collective-permute-done.4.refs_0_ = bf16[1,144,768]{2,1,0:T(8,128)(2,1)S(1)} collective-permute-done((bf16[1,144,768]{2,1,0:T(8,128)(2,1)S(1)}, bf16[1,144,768]{2,1,0:T(8,128)(2,1)S(1)}, u32[]{:S(2)}, u32[]{:S(2)}) %collective-permute-start.4) | collective-permute-done | bytes 221216 | tf_op jit(solution)/shard_map/ppermute | solution.py:31
  30.0 0.8 %score.1 = (f32[6,128,576]{2,1,0:T(8,128)S(1)}, bf16[6,144,576]{2,1,0:T(8,128)(2,1)S(1)}) custom-call(s32[4,4]{1,0:T(4,128)S(1)} %copy-done.5, s32[4,4]{1,0:T(4,128)S(1)} %copy-done.6, bf16[4,1,144,768]{3,2,1,0:T(8,128)(2,1)S(1)} %copy-done.1, bf16[1,144,768]{2,1,0:T(8,128)(2,1)S(1)} %collective-permute-done.4.refs_0_, ...), custom_call_target="tpu_custom_call" | custom-call | flops 127401984 | bytes 2903168 | tf_op jit(solution)/shard_map/score/pallas_call | solution.py:284
  30.8 1.5 %collective-permute-done.6.value_ref = bf16[1,144,384]{2,1,0:T(8,128)(2,1)S(1)} collective-permute-done((bf16[1,144,384]{2,1,0:T(8,128)(2,1)S(1)}, bf16[1,144,384]{2,1,0:T(8,128)(2,1)S(1)}, u32[]{:S(2)}, u32[]{:S(2)}) %collective-permute-start.6) | collective-permute-done | bytes 110624 | tf_op jit(solution)/shard_map/ppermute | solution.py:31
  32.4 0.5 %average.1 = (f32[4,144,384]{2,1,0:T(8,128)S(1)}, f32[1,576]{1,0:T(1,128)S(1)}) custom-call(f32[6,128,576]{2,1,0:T(8,128)S(1)} %get-tuple-element.42.acc_ref, bf16[6,144,576]{2,1,0:T(8,128)(2,1)S(1)} %get-tuple-element.43.w_ref, bf16[1,144,384]{2,1,0:T(8,128)(2,1)S(1)} %collective-permute-done.6.value_ref), custom_call_target="tpu_custom_call" | custom-call | flops 63700992 | bytes 2875392 | tf_op jit(solution)/shard_map/average/pallas_call | solution.py:284
  32.9 1.9 %collective-permute-done.7.value_ref = bf16[1,144,384]{2,1,0:T(8,128)(2,1)S(1)} collective-permute-done((bf16[1,144,384]{2,1,0:T(8,128)(2,1)S(1)}, bf16[1,144,384]{2,1,0:T(8,128)(2,1)S(1)}, u32[]{:S(2)}, u32[]{:S(2)}) %collective-permute-start.7) | collective-permute-done | bytes 110624 | tf_op jit(solution)/shard_map/ppermute | solution.py:31
  34.7 0.4 rest.1
  35.1 1.6 %collective-permute-start.8 = (f32[1,576]{1,0:T(1,128)S(1)}, f32[1,576]{1,0:T(1,128)S(1)}, u32[]{:S(2)}, u32[]{:S(2)}) collective-permute-start(f32[1,576]{1,0:T(1,128)S(1)} %get-tuple-element.47.square_in), channel_id=1, source_target_pairs={{0,2},{1,3},{2,0},{3,1},{4,6},{5,7},{6,4},{7,5},{8,10},{9,11},{10,... | collective-permute-start | bytes 6920 | tf_op jit(solution)/shard_map/ppermute | solution.py:40
  36.7 0.0 collective-permute-start.9
  36.7 0.3 turn.1
  37.0 0.7 %collective-permute-start.10 = (f32[1,576]{1,0:T(1,128)S(1)}, f32[1,576]{1,0:T(1,128)S(1)}, u32[]{:S(2)}, u32[]{:S(2)}) collective-permute-start(f32[1,576]{1,0:T(1,128)S(1)} %get-tuple-element.49.refs_0_), channel_id=1, source_target_pairs={{0,1},{1,0},{2,3},{3,2},{4,5},{5,4},{6,7},{7,6},{8,9},{9,8},{10,11... | collective-permute-start | bytes 6920 | tf_op jit(solution)/shard_map/ppermute | solution.py:40
  37.7 0.0 collective-permute-done.11.tail_ref
  37.7 0.0 copy-done.3
  37.7 1.4 %decode.1 = bf16[1,36,512]{2,1,0:T(8,128)(2,1)} custom-call(s32[1]{0:T(128)S(6)} %copy.11.fade_ref, bf16[36,512]{1,0:T(8,128)(2,1)S(1)} %get-tuple-element.50.hidden_ref, bf16[24,512]{1,0:T(8,128)(2,1)S(1)} %collective-permute-done.11.tail_ref, bf16[3,512,512]{2,1,0:T(8,128)(2,1)S(1)} %copy-done.3), custom_call_target="tpu_custom_call" | custom-call | flops 56623104 | bytes 1634308 | tf_op jit(solution)/shard_map/decode/pallas_call | solution.py:284
  39.1 0.0 collective-permute-done.10.refs_3_
  39.1 0.0 collective-permute-done.8.refs_1_
  39.2 0.5 %collective-permute-done.9.refs_2_ = f32[1,576]{1,0:T(1,128)S(1)} collective-permute-done((f32[1,576]{1,0:T(1,128)S(1)}, f32[1,576]{1,0:T(1,128)S(1)}, u32[]{:S(2)}, u32[]{:S(2)}) %collective-permute-start.9) | collective-permute-done | bytes 2336 | tf_op jit(solution)/shard_map/ppermute | solution.py:40
  39.7 1.1 %scale.1 = bf16[4,1,144,768]{3,2,1,0:T(8,128)(2,1)} custom-call(f32[4,144,384]{2,1,0:T(8,128)S(1)} %get-tuple-element.44.front_ref, f32[4,144,384]{2,1,0:T(8,128)S(1)} %get-tuple-element.48.back_ref, f32[1,576]{1,0:T(1,128)S(1)} %get-tuple-element.49.refs_0_, f32[1,576]{1,0:T(1,128)S(1)} %collective-permute-done.8.refs_1_, ...), custom_call_target="tpu_custom_call" | custom-call | flops 442368 | bytes 1778688 | tf_op jit(solution)/shard_map/scale/pallas_call | solution.py:284
  (5 shorter events, 0.0 us)
Async XLA Ops:
  0.6 15.2 %copy-start.7 = (bf16[2,1,144,768]{3,2,1,0:T(8,128)(2,1)S(1)}, bf16[2,1,144,768]{3,2,1,0:T(8,128)(2,1)}, u32[]{:S(2)}) copy-start(bf16[2,1,144,768]{3,2,1,0:T(8,128)(2,1)} %param.11) | copy-start | bytes 1327108
  0.6 15.1 %collective-permute-start = (bf16[2,1,144,768]{3,2,1,0:T(8,128)(2,1)}, bf16[2,1,144,768]{3,2,1,0:T(8,128)(2,1)S(1)}, u32[]{:S(2)}, u32[]{:S(2)}) collective-permute-start(bf16[2,1,144,768]{3,2,1,0:T(8,128)(2,1)} %param.11), channel_id=1, source_target_pairs={{0,8},{8,12},{1,9},{9,13},{2,10},{10,14},{3,11},{11,15},{16,24},{2... | collective-permute-start | bytes 1327112 | tf_op jit(solution)/shard_map/ppermute | solution.py:273
  6.6 8.5 %collective-permute-start.1 = (bf16[36,512]{1,0:T(8,128)(2,1)}, bf16[36,512]{1,0:T(8,128)(2,1)S(1)}, u32[]{:S(2)}, u32[]{:S(2)}) collective-permute-start(bf16[36,512]{1,0:T(8,128)(2,1)} %get-tuple-element.29), channel_id=1, source_target_pairs={{0,1},{1,0},{2,3},{3,2},{4,5},{5,4},{6,7},{7,6},{8,9},{9,8},{10,11... | collective-permute-start | bytes 110600 | tf_op jit(solution)/shard_map/ppermute | solution.py:40
  6.6 8.5 %collective-permute-start.2 = (bf16[36,512]{1,0:T(8,128)(2,1)}, bf16[36,512]{1,0:T(8,128)(2,1)S(1)}, u32[]{:S(2)}, u32[]{:S(2)}) collective-permute-start(bf16[36,512]{1,0:T(8,128)(2,1)} %get-tuple-element.30), channel_id=1, source_target_pairs={{0,2},{1,3},{2,0},{3,1},{4,6},{5,7},{6,4},{7,5},{8,10},{9,11},{10,... | collective-permute-start | bytes 110600 | tf_op jit(solution)/shard_map/ppermute | solution.py:40
  8.2 6.9 %collective-permute-start.3 = (bf16[36,512]{1,0:T(8,128)(2,1)}, bf16[36,512]{1,0:T(8,128)(2,1)S(1)}, u32[]{:S(2)}, u32[]{:S(2)}) collective-permute-start(bf16[36,512]{1,0:T(8,128)(2,1)} %get-tuple-element.31), channel_id=1, source_target_pairs={{0,3},{1,2},{2,1},{3,0},{4,7},{5,6},{6,5},{7,4},{8,11},{9,10},{10,... | collective-permute-start | bytes 110600 | tf_op jit(solution)/shard_map/ppermute | solution.py:40
  8.5 17.2 %collective-permute-start.5 = (bf16[2,1,144,768]{3,2,1,0:T(8,128)(2,1)}, bf16[2,1,144,768]{3,2,1,0:T(8,128)(2,1)S(1)}, u32[]{:S(2)}, u32[]{:S(2)}) collective-permute-start(bf16[2,1,144,768]{3,2,1,0:T(8,128)(2,1)} %param.11), channel_id=1, source_target_pairs={{4,12},{5,13},{6,14},{7,15},{20,28},{21,29},{22,30},{23,31}} | collective-permute-start | bytes 1327112 | tf_op jit(solution)/shard_map/ppermute | solution.py:273
  9.2 1.2 %copy-start = (bf16[4,1,144,768]{3,2,1,0:T(8,128)(2,1)S(1)}, bf16[4,1,144,768]{3,2,1,0:T(8,128)(2,1)}, u32[]{:S(2)}) copy-start(bf16[4,1,144,768]{3,2,1,0:T(8,128)(2,1)} %q_ref.7) | copy-start | bytes 2654212
  10.4 1.5 %copy-start.2 = (bf16[4,2,1,144,768]{4,3,2,1,0:T(8,128)(2,1)S(1)}, bf16[4,2,1,144,768]{4,3,2,1,0:T(8,128)(2,1)}, u32[]{:S(2)}) copy-start(bf16[4,2,1,144,768]{4,3,2,1,0:T(8,128)(2,1)} %kv_ref.1) | copy-start | bytes 5308420
  11.8 0.7 %copy-start.5 = (s32[4,4]{1,0:T(4,128)S(1)}, s32[4,4]{1,0:T(4,128)}, u32[]{:S(2)}) copy-start(s32[4,4]{1,0:T(4,128)} %step_ref.7) | copy-start | bytes 196
  12.5 2.6 %copy-start.4 = (bf16[36,512]{1,0:T(8,128)(2,1)S(1)}, bf16[36,512]{1,0:T(8,128)(2,1)}, u32[]{:S(2)}) copy-start(bf16[36,512]{1,0:T(8,128)(2,1)} %get-tuple-element.28.refs_0_) | copy-start | bytes 110596
  12.5 12.4 %copy-start.1 = (bf16[4,1,144,768]{3,2,1,0:T(8,128)(2,1)S(1)}, bf16[4,1,144,768]{3,2,1,0:T(8,128)(2,1)}, u32[]{:S(2)}) copy-start(bf16[4,1,144,768]{3,2,1,0:T(8,128)(2,1)} %q_ref.7) | copy-start | bytes 2654212
  12.5 12.4 %copy-start.6 = (s32[4,4]{1,0:T(4,128)S(1)}, s32[4,4]{1,0:T(4,128)}, u32[]{:S(2)}) copy-start(s32[4,4]{1,0:T(4,128)} %mask_ref.5) | copy-start | bytes 196
  15.8 14.2 %collective-permute-start.4 = (bf16[1,144,768]{2,1,0:T(8,128)(2,1)S(1)}, bf16[1,144,768]{2,1,0:T(8,128)(2,1)S(1)}, u32[]{:S(2)}, u32[]{:S(2)}) collective-permute-start(bf16[1,144,768]{2,1,0:T(8,128)(2,1)S(1)} %get-tuple-element.53), channel_id=1, source_target_pairs={{0,4},{4,8},{8,12},{1,5},{5,9},{9,13},{2,6},{6,10},{10,14},{3,7},{... | collective-permute-start | bytes 663560 | tf_op jit(solution)/shard_map/ppermute | solution.py:31
  18.5 13.9 %collective-permute-start.6 = (bf16[1,144,384]{2,1,0:T(8,128)(2,1)S(1)}, bf16[1,144,384]{2,1,0:T(8,128)(2,1)S(1)}, u32[]{:S(2)}, u32[]{:S(2)}) collective-permute-start(bf16[1,144,384]{2,1,0:T(8,128)(2,1)S(1)} %get-tuple-element.55), channel_id=1, source_target_pairs={{0,4},{4,8},{8,12},{1,5},{5,9},{9,13},{2,6},{6,10},{10,14},{3,7},{... | collective-permute-start | bytes 331784 | tf_op jit(solution)/shard_map/ppermute | solution.py:31
  20.4 14.3 %collective-permute-start.7 = (bf16[1,144,384]{2,1,0:T(8,128)(2,1)S(1)}, bf16[1,144,384]{2,1,0:T(8,128)(2,1)S(1)}, u32[]{:S(2)}, u32[]{:S(2)}) collective-permute-start(bf16[1,144,384]{2,1,0:T(8,128)(2,1)S(1)} %get-tuple-element.54), channel_id=1, source_target_pairs={{0,4},{4,8},{8,12},{1,5},{5,9},{9,13},{2,6},{6,10},{10,14},{3,7},{... | collective-permute-start | bytes 331784 | tf_op jit(solution)/shard_map/ppermute | solution.py:31
  23.0 14.7 %collective-permute-start.11 = (bf16[24,512]{1,0:T(8,128)(2,1)S(1)}, bf16[24,512]{1,0:T(8,128)(2,1)S(1)}, u32[]{:S(2)}, u32[]{:S(2)}) collective-permute-start(bf16[24,512]{1,0:T(8,128)(2,1)S(1)} %get-tuple-element.51), channel_id=1, source_target_pairs={{0,4},{4,8},{8,12},{1,5},{5,9},{9,13},{2,6},{6,10},{10,14},{3,7},{... | collective-permute-start | bytes 73736 | tf_op jit(solution)/shard_map/ppermute | solution.py:31
  34.7 3.0 %copy-start.3 = (bf16[3,512,512]{2,1,0:T(8,128)(2,1)S(1)}, bf16[3,512,512]{2,1,0:T(8,128)(2,1)}, u32[]{:S(2)}) copy-start(bf16[3,512,512]{2,1,0:T(8,128)(2,1)} %conv_ref.1) | copy-start | bytes 4718596
  35.1 4.0 %collective-permute-start.8 = (f32[1,576]{1,0:T(1,128)S(1)}, f32[1,576]{1,0:T(1,128)S(1)}, u32[]{:S(2)}, u32[]{:S(2)}) collective-permute-start(f32[1,576]{1,0:T(1,128)S(1)} %get-tuple-element.47.square_in), channel_id=1, source_target_pairs={{0,2},{1,3},{2,0},{3,1},{4,6},{5,7},{6,4},{7,5},{8,10},{9,11},{10,... | collective-permute-start | bytes 6920 | tf_op jit(solution)/shard_map/ppermute | solution.py:40
  36.7 3.0 %collective-permute-start.9 = (f32[1,576]{1,0:T(1,128)S(1)}, f32[1,576]{1,0:T(1,128)S(1)}, u32[]{:S(2)}, u32[]{:S(2)}) collective-permute-start(f32[1,576]{1,0:T(1,128)S(1)} %get-tuple-element.47.square_in), channel_id=1, source_target_pairs={{0,3},{1,2},{2,1},{3,0},{4,7},{5,6},{6,5},{7,4},{8,11},{9,10},{10,... | collective-permute-start | bytes 6920 | tf_op jit(solution)/shard_map/ppermute | solution.py:40
  37.0 2.2 %collective-permute-start.10 = (f32[1,576]{1,0:T(1,128)S(1)}, f32[1,576]{1,0:T(1,128)S(1)}, u32[]{:S(2)}, u32[]{:S(2)}) collective-permute-start(f32[1,576]{1,0:T(1,128)S(1)} %get-tuple-element.49.refs_0_), channel_id=1, source_target_pairs={{0,1},{1,0},{2,3},{3,2},{4,5},{5,4},{6,7},{7,6},{8,9},{9,8},{10,11... | collective-permute-start | bytes 6920 | tf_op jit(solution)/shard_map/ppermute | solution.py:40

commit v4 on v3

--- a/solution.py
+++ b/solution.py
@@ -253,10 +253,10 @@
         total = total + ref[...]
     inverse = lax.rsqrt(total / width + 1e-06)
     steps, rows, columns = out_ref.shape
-    spread = jnp.broadcast_to(inverse, (HD, steps * rows)).T
     copies = []
     for step in range(steps):
-        factor = spread[step * rows : (step + 1) * rows]
+        own = inverse[:, step * rows : (step + 1) * rows]
+        factor = jnp.broadcast_to(own, (HD, rows)).T
         place = 0
         for ref in (front_ref, back_ref):
             for first in range(0, ref.shape[2], HD):
@@ -423,7 +423,7 @@
 ):
     steps, _, rows, columns = query.shape
     heads = columns // HD
-    middle = (heads + 1) // 2 * HD
+    middle = -(-2 * heads // 3) * HD
     row_count = steps * rows
     span = lax.axis_size("span")
     axes = ("mp", "seq")

time: 41.1 us -> 41.1 us (level)
  no operation moved by 1% of the time
where the time goes in v4:
time: 41.1 us; the launch traced here: 40.7 us
  starting transfers between devices  16.8 us (41%)
  Pallas kernels  11 us (27%)
  waiting for transfers between devices  8 us (19%)
  local copies, waits for them, and re-layouts  3.36 us (8%)
  between operations  1.5 us (4%)
    pallas_call x11, Pallas kernels, plain_call(): pl.pallas_call(kernel, in_specs=list(in_specs) + [VMEM_SPEC] * (len(opera...  11 us
    ppermute x4, starting transfers between devices, hop(): lax.ppermute(value, axis, [(source, source + steps) for source in range(c...  8.35 us
    ppermute x4, waiting for transfers between devices, hop(): lax.ppermute(value, axis, [(source, source + steps) for source in range(c...  6.84 us
    ppermute x2, starting transfers between devices, send(): return lax.ppermute(value, 'span', pairs)  4.3 us
    ppermute x6, starting transfers between devices, swap(): return lax.ppermute(value, axes, pairs)  4.2 us
    unnamed x16, local copies, waits for them, and re-layouts  3.34 us
  transfers between devices with their start and end apart: 12, of which 5 were waited for; matrix products, arithmetic and copies ran while one was open for 0% of the time, Pallas kernels for 24%

profile of v4, /device:TPU:20, one launch (start us, length us, event | category | flops | bytes accessed | tf_op | source)
XLA Modules:
  0.0 40.7 jit_solution(2070947586497099310)
XLA Ops:
  0.6 0.0 copy-start.7
  0.6 3.6 %collective-permute-start = (bf16[2,1,144,768]{3,2,1,0:T(8,128)(2,1)}, bf16[2,1,144,768]{3,2,1,0:T(8,128)(2,1)S(1)}, u32[]{:S(2)}, u32[]{:S(2)}) collective-permute-start(bf16[2,1,144,768]{3,2,1,0:T(8,128)(2,1)} %param.11), channel_id=1, source_target_pairs={{0,8},{8,12},{1,9},{9,13},{2,10},{10,14},{3,11},{11,15},{16,24},{2... | collective-permute-start | bytes 1327112 | tf_op jit(solution)/shard_map/ppermute | solution.py:273
  4.3 2.3 %project.1 = (bf16[36,512]{1,0:T(8,128)(2,1)}, bf16[36,512]{1,0:T(8,128)(2,1)}, bf16[36,512]{1,0:T(8,128)(2,1)}, bf16[36,512]{1,0:T(8,128)(2,1)}) custom-call(bf16[1,144,768]{2,1,0:T(8,128)(2,1)} %x_hbm.1, bf16[768,512]{1,0:T(8,128)(2,1)} %w_hbm.1), custom_call_target="tpu_custom_call" | custom-call | flops 113246208 | bytes 1007616 | tf_op jit(solution)/shard_map/project/pallas_call | solution.py:284
  6.6 0.1 collective-permute-start.1
  6.6 1.6 %collective-permute-start.2 = (bf16[36,512]{1,0:T(8,128)(2,1)}, bf16[36,512]{1,0:T(8,128)(2,1)S(1)}, u32[]{:S(2)}, u32[]{:S(2)}) collective-permute-start(bf16[36,512]{1,0:T(8,128)(2,1)} %get-tuple-element.30), channel_id=1, source_target_pairs={{0,2},{1,3},{2,0},{3,1},{4,6},{5,7},{6,4},{7,5},{8,10},{9,11},{10,... | collective-permute-start | bytes 110600 | tf_op jit(solution)/shard_map/ppermute | solution.py:40
  8.2 0.3 collective-permute-start.3
  8.5 0.7 %collective-permute-start.5 = (bf16[2,1,144,768]{3,2,1,0:T(8,128)(2,1)}, bf16[2,1,144,768]{3,2,1,0:T(8,128)(2,1)S(1)}, u32[]{:S(2)}, u32[]{:S(2)}) collective-permute-start(bf16[2,1,144,768]{3,2,1,0:T(8,128)(2,1)} %param.11), channel_id=1, source_target_pairs={{4,12},{5,13},{6,14},{7,15},{20,28},{21,29},{22,30},{23,31}} | collective-permute-start | bytes 1327112 | tf_op jit(solution)/shard_map/ppermute | solution.py:273
  9.2 0.0 copy-start
  9.2 1.2 %copy-done = bf16[4,1,144,768]{3,2,1,0:T(8,128)(2,1)S(1)} copy-done((bf16[4,1,144,768]{3,2,1,0:T(8,128)(2,1)S(1)}, bf16[4,1,144,768]{3,2,1,0:T(8,128)(2,1)}, u32[]{:S(2)}) %copy-start) | copy-done | bytes 884760
  10.4 0.0 copy-start.2
  10.4 1.5 %copy-done.2 = bf16[4,2,1,144,768]{4,3,2,1,0:T(8,128)(2,1)S(1)} copy-done((bf16[4,2,1,144,768]{4,3,2,1,0:T(8,128)(2,1)S(1)}, bf16[4,2,1,144,768]{4,3,2,1,0:T(8,128)(2,1)}, u32[]{:S(2)}) %copy-start.2) | copy-done | bytes 1769496
  11.8 0.7 %copy-done.5 = s32[4,4]{1,0:T(4,128)S(1)} copy-done((s32[4,4]{1,0:T(4,128)S(1)}, s32[4,4]{1,0:T(4,128)}, u32[]{:S(2)}) %copy-start.5) | copy-done | bytes 88
  12.5 2.5 %own.1 = (f32[6,128,576]{2,1,0:T(8,128)S(1)}, f32[6,576]{1,0:T(8,128)S(1)}, f32[6,576]{1,0:T(8,128)S(1)}) custom-call(s32[4,4]{1,0:T(4,128)S(1)} %copy-done.5, bf16[4,1,144,768]{3,2,1,0:T(8,128)(2,1)S(1)} %copy-done, bf16[4,2,1,144,768]{4,3,2,1,0:T(8,128)(2,1)S(1)} %copy-done.2), custom_call_target="tpu_custom_call" | custom-call | flops 254803968 | bytes 2654272 | tf_op jit(solution)/shard_map/own/pallas_call | solution.py:284
  15.1 0.0 collective-permute-done.1.refs_1_
  15.1 0.0 collective-permute-done.2.refs_2_
  15.1 0.0 collective-permute-done.3.refs_3_
  15.1 0.0 copy-done.4
  15.1 0.1 gather.1
  15.3 0.5 %collective-permute-done.refs_0_ = bf16[2,1,144,768]{3,2,1,0:T(8,128)(2,1)S(1)} collective-permute-done((bf16[2,1,144,768]{3,2,1,0:T(8,128)(2,1)}, bf16[2,1,144,768]{3,2,1,0:T(8,128)(2,1)S(1)}, u32[]{:S(2)}, u32[]{:S(2)}) %collective-permute-start) | collective-permute-done | bytes 442400 | tf_op jit(solution)/shard_map/ppermute | solution.py:273
  15.8 0.0 copy-done.7
  15.8 0.1 select_bitcast_fusion
  15.8 2.6 %collective-permute-start.4 = (bf16[1,144,768]{2,1,0:T(8,128)(2,1)S(1)}, bf16[1,144,768]{2,1,0:T(8,128)(2,1)S(1)}, u32[]{:S(2)}, u32[]{:S(2)}) collective-permute-start(bf16[1,144,768]{2,1,0:T(8,128)(2,1)S(1)} %get-tuple-element.53), channel_id=1, source_target_pairs={{0,4},{4,8},{8,12},{1,5},{5,9},{9,13},{2,6},{6,10},{10,14},{3,7},{... | collective-permute-start | bytes 663560 | tf_op jit(solution)/shard_map/ppermute | solution.py:31
  18.5 1.9 %collective-permute-start.6 = (bf16[1,144,512]{2,1,0:T(8,128)(2,1)S(1)}, bf16[1,144,512]{2,1,0:T(8,128)(2,1)S(1)}, u32[]{:S(2)}, u32[]{:S(2)}) collective-permute-start(bf16[1,144,512]{2,1,0:T(8,128)(2,1)S(1)} %slice.24), channel_id=1, source_target_pairs={{0,4},{4,8},{8,12},{1,5},{5,9},{9,13},{2,6},{6,10},{10,14},{3,7},{... | collective-permute-start | bytes 442376 | tf_op jit(solution)/shard_map/ppermute | solution.py:31
  20.4 1.9 %collective-permute-start.7 = (bf16[1,144,256]{2,1,0:T(8,128)(2,1)S(1)}, bf16[1,144,256]{2,1,0:T(8,128)(2,1)S(1)}, u32[]{:S(2)}, u32[]{:S(2)}) collective-permute-start(bf16[1,144,256]{2,1,0:T(8,128)(2,1)S(1)} %slice.25), channel_id=1, source_target_pairs={{0,4},{4,8},{8,12},{1,5},{5,9},{9,13},{2,6},{6,10},{10,14},{3,7},{... | collective-permute-start | bytes 221192 | tf_op jit(solution)/shard_map/ppermute | solution.py:31
  23.0 1.9 %collective-permute-start.11 = (bf16[24,512]{1,0:T(8,128)(2,1)S(1)}, bf16[24,512]{1,0:T(8,128)(2,1)S(1)}, u32[]{:S(2)}, u32[]{:S(2)}) collective-permute-start(bf16[24,512]{1,0:T(8,128)(2,1)S(1)} %get-tuple-element.51), channel_id=1, source_target_pairs={{0,4},{4,8},{8,12},{1,5},{5,9},{9,13},{2,6},{6,10},{10,14},{3,7},{... | collective-permute-start | bytes 73736 | tf_op jit(solution)/shard_map/ppermute | solution.py:31
  24.9 0.0 copy-done.1
  24.9 0.0 copy-done.6
  24.9 0.7 %middle.2 = (f32[6,128,576]{2,1,0:T(8,128)S(1)}, f32[6,576]{1,0:T(8,128)S(1)}, f32[6,576]{1,0:T(8,128)S(1)}) custom-call(s32[4,4]{1,0:T(4,128)S(1)} %copy-done.5, s32[4,4]{1,0:T(4,128)S(1)} %copy-done.6, bf16[4,1,144,768]{3,2,1,0:T(8,128)(2,1)S(1)} %copy-done.1, bf16[2,1,144,768]{3,2,1,0:T(8,128)(2,1)S(1)} %collective-permute-done.refs_0_, ...), custom_call_target="tpu_custom_call" | custom-call | flops 254803968 | bytes 3124352 | tf_op jit(solution)/shard_map/middle/pallas_call | solution.py:284
  25.7 0.0 collective-permute-done.5.refs_0_
  25.7 0.7 %middle.3 = (f32[6,128,576]{2,1,0:T(8,128)S(1)}, f32[6,576]{1,0:T(8,128)S(1)}, f32[6,576]{1,0:T(8,128)S(1)}) custom-call(s32[4,4]{1,0:T(4,128)S(1)} %copy-done.5, s32[4,4]{1,0:T(4,128)S(1)} %copy-done.6, bf16[4,1,144,768]{3,2,1,0:T(8,128)(2,1)S(1)} %copy-done.1, bf16[2,1,144,768]{3,2,1,0:T(8,128)(2,1)S(1)} %collective-permute-done.5.refs_0_, ...), custom_call_target="tpu_custom_call" | custom-call | flops 254803968 | bytes 3124352 | tf_op jit(solution)/shard_map/middle/pallas_call | solution.py:284
  26.4 3.6 %collective-permute-done.4.refs_0_ = bf16[1,144,768]{2,1,0:T(8,128)(2,1)S(1)} collective-permute-done((bf16[1,144,768]{2,1,0:T(8,128)(2,1)S(1)}, bf16[1,144,768]{2,1,0:T(8,128)(2,1)S(1)}, u32[]{:S(2)}, u32[]{:S(2)}) %collective-permute-start.4) | collective-permute-done | bytes 221216 | tf_op jit(solution)/shard_map/ppermute | solution.py:31
  30.0 0.8 %score.1 = (f32[6,128,576]{2,1,0:T(8,128)S(1)}, bf16[6,144,576]{2,1,0:T(8,128)(2,1)S(1)}) custom-call(s32[4,4]{1,0:T(4,128)S(1)} %copy-done.5, s32[4,4]{1,0:T(4,128)S(1)} %copy-done.6, bf16[4,1,144,768]{3,2,1,0:T(8,128)(2,1)S(1)} %copy-done.1, bf16[1,144,768]{2,1,0:T(8,128)(2,1)S(1)} %collective-permute-done.4.refs_0_, ...), custom_call_target="tpu_custom_call" | custom-call | flops 127401984 | bytes 2903168 | tf_op jit(solution)/shard_map/score/pallas_call | solution.py:284
  30.8 2.3 %collective-permute-done.6.value_ref = bf16[1,144,512]{2,1,0:T(8,128)(2,1)S(1)} collective-permute-done((bf16[1,144,512]{2,1,0:T(8,128)(2,1)S(1)}, bf16[1,144,512]{2,1,0:T(8,128)(2,1)S(1)}, u32[]{:S(2)}, u32[]{:S(2)}) %collective-permute-start.6) | collective-permute-done | bytes 147488 | tf_op jit(solution)/shard_map/ppermute | solution.py:31
  33.2 0.6 %average.1 = (f32[4,144,512]{2,1,0:T(8,128)S(1)}, f32[1,576]{1,0:T(1,128)S(1)}) custom-call(f32[6,128,576]{2,1,0:T(8,128)S(1)} %get-tuple-element.42.acc_ref, bf16[6,144,576]{2,1,0:T(8,128)(2,1)S(1)} %get-tuple-element.43.w_ref, bf16[1,144,512]{2,1,0:T(8,128)(2,1)S(1)} %collective-permute-done.6.value_ref), custom_call_target="tpu_custom_call" | custom-call | flops 63700992 | bytes 2912256 | tf_op jit(solution)/shard_map/average/pallas_call | solution.py:284
  33.8 0.0 copy-start.3
  33.8 0.9 %collective-permute-done.7.value_ref = bf16[1,144,256]{2,1,0:T(8,128)(2,1)S(1)} collective-permute-done((bf16[1,144,256]{2,1,0:T(8,128)(2,1)S(1)}, bf16[1,144,256]{2,1,0:T(8,128)(2,1)S(1)}, u32[]{:S(2)}, u32[]{:S(2)}) %collective-permute-start.7) | collective-permute-done | bytes 73760 | tf_op jit(solution)/shard_map/ppermute | solution.py:31
  34.7 0.3 rest.1
  35.1 1.6 %collective-permute-start.8 = (f32[1,576]{1,0:T(1,128)S(1)}, f32[1,576]{1,0:T(1,128)S(1)}, u32[]{:S(2)}, u32[]{:S(2)}) collective-permute-start(f32[1,576]{1,0:T(1,128)S(1)} %get-tuple-element.47.square_in), channel_id=1, source_target_pairs={{0,2},{1,3},{2,0},{3,1},{4,6},{5,7},{6,4},{7,5},{8,10},{9,11},{10,... | collective-permute-start | bytes 6920 | tf_op jit(solution)/shard_map/ppermute | solution.py:40
  36.6 0.0 collective-permute-start.9
  36.6 0.2 turn.1
  36.9 0.7 %collective-permute-start.10 = (f32[1,576]{1,0:T(1,128)S(1)}, f32[1,576]{1,0:T(1,128)S(1)}, u32[]{:S(2)}, u32[]{:S(2)}) collective-permute-start(f32[1,576]{1,0:T(1,128)S(1)} %get-tuple-element.49.refs_0_), channel_id=1, source_target_pairs={{0,1},{1,0},{2,3},{3,2},{4,5},{5,4},{6,7},{7,6},{8,9},{9,8},{10,11... | collective-permute-start | bytes 6920 | tf_op jit(solution)/shard_map/ppermute | solution.py:40
  37.6 0.0 collective-permute-done.11.tail_ref
  37.6 0.0 copy-done.3
  37.6 1.4 %decode.1 = bf16[1,36,512]{2,1,0:T(8,128)(2,1)} custom-call(s32[1]{0:T(128)S(6)} %copy.11.fade_ref, bf16[36,512]{1,0:T(8,128)(2,1)S(1)} %get-tuple-element.50.hidden_ref, bf16[24,512]{1,0:T(8,128)(2,1)S(1)} %collective-permute-done.11.tail_ref, bf16[3,512,512]{2,1,0:T(8,128)(2,1)S(1)} %copy-done.3), custom_call_target="tpu_custom_call" | custom-call | flops 56623104 | bytes 1634308 | tf_op jit(solution)/shard_map/decode/pallas_call | solution.py:284
  39.0 0.0 collective-permute-done.10.refs_3_
  39.0 0.0 collective-permute-done.8.refs_1_
  39.0 0.6 %collective-permute-done.9.refs_2_ = f32[1,576]{1,0:T(1,128)S(1)} collective-permute-done((f32[1,576]{1,0:T(1,128)S(1)}, f32[1,576]{1,0:T(1,128)S(1)}, u32[]{:S(2)}, u32[]{:S(2)}) %collective-permute-start.9) | collective-permute-done | bytes 2336 | tf_op jit(solution)/shard_map/ppermute | solution.py:40
  39.6 1.1 %scale.1 = bf16[4,1,144,768]{3,2,1,0:T(8,128)(2,1)} custom-call(f32[4,144,512]{2,1,0:T(8,128)S(1)} %get-tuple-element.44.front_ref, f32[4,144,256]{2,1,0:T(8,128)S(1)} %get-tuple-element.48.back_ref, f32[1,576]{1,0:T(1,128)S(1)} %get-tuple-element.49.refs_0_, f32[1,576]{1,0:T(1,128)S(1)} %collective-permute-done.8.refs_1_, ...), custom_call_target="tpu_custom_call" | custom-call | flops 442368 | bytes 1778688 | tf_op jit(solution)/shard_map/scale/pallas_call | solution.py:284
  (6 shorter events, 0.0 us)
Async XLA Ops:
  0.6 15.2 %copy-start.7 = (bf16[2,1,144,768]{3,2,1,0:T(8,128)(2,1)S(1)}, bf16[2,1,144,768]{3,2,1,0:T(8,128)(2,1)}, u32[]{:S(2)}) copy-start(bf16[2,1,144,768]{3,2,1,0:T(8,128)(2,1)} %param.11) | copy-start | bytes 1327108
  0.6 15.1 %collective-permute-start = (bf16[2,1,144,768]{3,2,1,0:T(8,128)(2,1)}, bf16[2,1,144,768]{3,2,1,0:T(8,128)(2,1)S(1)}, u32[]{:S(2)}, u32[]{:S(2)}) collective-permute-start(bf16[2,1,144,768]{3,2,1,0:T(8,128)(2,1)} %param.11), channel_id=1, source_target_pairs={{0,8},{8,12},{1,9},{9,13},{2,10},{10,14},{3,11},{11,15},{16,24},{2... | collective-permute-start | bytes 1327112 | tf_op jit(solution)/shard_map/ppermute | solution.py:273
  6.6 8.5 %collective-permute-start.1 = (bf16[36,512]{1,0:T(8,128)(2,1)}, bf16[36,512]{1,0:T(8,128)(2,1)S(1)}, u32[]{:S(2)}, u32[]{:S(2)}) collective-permute-start(bf16[36,512]{1,0:T(8,128)(2,1)} %get-tuple-element.29), channel_id=1, source_target_pairs={{0,1},{1,0},{2,3},{3,2},{4,5},{5,4},{6,7},{7,6},{8,9},{9,8},{10,11... | collective-permute-start | bytes 110600 | tf_op jit(solution)/shard_map/ppermute | solution.py:40
  6.6 8.5 %collective-permute-start.2 = (bf16[36,512]{1,0:T(8,128)(2,1)}, bf16[36,512]{1,0:T(8,128)(2,1)S(1)}, u32[]{:S(2)}, u32[]{:S(2)}) collective-permute-start(bf16[36,512]{1,0:T(8,128)(2,1)} %get-tuple-element.30), channel_id=1, source_target_pairs={{0,2},{1,3},{2,0},{3,1},{4,6},{5,7},{6,4},{7,5},{8,10},{9,11},{10,... | collective-permute-start | bytes 110600 | tf_op jit(solution)/shard_map/ppermute | solution.py:40
  8.2 6.9 %collective-permute-start.3 = (bf16[36,512]{1,0:T(8,128)(2,1)}, bf16[36,512]{1,0:T(8,128)(2,1)S(1)}, u32[]{:S(2)}, u32[]{:S(2)}) collective-permute-start(bf16[36,512]{1,0:T(8,128)(2,1)} %get-tuple-element.31), channel_id=1, source_target_pairs={{0,3},{1,2},{2,1},{3,0},{4,7},{5,6},{6,5},{7,4},{8,11},{9,10},{10,... | collective-permute-start | bytes 110600 | tf_op jit(solution)/shard_map/ppermute | solution.py:40
  8.5 17.2 %collective-permute-start.5 = (bf16[2,1,144,768]{3,2,1,0:T(8,128)(2,1)}, bf16[2,1,144,768]{3,2,1,0:T(8,128)(2,1)S(1)}, u32[]{:S(2)}, u32[]{:S(2)}) collective-permute-start(bf16[2,1,144,768]{3,2,1,0:T(8,128)(2,1)} %param.11), channel_id=1, source_target_pairs={{4,12},{5,13},{6,14},{7,15},{20,28},{21,29},{22,30},{23,31}} | collective-permute-start | bytes 1327112 | tf_op jit(solution)/shard_map/ppermute | solution.py:273
  9.2 1.2 %copy-start = (bf16[4,1,144,768]{3,2,1,0:T(8,128)(2,1)S(1)}, bf16[4,1,144,768]{3,2,1,0:T(8,128)(2,1)}, u32[]{:S(2)}) copy-start(bf16[4,1,144,768]{3,2,1,0:T(8,128)(2,1)} %q_ref.7) | copy-start | bytes 2654212
  10.4 1.5 %copy-start.2 = (bf16[4,2,1,144,768]{4,3,2,1,0:T(8,128)(2,1)S(1)}, bf16[4,2,1,144,768]{4,3,2,1,0:T(8,128)(2,1)}, u32[]{:S(2)}) copy-start(bf16[4,2,1,144,768]{4,3,2,1,0:T(8,128)(2,1)} %kv_ref.1) | copy-start | bytes 5308420
  11.8 0.7 %copy-start.5 = (s32[4,4]{1,0:T(4,128)S(1)}, s32[4,4]{1,0:T(4,128)}, u32[]{:S(2)}) copy-start(s32[4,4]{1,0:T(4,128)} %step_ref.7) | copy-start | bytes 196
  12.5 2.6 %copy-start.4 = (bf16[36,512]{1,0:T(8,128)(2,1)S(1)}, bf16[36,512]{1,0:T(8,128)(2,1)}, u32[]{:S(2)}) copy-start(bf16[36,512]{1,0:T(8,128)(2,1)} %get-tuple-element.28.refs_0_) | copy-start | bytes 110596
  12.5 12.4 %copy-start.1 = (bf16[4,1,144,768]{3,2,1,0:T(8,128)(2,1)S(1)}, bf16[4,1,144,768]{3,2,1,0:T(8,128)(2,1)}, u32[]{:S(2)}) copy-start(bf16[4,1,144,768]{3,2,1,0:T(8,128)(2,1)} %q_ref.7) | copy-start | bytes 2654212
  12.5 12.4 %copy-start.6 = (s32[4,4]{1,0:T(4,128)S(1)}, s32[4,4]{1,0:T(4,128)}, u32[]{:S(2)}) copy-start(s32[4,4]{1,0:T(4,128)} %mask_ref.5) | copy-start | bytes 196
  15.8 14.2 %collective-permute-start.4 = (bf16[1,144,768]{2,1,0:T(8,128)(2,1)S(1)}, bf16[1,144,768]{2,1,0:T(8,128)(2,1)S(1)}, u32[]{:S(2)}, u32[]{:S(2)}) collective-permute-start(bf16[1,144,768]{2,1,0:T(8,128)(2,1)S(1)} %get-tuple-element.53), channel_id=1, source_target_pairs={{0,4},{4,8},{8,12},{1,5},{5,9},{9,13},{2,6},{6,10},{10,14},{3,7},{... | collective-permute-start | bytes 663560 | tf_op jit(solution)/shard_map/ppermute | solution.py:31
  18.5 14.7 %collective-permute-start.6 = (bf16[1,144,512]{2,1,0:T(8,128)(2,1)S(1)}, bf16[1,144,512]{2,1,0:T(8,128)(2,1)S(1)}, u32[]{:S(2)}, u32[]{:S(2)}) collective-permute-start(bf16[1,144,512]{2,1,0:T(8,128)(2,1)S(1)} %slice.24), channel_id=1, source_target_pairs={{0,4},{4,8},{8,12},{1,5},{5,9},{9,13},{2,6},{6,10},{10,14},{3,7},{... | collective-permute-start | bytes 442376 | tf_op jit(solution)/shard_map/ppermute | solution.py:31
  20.4 14.3 %collective-permute-start.7 = (bf16[1,144,256]{2,1,0:T(8,128)(2,1)S(1)}, bf16[1,144,256]{2,1,0:T(8,128)(2,1)S(1)}, u32[]{:S(2)}, u32[]{:S(2)}) collective-permute-start(bf16[1,144,256]{2,1,0:T(8,128)(2,1)S(1)} %slice.25), channel_id=1, source_target_pairs={{0,4},{4,8},{8,12},{1,5},{5,9},{9,13},{2,6},{6,10},{10,14},{3,7},{... | collective-permute-start | bytes 221192 | tf_op jit(solution)/shard_map/ppermute | solution.py:31
  23.0 14.6 %collective-permute-start.11 = (bf16[24,512]{1,0:T(8,128)(2,1)S(1)}, bf16[24,512]{1,0:T(8,128)(2,1)S(1)}, u32[]{:S(2)}, u32[]{:S(2)}) collective-permute-start(bf16[24,512]{1,0:T(8,128)(2,1)S(1)} %get-tuple-element.51), channel_id=1, source_target_pairs={{0,4},{4,8},{8,12},{1,5},{5,9},{9,13},{2,6},{6,10},{10,14},{3,7},{... | collective-permute-start | bytes 73736 | tf_op jit(solution)/shard_map/ppermute | solution.py:31
  33.8 3.8 %copy-start.3 = (bf16[3,512,512]{2,1,0:T(8,128)(2,1)S(1)}, bf16[3,512,512]{2,1,0:T(8,128)(2,1)}, u32[]{:S(2)}) copy-start(bf16[3,512,512]{2,1,0:T(8,128)(2,1)} %conv_ref.1) | copy-start | bytes 4718596
  35.1 3.9 %collective-permute-start.8 = (f32[1,576]{1,0:T(1,128)S(1)}, f32[1,576]{1,0:T(1,128)S(1)}, u32[]{:S(2)}, u32[]{:S(2)}) collective-permute-start(f32[1,576]{1,0:T(1,128)S(1)} %get-tuple-element.47.square_in), channel_id=1, source_target_pairs={{0,2},{1,3},{2,0},{3,1},{4,6},{5,7},{6,4},{7,5},{8,10},{9,11},{10,... | collective-permute-start | bytes 6920 | tf_op jit(solution)/shard_map/ppermute | solution.py:40
  36.6 3.0 %collective-permute-start.9 = (f32[1,576]{1,0:T(1,128)S(1)}, f32[1,576]{1,0:T(1,128)S(1)}, u32[]{:S(2)}, u32[]{:S(2)}) collective-permute-start(f32[1,576]{1,0:T(1,128)S(1)} %get-tuple-element.47.square_in), channel_id=1, source_target_pairs={{0,3},{1,2},{2,1},{3,0},{4,7},{5,6},{6,5},{7,4},{8,11},{9,10},{10,... | collective-permute-start | bytes 6920 | tf_op jit(solution)/shard_map/ppermute | solution.py:40
  36.9 2.1 %collective-permute-start.10 = (f32[1,576]{1,0:T(1,128)S(1)}, f32[1,576]{1,0:T(1,128)S(1)}, u32[]{:S(2)}, u32[]{:S(2)}) collective-permute-start(f32[1,576]{1,0:T(1,128)S(1)} %get-tuple-element.49.refs_0_), channel_id=1, source_target_pairs={{0,1},{1,0},{2,3},{3,2},{4,5},{5,4},{6,7},{7,6},{8,9},{9,8},{10,11... | collective-permute-start | bytes 6920 | tf_op jit(solution)/shard_map/ppermute | solution.py:40

commit v5 on v4

--- a/solution.py
+++ b/solution.py
@@ -239,11 +239,15 @@
     square_ref[...] = squares
 
 
-def turn_kernel(in_ref, square_in, out_ref, square_ref):
+def turn_kernel(in_ref, *refs):
+    square_refs, (out_ref, square_ref) = refs[:-2], refs[-2:]
     steps, rows, _ = out_ref.shape
+    squares = square_refs[0][...]
+    for ref in square_refs[1:]:
+        squares = squares + ref[...]
+    square_ref[...] = squares
     for head in range(in_ref.shape[0]):
         out_ref[:, :, head * HD : (head + 1) * HD] = in_ref[head].T.reshape(steps, rows, HD)
-    square_ref[...] = square_in[...]
 
 
 def scale_kernel(width, front_ref, back_ref, *refs):
@@ -423,7 +427,7 @@
 ):
     steps, _, rows, columns = query.shape
     heads = columns // HD
-    middle = -(-2 * heads // 3) * HD
+    middle = (heads - max(1, heads // 3)) * HD
     row_count = steps * rows
     span = lax.axis_size("span")
     axes = ("mp", "seq")
@@ -495,15 +499,15 @@
         pair_flops // 4,
         (acc, weights, values[1], squares),
     )
-    others = [swap(squares, axes, offset) for offset in range(2, lax.axis_size(axes))]
+    within = [swap(squares, "seq", offset) for offset in range(1, lax.axis_size("seq"))]
     back, squares = plain_call(
         turn_kernel,
         "turn",
         [jax.ShapeDtypeStruct((steps, rows, columns - middle), jnp.float32), square_shape],
         row_count * columns,
-        (averaged, squares),
-    )
-    others.append(swap(squares, axes, 1))
+        (averaged, squares, *within),
+    )
+    others = [swap(squares, "mp", offset) for offset in range(1, lax.axis_size("mp"))]
     decoded = decode(after(hidden, back), tail, conv_w, fade_count)
     attended = plain_call(
         functools.partial(scale_kernel, columns * lax.axis_size(axes)),

time: 41.1 us -> 41.6 us (1.012)
  Pallas kernels: 11 us -> 13.9 us
  waiting for transfers between devices: 8 us -> 6.25 us
  starting transfers between devices: 16.8 us -> 16.2 us
    pallas_call x11, Pallas kernels: 11 us -> 13.9 us  [plain_call(): pl.pallas_call(kernel, in_specs=list(in_specs) + [VMEM_SPEC] * (len(opera...]
    ppermute x4, waiting for transfers between devices: 6.84 us -> 4.56 us  [hop(): lax.ppermute(value, axis, [(source, source + steps) for source in range(c...]
    ppermute x6 -> x5, starting transfers between devices: 4.2 us -> 3.56 us  [swap(): return lax.ppermute(value, axes, pairs)]
    ppermute x6 -> x5, waiting for transfers between devices: 0.65 us -> 1.17 us  [swap(): return lax.ppermute(value, axes, pairs)]
  transfers between devices with their start and end apart: 12 -> 11, of which waited for: 5 -> 6; matrix products, arithmetic and copies ran while one was open for 0% -> 0% of each run, Pallas kernels for 24% -> 31%
where the time goes in v5:
time: 41.6 us; the launch traced here: 41.3 us
  starting transfers between devices  16.2 us (39%)
  Pallas kernels  13.9 us (33%)
  waiting for transfers between devices  6.25 us (15%)
  local copies, waits for them, and re-layouts  3.36 us (8%)
  between operations  1.5 us (4%)
    pallas_call x11, Pallas kernels, plain_call(): pl.pallas_call(kernel, in_specs=list(in_specs) + [VMEM_SPEC] * (len(opera...  13.9 us
    ppermute x4, starting transfers between devices, hop(): lax.ppermute(value, axis, [(source, source + steps) for source in range(c...  8.35 us
    ppermute x4, waiting for transfers between devices, hop(): lax.ppermute(value, axis, [(source, source + steps) for source in range(c...  4.56 us
    ppermute x2, starting transfers between devices, send(): return lax.ppermute(value, 'span', pairs)  4.3 us
    ppermute x5, starting transfers between devices, swap(): return lax.ppermute(value, axes, pairs)  3.56 us
    unnamed x16, local copies, waits for them, and re-layouts  3.34 us
    ppermute x5, waiting for transfers between devices, swap(): return lax.ppermute(value, axes, pairs)  1.17 us
  transfers between devices with their start and end apart: 11, of which 6 were waited for; matrix products, arithmetic and copies ran while one was open for 0% of the time, Pallas kernels for 31%

profile of v5, /device:TPU:20, one launch (start us, length us, event | category | flops | bytes accessed | tf_op | source)
XLA Modules:
  0.0 41.3 jit_solution(5977794053656265054)
XLA Ops:
  0.6 0.0 copy-start.7
  0.6 3.6 %collective-permute-start = (bf16[2,1,144,768]{3,2,1,0:T(8,128)(2,1)}, bf16[2,1,144,768]{3,2,1,0:T(8,128)(2,1)S(1)}, u32[]{:S(2)}, u32[]{:S(2)}) collective-permute-start(bf16[2,1,144,768]{3,2,1,0:T(8,128)(2,1)} %param.11), channel_id=1, source_target_pairs={{0,8},{8,12},{1,9},{9,13},{2,10},{10,14},{3,11},{11,15},{16,24},{2... | collective-permute-start | bytes 1327112 | tf_op jit(solution)/shard_map/ppermute | solution.py:277
  4.3 2.3 %project.1 = (bf16[36,512]{1,0:T(8,128)(2,1)}, bf16[36,512]{1,0:T(8,128)(2,1)}, bf16[36,512]{1,0:T(8,128)(2,1)}, bf16[36,512]{1,0:T(8,128)(2,1)}) custom-call(bf16[1,144,768]{2,1,0:T(8,128)(2,1)} %x_hbm.1, bf16[768,512]{1,0:T(8,128)(2,1)} %w_hbm.1), custom_call_target="tpu_custom_call" | custom-call | flops 113246208 | bytes 1007616 | tf_op jit(solution)/shard_map/project/pallas_call | solution.py:288
  6.6 0.1 collective-permute-start.1
  6.6 1.6 %collective-permute-start.2 = (bf16[36,512]{1,0:T(8,128)(2,1)}, bf16[36,512]{1,0:T(8,128)(2,1)S(1)}, u32[]{:S(2)}, u32[]{:S(2)}) collective-permute-start(bf16[36,512]{1,0:T(8,128)(2,1)} %get-tuple-element.30), channel_id=1, source_target_pairs={{0,2},{1,3},{2,0},{3,1},{4,6},{5,7},{6,4},{7,5},{8,10},{9,11},{10,... | collective-permute-start | bytes 110600 | tf_op jit(solution)/shard_map/ppermute | solution.py:40
  8.2 0.3 collective-permute-start.3
  8.5 0.7 %collective-permute-start.5 = (bf16[2,1,144,768]{3,2,1,0:T(8,128)(2,1)}, bf16[2,1,144,768]{3,2,1,0:T(8,128)(2,1)S(1)}, u32[]{:S(2)}, u32[]{:S(2)}) collective-permute-start(bf16[2,1,144,768]{3,2,1,0:T(8,128)(2,1)} %param.11), channel_id=1, source_target_pairs={{4,12},{5,13},{6,14},{7,15},{20,28},{21,29},{22,30},{23,31}} | collective-permute-start | bytes 1327112 | tf_op jit(solution)/shard_map/ppermute | solution.py:277
  9.2 0.0 copy-start
  9.2 1.2 %copy-done = bf16[4,1,144,768]{3,2,1,0:T(8,128)(2,1)S(1)} copy-done((bf16[4,1,144,768]{3,2,1,0:T(8,128)(2,1)S(1)}, bf16[4,1,144,768]{3,2,1,0:T(8,128)(2,1)}, u32[]{:S(2)}) %copy-start) | copy-done | bytes 884760
  10.4 1.5 %copy-done.2 = bf16[4,2,1,144,768]{4,3,2,1,0:T(8,128)(2,1)S(1)} copy-done((bf16[4,2,1,144,768]{4,3,2,1,0:T(8,128)(2,1)S(1)}, bf16[4,2,1,144,768]{4,3,2,1,0:T(8,128)(2,1)}, u32[]{:S(2)}) %copy-start.2) | copy-done | bytes 1769496
  11.8 0.0 copy-start.5
  11.8 0.7 %copy-done.5 = s32[4,4]{1,0:T(4,128)S(1)} copy-done((s32[4,4]{1,0:T(4,128)S(1)}, s32[4,4]{1,0:T(4,128)}, u32[]{:S(2)}) %copy-start.5) | copy-done | bytes 88
  12.5 0.0 copy-start.4
  12.5 0.0 copy-start.1
  12.5 2.5 %own.1 = (f32[6,128,576]{2,1,0:T(8,128)S(1)}, f32[6,576]{1,0:T(8,128)S(1)}, f32[6,576]{1,0:T(8,128)S(1)}) custom-call(s32[4,4]{1,0:T(4,128)S(1)} %copy-done.5, bf16[4,1,144,768]{3,2,1,0:T(8,128)(2,1)S(1)} %copy-done, bf16[4,2,1,144,768]{4,3,2,1,0:T(8,128)(2,1)S(1)} %copy-done.2), custom_call_target="tpu_custom_call" | custom-call | flops 254803968 | bytes 2654272 | tf_op jit(solution)/shard_map/own/pallas_call | solution.py:288
  15.1 0.0 collective-permute-done.1.refs_1_
  15.1 0.0 collective-permute-done.2.refs_2_
  15.1 0.0 collective-permute-done.3.refs_3_
  15.1 0.0 copy-done.4
  15.1 0.1 gather.1
  15.3 0.5 %collective-permute-done.refs_0_ = bf16[2,1,144,768]{3,2,1,0:T(8,128)(2,1)S(1)} collective-permute-done((bf16[2,1,144,768]{3,2,1,0:T(8,128)(2,1)}, bf16[2,1,144,768]{3,2,1,0:T(8,128)(2,1)S(1)}, u32[]{:S(2)}, u32[]{:S(2)}) %collective-permute-start) | collective-permute-done | bytes 442400 | tf_op jit(solution)/shard_map/ppermute | solution.py:277
  15.8 0.0 copy-done.7
  15.8 0.1 select_bitcast_fusion
  15.8 2.6 %collective-permute-start.4 = (bf16[1,144,768]{2,1,0:T(8,128)(2,1)S(1)}, bf16[1,144,768]{2,1,0:T(8,128)(2,1)S(1)}, u32[]{:S(2)}, u32[]{:S(2)}) collective-permute-start(bf16[1,144,768]{2,1,0:T(8,128)(2,1)S(1)} %get-tuple-element.53), channel_id=1, source_target_pairs={{0,4},{4,8},{8,12},{1,5},{5,9},{9,13},{2,6},{6,10},{10,14},{3,7},{... | collective-permute-start | bytes 663560 | tf_op jit(solution)/shard_map/ppermute | solution.py:31
  18.5 1.9 %collective-permute-start.6 = (bf16[1,144,512]{2,1,0:T(8,128)(2,1)S(1)}, bf16[1,144,512]{2,1,0:T(8,128)(2,1)S(1)}, u32[]{:S(2)}, u32[]{:S(2)}) collective-permute-start(bf16[1,144,512]{2,1,0:T(8,128)(2,1)S(1)} %slice.24), channel_id=1, source_target_pairs={{0,4},{4,8},{8,12},{1,5},{5,9},{9,13},{2,6},{6,10},{10,14},{3,7},{... | collective-permute-start | bytes 442376 | tf_op jit(solution)/shard_map/ppermute | solution.py:31
  20.4 1.9 %collective-permute-start.7 = (bf16[1,144,256]{2,1,0:T(8,128)(2,1)S(1)}, bf16[1,144,256]{2,1,0:T(8,128)(2,1)S(1)}, u32[]{:S(2)}, u32[]{:S(2)}) collective-permute-start(bf16[1,144,256]{2,1,0:T(8,128)(2,1)S(1)} %slice.25), channel_id=1, source_target_pairs={{0,4},{4,8},{8,12},{1,5},{5,9},{9,13},{2,6},{6,10},{10,14},{3,7},{... | collective-permute-start | bytes 221192 | tf_op jit(solution)/shard_map/ppermute | solution.py:31
  22.3 1.9 %collective-permute-start.10 = (bf16[24,512]{1,0:T(8,128)(2,1)S(1)}, bf16[24,512]{1,0:T(8,128)(2,1)S(1)}, u32[]{:S(2)}, u32[]{:S(2)}) collective-permute-start(bf16[24,512]{1,0:T(8,128)(2,1)S(1)} %get-tuple-element.51), channel_id=1, source_target_pairs={{0,4},{4,8},{8,12},{1,5},{5,9},{9,13},{2,6},{6,10},{10,14},{3,7},{... | collective-permute-start | bytes 73736 | tf_op jit(solution)/shard_map/ppermute | solution.py:31
  24.3 0.0 copy-done.1
  24.3 0.0 copy-done.6
  24.3 2.7 %middle.2 = (f32[6,128,576]{2,1,0:T(8,128)S(1)}, f32[6,576]{1,0:T(8,128)S(1)}, f32[6,576]{1,0:T(8,128)S(1)}) custom-call(s32[4,4]{1,0:T(4,128)S(1)} %copy-done.5, s32[4,4]{1,0:T(4,128)S(1)} %copy-done.6, bf16[4,1,144,768]{3,2,1,0:T(8,128)(2,1)S(1)} %copy-done.1, bf16[2,1,144,768]{3,2,1,0:T(8,128)(2,1)S(1)} %collective-permute-done.refs_0_, ...), custom_call_target="tpu_custom_call" | custom-call | flops 254803968 | bytes 3124352 | tf_op jit(solution)/shard_map/middle/pallas_call | solution.py:288
  27.0 0.0 collective-permute-done.5.refs_0_
  27.0 0.7 %middle.3 = (f32[6,128,576]{2,1,0:T(8,128)S(1)}, f32[6,576]{1,0:T(8,128)S(1)}, f32[6,576]{1,0:T(8,128)S(1)}) custom-call(s32[4,4]{1,0:T(4,128)S(1)} %copy-done.5, s32[4,4]{1,0:T(4,128)S(1)} %copy-done.6, bf16[4,1,144,768]{3,2,1,0:T(8,128)(2,1)S(1)} %copy-done.1, bf16[2,1,144,768]{3,2,1,0:T(8,128)(2,1)S(1)} %collective-permute-done.5.refs_0_, ...), custom_call_target="tpu_custom_call" | custom-call | flops 254803968 | bytes 3124352 | tf_op jit(solution)/shard_map/middle/pallas_call | solution.py:288
  27.8 2.2 %collective-permute-done.4.refs_0_ = bf16[1,144,768]{2,1,0:T(8,128)(2,1)S(1)} collective-permute-done((bf16[1,144,768]{2,1,0:T(8,128)(2,1)S(1)}, bf16[1,144,768]{2,1,0:T(8,128)(2,1)S(1)}, u32[]{:S(2)}, u32[]{:S(2)}) %collective-permute-start.4) | collective-permute-done | bytes 221216 | tf_op jit(solution)/shard_map/ppermute | solution.py:31
  30.0 1.8 %score.1 = (f32[6,128,576]{2,1,0:T(8,128)S(1)}, bf16[6,144,576]{2,1,0:T(8,128)(2,1)S(1)}) custom-call(s32[4,4]{1,0:T(4,128)S(1)} %copy-done.5, s32[4,4]{1,0:T(4,128)S(1)} %copy-done.6, bf16[4,1,144,768]{3,2,1,0:T(8,128)(2,1)S(1)} %copy-done.1, bf16[1,144,768]{2,1,0:T(8,128)(2,1)S(1)} %collective-permute-done.4.refs_0_, ...), custom_call_target="tpu_custom_call" | custom-call | flops 127401984 | bytes 2903168 | tf_op jit(solution)/shard_map/score/pallas_call | solution.py:288
  31.8 1.4 %collective-permute-done.6.value_ref = bf16[1,144,512]{2,1,0:T(8,128)(2,1)S(1)} collective-permute-done((bf16[1,144,512]{2,1,0:T(8,128)(2,1)S(1)}, bf16[1,144,512]{2,1,0:T(8,128)(2,1)S(1)}, u32[]{:S(2)}, u32[]{:S(2)}) %collective-permute-start.6) | collective-permute-done | bytes 147488 | tf_op jit(solution)/shard_map/ppermute | solution.py:31
  33.2 0.6 %average.1 = (f32[4,144,512]{2,1,0:T(8,128)S(1)}, f32[1,576]{1,0:T(1,128)S(1)}) custom-call(f32[6,128,576]{2,1,0:T(8,128)S(1)} %get-tuple-element.42.acc_ref, bf16[6,144,576]{2,1,0:T(8,128)(2,1)S(1)} %get-tuple-element.43.w_ref, bf16[1,144,512]{2,1,0:T(8,128)(2,1)S(1)} %collective-permute-done.6.value_ref), custom_call_target="tpu_custom_call" | custom-call | flops 63700992 | bytes 2912256 | tf_op jit(solution)/shard_map/average/pallas_call | solution.py:288
  33.8 0.0 copy-start.3
  33.8 0.9 %collective-permute-done.7.value_ref = bf16[1,144,256]{2,1,0:T(8,128)(2,1)S(1)} collective-permute-done((bf16[1,144,256]{2,1,0:T(8,128)(2,1)S(1)}, bf16[1,144,256]{2,1,0:T(8,128)(2,1)S(1)}, u32[]{:S(2)}, u32[]{:S(2)}) %collective-permute-start.7) | collective-permute-done | bytes 73760 | tf_op jit(solution)/shard_map/ppermute | solution.py:31
  34.7 0.3 rest.1
  35.1 0.1 collective-permute-start.8
  35.8 0.5 %collective-permute-done.8.refs_1_ = f32[1,576]{1,0:T(1,128)S(1)} collective-permute-done((f32[1,576]{1,0:T(1,128)S(1)}, f32[1,576]{1,0:T(1,128)S(1)}, u32[]{:S(2)}, u32[]{:S(2)}) %collective-permute-start.8) | collective-permute-done | bytes 2336 | tf_op jit(solution)/shard_map/ppermute | solution.py:40
  36.3 0.2 turn.1
  36.5 1.6 %collective-permute-start.9 = (f32[1,576]{1,0:T(1,128)S(1)}, f32[1,576]{1,0:T(1,128)S(1)}, u32[]{:S(2)}, u32[]{:S(2)}) collective-permute-start(f32[1,576]{1,0:T(1,128)S(1)} %get-tuple-element.49.refs_0_), channel_id=1, source_target_pairs={{0,2},{2,0},{1,3},{3,1},{4,6},{6,4},{5,7},{7,5},{8,10},{10,8},{9,1... | collective-permute-start | bytes 6920 | tf_op jit(solution)/shard_map/ppermute | solution.py:40
  38.1 0.0 collective-permute-done.10.tail_ref
  38.1 0.0 copy-done.3
  38.1 1.4 %decode.1 = bf16[1,36,512]{2,1,0:T(8,128)(2,1)} custom-call(s32[1]{0:T(128)S(6)} %copy.11.fade_ref, bf16[36,512]{1,0:T(8,128)(2,1)S(1)} %get-tuple-element.50.hidden_ref, bf16[24,512]{1,0:T(8,128)(2,1)S(1)} %collective-permute-done.10.tail_ref, bf16[3,512,512]{2,1,0:T(8,128)(2,1)S(1)} %copy-done.3), custom_call_target="tpu_custom_call" | custom-call | flops 56623104 | bytes 1634308 | tf_op jit(solution)/shard_map/decode/pallas_call | solution.py:288
  39.5 0.7 %collective-permute-done.9.refs_1_ = f32[1,576]{1,0:T(1,128)S(1)} collective-permute-done((f32[1,576]{1,0:T(1,128)S(1)}, f32[1,576]{1,0:T(1,128)S(1)}, u32[]{:S(2)}, u32[]{:S(2)}) %collective-permute-start.9) | collective-permute-done | bytes 2336 | tf_op jit(solution)/shard_map/ppermute | solution.py:40
  40.2 1.1 %scale.1 = bf16[4,1,144,768]{3,2,1,0:T(8,128)(2,1)} custom-call(f32[4,144,512]{2,1,0:T(8,128)S(1)} %get-tuple-element.44.front_ref, f32[4,144,256]{2,1,0:T(8,128)S(1)} %get-tuple-element.48.back_ref, f32[1,576]{1,0:T(1,128)S(1)} %get-tuple-element.49.refs_0_, f32[1,576]{1,0:T(1,128)S(1)} %collective-permute-done.9.refs_1_), custom_call_target="tpu_custom_call" | custom-call | flops 442368 | bytes 1774080 | tf_op jit(solution)/shard_map/scale/pallas_call | solution.py:288
  (4 shorter events, 0.0 us)
Async XLA Ops:
  0.6 15.2 %copy-start.7 = (bf16[2,1,144,768]{3,2,1,0:T(8,128)(2,1)S(1)}, bf16[2,1,144,768]{3,2,1,0:T(8,128)(2,1)}, u32[]{:S(2)}) copy-start(bf16[2,1,144,768]{3,2,1,0:T(8,128)(2,1)} %param.11) | copy-start | bytes 1327108
  0.6 15.1 %collective-permute-start = (bf16[2,1,144,768]{3,2,1,0:T(8,128)(2,1)}, bf16[2,1,144,768]{3,2,1,0:T(8,128)(2,1)S(1)}, u32[]{:S(2)}, u32[]{:S(2)}) collective-permute-start(bf16[2,1,144,768]{3,2,1,0:T(8,128)(2,1)} %param.11), channel_id=1, source_target_pairs={{0,8},{8,12},{1,9},{9,13},{2,10},{10,14},{3,11},{11,15},{16,24},{2... | collective-permute-start | bytes 1327112 | tf_op jit(solution)/shard_map/ppermute | solution.py:277
  6.6 8.5 %collective-permute-start.1 = (bf16[36,512]{1,0:T(8,128)(2,1)}, bf16[36,512]{1,0:T(8,128)(2,1)S(1)}, u32[]{:S(2)}, u32[]{:S(2)}) collective-permute-start(bf16[36,512]{1,0:T(8,128)(2,1)} %get-tuple-element.29), channel_id=1, source_target_pairs={{0,1},{1,0},{2,3},{3,2},{4,5},{5,4},{6,7},{7,6},{8,9},{9,8},{10,11... | collective-permute-start | bytes 110600 | tf_op jit(solution)/shard_map/ppermute | solution.py:40
  6.6 8.4 %collective-permute-start.2 = (bf16[36,512]{1,0:T(8,128)(2,1)}, bf16[36,512]{1,0:T(8,128)(2,1)S(1)}, u32[]{:S(2)}, u32[]{:S(2)}) collective-permute-start(bf16[36,512]{1,0:T(8,128)(2,1)} %get-tuple-element.30), channel_id=1, source_target_pairs={{0,2},{1,3},{2,0},{3,1},{4,6},{5,7},{6,4},{7,5},{8,10},{9,11},{10,... | collective-permute-start | bytes 110600 | tf_op jit(solution)/shard_map/ppermute | solution.py:40
  8.2 6.9 %collective-permute-start.3 = (bf16[36,512]{1,0:T(8,128)(2,1)}, bf16[36,512]{1,0:T(8,128)(2,1)S(1)}, u32[]{:S(2)}, u32[]{:S(2)}) collective-permute-start(bf16[36,512]{1,0:T(8,128)(2,1)} %get-tuple-element.31), channel_id=1, source_target_pairs={{0,3},{1,2},{2,1},{3,0},{4,7},{5,6},{6,5},{7,4},{8,11},{9,10},{10,... | collective-permute-start | bytes 110600 | tf_op jit(solution)/shard_map/ppermute | solution.py:40
  8.5 18.5 %collective-permute-start.5 = (bf16[2,1,144,768]{3,2,1,0:T(8,128)(2,1)}, bf16[2,1,144,768]{3,2,1,0:T(8,128)(2,1)S(1)}, u32[]{:S(2)}, u32[]{:S(2)}) collective-permute-start(bf16[2,1,144,768]{3,2,1,0:T(8,128)(2,1)} %param.11), channel_id=1, source_target_pairs={{4,12},{5,13},{6,14},{7,15},{20,28},{21,29},{22,30},{23,31}} | collective-permute-start | bytes 1327112 | tf_op jit(solution)/shard_map/ppermute | solution.py:277
  9.2 1.2 %copy-start = (bf16[4,1,144,768]{3,2,1,0:T(8,128)(2,1)S(1)}, bf16[4,1,144,768]{3,2,1,0:T(8,128)(2,1)}, u32[]{:S(2)}) copy-start(bf16[4,1,144,768]{3,2,1,0:T(8,128)(2,1)} %q_ref.7) | copy-start | bytes 2654212
  10.4 1.5 %copy-start.2 = (bf16[4,2,1,144,768]{4,3,2,1,0:T(8,128)(2,1)S(1)}, bf16[4,2,1,144,768]{4,3,2,1,0:T(8,128)(2,1)}, u32[]{:S(2)}) copy-start(bf16[4,2,1,144,768]{4,3,2,1,0:T(8,128)(2,1)} %kv_ref.1) | copy-start | bytes 5308420
  11.8 0.7 %copy-start.5 = (s32[4,4]{1,0:T(4,128)S(1)}, s32[4,4]{1,0:T(4,128)}, u32[]{:S(2)}) copy-start(s32[4,4]{1,0:T(4,128)} %step_ref.7) | copy-start | bytes 196
  12.5 2.6 %copy-start.4 = (bf16[36,512]{1,0:T(8,128)(2,1)S(1)}, bf16[36,512]{1,0:T(8,128)(2,1)}, u32[]{:S(2)}) copy-start(bf16[36,512]{1,0:T(8,128)(2,1)} %get-tuple-element.28.refs_0_) | copy-start | bytes 110596
  12.5 11.7 %copy-start.1 = (bf16[4,1,144,768]{3,2,1,0:T(8,128)(2,1)S(1)}, bf16[4,1,144,768]{3,2,1,0:T(8,128)(2,1)}, u32[]{:S(2)}) copy-start(bf16[4,1,144,768]{3,2,1,0:T(8,128)(2,1)} %q_ref.7) | copy-start | bytes 2654212
  12.5 11.7 %copy-start.6 = (s32[4,4]{1,0:T(4,128)S(1)}, s32[4,4]{1,0:T(4,128)}, u32[]{:S(2)}) copy-start(s32[4,4]{1,0:T(4,128)} %mask_ref.5) | copy-start | bytes 196
  15.8 14.2 %collective-permute-start.4 = (bf16[1,144,768]{2,1,0:T(8,128)(2,1)S(1)}, bf16[1,144,768]{2,1,0:T(8,128)(2,1)S(1)}, u32[]{:S(2)}, u32[]{:S(2)}) collective-permute-start(bf16[1,144,768]{2,1,0:T(8,128)(2,1)S(1)} %get-tuple-element.53), channel_id=1, source_target_pairs={{0,4},{4,8},{8,12},{1,5},{5,9},{9,13},{2,6},{6,10},{10,14},{3,7},{... | collective-permute-start | bytes 663560 | tf_op jit(solution)/shard_map/ppermute | solution.py:31
  18.5 14.7 %collective-permute-start.6 = (bf16[1,144,512]{2,1,0:T(8,128)(2,1)S(1)}, bf16[1,144,512]{2,1,0:T(8,128)(2,1)S(1)}, u32[]{:S(2)}, u32[]{:S(2)}) collective-permute-start(bf16[1,144,512]{2,1,0:T(8,128)(2,1)S(1)} %slice.24), channel_id=1, source_target_pairs={{0,4},{4,8},{8,12},{1,5},{5,9},{9,13},{2,6},{6,10},{10,14},{3,7},{... | collective-permute-start | bytes 442376 | tf_op jit(solution)/shard_map/ppermute | solution.py:31
  20.4 14.3 %collective-permute-start.7 = (bf16[1,144,256]{2,1,0:T(8,128)(2,1)S(1)}, bf16[1,144,256]{2,1,0:T(8,128)(2,1)S(1)}, u32[]{:S(2)}, u32[]{:S(2)}) collective-permute-start(bf16[1,144,256]{2,1,0:T(8,128)(2,1)S(1)} %slice.25), channel_id=1, source_target_pairs={{0,4},{4,8},{8,12},{1,5},{5,9},{9,13},{2,6},{6,10},{10,14},{3,7},{... | collective-permute-start | bytes 221192 | tf_op jit(solution)/shard_map/ppermute | solution.py:31
  22.3 15.8 %collective-permute-start.10 = (bf16[24,512]{1,0:T(8,128)(2,1)S(1)}, bf16[24,512]{1,0:T(8,128)(2,1)S(1)}, u32[]{:S(2)}, u32[]{:S(2)}) collective-permute-start(bf16[24,512]{1,0:T(8,128)(2,1)S(1)} %get-tuple-element.51), channel_id=1, source_target_pairs={{0,4},{4,8},{8,12},{1,5},{5,9},{9,13},{2,6},{6,10},{10,14},{3,7},{... | collective-permute-start | bytes 73736 | tf_op jit(solution)/shard_map/ppermute | solution.py:31
  33.8 4.3 %copy-start.3 = (bf16[3,512,512]{2,1,0:T(8,128)(2,1)S(1)}, bf16[3,512,512]{2,1,0:T(8,128)(2,1)}, u32[]{:S(2)}) copy-start(bf16[3,512,512]{2,1,0:T(8,128)(2,1)} %conv_ref.1) | copy-start | bytes 4718596
  35.1 1.2 %collective-permute-start.8 = (f32[1,576]{1,0:T(1,128)S(1)}, f32[1,576]{1,0:T(1,128)S(1)}, u32[]{:S(2)}, u32[]{:S(2)}) collective-permute-start(f32[1,576]{1,0:T(1,128)S(1)} %get-tuple-element.47.refs_0_), channel_id=1, source_target_pairs={{0,1},{1,0},{2,3},{3,2},{4,5},{5,4},{6,7},{7,6},{8,9},{9,8},{10,11... | collective-permute-start | bytes 6920 | tf_op jit(solution)/shard_map/ppermute | solution.py:40
  36.5 3.7 %collective-permute-start.9 = (f32[1,576]{1,0:T(1,128)S(1)}, f32[1,576]{1,0:T(1,128)S(1)}, u32[]{:S(2)}, u32[]{:S(2)}) collective-permute-start(f32[1,576]{1,0:T(1,128)S(1)} %get-tuple-element.49.refs_0_), channel_id=1, source_target_pairs={{0,2},{2,0},{1,3},{3,1},{4,6},{6,4},{5,7},{7,5},{8,10},{10,8},{9,1... | collective-permute-start | bytes 6920 | tf_op jit(solution)/shard_map/ppermute | solution.py:40

commit v6 on v4

--- a/solution.py
+++ b/solution.py
@@ -423,7 +423,7 @@
 ):
     steps, _, rows, columns = query.shape
     heads = columns // HD
-    middle = -(-2 * heads // 3) * HD
+    middle = (heads - max(1, heads // 3)) * HD
     row_count = steps * rows
     span = lax.axis_size("span")
     axes = ("mp", "seq")
@@ -495,7 +495,7 @@
         pair_flops // 4,
         (acc, weights, values[1], squares),
     )
-    others = [swap(squares, axes, offset) for offset in range(2, lax.axis_size(axes))]
+    others = [swap(squares, axes, offset) for offset in range(lax.axis_size(axes) - 1, 1, -1)]
     back, squares = plain_call(
         turn_kernel,
         "turn",

time: 41.1 us -> 41.3 us (level)
  waiting for transfers between devices: 8 us -> 8.46 us
    ppermute x6, waiting for transfers between devices: 0.65 us -> 1.1 us  [swap(): return lax.ppermute(value, axes, pairs)]
where the time goes in v6:
time: 41.3 us; the launch traced here: 40.9 us
  starting transfers between devices  16.6 us (40%)
  Pallas kernels  11 us (27%)
  waiting for transfers between devices  8.46 us (20%)
  local copies, waits for them, and re-layouts  3.36 us (8%)
  between operations  1.5 us (4%)
    pallas_call x11, Pallas kernels, plain_call(): pl.pallas_call(kernel, in_specs=list(in_specs) + [VMEM_SPEC] * (len(opera...  11 us
    ppermute x4, starting transfers between devices, hop(): lax.ppermute(value, axis, [(source, source + steps) for source in range(c...  8.35 us
    ppermute x4, waiting for transfers between devices, hop(): lax.ppermute(value, axis, [(source, source + steps) for source in range(c...  6.84 us
    ppermute x2, starting transfers between devices, send(): return lax.ppermute(value, 'span', pairs)  4.3 us
    ppermute x6, starting transfers between devices, swap(): return lax.ppermute(value, axes, pairs)  3.92 us
    unnamed x16, local copies, waits for them, and re-layouts  3.34 us
    ppermute x6, waiting for transfers between devices, swap(): return lax.ppermute(value, axes, pairs)  1.1 us
  transfers between devices with their start and end apart: 12, of which 5 were waited for; matrix products, arithmetic and copies ran while one was open for 0% of the time, Pallas kernels for 24%

profile of v6, /device:TPU:20, one launch (start us, length us, event | category | flops | bytes accessed | tf_op | source)
XLA Modules:
  0.0 40.9 jit_solution(11089205703549195986)
XLA Ops:
  0.6 0.0 copy-start.7
  0.6 3.6 %collective-permute-start = (bf16[2,1,144,768]{3,2,1,0:T(8,128)(2,1)}, bf16[2,1,144,768]{3,2,1,0:T(8,128)(2,1)S(1)}, u32[]{:S(2)}, u32[]{:S(2)}) collective-permute-start(bf16[2,1,144,768]{3,2,1,0:T(8,128)(2,1)} %param.11), channel_id=1, source_target_pairs={{0,8},{8,12},{1,9},{9,13},{2,10},{10,14},{3,11},{11,15},{16,24},{2... | collective-permute-start | bytes 1327112 | tf_op jit(solution)/shard_map/ppermute | solution.py:273
  4.3 2.3 %project.1 = (bf16[36,512]{1,0:T(8,128)(2,1)}, bf16[36,512]{1,0:T(8,128)(2,1)}, bf16[36,512]{1,0:T(8,128)(2,1)}, bf16[36,512]{1,0:T(8,128)(2,1)}) custom-call(bf16[1,144,768]{2,1,0:T(8,128)(2,1)} %x_hbm.1, bf16[768,512]{1,0:T(8,128)(2,1)} %w_hbm.1), custom_call_target="tpu_custom_call" | custom-call | flops 113246208 | bytes 1007616 | tf_op jit(solution)/shard_map/project/pallas_call | solution.py:284
  6.6 0.1 collective-permute-start.1
  6.6 1.6 %collective-permute-start.2 = (bf16[36,512]{1,0:T(8,128)(2,1)}, bf16[36,512]{1,0:T(8,128)(2,1)S(1)}, u32[]{:S(2)}, u32[]{:S(2)}) collective-permute-start(bf16[36,512]{1,0:T(8,128)(2,1)} %get-tuple-element.30), channel_id=1, source_target_pairs={{0,2},{1,3},{2,0},{3,1},{4,6},{5,7},{6,4},{7,5},{8,10},{9,11},{10,... | collective-permute-start | bytes 110600 | tf_op jit(solution)/shard_map/ppermute | solution.py:40
  8.2 0.3 collective-permute-start.3
  8.5 0.7 %collective-permute-start.5 = (bf16[2,1,144,768]{3,2,1,0:T(8,128)(2,1)}, bf16[2,1,144,768]{3,2,1,0:T(8,128)(2,1)S(1)}, u32[]{:S(2)}, u32[]{:S(2)}) collective-permute-start(bf16[2,1,144,768]{3,2,1,0:T(8,128)(2,1)} %param.11), channel_id=1, source_target_pairs={{4,12},{5,13},{6,14},{7,15},{20,28},{21,29},{22,30},{23,31}} | collective-permute-start | bytes 1327112 | tf_op jit(solution)/shard_map/ppermute | solution.py:273
  9.2 0.0 copy-start
  9.2 1.2 %copy-done = bf16[4,1,144,768]{3,2,1,0:T(8,128)(2,1)S(1)} copy-done((bf16[4,1,144,768]{3,2,1,0:T(8,128)(2,1)S(1)}, bf16[4,1,144,768]{3,2,1,0:T(8,128)(2,1)}, u32[]{:S(2)}) %copy-start) | copy-done | bytes 884760
  10.4 0.0 copy-start.2
  10.4 1.5 %copy-done.2 = bf16[4,2,1,144,768]{4,3,2,1,0:T(8,128)(2,1)S(1)} copy-done((bf16[4,2,1,144,768]{4,3,2,1,0:T(8,128)(2,1)S(1)}, bf16[4,2,1,144,768]{4,3,2,1,0:T(8,128)(2,1)}, u32[]{:S(2)}) %copy-start.2) | copy-done | bytes 1769496
  11.8 0.7 %copy-done.5 = s32[4,4]{1,0:T(4,128)S(1)} copy-done((s32[4,4]{1,0:T(4,128)S(1)}, s32[4,4]{1,0:T(4,128)}, u32[]{:S(2)}) %copy-start.5) | copy-done | bytes 88
  12.5 2.5 %own.1 = (f32[6,128,576]{2,1,0:T(8,128)S(1)}, f32[6,576]{1,0:T(8,128)S(1)}, f32[6,576]{1,0:T(8,128)S(1)}) custom-call(s32[4,4]{1,0:T(4,128)S(1)} %copy-done.5, bf16[4,1,144,768]{3,2,1,0:T(8,128)(2,1)S(1)} %copy-done, bf16[4,2,1,144,768]{4,3,2,1,0:T(8,128)(2,1)S(1)} %copy-done.2), custom_call_target="tpu_custom_call" | custom-call | flops 254803968 | bytes 2654272 | tf_op jit(solution)/shard_map/own/pallas_call | solution.py:284
  15.1 0.0 collective-permute-done.1.refs_1_
  15.1 0.0 collective-permute-done.2.refs_2_
  15.1 0.0 collective-permute-done.3.refs_3_
  15.1 0.0 copy-done.4
  15.1 0.1 gather.1
  15.3 0.5 %collective-permute-done.refs_0_ = bf16[2,1,144,768]{3,2,1,0:T(8,128)(2,1)S(1)} collective-permute-done((bf16[2,1,144,768]{3,2,1,0:T(8,128)(2,1)}, bf16[2,1,144,768]{3,2,1,0:T(8,128)(2,1)S(1)}, u32[]{:S(2)}, u32[]{:S(2)}) %collective-permute-start) | collective-permute-done | bytes 442400 | tf_op jit(solution)/shard_map/ppermute | solution.py:273
  15.8 0.0 copy-done.7
  15.8 0.1 select_bitcast_fusion
  15.8 2.6 %collective-permute-start.4 = (bf16[1,144,768]{2,1,0:T(8,128)(2,1)S(1)}, bf16[1,144,768]{2,1,0:T(8,128)(2,1)S(1)}, u32[]{:S(2)}, u32[]{:S(2)}) collective-permute-start(bf16[1,144,768]{2,1,0:T(8,128)(2,1)S(1)} %get-tuple-element.53), channel_id=1, source_target_pairs={{0,4},{4,8},{8,12},{1,5},{5,9},{9,13},{2,6},{6,10},{10,14},{3,7},{... | collective-permute-start | bytes 663560 | tf_op jit(solution)/shard_map/ppermute | solution.py:31
  18.5 1.9 %collective-permute-start.6 = (bf16[1,144,512]{2,1,0:T(8,128)(2,1)S(1)}, bf16[1,144,512]{2,1,0:T(8,128)(2,1)S(1)}, u32[]{:S(2)}, u32[]{:S(2)}) collective-permute-start(bf16[1,144,512]{2,1,0:T(8,128)(2,1)S(1)} %slice.24), channel_id=1, source_target_pairs={{0,4},{4,8},{8,12},{1,5},{5,9},{9,13},{2,6},{6,10},{10,14},{3,7},{... | collective-permute-start | bytes 442376 | tf_op jit(solution)/shard_map/ppermute | solution.py:31
  20.4 1.9 %collective-permute-start.7 = (bf16[1,144,256]{2,1,0:T(8,128)(2,1)S(1)}, bf16[1,144,256]{2,1,0:T(8,128)(2,1)S(1)}, u32[]{:S(2)}, u32[]{:S(2)}) collective-permute-start(bf16[1,144,256]{2,1,0:T(8,128)(2,1)S(1)} %slice.25), channel_id=1, source_target_pairs={{0,4},{4,8},{8,12},{1,5},{5,9},{9,13},{2,6},{6,10},{10,14},{3,7},{... | collective-permute-start | bytes 221192 | tf_op jit(solution)/shard_map/ppermute | solution.py:31
  23.0 1.9 %collective-permute-start.11 = (bf16[24,512]{1,0:T(8,128)(2,1)S(1)}, bf16[24,512]{1,0:T(8,128)(2,1)S(1)}, u32[]{:S(2)}, u32[]{:S(2)}) collective-permute-start(bf16[24,512]{1,0:T(8,128)(2,1)S(1)} %get-tuple-element.51), channel_id=1, source_target_pairs={{0,4},{4,8},{8,12},{1,5},{5,9},{9,13},{2,6},{6,10},{10,14},{3,7},{... | collective-permute-start | bytes 73736 | tf_op jit(solution)/shard_map/ppermute | solution.py:31
  24.9 0.0 copy-done.1
  24.9 0.0 copy-done.6
  24.9 0.7 %middle.2 = (f32[6,128,576]{2,1,0:T(8,128)S(1)}, f32[6,576]{1,0:T(8,128)S(1)}, f32[6,576]{1,0:T(8,128)S(1)}) custom-call(s32[4,4]{1,0:T(4,128)S(1)} %copy-done.5, s32[4,4]{1,0:T(4,128)S(1)} %copy-done.6, bf16[4,1,144,768]{3,2,1,0:T(8,128)(2,1)S(1)} %copy-done.1, bf16[2,1,144,768]{3,2,1,0:T(8,128)(2,1)S(1)} %collective-permute-done.refs_0_, ...), custom_call_target="tpu_custom_call" | custom-call | flops 254803968 | bytes 3124352 | tf_op jit(solution)/shard_map/middle/pallas_call | solution.py:284
  25.7 0.0 collective-permute-done.5.refs_0_
  25.7 0.7 %middle.3 = (f32[6,128,576]{2,1,0:T(8,128)S(1)}, f32[6,576]{1,0:T(8,128)S(1)}, f32[6,576]{1,0:T(8,128)S(1)}) custom-call(s32[4,4]{1,0:T(4,128)S(1)} %copy-done.5, s32[4,4]{1,0:T(4,128)S(1)} %copy-done.6, bf16[4,1,144,768]{3,2,1,0:T(8,128)(2,1)S(1)} %copy-done.1, bf16[2,1,144,768]{3,2,1,0:T(8,128)(2,1)S(1)} %collective-permute-done.5.refs_0_, ...), custom_call_target="tpu_custom_call" | custom-call | flops 254803968 | bytes 3124352 | tf_op jit(solution)/shard_map/middle/pallas_call | solution.py:284
  26.4 3.6 %collective-permute-done.4.refs_0_ = bf16[1,144,768]{2,1,0:T(8,128)(2,1)S(1)} collective-permute-done((bf16[1,144,768]{2,1,0:T(8,128)(2,1)S(1)}, bf16[1,144,768]{2,1,0:T(8,128)(2,1)S(1)}, u32[]{:S(2)}, u32[]{:S(2)}) %collective-permute-start.4) | collective-permute-done | bytes 221216 | tf_op jit(solution)/shard_map/ppermute | solution.py:31
  30.0 0.8 %score.1 = (f32[6,128,576]{2,1,0:T(8,128)S(1)}, bf16[6,144,576]{2,1,0:T(8,128)(2,1)S(1)}) custom-call(s32[4,4]{1,0:T(4,128)S(1)} %copy-done.5, s32[4,4]{1,0:T(4,128)S(1)} %copy-done.6, bf16[4,1,144,768]{3,2,1,0:T(8,128)(2,1)S(1)} %copy-done.1, bf16[1,144,768]{2,1,0:T(8,128)(2,1)S(1)} %collective-permute-done.4.refs_0_, ...), custom_call_target="tpu_custom_call" | custom-call | flops 127401984 | bytes 2903168 | tf_op jit(solution)/shard_map/score/pallas_call | solution.py:284
  30.8 2.3 %collective-permute-done.6.value_ref = bf16[1,144,512]{2,1,0:T(8,128)(2,1)S(1)} collective-permute-done((bf16[1,144,512]{2,1,0:T(8,128)(2,1)S(1)}, bf16[1,144,512]{2,1,0:T(8,128)(2,1)S(1)}, u32[]{:S(2)}, u32[]{:S(2)}) %collective-permute-start.6) | collective-permute-done | bytes 147488 | tf_op jit(solution)/shard_map/ppermute | solution.py:31
  33.2 0.6 %average.1 = (f32[4,144,512]{2,1,0:T(8,128)S(1)}, f32[1,576]{1,0:T(1,128)S(1)}) custom-call(f32[6,128,576]{2,1,0:T(8,128)S(1)} %get-tuple-element.42.acc_ref, bf16[6,144,576]{2,1,0:T(8,128)(2,1)S(1)} %get-tuple-element.43.w_ref, bf16[1,144,512]{2,1,0:T(8,128)(2,1)S(1)} %collective-permute-done.6.value_ref), custom_call_target="tpu_custom_call" | custom-call | flops 63700992 | bytes 2912256 | tf_op jit(solution)/shard_map/average/pallas_call | solution.py:284
  33.8 0.0 copy-start.3
  33.8 0.9 %collective-permute-done.7.value_ref = bf16[1,144,256]{2,1,0:T(8,128)(2,1)S(1)} collective-permute-done((bf16[1,144,256]{2,1,0:T(8,128)(2,1)S(1)}, bf16[1,144,256]{2,1,0:T(8,128)(2,1)S(1)}, u32[]{:S(2)}, u32[]{:S(2)}) %collective-permute-start.7) | collective-permute-done | bytes 73760 | tf_op jit(solution)/shard_map/ppermute | solution.py:31
  34.7 0.3 rest.1
  35.1 1.2 %collective-permute-start.8 = (f32[1,576]{1,0:T(1,128)S(1)}, f32[1,576]{1,0:T(1,128)S(1)}, u32[]{:S(2)}, u32[]{:S(2)}) collective-permute-start(f32[1,576]{1,0:T(1,128)S(1)} %get-tuple-element.47.square_in), channel_id=1, source_target_pairs={{0,3},{1,2},{2,1},{3,0},{4,7},{5,6},{6,5},{7,4},{8,11},{9,10},{10,... | collective-permute-start | bytes 6920 | tf_op jit(solution)/shard_map/ppermute | solution.py:40
  36.2 0.5 %collective-permute-start.9 = (f32[1,576]{1,0:T(1,128)S(1)}, f32[1,576]{1,0:T(1,128)S(1)}, u32[]{:S(2)}, u32[]{:S(2)}) collective-permute-start(f32[1,576]{1,0:T(1,128)S(1)} %get-tuple-element.47.square_in), channel_id=1, source_target_pairs={{0,2},{1,3},{2,0},{3,1},{4,6},{5,7},{6,4},{7,5},{8,10},{9,11},{10,... | collective-permute-start | bytes 6920 | tf_op jit(solution)/shard_map/ppermute | solution.py:40
  36.8 0.2 turn.1
  37.0 0.3 collective-permute-start.10
  37.3 0.0 collective-permute-done.11.tail_ref
  37.3 0.0 copy-done.3
  37.3 1.4 %decode.1 = bf16[1,36,512]{2,1,0:T(8,128)(2,1)} custom-call(s32[1]{0:T(128)S(6)} %copy.11.fade_ref, bf16[36,512]{1,0:T(8,128)(2,1)S(1)} %get-tuple-element.50.hidden_ref, bf16[24,512]{1,0:T(8,128)(2,1)S(1)} %collective-permute-done.11.tail_ref, bf16[3,512,512]{2,1,0:T(8,128)(2,1)S(1)} %copy-done.3), custom_call_target="tpu_custom_call" | custom-call | flops 56623104 | bytes 1634308 | tf_op jit(solution)/shard_map/decode/pallas_call | solution.py:284
  38.7 0.0 collective-permute-done.10.refs_3_
  38.7 0.0 collective-permute-done.8.refs_1_
  38.7 1.1 %collective-permute-done.9.refs_2_ = f32[1,576]{1,0:T(1,128)S(1)} collective-permute-done((f32[1,576]{1,0:T(1,128)S(1)}, f32[1,576]{1,0:T(1,128)S(1)}, u32[]{:S(2)}, u32[]{:S(2)}) %collective-permute-start.9) | collective-permute-done | bytes 2336 | tf_op jit(solution)/shard_map/ppermute | solution.py:40
  39.8 1.1 %scale.1 = bf16[4,1,144,768]{3,2,1,0:T(8,128)(2,1)} custom-call(f32[4,144,512]{2,1,0:T(8,128)S(1)} %get-tuple-element.44.front_ref, f32[4,144,256]{2,1,0:T(8,128)S(1)} %get-tuple-element.48.back_ref, f32[1,576]{1,0:T(1,128)S(1)} %get-tuple-element.49.refs_0_, f32[1,576]{1,0:T(1,128)S(1)} %collective-permute-done.8.refs_1_, ...), custom_call_target="tpu_custom_call" | custom-call | flops 442368 | bytes 1778688 | tf_op jit(solution)/shard_map/scale/pallas_call | solution.py:284
  (6 shorter events, 0.0 us)
Async XLA Ops:
  0.6 15.2 %copy-start.7 = (bf16[2,1,144,768]{3,2,1,0:T(8,128)(2,1)S(1)}, bf16[2,1,144,768]{3,2,1,0:T(8,128)(2,1)}, u32[]{:S(2)}) copy-start(bf16[2,1,144,768]{3,2,1,0:T(8,128)(2,1)} %param.11) | copy-start | bytes 1327108
  0.6 15.1 %collective-permute-start = (bf16[2,1,144,768]{3,2,1,0:T(8,128)(2,1)}, bf16[2,1,144,768]{3,2,1,0:T(8,128)(2,1)S(1)}, u32[]{:S(2)}, u32[]{:S(2)}) collective-permute-start(bf16[2,1,144,768]{3,2,1,0:T(8,128)(2,1)} %param.11), channel_id=1, source_target_pairs={{0,8},{8,12},{1,9},{9,13},{2,10},{10,14},{3,11},{11,15},{16,24},{2... | collective-permute-start | bytes 1327112 | tf_op jit(solution)/shard_map/ppermute | solution.py:273
  6.6 8.5 %collective-permute-start.1 = (bf16[36,512]{1,0:T(8,128)(2,1)}, bf16[36,512]{1,0:T(8,128)(2,1)S(1)}, u32[]{:S(2)}, u32[]{:S(2)}) collective-permute-start(bf16[36,512]{1,0:T(8,128)(2,1)} %get-tuple-element.29), channel_id=1, source_target_pairs={{0,1},{1,0},{2,3},{3,2},{4,5},{5,4},{6,7},{7,6},{8,9},{9,8},{10,11... | collective-permute-start | bytes 110600 | tf_op jit(solution)/shard_map/ppermute | solution.py:40
  6.6 8.5 %collective-permute-start.2 = (bf16[36,512]{1,0:T(8,128)(2,1)}, bf16[36,512]{1,0:T(8,128)(2,1)S(1)}, u32[]{:S(2)}, u32[]{:S(2)}) collective-permute-start(bf16[36,512]{1,0:T(8,128)(2,1)} %get-tuple-element.30), channel_id=1, source_target_pairs={{0,2},{1,3},{2,0},{3,1},{4,6},{5,7},{6,4},{7,5},{8,10},{9,11},{10,... | collective-permute-start | bytes 110600 | tf_op jit(solution)/shard_map/ppermute | solution.py:40
  8.2 6.9 %collective-permute-start.3 = (bf16[36,512]{1,0:T(8,128)(2,1)}, bf16[36,512]{1,0:T(8,128)(2,1)S(1)}, u32[]{:S(2)}, u32[]{:S(2)}) collective-permute-start(bf16[36,512]{1,0:T(8,128)(2,1)} %get-tuple-element.31), channel_id=1, source_target_pairs={{0,3},{1,2},{2,1},{3,0},{4,7},{5,6},{6,5},{7,4},{8,11},{9,10},{10,... | collective-permute-start | bytes 110600 | tf_op jit(solution)/shard_map/ppermute | solution.py:40
  8.5 17.2 %collective-permute-start.5 = (bf16[2,1,144,768]{3,2,1,0:T(8,128)(2,1)}, bf16[2,1,144,768]{3,2,1,0:T(8,128)(2,1)S(1)}, u32[]{:S(2)}, u32[]{:S(2)}) collective-permute-start(bf16[2,1,144,768]{3,2,1,0:T(8,128)(2,1)} %param.11), channel_id=1, source_target_pairs={{4,12},{5,13},{6,14},{7,15},{20,28},{21,29},{22,30},{23,31}} | collective-permute-start | bytes 1327112 | tf_op jit(solution)/shard_map/ppermute | solution.py:273
  9.2 1.2 %copy-start = (bf16[4,1,144,768]{3,2,1,0:T(8,128)(2,1)S(1)}, bf16[4,1,144,768]{3,2,1,0:T(8,128)(2,1)}, u32[]{:S(2)}) copy-start(bf16[4,1,144,768]{3,2,1,0:T(8,128)(2,1)} %q_ref.7) | copy-start | bytes 2654212
  10.4 1.5 %copy-start.2 = (bf16[4,2,1,144,768]{4,3,2,1,0:T(8,128)(2,1)S(1)}, bf16[4,2,1,144,768]{4,3,2,1,0:T(8,128)(2,1)}, u32[]{:S(2)}) copy-start(bf16[4,2,1,144,768]{4,3,2,1,0:T(8,128)(2,1)} %kv_ref.1) | copy-start | bytes 5308420
  11.8 0.7 %copy-start.5 = (s32[4,4]{1,0:T(4,128)S(1)}, s32[4,4]{1,0:T(4,128)}, u32[]{:S(2)}) copy-start(s32[4,4]{1,0:T(4,128)} %step_ref.7) | copy-start | bytes 196
  12.5 2.6 %copy-start.4 = (bf16[36,512]{1,0:T(8,128)(2,1)S(1)}, bf16[36,512]{1,0:T(8,128)(2,1)}, u32[]{:S(2)}) copy-start(bf16[36,512]{1,0:T(8,128)(2,1)} %get-tuple-element.28.refs_0_) | copy-start | bytes 110596
  12.5 12.4 %copy-start.1 = (bf16[4,1,144,768]{3,2,1,0:T(8,128)(2,1)S(1)}, bf16[4,1,144,768]{3,2,1,0:T(8,128)(2,1)}, u32[]{:S(2)}) copy-start(bf16[4,1,144,768]{3,2,1,0:T(8,128)(2,1)} %q_ref.7) | copy-start | bytes 2654212
  12.5 12.4 %copy-start.6 = (s32[4,4]{1,0:T(4,128)S(1)}, s32[4,4]{1,0:T(4,128)}, u32[]{:S(2)}) copy-start(s32[4,4]{1,0:T(4,128)} %mask_ref.5) | copy-start | bytes 196
  15.8 14.2 %collective-permute-start.4 = (bf16[1,144,768]{2,1,0:T(8,128)(2,1)S(1)}, bf16[1,144,768]{2,1,0:T(8,128)(2,1)S(1)}, u32[]{:S(2)}, u32[]{:S(2)}) collective-permute-start(bf16[1,144,768]{2,1,0:T(8,128)(2,1)S(1)} %get-tuple-element.53), channel_id=1, source_target_pairs={{0,4},{4,8},{8,12},{1,5},{5,9},{9,13},{2,6},{6,10},{10,14},{3,7},{... | collective-permute-start | bytes 663560 | tf_op jit(solution)/shard_map/ppermute | solution.py:31
  18.5 14.7 %collective-permute-start.6 = (bf16[1,144,512]{2,1,0:T(8,128)(2,1)S(1)}, bf16[1,144,512]{2,1,0:T(8,128)(2,1)S(1)}, u32[]{:S(2)}, u32[]{:S(2)}) collective-permute-start(bf16[1,144,512]{2,1,0:T(8,128)(2,1)S(1)} %slice.24), channel_id=1, source_target_pairs={{0,4},{4,8},{8,12},{1,5},{5,9},{9,13},{2,6},{6,10},{10,14},{3,7},{... | collective-permute-start | bytes 442376 | tf_op jit(solution)/shard_map/ppermute | solution.py:31
  20.4 14.3 %collective-permute-start.7 = (bf16[1,144,256]{2,1,0:T(8,128)(2,1)S(1)}, bf16[1,144,256]{2,1,0:T(8,128)(2,1)S(1)}, u32[]{:S(2)}, u32[]{:S(2)}) collective-permute-start(bf16[1,144,256]{2,1,0:T(8,128)(2,1)S(1)} %slice.25), channel_id=1, source_target_pairs={{0,4},{4,8},{8,12},{1,5},{5,9},{9,13},{2,6},{6,10},{10,14},{3,7},{... | collective-permute-start | bytes 221192 | tf_op jit(solution)/shard_map/ppermute | solution.py:31
  23.0 14.3 %collective-permute-start.11 = (bf16[24,512]{1,0:T(8,128)(2,1)S(1)}, bf16[24,512]{1,0:T(8,128)(2,1)S(1)}, u32[]{:S(2)}, u32[]{:S(2)}) collective-permute-start(bf16[24,512]{1,0:T(8,128)(2,1)S(1)} %get-tuple-element.51), channel_id=1, source_target_pairs={{0,4},{4,8},{8,12},{1,5},{5,9},{9,13},{2,6},{6,10},{10,14},{3,7},{... | collective-permute-start | bytes 73736 | tf_op jit(solution)/shard_map/ppermute | solution.py:31
  33.8 3.5 %copy-start.3 = (bf16[3,512,512]{2,1,0:T(8,128)(2,1)S(1)}, bf16[3,512,512]{2,1,0:T(8,128)(2,1)}, u32[]{:S(2)}) copy-start(bf16[3,512,512]{2,1,0:T(8,128)(2,1)} %conv_ref.1) | copy-start | bytes 4718596
  35.1 3.7 %collective-permute-start.8 = (f32[1,576]{1,0:T(1,128)S(1)}, f32[1,576]{1,0:T(1,128)S(1)}, u32[]{:S(2)}, u32[]{:S(2)}) collective-permute-start(f32[1,576]{1,0:T(1,128)S(1)} %get-tuple-element.47.square_in), channel_id=1, source_target_pairs={{0,3},{1,2},{2,1},{3,0},{4,7},{5,6},{6,5},{7,4},{8,11},{9,10},{10,... | collective-permute-start | bytes 6920 | tf_op jit(solution)/shard_map/ppermute | solution.py:40
  36.2 3.6 %collective-permute-start.9 = (f32[1,576]{1,0:T(1,128)S(1)}, f32[1,576]{1,0:T(1,128)S(1)}, u32[]{:S(2)}, u32[]{:S(2)}) collective-permute-start(f32[1,576]{1,0:T(1,128)S(1)} %get-tuple-element.47.square_in), channel_id=1, source_target_pairs={{0,2},{1,3},{2,0},{3,1},{4,6},{5,7},{6,4},{7,5},{8,10},{9,11},{10,... | collective-permute-start | bytes 6920 | tf_op jit(solution)/shard_map/ppermute | solution.py:40
  37.0 1.7 %collective-permute-start.10 = (f32[1,576]{1,0:T(1,128)S(1)}, f32[1,576]{1,0:T(1,128)S(1)}, u32[]{:S(2)}, u32[]{:S(2)}) collective-permute-start(f32[1,576]{1,0:T(1,128)S(1)} %get-tuple-element.49.refs_0_), channel_id=1, source_target_pairs={{0,1},{1,0},{2,3},{3,2},{4,5},{5,4},{6,7},{7,6},{8,9},{9,8},{10,11... | collective-permute-start | bytes 6920 | tf_op jit(solution)/shard_map/ppermute | solution.py:40

commit v7 on v6

--- a/solution.py
+++ b/solution.py
@@ -441,7 +441,7 @@
         own_kernel,
         "own",
         [acc_shape, stat_shape, stat_shape],
-        pair_flops,
+        3 * pair_flops,
         (step_index, query, noisy_kv),
         [SMEM_SPEC],
     )
@@ -495,7 +495,7 @@
         pair_flops // 4,
         (acc, weights, values[1], squares),
     )
-    others = [swap(squares, axes, offset) for offset in range(lax.axis_size(axes) - 1, 1, -1)]
+    others = [swap(squares, axes, offset) for offset in range(2, lax.axis_size(axes))]
     back, squares = plain_call(
         turn_kernel,
         "turn",

time: 41.3 us -> 41.1 us (level)
  waiting for transfers between devices: 8.46 us -> 6.09 us
  Pallas kernels: 11 us -> 12.9 us
    pallas_call x11, Pallas kernels: 11 us -> 12.9 us  [plain_call(): pl.pallas_call(kernel, in_specs=list(in_specs) + [VMEM_SPEC] * (len(opera...]
    ppermute x4, waiting for transfers between devices: 6.84 us -> 4.93 us  [hop(): lax.ppermute(value, axis, [(source, source + steps) for source in range(c...]
    ppermute x6, waiting for transfers between devices: 1.1 us -> 0.65 us  [swap(): return lax.ppermute(value, axes, pairs)]
  transfers between devices with their start and end apart: 12 -> 12, of which waited for: 5 -> 5; matrix products, arithmetic and copies ran while one was open for 0% -> 0% of each run, Pallas kernels for 24% -> 29%
where the time goes in v7:
time: 41.1 us; the launch traced here: 40.8 us
  starting transfers between devices  16.9 us (41%)
  Pallas kernels  12.9 us (31%)
  waiting for transfers between devices  6.09 us (15%)
  local copies, waits for them, and re-layouts  3.36 us (8%)
  between operations  1.48 us (4%)
    pallas_call x11, Pallas kernels, plain_call(): pl.pallas_call(kernel, in_specs=list(in_specs) + [VMEM_SPEC] * (len(opera...  12.9 us
    ppermute x4, starting transfers between devices, hop(): lax.ppermute(value, axis, [(source, source + steps) for source in range(c...  8.35 us
    ppermute x4, waiting for transfers between devices, hop(): lax.ppermute(value, axis, [(source, source + steps) for source in range(c...  4.93 us
    ppermute x2, starting transfers between devices, send(): return lax.ppermute(value, 'span', pairs)  4.3 us
    ppermute x6, starting transfers between devices, swap(): return lax.ppermute(value, axes, pairs)  4.2 us
    unnamed x16, local copies, waits for them, and re-layouts  3.34 us
  transfers between devices with their start and end apart: 12, of which 5 were waited for; matrix products, arithmetic and copies ran while one was open for 0% of the time, Pallas kernels for 29%

profile of v7, /device:TPU:20, one launch (start us, length us, event | category | flops | bytes accessed | tf_op | source)
XLA Modules:
  0.0 40.8 jit_solution(6453196812698960313)
XLA Ops:
  0.6 0.0 copy-start.7
  0.6 3.6 %collective-permute-start = (bf16[2,1,144,768]{3,2,1,0:T(8,128)(2,1)}, bf16[2,1,144,768]{3,2,1,0:T(8,128)(2,1)S(1)}, u32[]{:S(2)}, u32[]{:S(2)}) collective-permute-start(bf16[2,1,144,768]{3,2,1,0:T(8,128)(2,1)} %param.11), channel_id=1, source_target_pairs={{0,8},{8,12},{1,9},{9,13},{2,10},{10,14},{3,11},{11,15},{16,24},{2... | collective-permute-start | bytes 1327112 | tf_op jit(solution)/shard_map/ppermute | solution.py:273
  4.3 0.7 %collective-permute-start.5 = (bf16[2,1,144,768]{3,2,1,0:T(8,128)(2,1)}, bf16[2,1,144,768]{3,2,1,0:T(8,128)(2,1)S(1)}, u32[]{:S(2)}, u32[]{:S(2)}) collective-permute-start(bf16[2,1,144,768]{3,2,1,0:T(8,128)(2,1)} %param.11), channel_id=1, source_target_pairs={{4,12},{5,13},{6,14},{7,15},{20,28},{21,29},{22,30},{23,31}} | collective-permute-start | bytes 1327112 | tf_op jit(solution)/shard_map/ppermute | solution.py:273
  5.0 2.3 %project.1 = (bf16[36,512]{1,0:T(8,128)(2,1)}, bf16[36,512]{1,0:T(8,128)(2,1)}, bf16[36,512]{1,0:T(8,128)(2,1)}, bf16[36,512]{1,0:T(8,128)(2,1)}) custom-call(bf16[1,144,768]{2,1,0:T(8,128)(2,1)} %x_hbm.1, bf16[768,512]{1,0:T(8,128)(2,1)} %w_hbm.1), custom_call_target="tpu_custom_call" | custom-call | flops 113246208 | bytes 1007616 | tf_op jit(solution)/shard_map/project/pallas_call | solution.py:284
  7.3 0.1 collective-permute-start.1
  7.3 1.6 %collective-permute-start.2 = (bf16[36,512]{1,0:T(8,128)(2,1)}, bf16[36,512]{1,0:T(8,128)(2,1)S(1)}, u32[]{:S(2)}, u32[]{:S(2)}) collective-permute-start(bf16[36,512]{1,0:T(8,128)(2,1)} %get-tuple-element.30), channel_id=1, source_target_pairs={{0,2},{1,3},{2,0},{3,1},{4,6},{5,7},{6,4},{7,5},{8,10},{9,11},{10,... | collective-permute-start | bytes 110600 | tf_op jit(solution)/shard_map/ppermute | solution.py:40
  8.9 0.3 collective-permute-start.3
  9.2 0.0 copy-start
  9.2 1.2 %copy-done = bf16[4,1,144,768]{3,2,1,0:T(8,128)(2,1)S(1)} copy-done((bf16[4,1,144,768]{3,2,1,0:T(8,128)(2,1)S(1)}, bf16[4,1,144,768]{3,2,1,0:T(8,128)(2,1)}, u32[]{:S(2)}) %copy-start) | copy-done | bytes 884760
  10.4 0.0 copy-start.4
  10.4 0.7 %copy-done.4 = s32[4,4]{1,0:T(4,128)S(1)} copy-done((s32[4,4]{1,0:T(4,128)S(1)}, s32[4,4]{1,0:T(4,128)}, u32[]{:S(2)}) %copy-start.4) | copy-done | bytes 88
  11.1 1.5 %copy-done.6 = bf16[4,2,1,144,768]{4,3,2,1,0:T(8,128)(2,1)S(1)} copy-done((bf16[4,2,1,144,768]{4,3,2,1,0:T(8,128)(2,1)S(1)}, bf16[4,2,1,144,768]{4,3,2,1,0:T(8,128)(2,1)}, u32[]{:S(2)}) %copy-start.6) | copy-done | bytes 1769496
  12.5 2.5 %own.1 = (f32[6,128,576]{2,1,0:T(8,128)S(1)}, f32[6,576]{1,0:T(8,128)S(1)}, f32[6,576]{1,0:T(8,128)S(1)}) custom-call(s32[4,4]{1,0:T(4,128)S(1)} %copy-done.4, bf16[4,1,144,768]{3,2,1,0:T(8,128)(2,1)S(1)} %copy-done, bf16[4,2,1,144,768]{4,3,2,1,0:T(8,128)(2,1)S(1)} %copy-done.6), custom_call_target="tpu_custom_call" | custom-call | flops 764411904 | bytes 2654272 | tf_op jit(solution)/shard_map/own/pallas_call | solution.py:284
  15.1 0.0 collective-permute-done.1.refs_1_
  15.1 0.0 collective-permute-done.2.refs_2_
  15.1 0.0 collective-permute-done.3.refs_3_
  15.1 0.0 copy-done.3
  15.1 0.1 gather.1
  15.3 0.5 %collective-permute-done.refs_0_ = bf16[2,1,144,768]{3,2,1,0:T(8,128)(2,1)S(1)} collective-permute-done((bf16[2,1,144,768]{3,2,1,0:T(8,128)(2,1)}, bf16[2,1,144,768]{3,2,1,0:T(8,128)(2,1)S(1)}, u32[]{:S(2)}, u32[]{:S(2)}) %collective-permute-start) | collective-permute-done | bytes 442400 | tf_op jit(solution)/shard_map/ppermute | solution.py:273
  15.8 0.0 copy-done.7
  15.8 0.1 select_bitcast_fusion
  15.8 2.6 %collective-permute-start.4 = (bf16[1,144,768]{2,1,0:T(8,128)(2,1)S(1)}, bf16[1,144,768]{2,1,0:T(8,128)(2,1)S(1)}, u32[]{:S(2)}, u32[]{:S(2)}) collective-permute-start(bf16[1,144,768]{2,1,0:T(8,128)(2,1)S(1)} %get-tuple-element.53), channel_id=1, source_target_pairs={{0,4},{4,8},{8,12},{1,5},{5,9},{9,13},{2,6},{6,10},{10,14},{3,7},{... | collective-permute-start | bytes 663560 | tf_op jit(solution)/shard_map/ppermute | solution.py:31
  18.5 1.9 %collective-permute-start.6 = (bf16[1,144,512]{2,1,0:T(8,128)(2,1)S(1)}, bf16[1,144,512]{2,1,0:T(8,128)(2,1)S(1)}, u32[]{:S(2)}, u32[]{:S(2)}) collective-permute-start(bf16[1,144,512]{2,1,0:T(8,128)(2,1)S(1)} %slice.24), channel_id=1, source_target_pairs={{0,4},{4,8},{8,12},{1,5},{5,9},{9,13},{2,6},{6,10},{10,14},{3,7},{... | collective-permute-start | bytes 442376 | tf_op jit(solution)/shard_map/ppermute | solution.py:31
  20.4 1.9 %collective-permute-start.7 = (bf16[1,144,256]{2,1,0:T(8,128)(2,1)S(1)}, bf16[1,144,256]{2,1,0:T(8,128)(2,1)S(1)}, u32[]{:S(2)}, u32[]{:S(2)}) collective-permute-start(bf16[1,144,256]{2,1,0:T(8,128)(2,1)S(1)} %slice.25), channel_id=1, source_target_pairs={{0,4},{4,8},{8,12},{1,5},{5,9},{9,13},{2,6},{6,10},{10,14},{3,7},{... | collective-permute-start | bytes 221192 | tf_op jit(solution)/shard_map/ppermute | solution.py:31
  23.0 1.9 %collective-permute-start.11 = (bf16[24,512]{1,0:T(8,128)(2,1)S(1)}, bf16[24,512]{1,0:T(8,128)(2,1)S(1)}, u32[]{:S(2)}, u32[]{:S(2)}) collective-permute-start(bf16[24,512]{1,0:T(8,128)(2,1)S(1)} %get-tuple-element.51), channel_id=1, source_target_pairs={{0,4},{4,8},{8,12},{1,5},{5,9},{9,13},{2,6},{6,10},{10,14},{3,7},{... | collective-permute-start | bytes 73736 | tf_op jit(solution)/shard_map/ppermute | solution.py:31
  24.9 0.0 copy-done.1
  24.9 0.0 copy-done.5
  24.9 2.7 %middle.2 = (f32[6,128,576]{2,1,0:T(8,128)S(1)}, f32[6,576]{1,0:T(8,128)S(1)}, f32[6,576]{1,0:T(8,128)S(1)}) custom-call(s32[4,4]{1,0:T(4,128)S(1)} %copy-done.4, s32[4,4]{1,0:T(4,128)S(1)} %copy-done.5, bf16[4,1,144,768]{3,2,1,0:T(8,128)(2,1)S(1)} %copy-done.1, bf16[2,1,144,768]{3,2,1,0:T(8,128)(2,1)S(1)} %collective-permute-done.refs_0_, ...), custom_call_target="tpu_custom_call" | custom-call | flops 254803968 | bytes 3124352 | tf_op jit(solution)/shard_map/middle/pallas_call | solution.py:284
  27.6 0.0 collective-permute-done.5.refs_0_
  27.6 0.7 %middle.3 = (f32[6,128,576]{2,1,0:T(8,128)S(1)}, f32[6,576]{1,0:T(8,128)S(1)}, f32[6,576]{1,0:T(8,128)S(1)}) custom-call(s32[4,4]{1,0:T(4,128)S(1)} %copy-done.4, s32[4,4]{1,0:T(4,128)S(1)} %copy-done.5, bf16[4,1,144,768]{3,2,1,0:T(8,128)(2,1)S(1)} %copy-done.1, bf16[2,1,144,768]{3,2,1,0:T(8,128)(2,1)S(1)} %collective-permute-done.5.refs_0_, ...), custom_call_target="tpu_custom_call" | custom-call | flops 254803968 | bytes 3124352 | tf_op jit(solution)/shard_map/middle/pallas_call | solution.py:284
  28.4 1.7 %collective-permute-done.4.refs_0_ = bf16[1,144,768]{2,1,0:T(8,128)(2,1)S(1)} collective-permute-done((bf16[1,144,768]{2,1,0:T(8,128)(2,1)S(1)}, bf16[1,144,768]{2,1,0:T(8,128)(2,1)S(1)}, u32[]{:S(2)}, u32[]{:S(2)}) %collective-permute-start.4) | collective-permute-done | bytes 221216 | tf_op jit(solution)/shard_map/ppermute | solution.py:31
  30.0 0.8 %score.1 = (f32[6,128,576]{2,1,0:T(8,128)S(1)}, bf16[6,144,576]{2,1,0:T(8,128)(2,1)S(1)}) custom-call(s32[4,4]{1,0:T(4,128)S(1)} %copy-done.4, s32[4,4]{1,0:T(4,128)S(1)} %copy-done.5, bf16[4,1,144,768]{3,2,1,0:T(8,128)(2,1)S(1)} %copy-done.1, bf16[1,144,768]{2,1,0:T(8,128)(2,1)S(1)} %collective-permute-done.4.refs_0_, ...), custom_call_target="tpu_custom_call" | custom-call | flops 127401984 | bytes 2903168 | tf_op jit(solution)/shard_map/score/pallas_call | solution.py:284
  30.9 2.3 %collective-permute-done.6.value_ref = bf16[1,144,512]{2,1,0:T(8,128)(2,1)S(1)} collective-permute-done((bf16[1,144,512]{2,1,0:T(8,128)(2,1)S(1)}, bf16[1,144,512]{2,1,0:T(8,128)(2,1)S(1)}, u32[]{:S(2)}, u32[]{:S(2)}) %collective-permute-start.6) | collective-permute-done | bytes 147488 | tf_op jit(solution)/shard_map/ppermute | solution.py:31
  33.2 0.6 %average.1 = (f32[4,144,512]{2,1,0:T(8,128)S(1)}, f32[1,576]{1,0:T(1,128)S(1)}) custom-call(f32[6,128,576]{2,1,0:T(8,128)S(1)} %get-tuple-element.42.acc_ref, bf16[6,144,576]{2,1,0:T(8,128)(2,1)S(1)} %get-tuple-element.43.w_ref, bf16[1,144,512]{2,1,0:T(8,128)(2,1)S(1)} %collective-permute-done.6.value_ref), custom_call_target="tpu_custom_call" | custom-call | flops 63700992 | bytes 2912256 | tf_op jit(solution)/shard_map/average/pallas_call | solution.py:284
  33.8 0.0 copy-start.2
  33.8 0.9 %collective-permute-done.7.value_ref = bf16[1,144,256]{2,1,0:T(8,128)(2,1)S(1)} collective-permute-done((bf16[1,144,256]{2,1,0:T(8,128)(2,1)S(1)}, bf16[1,144,256]{2,1,0:T(8,128)(2,1)S(1)}, u32[]{:S(2)}, u32[]{:S(2)}) %collective-permute-start.7) | collective-permute-done | bytes 73760 | tf_op jit(solution)/shard_map/ppermute | solution.py:31
  34.8 0.3 rest.1
  35.1 1.6 %collective-permute-start.8 = (f32[1,576]{1,0:T(1,128)S(1)}, f32[1,576]{1,0:T(1,128)S(1)}, u32[]{:S(2)}, u32[]{:S(2)}) collective-permute-start(f32[1,576]{1,0:T(1,128)S(1)} %get-tuple-element.47.square_in), channel_id=1, source_target_pairs={{0,2},{1,3},{2,0},{3,1},{4,6},{5,7},{6,4},{7,5},{8,10},{9,11},{10,... | collective-permute-start | bytes 6920 | tf_op jit(solution)/shard_map/ppermute | solution.py:40
  36.7 0.0 collective-permute-start.9
  36.7 0.2 turn.1
  36.9 0.7 %collective-permute-start.10 = (f32[1,576]{1,0:T(1,128)S(1)}, f32[1,576]{1,0:T(1,128)S(1)}, u32[]{:S(2)}, u32[]{:S(2)}) collective-permute-start(f32[1,576]{1,0:T(1,128)S(1)} %get-tuple-element.49.refs_0_), channel_id=1, source_target_pairs={{0,1},{1,0},{2,3},{3,2},{4,5},{5,4},{6,7},{7,6},{8,9},{9,8},{10,11... | collective-permute-start | bytes 6920 | tf_op jit(solution)/shard_map/ppermute | solution.py:40
  37.6 0.0 collective-permute-done.11.tail_ref
  37.6 0.0 copy-done.2
  37.6 1.4 %decode.1 = bf16[1,36,512]{2,1,0:T(8,128)(2,1)} custom-call(s32[1]{0:T(128)S(6)} %copy.11.fade_ref, bf16[36,512]{1,0:T(8,128)(2,1)S(1)} %get-tuple-element.50.hidden_ref, bf16[24,512]{1,0:T(8,128)(2,1)S(1)} %collective-permute-done.11.tail_ref, bf16[3,512,512]{2,1,0:T(8,128)(2,1)S(1)} %copy-done.2), custom_call_target="tpu_custom_call" | custom-call | flops 56623104 | bytes 1634308 | tf_op jit(solution)/shard_map/decode/pallas_call | solution.py:284
  39.0 0.0 collective-permute-done.10.refs_3_
  39.0 0.0 collective-permute-done.8.refs_1_
  39.0 0.6 %collective-permute-done.9.refs_2_ = f32[1,576]{1,0:T(1,128)S(1)} collective-permute-done((f32[1,576]{1,0:T(1,128)S(1)}, f32[1,576]{1,0:T(1,128)S(1)}, u32[]{:S(2)}, u32[]{:S(2)}) %collective-permute-start.9) | collective-permute-done | bytes 2336 | tf_op jit(solution)/shard_map/ppermute | solution.py:40
  39.7 1.1 %scale.1 = bf16[4,1,144,768]{3,2,1,0:T(8,128)(2,1)} custom-call(f32[4,144,512]{2,1,0:T(8,128)S(1)} %get-tuple-element.44.front_ref, f32[4,144,256]{2,1,0:T(8,128)S(1)} %get-tuple-element.48.back_ref, f32[1,576]{1,0:T(1,128)S(1)} %get-tuple-element.49.refs_0_, f32[1,576]{1,0:T(1,128)S(1)} %collective-permute-done.8.refs_1_, ...), custom_call_target="tpu_custom_call" | custom-call | flops 442368 | bytes 1778688 | tf_op jit(solution)/shard_map/scale/pallas_call | solution.py:284
  (6 shorter events, 0.0 us)
Async XLA Ops:
  0.6 15.2 %copy-start.7 = (bf16[2,1,144,768]{3,2,1,0:T(8,128)(2,1)S(1)}, bf16[2,1,144,768]{3,2,1,0:T(8,128)(2,1)}, u32[]{:S(2)}) copy-start(bf16[2,1,144,768]{3,2,1,0:T(8,128)(2,1)} %param.11) | copy-start | bytes 1327108
  0.6 15.1 %collective-permute-start = (bf16[2,1,144,768]{3,2,1,0:T(8,128)(2,1)}, bf16[2,1,144,768]{3,2,1,0:T(8,128)(2,1)S(1)}, u32[]{:S(2)}, u32[]{:S(2)}) collective-permute-start(bf16[2,1,144,768]{3,2,1,0:T(8,128)(2,1)} %param.11), channel_id=1, source_target_pairs={{0,8},{8,12},{1,9},{9,13},{2,10},{10,14},{3,11},{11,15},{16,24},{2... | collective-permute-start | bytes 1327112 | tf_op jit(solution)/shard_map/ppermute | solution.py:273
  4.3 23.4 %collective-permute-start.5 = (bf16[2,1,144,768]{3,2,1,0:T(8,128)(2,1)}, bf16[2,1,144,768]{3,2,1,0:T(8,128)(2,1)S(1)}, u32[]{:S(2)}, u32[]{:S(2)}) collective-permute-start(bf16[2,1,144,768]{3,2,1,0:T(8,128)(2,1)} %param.11), channel_id=1, source_target_pairs={{4,12},{5,13},{6,14},{7,15},{20,28},{21,29},{22,30},{23,31}} | collective-permute-start | bytes 1327112 | tf_op jit(solution)/shard_map/ppermute | solution.py:273
  7.3 7.8 %collective-permute-start.1 = (bf16[36,512]{1,0:T(8,128)(2,1)}, bf16[36,512]{1,0:T(8,128)(2,1)S(1)}, u32[]{:S(2)}, u32[]{:S(2)}) collective-permute-start(bf16[36,512]{1,0:T(8,128)(2,1)} %get-tuple-element.29), channel_id=1, source_target_pairs={{0,1},{1,0},{2,3},{3,2},{4,5},{5,4},{6,7},{7,6},{8,9},{9,8},{10,11... | collective-permute-start | bytes 110600 | tf_op jit(solution)/shard_map/ppermute | solution.py:40
  7.3 7.8 %collective-permute-start.2 = (bf16[36,512]{1,0:T(8,128)(2,1)}, bf16[36,512]{1,0:T(8,128)(2,1)S(1)}, u32[]{:S(2)}, u32[]{:S(2)}) collective-permute-start(bf16[36,512]{1,0:T(8,128)(2,1)} %get-tuple-element.30), channel_id=1, source_target_pairs={{0,2},{1,3},{2,0},{3,1},{4,6},{5,7},{6,4},{7,5},{8,10},{9,11},{10,... | collective-permute-start | bytes 110600 | tf_op jit(solution)/shard_map/ppermute | solution.py:40
  8.9 6.2 %collective-permute-start.3 = (bf16[36,512]{1,0:T(8,128)(2,1)}, bf16[36,512]{1,0:T(8,128)(2,1)S(1)}, u32[]{:S(2)}, u32[]{:S(2)}) collective-permute-start(bf16[36,512]{1,0:T(8,128)(2,1)} %get-tuple-element.31), channel_id=1, source_target_pairs={{0,3},{1,2},{2,1},{3,0},{4,7},{5,6},{6,5},{7,4},{8,11},{9,10},{10,... | collective-permute-start | bytes 110600 | tf_op jit(solution)/shard_map/ppermute | solution.py:40
  9.2 1.2 %copy-start = (bf16[4,1,144,768]{3,2,1,0:T(8,128)(2,1)S(1)}, bf16[4,1,144,768]{3,2,1,0:T(8,128)(2,1)}, u32[]{:S(2)}) copy-start(bf16[4,1,144,768]{3,2,1,0:T(8,128)(2,1)} %q_ref.7) | copy-start | bytes 2654212
  10.4 0.7 %copy-start.4 = (s32[4,4]{1,0:T(4,128)S(1)}, s32[4,4]{1,0:T(4,128)}, u32[]{:S(2)}) copy-start(s32[4,4]{1,0:T(4,128)} %step_ref.7) | copy-start | bytes 196
  11.0 1.5 %copy-start.6 = (bf16[4,2,1,144,768]{4,3,2,1,0:T(8,128)(2,1)S(1)}, bf16[4,2,1,144,768]{4,3,2,1,0:T(8,128)(2,1)}, u32[]{:S(2)}) copy-start(bf16[4,2,1,144,768]{4,3,2,1,0:T(8,128)(2,1)} %kv_ref.1) | copy-start | bytes 5308420
  12.5 2.6 %copy-start.3 = (bf16[36,512]{1,0:T(8,128)(2,1)S(1)}, bf16[36,512]{1,0:T(8,128)(2,1)}, u32[]{:S(2)}) copy-start(bf16[36,512]{1,0:T(8,128)(2,1)} %get-tuple-element.28.refs_0_) | copy-start | bytes 110596
  12.5 12.4 %copy-start.1 = (bf16[4,1,144,768]{3,2,1,0:T(8,128)(2,1)S(1)}, bf16[4,1,144,768]{3,2,1,0:T(8,128)(2,1)}, u32[]{:S(2)}) copy-start(bf16[4,1,144,768]{3,2,1,0:T(8,128)(2,1)} %q_ref.7) | copy-start | bytes 2654212
  12.5 12.4 %copy-start.5 = (s32[4,4]{1,0:T(4,128)S(1)}, s32[4,4]{1,0:T(4,128)}, u32[]{:S(2)}) copy-start(s32[4,4]{1,0:T(4,128)} %mask_ref.5) | copy-start | bytes 196
  15.8 14.2 %collective-permute-start.4 = (bf16[1,144,768]{2,1,0:T(8,128)(2,1)S(1)}, bf16[1,144,768]{2,1,0:T(8,128)(2,1)S(1)}, u32[]{:S(2)}, u32[]{:S(2)}) collective-permute-start(bf16[1,144,768]{2,1,0:T(8,128)(2,1)S(1)} %get-tuple-element.53), channel_id=1, source_target_pairs={{0,4},{4,8},{8,12},{1,5},{5,9},{9,13},{2,6},{6,10},{10,14},{3,7},{... | collective-permute-start | bytes 663560 | tf_op jit(solution)/shard_map/ppermute | solution.py:31
  18.5 14.7 %collective-permute-start.6 = (bf16[1,144,512]{2,1,0:T(8,128)(2,1)S(1)}, bf16[1,144,512]{2,1,0:T(8,128)(2,1)S(1)}, u32[]{:S(2)}, u32[]{:S(2)}) collective-permute-start(bf16[1,144,512]{2,1,0:T(8,128)(2,1)S(1)} %slice.24), channel_id=1, source_target_pairs={{0,4},{4,8},{8,12},{1,5},{5,9},{9,13},{2,6},{6,10},{10,14},{3,7},{... | collective-permute-start | bytes 442376 | tf_op jit(solution)/shard_map/ppermute | solution.py:31
  20.4 14.4 %collective-permute-start.7 = (bf16[1,144,256]{2,1,0:T(8,128)(2,1)S(1)}, bf16[1,144,256]{2,1,0:T(8,128)(2,1)S(1)}, u32[]{:S(2)}, u32[]{:S(2)}) collective-permute-start(bf16[1,144,256]{2,1,0:T(8,128)(2,1)S(1)} %slice.25), channel_id=1, source_target_pairs={{0,4},{4,8},{8,12},{1,5},{5,9},{9,13},{2,6},{6,10},{10,14},{3,7},{... | collective-permute-start | bytes 221192 | tf_op jit(solution)/shard_map/ppermute | solution.py:31
  23.0 14.6 %collective-permute-start.11 = (bf16[24,512]{1,0:T(8,128)(2,1)S(1)}, bf16[24,512]{1,0:T(8,128)(2,1)S(1)}, u32[]{:S(2)}, u32[]{:S(2)}) collective-permute-start(bf16[24,512]{1,0:T(8,128)(2,1)S(1)} %get-tuple-element.51), channel_id=1, source_target_pairs={{0,4},{4,8},{8,12},{1,5},{5,9},{9,13},{2,6},{6,10},{10,14},{3,7},{... | collective-permute-start | bytes 73736 | tf_op jit(solution)/shard_map/ppermute | solution.py:31
  33.8 3.8 %copy-start.2 = (bf16[3,512,512]{2,1,0:T(8,128)(2,1)S(1)}, bf16[3,512,512]{2,1,0:T(8,128)(2,1)}, u32[]{:S(2)}) copy-start(bf16[3,512,512]{2,1,0:T(8,128)(2,1)} %conv_ref.1) | copy-start | bytes 4718596
  35.1 3.9 %collective-permute-start.8 = (f32[1,576]{1,0:T(1,128)S(1)}, f32[1,576]{1,0:T(1,128)S(1)}, u32[]{:S(2)}, u32[]{:S(2)}) collective-permute-start(f32[1,576]{1,0:T(1,128)S(1)} %get-tuple-element.47.square_in), channel_id=1, source_target_pairs={{0,2},{1,3},{2,0},{3,1},{4,6},{5,7},{6,4},{7,5},{8,10},{9,11},{10,... | collective-permute-start | bytes 6920 | tf_op jit(solution)/shard_map/ppermute | solution.py:40
  36.7 3.0 %collective-permute-start.9 = (f32[1,576]{1,0:T(1,128)S(1)}, f32[1,576]{1,0:T(1,128)S(1)}, u32[]{:S(2)}, u32[]{:S(2)}) collective-permute-start(f32[1,576]{1,0:T(1,128)S(1)} %get-tuple-element.47.square_in), channel_id=1, source_target_pairs={{0,3},{1,2},{2,1},{3,0},{4,7},{5,6},{6,5},{7,4},{8,11},{9,10},{10,... | collective-permute-start | bytes 6920 | tf_op jit(solution)/shard_map/ppermute | solution.py:40
  36.9 2.1 %collective-permute-start.10 = (f32[1,576]{1,0:T(1,128)S(1)}, f32[1,576]{1,0:T(1,128)S(1)}, u32[]{:S(2)}, u32[]{:S(2)}) collective-permute-start(f32[1,576]{1,0:T(1,128)S(1)} %get-tuple-element.49.refs_0_), channel_id=1, source_target_pairs={{0,1},{1,0},{2,3},{3,2},{4,5},{5,4},{6,7},{7,6},{8,9},{9,8},{10,11... | collective-permute-start | bytes 6920 | tf_op jit(solution)/shard_map/ppermute | solution.py:40

commit v8 on v6

--- a/solution.py
+++ b/solution.py
@@ -239,11 +239,10 @@
     square_ref[...] = squares
 
 
-def turn_kernel(in_ref, square_in, out_ref, square_ref):
+def turn_kernel(in_ref, out_ref):
     steps, rows, _ = out_ref.shape
     for head in range(in_ref.shape[0]):
         out_ref[:, :, head * HD : (head + 1) * HD] = in_ref[head].T.reshape(steps, rows, HD)
-    square_ref[...] = square_in[...]
 
 
 def scale_kernel(width, front_ref, back_ref, *refs):
@@ -288,7 +287,7 @@
         out_shape=out_shape,
         scratch_shapes=list(scratch),
         compiler_params=pltpu.CompilerParams(vmem_limit_bytes=limit),
-        cost_estimate=cost(flops, nbytes),
+        cost_estimate=cost(10 * flops, nbytes),
         name=name,
     )(*operands)
 
@@ -481,12 +480,13 @@
         [SMEM_SPEC] * 2,
     )
     square_shape = jax.ShapeDtypeStruct((1, row_count), jnp.float32)
+    decoded = decode(after(hidden, weights), tail, conv_w, fade_count)
     front, squares = plain_call(
         functools.partial(average_kernel, 0, middle // HD),
         "average",
         [jax.ShapeDtypeStruct((steps, rows, middle), jnp.float32), square_shape],
         pair_flops // 4,
-        (acc, weights, values[0]),
+        (after(acc, decoded), weights, values[0]),
     )
     averaged, squares = plain_call(
         functools.partial(rest_kernel, middle // HD, heads),
@@ -495,16 +495,14 @@
         pair_flops // 4,
         (acc, weights, values[1], squares),
     )
-    others = [swap(squares, axes, offset) for offset in range(lax.axis_size(axes) - 1, 1, -1)]
-    back, squares = plain_call(
+    others = [swap(squares, axes, offset) for offset in range(1, lax.axis_size(axes))]
+    back = plain_call(
         turn_kernel,
         "turn",
-        [jax.ShapeDtypeStruct((steps, rows, columns - middle), jnp.float32), square_shape],
+        [jax.ShapeDtypeStruct((steps, rows, columns - middle), jnp.float32)],
         row_count * columns,
-        (averaged, squares),
-    )
-    others.append(swap(squares, axes, 1))
-    decoded = decode(after(hidden, back), tail, conv_w, fade_count)
+        (averaged,),
+    )[0]
     attended = plain_call(
         functools.partial(scale_kernel, columns * lax.axis_size(axes)),
         "scale",

time: 41.3 us -> 41.8 us (1.012)
  waiting for transfers between devices: 8.46 us -> 6.5 us
  Pallas kernels: 11 us -> 12.3 us
  other arithmetic: 0.06 us -> 1.1 us
  local copies, waits for them, and re-layouts: 3.36 us -> 2.88 us
    ppermute x4, waiting for transfers between devices: 6.84 us -> 4.34 us  [hop(): lax.ppermute(value, axis, [(source, source + steps) for source in range(c...]
    pallas_call x11, Pallas kernels: 11 us -> 12.3 us  [plain_call(): pl.pallas_call(kernel, in_specs=list(in_specs) + [VMEM_SPEC] * (len(opera...]
    ppermute x6, waiting for transfers between devices: 1.1 us -> 2.15 us  [swap(): return lax.ppermute(value, axes, pairs)]
    select_n x1, other arithmetic: 0.06 us -> 1.1 us  [per_device(): jnp.where(forwards, near[which], clean_kv[which])]
    ppermute x2, starting transfers between devices: 4.3 us -> 5.2 us  [send(): return lax.ppermute(value, 'span', pairs)]
    ppermute x4, starting transfers between devices: 8.35 us -> 7.68 us  [hop(): lax.ppermute(value, axis, [(source, source + steps) for source in range(c...]
    ppermute x2, waiting for transfers between devices: 0.52 us -> 0.01 us  [send(): return lax.ppermute(value, 'span', pairs)]
    unnamed x16, local copies, waits for them, and re-layouts: 3.34 us -> 2.86 us
  transfers between devices with their start and end apart: 12 -> 12, of which waited for: 5 -> 4; matrix products, arithmetic and copies ran while one was open for 0% -> 3% of each run, Pallas kernels for 24% -> 27%
where the time goes in v8:
time: 41.8 us; the launch traced here: 41.3 us
  starting transfers between devices  17 us (41%)
  Pallas kernels  12.3 us (29%)
  waiting for transfers between devices  6.5 us (16%)
  local copies, waits for them, and re-layouts  2.88 us (7%)
  between operations  1.52 us (4%)
  other arithmetic  1.1 us (3%)
    pallas_call x11, Pallas kernels, plain_call(): pl.pallas_call(kernel, in_specs=list(in_specs) + [VMEM_SPEC] * (len(opera...  12.3 us
    ppermute x4, starting transfers between devices, hop(): lax.ppermute(value, axis, [(source, source + steps) for source in range(c...  7.68 us
    ppermute x2, starting transfers between devices, send(): return lax.ppermute(value, 'span', pairs)  5.2 us
    ppermute x4, waiting for transfers between devices, hop(): lax.ppermute(value, axis, [(source, source + steps) for source in range(c...  4.34 us
    ppermute x6, starting transfers between devices, swap(): return lax.ppermute(value, axes, pairs)  4.14 us
    unnamed x16, local copies, waits for them, and re-layouts  2.86 us
    ppermute x6, waiting for transfers between devices, swap(): return lax.ppermute(value, axes, pairs)  2.15 us
    select_n x1, other arithmetic, per_device(): jnp.where(forwards, near[which], clean_kv[which])  1.1 us
  transfers between devices with their start and end apart: 12, of which 4 were waited for; matrix products, arithmetic and copies ran while one was open for 3% of the time, Pallas kernels for 27%

profile of v8, /device:TPU:20, one launch (start us, length us, event | category | flops | bytes accessed | tf_op | source)
XLA Modules:
  0.0 41.3 jit_solution(17363178329756907173)
XLA Ops:
  0.6 0.0 copy-start.1
  0.6 0.0 copy-start.4
  0.7 0.0 copy-start.3
  0.7 3.8 %collective-permute-start = (bf16[2,1,144,768]{3,2,1,0:T(8,128)(2,1)}, bf16[2,1,144,768]{3,2,1,0:T(8,128)(2,1)S(1)}, u32[]{:S(2)}, u32[]{:S(2)}) collective-permute-start(bf16[2,1,144,768]{3,2,1,0:T(8,128)(2,1)} %param.11), channel_id=1, source_target_pairs={{0,8},{8,12},{1,9},{9,13},{2,10},{10,14},{3,11},{11,15},{16,24},{2... | collective-permute-start | bytes 1327112 | tf_op jit(solution)/shard_map/ppermute | solution.py:272
  4.4 1.4 %collective-permute-start.5 = (bf16[2,1,144,768]{3,2,1,0:T(8,128)(2,1)}, bf16[2,1,144,768]{3,2,1,0:T(8,128)(2,1)}, u32[]{:S(2)}, u32[]{:S(2)}) collective-permute-start(bf16[2,1,144,768]{3,2,1,0:T(8,128)(2,1)} %param.11), channel_id=1, source_target_pairs={{4,12},{5,13},{6,14},{7,15},{20,28},{21,29},{22,30},{23,31}} | collective-permute-start | bytes 1327112 | tf_op jit(solution)/shard_map/ppermute | solution.py:272
  5.9 2.3 %project.1 = (bf16[36,512]{1,0:T(8,128)(2,1)}, bf16[36,512]{1,0:T(8,128)(2,1)}, bf16[36,512]{1,0:T(8,128)(2,1)}, bf16[36,512]{1,0:T(8,128)(2,1)}) custom-call(bf16[1,144,768]{2,1,0:T(8,128)(2,1)} %x_hbm.1, bf16[768,512]{1,0:T(8,128)(2,1)} %w_hbm.1), custom_call_target="tpu_custom_call" | custom-call | flops 1132462080 | bytes 1007616 | tf_op jit(solution)/shard_map/project/pallas_call | solution.py:283
  8.2 0.1 collective-permute-start.1
  8.2 1.6 %collective-permute-start.2 = (bf16[36,512]{1,0:T(8,128)(2,1)}, bf16[36,512]{1,0:T(8,128)(2,1)S(1)}, u32[]{:S(2)}, u32[]{:S(2)}) collective-permute-start(bf16[36,512]{1,0:T(8,128)(2,1)} %get-tuple-element.29), channel_id=1, source_target_pairs={{0,2},{1,3},{2,0},{3,1},{4,6},{5,7},{6,4},{7,5},{8,10},{9,11},{10,... | collective-permute-start | bytes 110600 | tf_op jit(solution)/shard_map/ppermute | solution.py:40
  9.8 0.3 collective-permute-start.3
  10.1 0.0 copy-done.1
  10.1 0.0 copy-done.4
  10.1 0.0 copy-done.3
  10.1 2.5 %own.1 = (f32[6,128,576]{2,1,0:T(8,128)S(1)}, f32[6,576]{1,0:T(8,128)S(1)}, f32[6,576]{1,0:T(8,128)S(1)}) custom-call(s32[4,4]{1,0:T(4,128)S(1)} %copy-done.4, bf16[4,1,144,768]{3,2,1,0:T(8,128)(2,1)S(1)} %copy-done.3, bf16[4,2,1,144,768]{4,3,2,1,0:T(8,128)(2,1)S(1)} %copy-done.1), custom_call_target="tpu_custom_call" | custom-call | flops 2548039680 | bytes 2654272 | tf_op jit(solution)/shard_map/own/pallas_call | solution.py:283
  12.7 0.0 copy-start.6
  12.7 1.3 %copy-done.6 = f32[6,128,576]{2,1,0:T(8,128)} copy-done((f32[6,128,576]{2,1,0:T(8,128)}, f32[6,128,576]{2,1,0:T(8,128)S(1)}, u32[]{:S(2)}) %copy-start.6) | copy-done | bytes 1769496
  14.6 0.0 collective-permute-done.1.refs_1_
  14.6 0.0 collective-permute-done.2.refs_2_
  14.6 0.0 collective-permute-done.3.refs_3_
  14.6 0.0 copy-done
  14.7 0.1 gather.1
  14.8 1.9 %collective-permute-start.6 = (bf16[24,512]{1,0:T(8,128)(2,1)S(1)}, bf16[24,512]{1,0:T(8,128)(2,1)S(1)}, u32[]{:S(2)}, u32[]{:S(2)}) collective-permute-start(bf16[24,512]{1,0:T(8,128)(2,1)S(1)} %get-tuple-element.44), channel_id=1, source_target_pairs={{0,4},{4,8},{8,12},{1,5},{5,9},{9,13},{2,6},{6,10},{10,14},{3,7},{... | collective-permute-start | bytes 73736 | tf_op jit(solution)/shard_map/ppermute | solution.py:31
  16.7 0.0 collective-permute-done.refs_0_
  16.7 1.1 %select_bitcast_fusion = (bf16[1,144,768]{2,1,0:T(8,128)(2,1)S(1)}, bf16[1,144,768]{2,1,0:T(8,128)(2,1)S(1)}) fusion(bf16[2,1,144,768]{3,2,1,0:T(8,128)(2,1)} %param.11, bf16[2,1,144,768]{3,2,1,0:T(8,128)(2,1)S(1)} %collective-permute-done.refs_0_, pred[]{:T(512)S(6)} %eq.3), kind=kLoop, calls=%fused_computation | loop fusion | flops 221184 | bytes 1327105 | tf_op jit(solution)/shard_map/jit(_where)/select_n | solution.py:452
  17.9 1.9 %collective-permute-start.4 = (bf16[1,144,768]{2,1,0:T(8,128)(2,1)S(1)}, bf16[1,144,768]{2,1,0:T(8,128)(2,1)S(1)}, u32[]{:S(2)}, u32[]{:S(2)}) collective-permute-start(bf16[1,144,768]{2,1,0:T(8,128)(2,1)S(1)} %get-tuple-element.51), channel_id=1, source_target_pairs={{0,4},{4,8},{8,12},{1,5},{5,9},{9,13},{2,6},{6,10},{10,14},{3,7},{... | collective-permute-start | bytes 663560 | tf_op jit(solution)/shard_map/ppermute | solution.py:31
  19.8 1.9 %collective-permute-start.7 = (bf16[1,144,512]{2,1,0:T(8,128)(2,1)S(1)}, bf16[1,144,512]{2,1,0:T(8,128)(2,1)S(1)}, u32[]{:S(2)}, u32[]{:S(2)}) collective-permute-start(bf16[1,144,512]{2,1,0:T(8,128)(2,1)S(1)} %slice.24), channel_id=1, source_target_pairs={{0,4},{4,8},{8,12},{1,5},{5,9},{9,13},{2,6},{6,10},{10,14},{3,7},{... | collective-permute-start | bytes 442376 | tf_op jit(solution)/shard_map/ppermute | solution.py:31
  21.7 1.9 %collective-permute-start.8 = (bf16[1,144,256]{2,1,0:T(8,128)(2,1)S(1)}, bf16[1,144,256]{2,1,0:T(8,128)(2,1)S(1)}, u32[]{:S(2)}, u32[]{:S(2)}) collective-permute-start(bf16[1,144,256]{2,1,0:T(8,128)(2,1)S(1)} %slice.25), channel_id=1, source_target_pairs={{0,4},{4,8},{8,12},{1,5},{5,9},{9,13},{2,6},{6,10},{10,14},{3,7},{... | collective-permute-start | bytes 221192 | tf_op jit(solution)/shard_map/ppermute | solution.py:31
  23.7 0.0 copy-done.5
  23.7 1.5 %copy-done.7 = f32[6,128,576]{2,1,0:T(8,128)S(1)} copy-done((f32[6,128,576]{2,1,0:T(8,128)S(1)}, f32[6,128,576]{2,1,0:T(8,128)}, u32[]{:S(2)}) %copy-start.7) | copy-done | bytes 1769496
  25.2 0.7 %middle.2 = (f32[6,128,576]{2,1,0:T(8,128)S(1)}, f32[6,576]{1,0:T(8,128)S(1)}, f32[6,576]{1,0:T(8,128)S(1)}) custom-call(s32[4,4]{1,0:T(4,128)S(1)} %copy-done.4, s32[4,4]{1,0:T(4,128)S(1)} %copy-done.5, bf16[4,1,144,768]{3,2,1,0:T(8,128)(2,1)S(1)} %copy-done.3, bf16[2,1,144,768]{3,2,1,0:T(8,128)(2,1)S(1)} %collective-permute-done.refs_0_, ...), custom_call_target="tpu_custom_call" | custom-call | flops 2548039680 | bytes 3124352 | tf_op jit(solution)/shard_map/middle/pallas_call | solution.py:283
  26.0 0.0 collective-permute-done.5.refs_0_
  26.0 1.2 %middle.3 = (f32[6,128,576]{2,1,0:T(8,128)S(1)}, f32[6,576]{1,0:T(8,128)S(1)}, f32[6,576]{1,0:T(8,128)S(1)}) custom-call(s32[4,4]{1,0:T(4,128)S(1)} %copy-done.4, s32[4,4]{1,0:T(4,128)S(1)} %copy-done.5, bf16[4,1,144,768]{3,2,1,0:T(8,128)(2,1)S(1)} %copy-done.3, bf16[2,1,144,768]{3,2,1,0:T(8,128)(2,1)} %collective-permute-done.5.refs_0_, ...), custom_call_target="tpu_custom_call" | custom-call | flops 2548039680 | bytes 3124352 | tf_op jit(solution)/shard_map/middle/pallas_call | solution.py:283
  27.2 3.6 %collective-permute-done.4.refs_0_ = bf16[1,144,768]{2,1,0:T(8,128)(2,1)S(1)} collective-permute-done((bf16[1,144,768]{2,1,0:T(8,128)(2,1)S(1)}, bf16[1,144,768]{2,1,0:T(8,128)(2,1)S(1)}, u32[]{:S(2)}, u32[]{:S(2)}) %collective-permute-start.4) | collective-permute-done | bytes 221216 | tf_op jit(solution)/shard_map/ppermute | solution.py:31
  30.7 1.8 %score.1 = (f32[6,128,576]{2,1,0:T(8,128)S(1)}, bf16[6,144,576]{2,1,0:T(8,128)(2,1)S(1)}) custom-call(s32[4,4]{1,0:T(4,128)S(1)} %copy-done.4, s32[4,4]{1,0:T(4,128)S(1)} %copy-done.5, bf16[4,1,144,768]{3,2,1,0:T(8,128)(2,1)S(1)} %copy-done.3, bf16[1,144,768]{2,1,0:T(8,128)(2,1)S(1)} %collective-permute-done.4.refs_0_, ...), custom_call_target="tpu_custom_call" | custom-call | flops 1274019840 | bytes 2903168 | tf_op jit(solution)/shard_map/score/pallas_call | solution.py:283
  32.5 0.0 collective-permute-done.6.tail_ref
  32.5 0.0 copy-done.2
  32.5 1.4 %decode.1 = bf16[1,36,512]{2,1,0:T(8,128)(2,1)} custom-call(s32[1]{0:T(128)S(6)} %copy.11.fade_ref, bf16[36,512]{1,0:T(8,128)(2,1)S(1)} %get-tuple-element.43.hidden_ref, bf16[24,512]{1,0:T(8,128)(2,1)S(1)} %collective-permute-done.6.tail_ref, bf16[3,512,512]{2,1,0:T(8,128)(2,1)S(1)} %copy-done.2), custom_call_target="tpu_custom_call" | custom-call | flops 566231040 | bytes 1634308 | tf_op jit(solution)/shard_map/decode/pallas_call | solution.py:283
  34.0 0.0 collective-permute-done.7.value_ref
  34.0 0.6 %average.1 = (f32[4,144,512]{2,1,0:T(8,128)S(1)}, f32[1,576]{1,0:T(1,128)S(1)}) custom-call(f32[6,128,576]{2,1,0:T(8,128)S(1)} %get-tuple-element.45.acc_ref, bf16[6,144,576]{2,1,0:T(8,128)(2,1)S(1)} %get-tuple-element.42.w_ref, bf16[1,144,512]{2,1,0:T(8,128)(2,1)S(1)} %collective-permute-done.7.value_ref), custom_call_target="tpu_custom_call" | custom-call | flops 637009920 | bytes 2912256 | tf_op jit(solution)/shard_map/average/pallas_call | solution.py:283
  34.6 0.8 %collective-permute-done.8.value_ref = bf16[1,144,256]{2,1,0:T(8,128)(2,1)S(1)} collective-permute-done((bf16[1,144,256]{2,1,0:T(8,128)(2,1)S(1)}, bf16[1,144,256]{2,1,0:T(8,128)(2,1)S(1)}, u32[]{:S(2)}, u32[]{:S(2)}) %collective-permute-start.8) | collective-permute-done | bytes 73760 | tf_op jit(solution)/shard_map/ppermute | solution.py:31
  35.4 0.3 rest.1
  35.7 1.6 %collective-permute-start.10 = (f32[1,576]{1,0:T(1,128)S(1)}, f32[1,576]{1,0:T(1,128)S(1)}, u32[]{:S(2)}, u32[]{:S(2)}) collective-permute-start(f32[1,576]{1,0:T(1,128)S(1)} %get-tuple-element.49.refs_0_), channel_id=1, source_target_pairs={{0,2},{1,3},{2,0},{3,1},{4,6},{5,7},{6,4},{7,5},{8,10},{9,11},{10,... | collective-permute-start | bytes 6920 | tf_op jit(solution)/shard_map/ppermute | solution.py:40
  37.2 0.0 collective-permute-start.11
  37.3 0.6 %collective-permute-start.9 = (f32[1,576]{1,0:T(1,128)S(1)}, f32[1,576]{1,0:T(1,128)S(1)}, u32[]{:S(2)}, u32[]{:S(2)}) collective-permute-start(f32[1,576]{1,0:T(1,128)S(1)} %get-tuple-element.49.refs_0_), channel_id=1, source_target_pairs={{0,1},{1,0},{2,3},{3,2},{4,5},{5,4},{6,7},{7,6},{8,9},{9,8},{10,11... | collective-permute-start | bytes 6920 | tf_op jit(solution)/shard_map/ppermute | solution.py:40
  37.9 0.2 turn.1.back_ref
  38.1 1.2 %collective-permute-done.10.refs_2_ = f32[1,576]{1,0:T(1,128)S(1)} collective-permute-done((f32[1,576]{1,0:T(1,128)S(1)}, f32[1,576]{1,0:T(1,128)S(1)}, u32[]{:S(2)}, u32[]{:S(2)}) %collective-permute-start.10) | collective-permute-done | bytes 2336 | tf_op jit(solution)/shard_map/ppermute | solution.py:40
  39.3 0.9 %collective-permute-done.11.refs_3_ = f32[1,576]{1,0:T(1,128)S(1)} collective-permute-done((f32[1,576]{1,0:T(1,128)S(1)}, f32[1,576]{1,0:T(1,128)S(1)}, u32[]{:S(2)}, u32[]{:S(2)}) %collective-permute-start.11) | collective-permute-done | bytes 2336 | tf_op jit(solution)/shard_map/ppermute | solution.py:40
  40.3 0.0 collective-permute-done.9.refs_1_
  40.3 1.1 %scale.1 = bf16[4,1,144,768]{3,2,1,0:T(8,128)(2,1)} custom-call(f32[4,144,512]{2,1,0:T(8,128)S(1)} %get-tuple-element.46.front_ref, f32[4,144,256]{2,1,0:T(8,128)S(1)} %turn.1.back_ref, f32[1,576]{1,0:T(1,128)S(1)} %get-tuple-element.49.refs_0_, f32[1,576]{1,0:T(1,128)S(1)} %collective-permute-done.9.refs_1_, f32[1,576]{1,0:T(1,128)S(1)} %collective-permute-done.10.refs_2_, ...), custom_call_target="tpu_custom_call" | custom-call | flops 4423680 | bytes 1778688 | tf_op jit(solution)/shard_map/scale/pallas_call | solution.py:283
  (6 shorter events, 0.0 us)
Async XLA Ops:
  0.6 9.5 %copy-start.1 = (bf16[4,2,1,144,768]{4,3,2,1,0:T(8,128)(2,1)S(1)}, bf16[4,2,1,144,768]{4,3,2,1,0:T(8,128)(2,1)}, u32[]{:S(2)}) copy-start(bf16[4,2,1,144,768]{4,3,2,1,0:T(8,128)(2,1)} %kv_ref.1) | copy-start | bytes 5308420
  0.6 9.5 %copy-start.4 = (s32[4,4]{1,0:T(4,128)S(1)}, s32[4,4]{1,0:T(4,128)}, u32[]{:S(2)}) copy-start(s32[4,4]{1,0:T(4,128)} %step_ref.7) | copy-start | bytes 196
  0.7 9.5 %copy-start.3 = (bf16[4,1,144,768]{3,2,1,0:T(8,128)(2,1)S(1)}, bf16[4,1,144,768]{3,2,1,0:T(8,128)(2,1)}, u32[]{:S(2)}) copy-start(bf16[4,1,144,768]{3,2,1,0:T(8,128)(2,1)} %q_ref.7) | copy-start | bytes 2654212
  0.7 16.1 %collective-permute-start = (bf16[2,1,144,768]{3,2,1,0:T(8,128)(2,1)}, bf16[2,1,144,768]{3,2,1,0:T(8,128)(2,1)S(1)}, u32[]{:S(2)}, u32[]{:S(2)}) collective-permute-start(bf16[2,1,144,768]{3,2,1,0:T(8,128)(2,1)} %param.11), channel_id=1, source_target_pairs={{0,8},{8,12},{1,9},{9,13},{2,10},{10,14},{3,11},{11,15},{16,24},{2... | collective-permute-start | bytes 1327112 | tf_op jit(solution)/shard_map/ppermute | solution.py:272
  4.4 21.5 %collective-permute-start.5 = (bf16[2,1,144,768]{3,2,1,0:T(8,128)(2,1)}, bf16[2,1,144,768]{3,2,1,0:T(8,128)(2,1)}, u32[]{:S(2)}, u32[]{:S(2)}) collective-permute-start(bf16[2,1,144,768]{3,2,1,0:T(8,128)(2,1)} %param.11), channel_id=1, source_target_pairs={{4,12},{5,13},{6,14},{7,15},{20,28},{21,29},{22,30},{23,31}} | collective-permute-start | bytes 1327112 | tf_op jit(solution)/shard_map/ppermute | solution.py:272
  8.2 6.5 %collective-permute-start.1 = (bf16[36,512]{1,0:T(8,128)(2,1)}, bf16[36,512]{1,0:T(8,128)(2,1)S(1)}, u32[]{:S(2)}, u32[]{:S(2)}) collective-permute-start(bf16[36,512]{1,0:T(8,128)(2,1)} %get-tuple-element.28), channel_id=1, source_target_pairs={{0,1},{1,0},{2,3},{3,2},{4,5},{5,4},{6,7},{7,6},{8,9},{9,8},{10,11... | collective-permute-start | bytes 110600 | tf_op jit(solution)/shard_map/ppermute | solution.py:40
  8.2 6.4 %collective-permute-start.2 = (bf16[36,512]{1,0:T(8,128)(2,1)}, bf16[36,512]{1,0:T(8,128)(2,1)S(1)}, u32[]{:S(2)}, u32[]{:S(2)}) collective-permute-start(bf16[36,512]{1,0:T(8,128)(2,1)} %get-tuple-element.29), channel_id=1, source_target_pairs={{0,2},{1,3},{2,0},{3,1},{4,6},{5,7},{6,4},{7,5},{8,10},{9,11},{10,... | collective-permute-start | bytes 110600 | tf_op jit(solution)/shard_map/ppermute | solution.py:40
  9.8 4.9 %copy-start = (bf16[36,512]{1,0:T(8,128)(2,1)S(1)}, bf16[36,512]{1,0:T(8,128)(2,1)}, u32[]{:S(2)}) copy-start(bf16[36,512]{1,0:T(8,128)(2,1)} %get-tuple-element.27.refs_0_) | copy-start | bytes 110596
  9.8 13.9 %copy-start.5 = (s32[4,4]{1,0:T(4,128)S(1)}, s32[4,4]{1,0:T(4,128)}, u32[]{:S(2)}) copy-start(s32[4,4]{1,0:T(4,128)} %mask_ref.5) | copy-start | bytes 196
  9.8 4.8 %collective-permute-start.3 = (bf16[36,512]{1,0:T(8,128)(2,1)}, bf16[36,512]{1,0:T(8,128)(2,1)S(1)}, u32[]{:S(2)}, u32[]{:S(2)}) collective-permute-start(bf16[36,512]{1,0:T(8,128)(2,1)} %get-tuple-element.30), channel_id=1, source_target_pairs={{0,3},{1,2},{2,1},{3,0},{4,7},{5,6},{6,5},{7,4},{8,11},{9,10},{10,... | collective-permute-start | bytes 110600 | tf_op jit(solution)/shard_map/ppermute | solution.py:40
  12.7 1.3 %copy-start.6 = (f32[6,128,576]{2,1,0:T(8,128)}, f32[6,128,576]{2,1,0:T(8,128)S(1)}, u32[]{:S(2)}) copy-start(f32[6,128,576]{2,1,0:T(8,128)S(1)} %get-tuple-element.26.refs_1_) | copy-start | bytes 5308420
  14.8 17.7 %collective-permute-start.6 = (bf16[24,512]{1,0:T(8,128)(2,1)S(1)}, bf16[24,512]{1,0:T(8,128)(2,1)S(1)}, u32[]{:S(2)}, u32[]{:S(2)}) collective-permute-start(bf16[24,512]{1,0:T(8,128)(2,1)S(1)} %get-tuple-element.44), channel_id=1, source_target_pairs={{0,4},{4,8},{8,12},{1,5},{5,9},{9,13},{2,6},{6,10},{10,14},{3,7},{... | collective-permute-start | bytes 73736 | tf_op jit(solution)/shard_map/ppermute | solution.py:31
  17.9 12.8 %collective-permute-start.4 = (bf16[1,144,768]{2,1,0:T(8,128)(2,1)S(1)}, bf16[1,144,768]{2,1,0:T(8,128)(2,1)S(1)}, u32[]{:S(2)}, u32[]{:S(2)}) collective-permute-start(bf16[1,144,768]{2,1,0:T(8,128)(2,1)S(1)} %get-tuple-element.51), channel_id=1, source_target_pairs={{0,4},{4,8},{8,12},{1,5},{5,9},{9,13},{2,6},{6,10},{10,14},{3,7},{... | collective-permute-start | bytes 663560 | tf_op jit(solution)/shard_map/ppermute | solution.py:31
  19.8 14.2 %collective-permute-start.7 = (bf16[1,144,512]{2,1,0:T(8,128)(2,1)S(1)}, bf16[1,144,512]{2,1,0:T(8,128)(2,1)S(1)}, u32[]{:S(2)}, u32[]{:S(2)}) collective-permute-start(bf16[1,144,512]{2,1,0:T(8,128)(2,1)S(1)} %slice.24), channel_id=1, source_target_pairs={{0,4},{4,8},{8,12},{1,5},{5,9},{9,13},{2,6},{6,10},{10,14},{3,7},{... | collective-permute-start | bytes 442376 | tf_op jit(solution)/shard_map/ppermute | solution.py:31
  21.7 13.6 %collective-permute-start.8 = (bf16[1,144,256]{2,1,0:T(8,128)(2,1)S(1)}, bf16[1,144,256]{2,1,0:T(8,128)(2,1)S(1)}, u32[]{:S(2)}, u32[]{:S(2)}) collective-permute-start(bf16[1,144,256]{2,1,0:T(8,128)(2,1)S(1)} %slice.25), channel_id=1, source_target_pairs={{0,4},{4,8},{8,12},{1,5},{5,9},{9,13},{2,6},{6,10},{10,14},{3,7},{... | collective-permute-start | bytes 221192 | tf_op jit(solution)/shard_map/ppermute | solution.py:31
  23.7 1.5 %copy-start.7 = (f32[6,128,576]{2,1,0:T(8,128)S(1)}, f32[6,128,576]{2,1,0:T(8,128)}, u32[]{:S(2)}) copy-start(f32[6,128,576]{2,1,0:T(8,128)} %copy-done.6) | copy-start | bytes 5308420
  30.7 1.8 %copy-start.2 = (bf16[3,512,512]{2,1,0:T(8,128)(2,1)S(1)}, bf16[3,512,512]{2,1,0:T(8,128)(2,1)}, u32[]{:S(2)}) copy-start(bf16[3,512,512]{2,1,0:T(8,128)(2,1)} %conv_ref.1) | copy-start | bytes 4718596
  35.7 3.7 %collective-permute-start.10 = (f32[1,576]{1,0:T(1,128)S(1)}, f32[1,576]{1,0:T(1,128)S(1)}, u32[]{:S(2)}, u32[]{:S(2)}) collective-permute-start(f32[1,576]{1,0:T(1,128)S(1)} %get-tuple-element.49.refs_0_), channel_id=1, source_target_pairs={{0,2},{1,3},{2,0},{3,1},{4,6},{5,7},{6,4},{7,5},{8,10},{9,11},{10,... | collective-permute-start | bytes 6920 | tf_op jit(solution)/shard_map/ppermute | solution.py:40
  37.2 3.0 %collective-permute-start.11 = (f32[1,576]{1,0:T(1,128)S(1)}, f32[1,576]{1,0:T(1,128)S(1)}, u32[]{:S(2)}, u32[]{:S(2)}) collective-permute-start(f32[1,576]{1,0:T(1,128)S(1)} %get-tuple-element.49.refs_0_), channel_id=1, source_target_pairs={{0,3},{1,2},{2,1},{3,0},{4,7},{5,6},{6,5},{7,4},{8,11},{9,10},{10,... | collective-permute-start | bytes 6920 | tf_op jit(solution)/shard_map/ppermute | solution.py:40
  37.3 3.0 %collective-permute-start.9 = (f32[1,576]{1,0:T(1,128)S(1)}, f32[1,576]{1,0:T(1,128)S(1)}, u32[]{:S(2)}, u32[]{:S(2)}) collective-permute-start(f32[1,576]{1,0:T(1,128)S(1)} %get-tuple-element.49.refs_0_), channel_id=1, source_target_pairs={{0,1},{1,0},{2,3},{3,2},{4,5},{5,4},{6,7},{7,6},{8,9},{9,8},{10,11... | collective-permute-start | bytes 6920 | tf_op jit(solution)/shard_map/ppermute | solution.py:40

commit v9 on v5

--- a/solution.py
+++ b/solution.py
@@ -38,6 +38,16 @@
     else:
         pairs = [(source, (source + offset) % count) for source in range(count)]
     return lax.ppermute(value, axes, pairs)
+
+
+def cross(value, offset):
+    chips, cores = lax.axis_size("mp"), lax.axis_size("seq")
+    pairs = [
+        (chip * cores + core, (chip + offset) % chips * cores + (core + 1) % cores)
+        for chip in range(chips)
+        for core in range(cores)
+    ]
+    return lax.ppermute(value, ("mp", "seq"), pairs)
 
 
 def target_of(axes, offset):
@@ -507,7 +517,7 @@
         row_count * columns,
         (averaged, squares, *within),
     )
-    others = [swap(squares, "mp", offset) for offset in range(1, lax.axis_size("mp"))]
+    others = [cross(squares, offset) for offset in range(1, lax.axis_size("mp"))]
     decoded = decode(after(hidden, back), tail, conv_w, fade_count)
     attended = plain_call(
         functools.partial(scale_kernel, columns * lax.axis_size(axes)),

time: 41.6 us -> 41.4 us (level)
    ppermute x5 -> x4, starting transfers between devices: 3.56 us -> 2 us  [swap(): return lax.ppermute(value, axes, pairs)]
    ppermute x0 -> x1, starting transfers between devices: none -> 1.33 us  [cross(): return lax.ppermute(value, ('mp', 'seq'), pairs)]
    ppermute x5 -> x4, waiting for transfers between devices: 1.17 us -> 0.51 us  [swap(): return lax.ppermute(value, axes, pairs)]
where the time goes in v9:
time: 41.4 us; the launch traced here: 40.7 us
  starting transfers between devices  16 us (39%)
  Pallas kernels  13.9 us (34%)
  waiting for transfers between devices  5.91 us (14%)
  local copies, waits for them, and re-layouts  3.36 us (8%)
  between operations  1.5 us (4%)
    pallas_call x11, Pallas kernels, plain_call(): pl.pallas_call(kernel, in_specs=list(in_specs) + [VMEM_SPEC] * (len(opera...  13.9 us
    ppermute x4, starting transfers between devices, hop(): lax.ppermute(value, axis, [(source, source + steps) for source in range(c...  8.35 us
    ppermute x4, waiting for transfers between devices, hop(): lax.ppermute(value, axis, [(source, source + steps) for source in range(c...  4.56 us
    ppermute x2, starting transfers between devices, send(): return lax.ppermute(value, 'span', pairs)  4.3 us
    unnamed x16, local copies, waits for them, and re-layouts  3.34 us
    ppermute x4, starting transfers between devices, swap(): return lax.ppermute(value, axes, pairs)  2 us
    ppermute x1, starting transfers between devices, cross(): return lax.ppermute(value, ('mp', 'seq'), pairs)  1.33 us
  transfers between devices with their start and end apart: 11, of which 6 were waited for; matrix products, arithmetic and copies ran while one was open for 0% of the time, Pallas kernels for 31%

profile of v9, /device:TPU:20, one launch (start us, length us, event | category | flops | bytes accessed | tf_op | source)
XLA Modules:
  0.0 40.7 jit_solution(16231326324087115026)
XLA Ops:
  0.6 0.0 copy-start.7
  0.6 3.6 %collective-permute-start = (bf16[2,1,144,768]{3,2,1,0:T(8,128)(2,1)}, bf16[2,1,144,768]{3,2,1,0:T(8,128)(2,1)S(1)}, u32[]{:S(2)}, u32[]{:S(2)}) collective-permute-start(bf16[2,1,144,768]{3,2,1,0:T(8,128)(2,1)} %param.11), channel_id=1, source_target_pairs={{0,8},{8,12},{1,9},{9,13},{2,10},{10,14},{3,11},{11,15},{16,24},{2... | collective-permute-start | bytes 1327112 | tf_op jit(solution)/shard_map/ppermute | solution.py:287
  4.3 2.3 %project.1 = (bf16[36,512]{1,0:T(8,128)(2,1)}, bf16[36,512]{1,0:T(8,128)(2,1)}, bf16[36,512]{1,0:T(8,128)(2,1)}, bf16[36,512]{1,0:T(8,128)(2,1)}) custom-call(bf16[1,144,768]{2,1,0:T(8,128)(2,1)} %x_hbm.1, bf16[768,512]{1,0:T(8,128)(2,1)} %w_hbm.1), custom_call_target="tpu_custom_call" | custom-call | flops 113246208 | bytes 1007616 | tf_op jit(solution)/shard_map/project/pallas_call | solution.py:298
  6.6 0.1 collective-permute-start.1
  6.6 1.6 %collective-permute-start.2 = (bf16[36,512]{1,0:T(8,128)(2,1)}, bf16[36,512]{1,0:T(8,128)(2,1)S(1)}, u32[]{:S(2)}, u32[]{:S(2)}) collective-permute-start(bf16[36,512]{1,0:T(8,128)(2,1)} %get-tuple-element.30), channel_id=1, source_target_pairs={{0,2},{1,3},{2,0},{3,1},{4,6},{5,7},{6,4},{7,5},{8,10},{9,11},{10,... | collective-permute-start | bytes 110600 | tf_op jit(solution)/shard_map/ppermute | solution.py:40
  8.2 0.3 collective-permute-start.3
  8.5 0.7 %collective-permute-start.5 = (bf16[2,1,144,768]{3,2,1,0:T(8,128)(2,1)}, bf16[2,1,144,768]{3,2,1,0:T(8,128)(2,1)S(1)}, u32[]{:S(2)}, u32[]{:S(2)}) collective-permute-start(bf16[2,1,144,768]{3,2,1,0:T(8,128)(2,1)} %param.11), channel_id=1, source_target_pairs={{4,12},{5,13},{6,14},{7,15},{20,28},{21,29},{22,30},{23,31}} | collective-permute-start | bytes 1327112 | tf_op jit(solution)/shard_map/ppermute | solution.py:287
  9.2 0.0 copy-start
  9.2 1.2 %copy-done = bf16[4,1,144,768]{3,2,1,0:T(8,128)(2,1)S(1)} copy-done((bf16[4,1,144,768]{3,2,1,0:T(8,128)(2,1)S(1)}, bf16[4,1,144,768]{3,2,1,0:T(8,128)(2,1)}, u32[]{:S(2)}) %copy-start) | copy-done | bytes 884760
  10.4 1.5 %copy-done.2 = bf16[4,2,1,144,768]{4,3,2,1,0:T(8,128)(2,1)S(1)} copy-done((bf16[4,2,1,144,768]{4,3,2,1,0:T(8,128)(2,1)S(1)}, bf16[4,2,1,144,768]{4,3,2,1,0:T(8,128)(2,1)}, u32[]{:S(2)}) %copy-start.2) | copy-done | bytes 1769496
  11.8 0.0 copy-start.5
  11.8 0.7 %copy-done.5 = s32[4,4]{1,0:T(4,128)S(1)} copy-done((s32[4,4]{1,0:T(4,128)S(1)}, s32[4,4]{1,0:T(4,128)}, u32[]{:S(2)}) %copy-start.5) | copy-done | bytes 88
  12.5 0.0 copy-start.4
  12.5 0.0 copy-start.1
  12.5 2.5 %own.1 = (f32[6,128,576]{2,1,0:T(8,128)S(1)}, f32[6,576]{1,0:T(8,128)S(1)}, f32[6,576]{1,0:T(8,128)S(1)}) custom-call(s32[4,4]{1,0:T(4,128)S(1)} %copy-done.5, bf16[4,1,144,768]{3,2,1,0:T(8,128)(2,1)S(1)} %copy-done, bf16[4,2,1,144,768]{4,3,2,1,0:T(8,128)(2,1)S(1)} %copy-done.2), custom_call_target="tpu_custom_call" | custom-call | flops 254803968 | bytes 2654272 | tf_op jit(solution)/shard_map/own/pallas_call | solution.py:298
  15.1 0.0 collective-permute-done.1.refs_1_
  15.1 0.0 collective-permute-done.2.refs_2_
  15.1 0.0 collective-permute-done.3.refs_3_
  15.1 0.0 copy-done.4
  15.1 0.1 gather.1
  15.3 0.5 %collective-permute-done.refs_0_ = bf16[2,1,144,768]{3,2,1,0:T(8,128)(2,1)S(1)} collective-permute-done((bf16[2,1,144,768]{3,2,1,0:T(8,128)(2,1)}, bf16[2,1,144,768]{3,2,1,0:T(8,128)(2,1)S(1)}, u32[]{:S(2)}, u32[]{:S(2)}) %collective-permute-start) | collective-permute-done | bytes 442400 | tf_op jit(solution)/shard_map/ppermute | solution.py:287
  15.8 0.0 copy-done.7
  15.8 0.1 select_bitcast_fusion
  15.8 2.6 %collective-permute-start.4 = (bf16[1,144,768]{2,1,0:T(8,128)(2,1)S(1)}, bf16[1,144,768]{2,1,0:T(8,128)(2,1)S(1)}, u32[]{:S(2)}, u32[]{:S(2)}) collective-permute-start(bf16[1,144,768]{2,1,0:T(8,128)(2,1)S(1)} %get-tuple-element.53), channel_id=1, source_target_pairs={{0,4},{4,8},{8,12},{1,5},{5,9},{9,13},{2,6},{6,10},{10,14},{3,7},{... | collective-permute-start | bytes 663560 | tf_op jit(solution)/shard_map/ppermute | solution.py:31
  18.5 1.9 %collective-permute-start.6 = (bf16[1,144,512]{2,1,0:T(8,128)(2,1)S(1)}, bf16[1,144,512]{2,1,0:T(8,128)(2,1)S(1)}, u32[]{:S(2)}, u32[]{:S(2)}) collective-permute-start(bf16[1,144,512]{2,1,0:T(8,128)(2,1)S(1)} %slice.24), channel_id=1, source_target_pairs={{0,4},{4,8},{8,12},{1,5},{5,9},{9,13},{2,6},{6,10},{10,14},{3,7},{... | collective-permute-start | bytes 442376 | tf_op jit(solution)/shard_map/ppermute | solution.py:31
  20.4 1.9 %collective-permute-start.7 = (bf16[1,144,256]{2,1,0:T(8,128)(2,1)S(1)}, bf16[1,144,256]{2,1,0:T(8,128)(2,1)S(1)}, u32[]{:S(2)}, u32[]{:S(2)}) collective-permute-start(bf16[1,144,256]{2,1,0:T(8,128)(2,1)S(1)} %slice.25), channel_id=1, source_target_pairs={{0,4},{4,8},{8,12},{1,5},{5,9},{9,13},{2,6},{6,10},{10,14},{3,7},{... | collective-permute-start | bytes 221192 | tf_op jit(solution)/shard_map/ppermute | solution.py:31
  22.3 1.9 %collective-permute-start.10 = (bf16[24,512]{1,0:T(8,128)(2,1)S(1)}, bf16[24,512]{1,0:T(8,128)(2,1)S(1)}, u32[]{:S(2)}, u32[]{:S(2)}) collective-permute-start(bf16[24,512]{1,0:T(8,128)(2,1)S(1)} %get-tuple-element.51), channel_id=1, source_target_pairs={{0,4},{4,8},{8,12},{1,5},{5,9},{9,13},{2,6},{6,10},{10,14},{3,7},{... | collective-permute-start | bytes 73736 | tf_op jit(solution)/shard_map/ppermute | solution.py:31
  24.3 0.0 copy-done.1
  24.3 0.0 copy-done.6
  24.3 2.7 %middle.2 = (f32[6,128,576]{2,1,0:T(8,128)S(1)}, f32[6,576]{1,0:T(8,128)S(1)}, f32[6,576]{1,0:T(8,128)S(1)}) custom-call(s32[4,4]{1,0:T(4,128)S(1)} %copy-done.5, s32[4,4]{1,0:T(4,128)S(1)} %copy-done.6, bf16[4,1,144,768]{3,2,1,0:T(8,128)(2,1)S(1)} %copy-done.1, bf16[2,1,144,768]{3,2,1,0:T(8,128)(2,1)S(1)} %collective-permute-done.refs_0_, ...), custom_call_target="tpu_custom_call" | custom-call | flops 254803968 | bytes 3124352 | tf_op jit(solution)/shard_map/middle/pallas_call | solution.py:298
  27.0 0.0 collective-permute-done.5.refs_0_
  27.0 0.7 %middle.3 = (f32[6,128,576]{2,1,0:T(8,128)S(1)}, f32[6,576]{1,0:T(8,128)S(1)}, f32[6,576]{1,0:T(8,128)S(1)}) custom-call(s32[4,4]{1,0:T(4,128)S(1)} %copy-done.5, s32[4,4]{1,0:T(4,128)S(1)} %copy-done.6, bf16[4,1,144,768]{3,2,1,0:T(8,128)(2,1)S(1)} %copy-done.1, bf16[2,1,144,768]{3,2,1,0:T(8,128)(2,1)S(1)} %collective-permute-done.5.refs_0_, ...), custom_call_target="tpu_custom_call" | custom-call | flops 254803968 | bytes 3124352 | tf_op jit(solution)/shard_map/middle/pallas_call | solution.py:298
  27.8 2.2 %collective-permute-done.4.refs_0_ = bf16[1,144,768]{2,1,0:T(8,128)(2,1)S(1)} collective-permute-done((bf16[1,144,768]{2,1,0:T(8,128)(2,1)S(1)}, bf16[1,144,768]{2,1,0:T(8,128)(2,1)S(1)}, u32[]{:S(2)}, u32[]{:S(2)}) %collective-permute-start.4) | collective-permute-done | bytes 221216 | tf_op jit(solution)/shard_map/ppermute | solution.py:31
  30.0 1.8 %score.1 = (f32[6,128,576]{2,1,0:T(8,128)S(1)}, bf16[6,144,576]{2,1,0:T(8,128)(2,1)S(1)}) custom-call(s32[4,4]{1,0:T(4,128)S(1)} %copy-done.5, s32[4,4]{1,0:T(4,128)S(1)} %copy-done.6, bf16[4,1,144,768]{3,2,1,0:T(8,128)(2,1)S(1)} %copy-done.1, bf16[1,144,768]{2,1,0:T(8,128)(2,1)S(1)} %collective-permute-done.4.refs_0_, ...), custom_call_target="tpu_custom_call" | custom-call | flops 127401984 | bytes 2903168 | tf_op jit(solution)/shard_map/score/pallas_call | solution.py:298
  31.8 1.4 %collective-permute-done.6.value_ref = bf16[1,144,512]{2,1,0:T(8,128)(2,1)S(1)} collective-permute-done((bf16[1,144,512]{2,1,0:T(8,128)(2,1)S(1)}, bf16[1,144,512]{2,1,0:T(8,128)(2,1)S(1)}, u32[]{:S(2)}, u32[]{:S(2)}) %collective-permute-start.6) | collective-permute-done | bytes 147488 | tf_op jit(solution)/shard_map/ppermute | solution.py:31
  33.2 0.6 %average.1 = (f32[4,144,512]{2,1,0:T(8,128)S(1)}, f32[1,576]{1,0:T(1,128)S(1)}) custom-call(f32[6,128,576]{2,1,0:T(8,128)S(1)} %get-tuple-element.42.acc_ref, bf16[6,144,576]{2,1,0:T(8,128)(2,1)S(1)} %get-tuple-element.43.w_ref, bf16[1,144,512]{2,1,0:T(8,128)(2,1)S(1)} %collective-permute-done.6.value_ref), custom_call_target="tpu_custom_call" | custom-call | flops 63700992 | bytes 2912256 | tf_op jit(solution)/shard_map/average/pallas_call | solution.py:298
  33.8 0.0 copy-start.3
  33.8 0.9 %collective-permute-done.7.value_ref = bf16[1,144,256]{2,1,0:T(8,128)(2,1)S(1)} collective-permute-done((bf16[1,144,256]{2,1,0:T(8,128)(2,1)S(1)}, bf16[1,144,256]{2,1,0:T(8,128)(2,1)S(1)}, u32[]{:S(2)}, u32[]{:S(2)}) %collective-permute-start.7) | collective-permute-done | bytes 73760 | tf_op jit(solution)/shard_map/ppermute | solution.py:31
  34.7 0.3 rest.1
  35.1 0.1 collective-permute-start.8
  35.8 0.5 %collective-permute-done.8.refs_1_ = f32[1,576]{1,0:T(1,128)S(1)} collective-permute-done((f32[1,576]{1,0:T(1,128)S(1)}, f32[1,576]{1,0:T(1,128)S(1)}, u32[]{:S(2)}, u32[]{:S(2)}) %collective-permute-start.8) | collective-permute-done | bytes 2336 | tf_op jit(solution)/shard_map/ppermute | solution.py:40
  36.3 0.2 turn.1
  36.5 1.3 %collective-permute-start.9 = (f32[1,576]{1,0:T(1,128)S(1)}, f32[1,576]{1,0:T(1,128)S(1)}, u32[]{:S(2)}, u32[]{:S(2)}) collective-permute-start(f32[1,576]{1,0:T(1,128)S(1)} %get-tuple-element.49.refs_0_), channel_id=1, source_target_pairs={{0,3},{1,2},{2,1},{3,0},{4,7},{5,6},{6,5},{7,4},{8,11},{9,10},{10,... | collective-permute-start | bytes 6920 | tf_op jit(solution)/shard_map/ppermute | solution.py:50
  37.9 0.0 collective-permute-done.10.tail_ref
  37.9 0.0 copy-done.3
  37.9 1.4 %decode.1 = bf16[1,36,512]{2,1,0:T(8,128)(2,1)} custom-call(s32[1]{0:T(128)S(6)} %copy.11.fade_ref, bf16[36,512]{1,0:T(8,128)(2,1)S(1)} %get-tuple-element.50.hidden_ref, bf16[24,512]{1,0:T(8,128)(2,1)S(1)} %collective-permute-done.10.tail_ref, bf16[3,512,512]{2,1,0:T(8,128)(2,1)S(1)} %copy-done.3), custom_call_target="tpu_custom_call" | custom-call | flops 56623104 | bytes 1634308 | tf_op jit(solution)/shard_map/decode/pallas_call | solution.py:298
  39.3 0.3 collective-permute-done.9.refs_1_
  39.6 1.1 %scale.1 = bf16[4,1,144,768]{3,2,1,0:T(8,128)(2,1)} custom-call(f32[4,144,512]{2,1,0:T(8,128)S(1)} %get-tuple-element.44.front_ref, f32[4,144,256]{2,1,0:T(8,128)S(1)} %get-tuple-element.48.back_ref, f32[1,576]{1,0:T(1,128)S(1)} %get-tuple-element.49.refs_0_, f32[1,576]{1,0:T(1,128)S(1)} %collective-permute-done.9.refs_1_), custom_call_target="tpu_custom_call" | custom-call | flops 442368 | bytes 1774080 | tf_op jit(solution)/shard_map/scale/pallas_call | solution.py:298
  (4 shorter events, 0.0 us)
Async XLA Ops:
  0.6 15.2 %copy-start.7 = (bf16[2,1,144,768]{3,2,1,0:T(8,128)(2,1)S(1)}, bf16[2,1,144,768]{3,2,1,0:T(8,128)(2,1)}, u32[]{:S(2)}) copy-start(bf16[2,1,144,768]{3,2,1,0:T(8,128)(2,1)} %param.11) | copy-start | bytes 1327108
  0.6 15.1 %collective-permute-start = (bf16[2,1,144,768]{3,2,1,0:T(8,128)(2,1)}, bf16[2,1,144,768]{3,2,1,0:T(8,128)(2,1)S(1)}, u32[]{:S(2)}, u32[]{:S(2)}) collective-permute-start(bf16[2,1,144,768]{3,2,1,0:T(8,128)(2,1)} %param.11), channel_id=1, source_target_pairs={{0,8},{8,12},{1,9},{9,13},{2,10},{10,14},{3,11},{11,15},{16,24},{2... | collective-permute-start | bytes 1327112 | tf_op jit(solution)/shard_map/ppermute | solution.py:287
  6.6 8.5 %collective-permute-start.1 = (bf16[36,512]{1,0:T(8,128)(2,1)}, bf16[36,512]{1,0:T(8,128)(2,1)S(1)}, u32[]{:S(2)}, u32[]{:S(2)}) collective-permute-start(bf16[36,512]{1,0:T(8,128)(2,1)} %get-tuple-element.29), channel_id=1, source_target_pairs={{0,1},{1,0},{2,3},{3,2},{4,5},{5,4},{6,7},{7,6},{8,9},{9,8},{10,11... | collective-permute-start | bytes 110600 | tf_op jit(solution)/shard_map/ppermute | solution.py:40
  6.6 8.4 %collective-permute-start.2 = (bf16[36,512]{1,0:T(8,128)(2,1)}, bf16[36,512]{1,0:T(8,128)(2,1)S(1)}, u32[]{:S(2)}, u32[]{:S(2)}) collective-permute-start(bf16[36,512]{1,0:T(8,128)(2,1)} %get-tuple-element.30), channel_id=1, source_target_pairs={{0,2},{1,3},{2,0},{3,1},{4,6},{5,7},{6,4},{7,5},{8,10},{9,11},{10,... | collective-permute-start | bytes 110600 | tf_op jit(solution)/shard_map/ppermute | solution.py:40
  8.2 6.9 %collective-permute-start.3 = (bf16[36,512]{1,0:T(8,128)(2,1)}, bf16[36,512]{1,0:T(8,128)(2,1)S(1)}, u32[]{:S(2)}, u32[]{:S(2)}) collective-permute-start(bf16[36,512]{1,0:T(8,128)(2,1)} %get-tuple-element.31), channel_id=1, source_target_pairs={{0,3},{1,2},{2,1},{3,0},{4,7},{5,6},{6,5},{7,4},{8,11},{9,10},{10,... | collective-permute-start | bytes 110600 | tf_op jit(solution)/shard_map/ppermute | solution.py:40
  8.5 18.5 %collective-permute-start.5 = (bf16[2,1,144,768]{3,2,1,0:T(8,128)(2,1)}, bf16[2,1,144,768]{3,2,1,0:T(8,128)(2,1)S(1)}, u32[]{:S(2)}, u32[]{:S(2)}) collective-permute-start(bf16[2,1,144,768]{3,2,1,0:T(8,128)(2,1)} %param.11), channel_id=1, source_target_pairs={{4,12},{5,13},{6,14},{7,15},{20,28},{21,29},{22,30},{23,31}} | collective-permute-start | bytes 1327112 | tf_op jit(solution)/shard_map/ppermute | solution.py:287
  9.2 1.2 %copy-start = (bf16[4,1,144,768]{3,2,1,0:T(8,128)(2,1)S(1)}, bf16[4,1,144,768]{3,2,1,0:T(8,128)(2,1)}, u32[]{:S(2)}) copy-start(bf16[4,1,144,768]{3,2,1,0:T(8,128)(2,1)} %q_ref.7) | copy-start | bytes 2654212
  10.4 1.5 %copy-start.2 = (bf16[4,2,1,144,768]{4,3,2,1,0:T(8,128)(2,1)S(1)}, bf16[4,2,1,144,768]{4,3,2,1,0:T(8,128)(2,1)}, u32[]{:S(2)}) copy-start(bf16[4,2,1,144,768]{4,3,2,1,0:T(8,128)(2,1)} %kv_ref.1) | copy-start | bytes 5308420
  11.8 0.7 %copy-start.5 = (s32[4,4]{1,0:T(4,128)S(1)}, s32[4,4]{1,0:T(4,128)}, u32[]{:S(2)}) copy-start(s32[4,4]{1,0:T(4,128)} %step_ref.7) | copy-start | bytes 196
  12.5 2.6 %copy-start.4 = (bf16[36,512]{1,0:T(8,128)(2,1)S(1)}, bf16[36,512]{1,0:T(8,128)(2,1)}, u32[]{:S(2)}) copy-start(bf16[36,512]{1,0:T(8,128)(2,1)} %get-tuple-element.28.refs_0_) | copy-start | bytes 110596
  12.5 11.7 %copy-start.1 = (bf16[4,1,144,768]{3,2,1,0:T(8,128)(2,1)S(1)}, bf16[4,1,144,768]{3,2,1,0:T(8,128)(2,1)}, u32[]{:S(2)}) copy-start(bf16[4,1,144,768]{3,2,1,0:T(8,128)(2,1)} %q_ref.7) | copy-start | bytes 2654212
  12.5 11.7 %copy-start.6 = (s32[4,4]{1,0:T(4,128)S(1)}, s32[4,4]{1,0:T(4,128)}, u32[]{:S(2)}) copy-start(s32[4,4]{1,0:T(4,128)} %mask_ref.5) | copy-start | bytes 196
  15.8 14.2 %collective-permute-start.4 = (bf16[1,144,768]{2,1,0:T(8,128)(2,1)S(1)}, bf16[1,144,768]{2,1,0:T(8,128)(2,1)S(1)}, u32[]{:S(2)}, u32[]{:S(2)}) collective-permute-start(bf16[1,144,768]{2,1,0:T(8,128)(2,1)S(1)} %get-tuple-element.53), channel_id=1, source_target_pairs={{0,4},{4,8},{8,12},{1,5},{5,9},{9,13},{2,6},{6,10},{10,14},{3,7},{... | collective-permute-start | bytes 663560 | tf_op jit(solution)/shard_map/ppermute | solution.py:31
  18.5 14.7 %collective-permute-start.6 = (bf16[1,144,512]{2,1,0:T(8,128)(2,1)S(1)}, bf16[1,144,512]{2,1,0:T(8,128)(2,1)S(1)}, u32[]{:S(2)}, u32[]{:S(2)}) collective-permute-start(bf16[1,144,512]{2,1,0:T(8,128)(2,1)S(1)} %slice.24), channel_id=1, source_target_pairs={{0,4},{4,8},{8,12},{1,5},{5,9},{9,13},{2,6},{6,10},{10,14},{3,7},{... | collective-permute-start | bytes 442376 | tf_op jit(solution)/shard_map/ppermute | solution.py:31
  20.4 14.3 %collective-permute-start.7 = (bf16[1,144,256]{2,1,0:T(8,128)(2,1)S(1)}, bf16[1,144,256]{2,1,0:T(8,128)(2,1)S(1)}, u32[]{:S(2)}, u32[]{:S(2)}) collective-permute-start(bf16[1,144,256]{2,1,0:T(8,128)(2,1)S(1)} %slice.25), channel_id=1, source_target_pairs={{0,4},{4,8},{8,12},{1,5},{5,9},{9,13},{2,6},{6,10},{10,14},{3,7},{... | collective-permute-start | bytes 221192 | tf_op jit(solution)/shard_map/ppermute | solution.py:31
  22.3 15.5 %collective-permute-start.10 = (bf16[24,512]{1,0:T(8,128)(2,1)S(1)}, bf16[24,512]{1,0:T(8,128)(2,1)S(1)}, u32[]{:S(2)}, u32[]{:S(2)}) collective-permute-start(bf16[24,512]{1,0:T(8,128)(2,1)S(1)} %get-tuple-element.51), channel_id=1, source_target_pairs={{0,4},{4,8},{8,12},{1,5},{5,9},{9,13},{2,6},{6,10},{10,14},{3,7},{... | collective-permute-start | bytes 73736 | tf_op jit(solution)/shard_map/ppermute | solution.py:31
  33.8 4.1 %copy-start.3 = (bf16[3,512,512]{2,1,0:T(8,128)(2,1)S(1)}, bf16[3,512,512]{2,1,0:T(8,128)(2,1)}, u32[]{:S(2)}) copy-start(bf16[3,512,512]{2,1,0:T(8,128)(2,1)} %conv_ref.1) | copy-start | bytes 4718596
  35.1 1.2 %collective-permute-start.8 = (f32[1,576]{1,0:T(1,128)S(1)}, f32[1,576]{1,0:T(1,128)S(1)}, u32[]{:S(2)}, u32[]{:S(2)}) collective-permute-start(f32[1,576]{1,0:T(1,128)S(1)} %get-tuple-element.47.refs_0_), channel_id=1, source_target_pairs={{0,1},{1,0},{2,3},{3,2},{4,5},{5,4},{6,7},{7,6},{8,9},{9,8},{10,11... | collective-permute-start | bytes 6920 | tf_op jit(solution)/shard_map/ppermute | solution.py:40
  36.5 3.1 %collective-permute-start.9 = (f32[1,576]{1,0:T(1,128)S(1)}, f32[1,576]{1,0:T(1,128)S(1)}, u32[]{:S(2)}, u32[]{:S(2)}) collective-permute-start(f32[1,576]{1,0:T(1,128)S(1)} %get-tuple-element.49.refs_0_), channel_id=1, source_target_pairs={{0,3},{1,2},{2,1},{3,0},{4,7},{5,6},{6,5},{7,4},{8,11},{9,10},{10,... | collective-permute-start | bytes 6920 | tf_op jit(solution)/shard_map/ppermute | solution.py:50

commit v10 on v4

--- a/solution.py
+++ b/solution.py
@@ -423,7 +423,7 @@
 ):
     steps, _, rows, columns = query.shape
     heads = columns // HD
-    middle = -(-2 * heads // 3) * HD
+    middle = max(1, heads - 1) * HD
     row_count = steps * rows
     span = lax.axis_size("span")
     axes = ("mp", "seq")

time: 41.1 us -> 41.5 us (level)
  Pallas kernels: 11 us -> 12 us
  waiting for transfers between devices: 8 us -> 7.38 us
    pallas_call x11, Pallas kernels: 11 us -> 12 us  [plain_call(): pl.pallas_call(kernel, in_specs=list(in_specs) + [VMEM_SPEC] * (len(opera...]
    ppermute x4, waiting for transfers between devices: 6.84 us -> 6.13 us  [hop(): lax.ppermute(value, axis, [(source, source + steps) for source in range(c...]
  transfers between devices with their start and end apart: 12 -> 12, of which waited for: 5 -> 5; matrix products, arithmetic and copies ran while one was open for 0% -> 0% of each run, Pallas kernels for 24% -> 27%
where the time goes in v10:
time: 41.5 us; the launch traced here: 41.1 us
  starting transfers between devices  16.8 us (40%)
  Pallas kernels  12 us (29%)
  waiting for transfers between devices  7.38 us (18%)
  local copies, waits for them, and re-layouts  3.37 us (8%)
  between operations  1.5 us (4%)
    pallas_call x11, Pallas kernels, plain_call(): pl.pallas_call(kernel, in_specs=list(in_specs) + [VMEM_SPEC] * (len(opera...  12 us
    ppermute x4, starting transfers between devices, hop(): lax.ppermute(value, axis, [(source, source + steps) for source in range(c...  8.35 us
    ppermute x4, waiting for transfers between devices, hop(): lax.ppermute(value, axis, [(source, source + steps) for source in range(c...  6.13 us
    ppermute x2, starting transfers between devices, send(): return lax.ppermute(value, 'span', pairs)  4.3 us
    ppermute x6, starting transfers between devices, swap(): return lax.ppermute(value, axes, pairs)  4.2 us
    unnamed x16, local copies, waits for them, and re-layouts  3.34 us
  transfers between devices with their start and end apart: 12, of which 5 were waited for; matrix products, arithmetic and copies ran while one was open for 0% of the time, Pallas kernels for 27%

profile of v10, /device:TPU:20, one launch (start us, length us, event | category | flops | bytes accessed | tf_op | source)
XLA Modules:
  0.0 41.1 jit_solution(11945191538104703254)
XLA Ops:
  0.6 0.0 copy-start.7
  0.6 3.6 %collective-permute-start = (bf16[2,1,144,768]{3,2,1,0:T(8,128)(2,1)}, bf16[2,1,144,768]{3,2,1,0:T(8,128)(2,1)S(1)}, u32[]{:S(2)}, u32[]{:S(2)}) collective-permute-start(bf16[2,1,144,768]{3,2,1,0:T(8,128)(2,1)} %param.11), channel_id=1, source_target_pairs={{0,8},{8,12},{1,9},{9,13},{2,10},{10,14},{3,11},{11,15},{16,24},{2... | collective-permute-start | bytes 1327112 | tf_op jit(solution)/shard_map/ppermute | solution.py:273
  4.3 2.3 %project.1 = (bf16[36,512]{1,0:T(8,128)(2,1)}, bf16[36,512]{1,0:T(8,128)(2,1)}, bf16[36,512]{1,0:T(8,128)(2,1)}, bf16[36,512]{1,0:T(8,128)(2,1)}) custom-call(bf16[1,144,768]{2,1,0:T(8,128)(2,1)} %x_hbm.1, bf16[768,512]{1,0:T(8,128)(2,1)} %w_hbm.1), custom_call_target="tpu_custom_call" | custom-call | flops 113246208 | bytes 1007616 | tf_op jit(solution)/shard_map/project/pallas_call | solution.py:284
  6.6 0.1 collective-permute-start.1
  6.6 1.6 %collective-permute-start.2 = (bf16[36,512]{1,0:T(8,128)(2,1)}, bf16[36,512]{1,0:T(8,128)(2,1)S(1)}, u32[]{:S(2)}, u32[]{:S(2)}) collective-permute-start(bf16[36,512]{1,0:T(8,128)(2,1)} %get-tuple-element.30), channel_id=1, source_target_pairs={{0,2},{1,3},{2,0},{3,1},{4,6},{5,7},{6,4},{7,5},{8,10},{9,11},{10,... | collective-permute-start | bytes 110600 | tf_op jit(solution)/shard_map/ppermute | solution.py:40
  8.2 0.3 collective-permute-start.3
  8.5 0.7 %collective-permute-start.5 = (bf16[2,1,144,768]{3,2,1,0:T(8,128)(2,1)}, bf16[2,1,144,768]{3,2,1,0:T(8,128)(2,1)S(1)}, u32[]{:S(2)}, u32[]{:S(2)}) collective-permute-start(bf16[2,1,144,768]{3,2,1,0:T(8,128)(2,1)} %param.11), channel_id=1, source_target_pairs={{4,12},{5,13},{6,14},{7,15},{20,28},{21,29},{22,30},{23,31}} | collective-permute-start | bytes 1327112 | tf_op jit(solution)/shard_map/ppermute | solution.py:273
  9.2 0.0 copy-start
  9.2 1.2 %copy-done = bf16[4,1,144,768]{3,2,1,0:T(8,128)(2,1)S(1)} copy-done((bf16[4,1,144,768]{3,2,1,0:T(8,128)(2,1)S(1)}, bf16[4,1,144,768]{3,2,1,0:T(8,128)(2,1)}, u32[]{:S(2)}) %copy-start) | copy-done | bytes 884760
  10.4 1.5 %copy-done.2 = bf16[4,2,1,144,768]{4,3,2,1,0:T(8,128)(2,1)S(1)} copy-done((bf16[4,2,1,144,768]{4,3,2,1,0:T(8,128)(2,1)S(1)}, bf16[4,2,1,144,768]{4,3,2,1,0:T(8,128)(2,1)}, u32[]{:S(2)}) %copy-start.2) | copy-done | bytes 1769496
  11.8 0.0 copy-start.5
  11.8 0.7 %copy-done.5 = s32[4,4]{1,0:T(4,128)S(1)} copy-done((s32[4,4]{1,0:T(4,128)S(1)}, s32[4,4]{1,0:T(4,128)}, u32[]{:S(2)}) %copy-start.5) | copy-done | bytes 88
  12.5 2.5 %own.1 = (f32[6,128,576]{2,1,0:T(8,128)S(1)}, f32[6,576]{1,0:T(8,128)S(1)}, f32[6,576]{1,0:T(8,128)S(1)}) custom-call(s32[4,4]{1,0:T(4,128)S(1)} %copy-done.5, bf16[4,1,144,768]{3,2,1,0:T(8,128)(2,1)S(1)} %copy-done, bf16[4,2,1,144,768]{4,3,2,1,0:T(8,128)(2,1)S(1)} %copy-done.2), custom_call_target="tpu_custom_call" | custom-call | flops 254803968 | bytes 2654272 | tf_op jit(solution)/shard_map/own/pallas_call | solution.py:284
  15.1 0.0 collective-permute-done.1.refs_1_
  15.1 0.0 collective-permute-done.2.refs_2_
  15.1 0.0 collective-permute-done.3.refs_3_
  15.1 0.0 copy-done.4
  15.1 0.1 gather.1
  15.3 0.5 %collective-permute-done.refs_0_ = bf16[2,1,144,768]{3,2,1,0:T(8,128)(2,1)S(1)} collective-permute-done((bf16[2,1,144,768]{3,2,1,0:T(8,128)(2,1)}, bf16[2,1,144,768]{3,2,1,0:T(8,128)(2,1)S(1)}, u32[]{:S(2)}, u32[]{:S(2)}) %collective-permute-start) | collective-permute-done | bytes 442400 | tf_op jit(solution)/shard_map/ppermute | solution.py:273
  15.8 0.0 copy-done.7
  15.8 0.1 select_bitcast_fusion
  15.8 2.6 %collective-permute-start.4 = (bf16[1,144,768]{2,1,0:T(8,128)(2,1)S(1)}, bf16[1,144,768]{2,1,0:T(8,128)(2,1)S(1)}, u32[]{:S(2)}, u32[]{:S(2)}) collective-permute-start(bf16[1,144,768]{2,1,0:T(8,128)(2,1)S(1)} %get-tuple-element.53), channel_id=1, source_target_pairs={{0,4},{4,8},{8,12},{1,5},{5,9},{9,13},{2,6},{6,10},{10,14},{3,7},{... | collective-permute-start | bytes 663560 | tf_op jit(solution)/shard_map/ppermute | solution.py:31
  18.5 1.9 %collective-permute-start.6 = (bf16[1,144,640]{2,1,0:T(8,128)(2,1)S(1)}, bf16[1,144,640]{2,1,0:T(8,128)(2,1)S(1)}, u32[]{:S(2)}, u32[]{:S(2)}) collective-permute-start(bf16[1,144,640]{2,1,0:T(8,128)(2,1)S(1)} %slice.24), channel_id=1, source_target_pairs={{0,4},{4,8},{8,12},{1,5},{5,9},{9,13},{2,6},{6,10},{10,14},{3,7},{... | collective-permute-start | bytes 552968 | tf_op jit(solution)/shard_map/ppermute | solution.py:31
  21.0 1.9 %collective-permute-start.11 = (bf16[24,512]{1,0:T(8,128)(2,1)S(1)}, bf16[24,512]{1,0:T(8,128)(2,1)S(1)}, u32[]{:S(2)}, u32[]{:S(2)}) collective-permute-start(bf16[24,512]{1,0:T(8,128)(2,1)S(1)} %get-tuple-element.51), channel_id=1, source_target_pairs={{0,4},{4,8},{8,12},{1,5},{5,9},{9,13},{2,6},{6,10},{10,14},{3,7},{... | collective-permute-start | bytes 73736 | tf_op jit(solution)/shard_map/ppermute | solution.py:31
  23.0 1.9 %collective-permute-start.7 = (bf16[1,144,128]{2,1,0:T(8,128)(2,1)S(1)}, bf16[1,144,128]{2,1,0:T(8,128)(2,1)S(1)}, u32[]{:S(2)}, u32[]{:S(2)}) collective-permute-start(bf16[1,144,128]{2,1,0:T(8,128)(2,1)S(1)} %slice.25), channel_id=1, source_target_pairs={{0,4},{4,8},{8,12},{1,5},{5,9},{9,13},{2,6},{6,10},{10,14},{3,7},{... | collective-permute-start | bytes 110600 | tf_op jit(solution)/shard_map/ppermute | solution.py:31
  24.9 0.0 copy-done.1
  24.9 0.0 copy-done.6
  24.9 0.7 %middle.2 = (f32[6,128,576]{2,1,0:T(8,128)S(1)}, f32[6,576]{1,0:T(8,128)S(1)}, f32[6,576]{1,0:T(8,128)S(1)}) custom-call(s32[4,4]{1,0:T(4,128)S(1)} %copy-done.5, s32[4,4]{1,0:T(4,128)S(1)} %copy-done.6, bf16[4,1,144,768]{3,2,1,0:T(8,128)(2,1)S(1)} %copy-done.1, bf16[2,1,144,768]{3,2,1,0:T(8,128)(2,1)S(1)} %collective-permute-done.refs_0_, ...), custom_call_target="tpu_custom_call" | custom-call | flops 254803968 | bytes 3124352 | tf_op jit(solution)/shard_map/middle/pallas_call | solution.py:284
  25.7 0.0 collective-permute-done.5.refs_0_
  25.7 0.7 %middle.3 = (f32[6,128,576]{2,1,0:T(8,128)S(1)}, f32[6,576]{1,0:T(8,128)S(1)}, f32[6,576]{1,0:T(8,128)S(1)}) custom-call(s32[4,4]{1,0:T(4,128)S(1)} %copy-done.5, s32[4,4]{1,0:T(4,128)S(1)} %copy-done.6, bf16[4,1,144,768]{3,2,1,0:T(8,128)(2,1)S(1)} %copy-done.1, bf16[2,1,144,768]{3,2,1,0:T(8,128)(2,1)S(1)} %collective-permute-done.5.refs_0_, ...), custom_call_target="tpu_custom_call" | custom-call | flops 254803968 | bytes 3124352 | tf_op jit(solution)/shard_map/middle/pallas_call | solution.py:284
  26.4 3.6 %collective-permute-done.4.refs_0_ = bf16[1,144,768]{2,1,0:T(8,128)(2,1)S(1)} collective-permute-done((bf16[1,144,768]{2,1,0:T(8,128)(2,1)S(1)}, bf16[1,144,768]{2,1,0:T(8,128)(2,1)S(1)}, u32[]{:S(2)}, u32[]{:S(2)}) %collective-permute-start.4) | collective-permute-done | bytes 221216 | tf_op jit(solution)/shard_map/ppermute | solution.py:31
  30.0 1.8 %score.1 = (f32[6,128,576]{2,1,0:T(8,128)S(1)}, bf16[6,144,576]{2,1,0:T(8,128)(2,1)S(1)}) custom-call(s32[4,4]{1,0:T(4,128)S(1)} %copy-done.5, s32[4,4]{1,0:T(4,128)S(1)} %copy-done.6, bf16[4,1,144,768]{3,2,1,0:T(8,128)(2,1)S(1)} %copy-done.1, bf16[1,144,768]{2,1,0:T(8,128)(2,1)S(1)} %collective-permute-done.4.refs_0_, ...), custom_call_target="tpu_custom_call" | custom-call | flops 127401984 | bytes 2903168 | tf_op jit(solution)/shard_map/score/pallas_call | solution.py:284
  31.8 2.2 %collective-permute-done.6.value_ref = bf16[1,144,640]{2,1,0:T(8,128)(2,1)S(1)} collective-permute-done((bf16[1,144,640]{2,1,0:T(8,128)(2,1)S(1)}, bf16[1,144,640]{2,1,0:T(8,128)(2,1)S(1)}, u32[]{:S(2)}, u32[]{:S(2)}) %collective-permute-start.6) | collective-permute-done | bytes 184352 | tf_op jit(solution)/shard_map/ppermute | solution.py:31
  34.0 0.8 %average.1 = (f32[4,144,640]{2,1,0:T(8,128)S(1)}, f32[1,576]{1,0:T(1,128)S(1)}) custom-call(f32[6,128,576]{2,1,0:T(8,128)S(1)} %get-tuple-element.42.acc_ref, bf16[6,144,576]{2,1,0:T(8,128)(2,1)S(1)} %get-tuple-element.43.w_ref, bf16[1,144,640]{2,1,0:T(8,128)(2,1)S(1)} %collective-permute-done.6.value_ref), custom_call_target="tpu_custom_call" | custom-call | flops 63700992 | bytes 2949120 | tf_op jit(solution)/shard_map/average/pallas_call | solution.py:284
  34.8 0.0 copy-start.3
  34.8 0.4 collective-permute-done.7.value_ref
  35.2 0.3 rest.1
  35.5 1.6 %collective-permute-start.8 = (f32[1,576]{1,0:T(1,128)S(1)}, f32[1,576]{1,0:T(1,128)S(1)}, u32[]{:S(2)}, u32[]{:S(2)}) collective-permute-start(f32[1,576]{1,0:T(1,128)S(1)} %get-tuple-element.47.square_in), channel_id=1, source_target_pairs={{0,2},{1,3},{2,0},{3,1},{4,6},{5,7},{6,4},{7,5},{8,10},{9,11},{10,... | collective-permute-start | bytes 6920 | tf_op jit(solution)/shard_map/ppermute | solution.py:40
  37.0 0.0 collective-permute-start.9
  37.0 0.1 turn.1
  37.2 0.7 %collective-permute-start.10 = (f32[1,576]{1,0:T(1,128)S(1)}, f32[1,576]{1,0:T(1,128)S(1)}, u32[]{:S(2)}, u32[]{:S(2)}) collective-permute-start(f32[1,576]{1,0:T(1,128)S(1)} %get-tuple-element.49.refs_0_), channel_id=1, source_target_pairs={{0,1},{1,0},{2,3},{3,2},{4,5},{5,4},{6,7},{7,6},{8,9},{9,8},{10,11... | collective-permute-start | bytes 6920 | tf_op jit(solution)/shard_map/ppermute | solution.py:40
  37.9 0.0 collective-permute-done.11.tail_ref
  37.9 0.0 copy-done.3
  37.9 1.4 %decode.1 = bf16[1,36,512]{2,1,0:T(8,128)(2,1)} custom-call(s32[1]{0:T(128)S(6)} %copy.11.fade_ref, bf16[36,512]{1,0:T(8,128)(2,1)S(1)} %get-tuple-element.50.hidden_ref, bf16[24,512]{1,0:T(8,128)(2,1)S(1)} %collective-permute-done.11.tail_ref, bf16[3,512,512]{2,1,0:T(8,128)(2,1)S(1)} %copy-done.3), custom_call_target="tpu_custom_call" | custom-call | flops 56623104 | bytes 1634308 | tf_op jit(solution)/shard_map/decode/pallas_call | solution.py:284
  39.3 0.0 collective-permute-done.10.refs_3_
  39.3 0.0 collective-permute-done.8.refs_1_
  39.3 0.7 %collective-permute-done.9.refs_2_ = f32[1,576]{1,0:T(1,128)S(1)} collective-permute-done((f32[1,576]{1,0:T(1,128)S(1)}, f32[1,576]{1,0:T(1,128)S(1)}, u32[]{:S(2)}, u32[]{:S(2)}) %collective-permute-start.9) | collective-permute-done | bytes 2336 | tf_op jit(solution)/shard_map/ppermute | solution.py:40
  40.1 1.1 %scale.1 = bf16[4,1,144,768]{3,2,1,0:T(8,128)(2,1)} custom-call(f32[4,144,640]{2,1,0:T(8,128)S(1)} %get-tuple-element.44.front_ref, f32[4,144,128]{2,1,0:T(8,128)S(1)} %get-tuple-element.48.back_ref, f32[1,576]{1,0:T(1,128)S(1)} %get-tuple-element.49.refs_0_, f32[1,576]{1,0:T(1,128)S(1)} %collective-permute-done.8.refs_1_, ...), custom_call_target="tpu_custom_call" | custom-call | flops 442368 | bytes 1778688 | tf_op jit(solution)/shard_map/scale/pallas_call | solution.py:284
  (6 shorter events, 0.0 us)
Async XLA Ops:
  0.6 15.2 %copy-start.7 = (bf16[2,1,144,768]{3,2,1,0:T(8,128)(2,1)S(1)}, bf16[2,1,144,768]{3,2,1,0:T(8,128)(2,1)}, u32[]{:S(2)}) copy-start(bf16[2,1,144,768]{3,2,1,0:T(8,128)(2,1)} %param.11) | copy-start | bytes 1327108
  0.6 15.1 %collective-permute-start = (bf16[2,1,144,768]{3,2,1,0:T(8,128)(2,1)}, bf16[2,1,144,768]{3,2,1,0:T(8,128)(2,1)S(1)}, u32[]{:S(2)}, u32[]{:S(2)}) collective-permute-start(bf16[2,1,144,768]{3,2,1,0:T(8,128)(2,1)} %param.11), channel_id=1, source_target_pairs={{0,8},{8,12},{1,9},{9,13},{2,10},{10,14},{3,11},{11,15},{16,24},{2... | collective-permute-start | bytes 1327112 | tf_op jit(solution)/shard_map/ppermute | solution.py:273
  6.6 8.5 %collective-permute-start.1 = (bf16[36,512]{1,0:T(8,128)(2,1)}, bf16[36,512]{1,0:T(8,128)(2,1)S(1)}, u32[]{:S(2)}, u32[]{:S(2)}) collective-permute-start(bf16[36,512]{1,0:T(8,128)(2,1)} %get-tuple-element.29), channel_id=1, source_target_pairs={{0,1},{1,0},{2,3},{3,2},{4,5},{5,4},{6,7},{7,6},{8,9},{9,8},{10,11... | collective-permute-start | bytes 110600 | tf_op jit(solution)/shard_map/ppermute | solution.py:40
  6.6 8.5 %collective-permute-start.2 = (bf16[36,512]{1,0:T(8,128)(2,1)}, bf16[36,512]{1,0:T(8,128)(2,1)S(1)}, u32[]{:S(2)}, u32[]{:S(2)}) collective-permute-start(bf16[36,512]{1,0:T(8,128)(2,1)} %get-tuple-element.30), channel_id=1, source_target_pairs={{0,2},{1,3},{2,0},{3,1},{4,6},{5,7},{6,4},{7,5},{8,10},{9,11},{10,... | collective-permute-start | bytes 110600 | tf_op jit(solution)/shard_map/ppermute | solution.py:40
  8.2 6.9 %collective-permute-start.3 = (bf16[36,512]{1,0:T(8,128)(2,1)}, bf16[36,512]{1,0:T(8,128)(2,1)S(1)}, u32[]{:S(2)}, u32[]{:S(2)}) collective-permute-start(bf16[36,512]{1,0:T(8,128)(2,1)} %get-tuple-element.31), channel_id=1, source_target_pairs={{0,3},{1,2},{2,1},{3,0},{4,7},{5,6},{6,5},{7,4},{8,11},{9,10},{10,... | collective-permute-start | bytes 110600 | tf_op jit(solution)/shard_map/ppermute | solution.py:40
  8.5 17.2 %collective-permute-start.5 = (bf16[2,1,144,768]{3,2,1,0:T(8,128)(2,1)}, bf16[2,1,144,768]{3,2,1,0:T(8,128)(2,1)S(1)}, u32[]{:S(2)}, u32[]{:S(2)}) collective-permute-start(bf16[2,1,144,768]{3,2,1,0:T(8,128)(2,1)} %param.11), channel_id=1, source_target_pairs={{4,12},{5,13},{6,14},{7,15},{20,28},{21,29},{22,30},{23,31}} | collective-permute-start | bytes 1327112 | tf_op jit(solution)/shard_map/ppermute | solution.py:273
  9.2 1.2 %copy-start = (bf16[4,1,144,768]{3,2,1,0:T(8,128)(2,1)S(1)}, bf16[4,1,144,768]{3,2,1,0:T(8,128)(2,1)}, u32[]{:S(2)}) copy-start(bf16[4,1,144,768]{3,2,1,0:T(8,128)(2,1)} %q_ref.7) | copy-start | bytes 2654212
  10.4 1.5 %copy-start.2 = (bf16[4,2,1,144,768]{4,3,2,1,0:T(8,128)(2,1)S(1)}, bf16[4,2,1,144,768]{4,3,2,1,0:T(8,128)(2,1)}, u32[]{:S(2)}) copy-start(bf16[4,2,1,144,768]{4,3,2,1,0:T(8,128)(2,1)} %kv_ref.1) | copy-start | bytes 5308420
  11.8 0.7 %copy-start.5 = (s32[4,4]{1,0:T(4,128)S(1)}, s32[4,4]{1,0:T(4,128)}, u32[]{:S(2)}) copy-start(s32[4,4]{1,0:T(4,128)} %step_ref.7) | copy-start | bytes 196
  12.5 2.6 %copy-start.4 = (bf16[36,512]{1,0:T(8,128)(2,1)S(1)}, bf16[36,512]{1,0:T(8,128)(2,1)}, u32[]{:S(2)}) copy-start(bf16[36,512]{1,0:T(8,128)(2,1)} %get-tuple-element.28.refs_0_) | copy-start | bytes 110596
  12.5 12.4 %copy-start.1 = (bf16[4,1,144,768]{3,2,1,0:T(8,128)(2,1)S(1)}, bf16[4,1,144,768]{3,2,1,0:T(8,128)(2,1)}, u32[]{:S(2)}) copy-start(bf16[4,1,144,768]{3,2,1,0:T(8,128)(2,1)} %q_ref.7) | copy-start | bytes 2654212
  12.5 12.4 %copy-start.6 = (s32[4,4]{1,0:T(4,128)S(1)}, s32[4,4]{1,0:T(4,128)}, u32[]{:S(2)}) copy-start(s32[4,4]{1,0:T(4,128)} %mask_ref.5) | copy-start | bytes 196
  15.8 14.2 %collective-permute-start.4 = (bf16[1,144,768]{2,1,0:T(8,128)(2,1)S(1)}, bf16[1,144,768]{2,1,0:T(8,128)(2,1)S(1)}, u32[]{:S(2)}, u32[]{:S(2)}) collective-permute-start(bf16[1,144,768]{2,1,0:T(8,128)(2,1)S(1)} %get-tuple-element.53), channel_id=1, source_target_pairs={{0,4},{4,8},{8,12},{1,5},{5,9},{9,13},{2,6},{6,10},{10,14},{3,7},{... | collective-permute-start | bytes 663560 | tf_op jit(solution)/shard_map/ppermute | solution.py:31
  18.5 15.5 %collective-permute-start.6 = (bf16[1,144,640]{2,1,0:T(8,128)(2,1)S(1)}, bf16[1,144,640]{2,1,0:T(8,128)(2,1)S(1)}, u32[]{:S(2)}, u32[]{:S(2)}) collective-permute-start(bf16[1,144,640]{2,1,0:T(8,128)(2,1)S(1)} %slice.24), channel_id=1, source_target_pairs={{0,4},{4,8},{8,12},{1,5},{5,9},{9,13},{2,6},{6,10},{10,14},{3,7},{... | collective-permute-start | bytes 552968 | tf_op jit(solution)/shard_map/ppermute | solution.py:31
  21.0 16.9 %collective-permute-start.11 = (bf16[24,512]{1,0:T(8,128)(2,1)S(1)}, bf16[24,512]{1,0:T(8,128)(2,1)S(1)}, u32[]{:S(2)}, u32[]{:S(2)}) collective-permute-start(bf16[24,512]{1,0:T(8,128)(2,1)S(1)} %get-tuple-element.51), channel_id=1, source_target_pairs={{0,4},{4,8},{8,12},{1,5},{5,9},{9,13},{2,6},{6,10},{10,14},{3,7},{... | collective-permute-start | bytes 73736 | tf_op jit(solution)/shard_map/ppermute | solution.py:31
  23.0 12.2 %collective-permute-start.7 = (bf16[1,144,128]{2,1,0:T(8,128)(2,1)S(1)}, bf16[1,144,128]{2,1,0:T(8,128)(2,1)S(1)}, u32[]{:S(2)}, u32[]{:S(2)}) collective-permute-start(bf16[1,144,128]{2,1,0:T(8,128)(2,1)S(1)} %slice.25), channel_id=1, source_target_pairs={{0,4},{4,8},{8,12},{1,5},{5,9},{9,13},{2,6},{6,10},{10,14},{3,7},{... | collective-permute-start | bytes 110600 | tf_op jit(solution)/shard_map/ppermute | solution.py:31
  34.8 3.1 %copy-start.3 = (bf16[3,512,512]{2,1,0:T(8,128)(2,1)S(1)}, bf16[3,512,512]{2,1,0:T(8,128)(2,1)}, u32[]{:S(2)}) copy-start(bf16[3,512,512]{2,1,0:T(8,128)(2,1)} %conv_ref.1) | copy-start | bytes 4718596
  35.5 3.9 %collective-permute-start.8 = (f32[1,576]{1,0:T(1,128)S(1)}, f32[1,576]{1,0:T(1,128)S(1)}, u32[]{:S(2)}, u32[]{:S(2)}) collective-permute-start(f32[1,576]{1,0:T(1,128)S(1)} %get-tuple-element.47.square_in), channel_id=1, source_target_pairs={{0,2},{1,3},{2,0},{3,1},{4,6},{5,7},{6,4},{7,5},{8,10},{9,11},{10,... | collective-permute-start | bytes 6920 | tf_op jit(solution)/shard_map/ppermute | solution.py:40
  37.0 3.0 %collective-permute-start.9 = (f32[1,576]{1,0:T(1,128)S(1)}, f32[1,576]{1,0:T(1,128)S(1)}, u32[]{:S(2)}, u32[]{:S(2)}) collective-permute-start(f32[1,576]{1,0:T(1,128)S(1)} %get-tuple-element.47.square_in), channel_id=1, source_target_pairs={{0,3},{1,2},{2,1},{3,0},{4,7},{5,6},{6,5},{7,4},{8,11},{9,10},{10,... | collective-permute-start | bytes 6920 | tf_op jit(solution)/shard_map/ppermute | solution.py:40
  37.2 2.1 %collective-permute-start.10 = (f32[1,576]{1,0:T(1,128)S(1)}, f32[1,576]{1,0:T(1,128)S(1)}, u32[]{:S(2)}, u32[]{:S(2)}) collective-permute-start(f32[1,576]{1,0:T(1,128)S(1)} %get-tuple-element.49.refs_0_), channel_id=1, source_target_pairs={{0,1},{1,0},{2,3},{3,2},{4,5},{5,4},{6,7},{7,6},{8,9},{9,8},{10,11... | collective-permute-start | bytes 6920 | tf_op jit(solution)/shard_map/ppermute | solution.py:40

commit v11 on v3

--- a/solution.py
+++ b/solution.py
@@ -213,8 +213,11 @@
 
 
 def average_head(head, acc_ref, w_ref, value_ref, first):
-    if value_ref.shape[-1] == acc_ref.shape[0] * HD:
+    width = acc_ref.shape[0] * HD
+    if value_ref.shape[-1] == width:
         first = 0
+    if value_ref.shape[-1] > width:
+        first = -acc_ref.shape[0]
     cut = slice((head - first) * HD, (head - first + 1) * HD)
     return acc_ref[head] + tn_dot(half(value_ref, 1, cut), w_ref[head])
 
@@ -451,10 +454,11 @@
         near = after(near, carry[0], hidden)
         forwards = lax.axis_index("span") == 2
         passed = [jnp.where(forwards, near[which], clean_kv[which]) for which in range(2)]
-        passed = [passed[0], passed[1][:, :, :middle], passed[1][:, :, middle:]]
+        front = jnp.concatenate([passed[0], passed[1][:, :, :middle]], 2)
+        passed = [front, passed[1][:, :, middle:]]
         passed = [hop(block, "span", 1) for block in passed]
         early = [(near, {2: 0, 3: 2}), (direct, {3: 1})]
-        keys, *values = passed
+        keys, values = passed[0], passed
         last_plan = {1: 0, 2: 1, 3: 0}
     else:
         ring = [near]

time: 41.1 us -> 41.1 us (level)
  Pallas kernels: 11 us -> 13 us
  starting transfers between devices: 16.8 us -> 14.9 us
    pallas_call x11, Pallas kernels: 11 us -> 13 us  [plain_call(): pl.pallas_call(kernel, in_specs=list(in_specs) + [VMEM_SPEC] * (len(opera...]
    ppermute x4 -> x3, starting transfers between devices: 8.35 us -> 6.43 us  [hop(): lax.ppermute(value, axis, [(source, source + steps) for source in range(c...]
    ppermute x4 -> x3, waiting for transfers between devices: 6.97 us -> 6.86 us  [hop(): lax.ppermute(value, axis, [(source, source + steps) for source in range(c...]
  transfers between devices with their start and end apart: 12 -> 11, of which waited for: 5 -> 4; matrix products, arithmetic and copies ran while one was open for 0% -> 0% of each run, Pallas kernels for 24% -> 29%
where the time goes in v11:
time: 41.1 us; the launch traced here: 40.8 us
  starting transfers between devices  14.9 us (36%)
  Pallas kernels  13 us (32%)
  waiting for transfers between devices  7.91 us (19%)
  local copies, waits for them, and re-layouts  3.37 us (8%)
  between operations  1.49 us (4%)
    pallas_call x11, Pallas kernels, plain_call(): pl.pallas_call(kernel, in_specs=list(in_specs) + [VMEM_SPEC] * (len(opera...  13 us
    ppermute x3, waiting for transfers between devices, hop(): lax.ppermute(value, axis, [(source, source + steps) for source in range(c...  6.86 us
    ppermute x3, starting transfers between devices, hop(): lax.ppermute(value, axis, [(source, source + steps) for source in range(c...  6.43 us
    ppermute x2, starting transfers between devices, send(): return lax.ppermute(value, 'span', pairs)  4.3 us
    ppermute x6, starting transfers between devices, swap(): return lax.ppermute(value, axes, pairs)  4.2 us
    unnamed x16, local copies, waits for them, and re-layouts  3.35 us
  transfers between devices with their start and end apart: 11, of which 4 were waited for; matrix products, arithmetic and copies ran while one was open for 0% of the time, Pallas kernels for 29%

profile of v11, /device:TPU:20, one launch (start us, length us, event | category | flops | bytes accessed | tf_op | source)
XLA Modules:
  0.0 40.8 jit_solution(17700625519787357680)
XLA Ops:
  0.6 0.0 copy-start.7
  0.6 3.6 %collective-permute-start = (bf16[2,1,144,768]{3,2,1,0:T(8,128)(2,1)}, bf16[2,1,144,768]{3,2,1,0:T(8,128)(2,1)S(1)}, u32[]{:S(2)}, u32[]{:S(2)}) collective-permute-start(bf16[2,1,144,768]{3,2,1,0:T(8,128)(2,1)} %param.11), channel_id=1, source_target_pairs={{0,8},{8,12},{1,9},{9,13},{2,10},{10,14},{3,11},{11,15},{16,24},{2... | collective-permute-start | bytes 1327112 | tf_op jit(solution)/shard_map/ppermute | solution.py:276
  4.3 2.3 %project.1 = (bf16[36,512]{1,0:T(8,128)(2,1)}, bf16[36,512]{1,0:T(8,128)(2,1)}, bf16[36,512]{1,0:T(8,128)(2,1)}, bf16[36,512]{1,0:T(8,128)(2,1)}) custom-call(bf16[1,144,768]{2,1,0:T(8,128)(2,1)} %x_hbm.1, bf16[768,512]{1,0:T(8,128)(2,1)} %w_hbm.1), custom_call_target="tpu_custom_call" | custom-call | flops 113246208 | bytes 1007616 | tf_op jit(solution)/shard_map/project/pallas_call | solution.py:287
  6.6 0.1 collective-permute-start.1
  6.6 1.6 %collective-permute-start.2 = (bf16[36,512]{1,0:T(8,128)(2,1)}, bf16[36,512]{1,0:T(8,128)(2,1)S(1)}, u32[]{:S(2)}, u32[]{:S(2)}) collective-permute-start(bf16[36,512]{1,0:T(8,128)(2,1)} %get-tuple-element.30), channel_id=1, source_target_pairs={{0,2},{1,3},{2,0},{3,1},{4,6},{5,7},{6,4},{7,5},{8,10},{9,11},{10,... | collective-permute-start | bytes 110600 | tf_op jit(solution)/shard_map/ppermute | solution.py:40
  8.2 0.3 collective-permute-start.3
  8.5 0.7 %collective-permute-start.5 = (bf16[2,1,144,768]{3,2,1,0:T(8,128)(2,1)}, bf16[2,1,144,768]{3,2,1,0:T(8,128)(2,1)S(1)}, u32[]{:S(2)}, u32[]{:S(2)}) collective-permute-start(bf16[2,1,144,768]{3,2,1,0:T(8,128)(2,1)} %param.11), channel_id=1, source_target_pairs={{4,12},{5,13},{6,14},{7,15},{20,28},{21,29},{22,30},{23,31}} | collective-permute-start | bytes 1327112 | tf_op jit(solution)/shard_map/ppermute | solution.py:276
  9.2 0.0 copy-start
  9.2 1.2 %copy-done = bf16[4,1,144,768]{3,2,1,0:T(8,128)(2,1)S(1)} copy-done((bf16[4,1,144,768]{3,2,1,0:T(8,128)(2,1)S(1)}, bf16[4,1,144,768]{3,2,1,0:T(8,128)(2,1)}, u32[]{:S(2)}) %copy-start) | copy-done | bytes 884760
  10.4 0.0 copy-start.2
  10.4 1.5 %copy-done.2 = bf16[4,2,1,144,768]{4,3,2,1,0:T(8,128)(2,1)S(1)} copy-done((bf16[4,2,1,144,768]{4,3,2,1,0:T(8,128)(2,1)S(1)}, bf16[4,2,1,144,768]{4,3,2,1,0:T(8,128)(2,1)}, u32[]{:S(2)}) %copy-start.2) | copy-done | bytes 1769496
  11.8 0.0 copy-start.5
  11.8 0.7 %copy-done.5 = s32[4,4]{1,0:T(4,128)S(1)} copy-done((s32[4,4]{1,0:T(4,128)S(1)}, s32[4,4]{1,0:T(4,128)}, u32[]{:S(2)}) %copy-start.5) | copy-done | bytes 88
  12.5 2.5 %own.1 = (f32[6,128,576]{2,1,0:T(8,128)S(1)}, f32[6,576]{1,0:T(8,128)S(1)}, f32[6,576]{1,0:T(8,128)S(1)}) custom-call(s32[4,4]{1,0:T(4,128)S(1)} %copy-done.5, bf16[4,1,144,768]{3,2,1,0:T(8,128)(2,1)S(1)} %copy-done, bf16[4,2,1,144,768]{4,3,2,1,0:T(8,128)(2,1)S(1)} %copy-done.2), custom_call_target="tpu_custom_call" | custom-call | flops 254803968 | bytes 2654272 | tf_op jit(solution)/shard_map/own/pallas_call | solution.py:287
  15.1 0.0 copy-start.1
  15.1 0.0 copy-start.6
  15.1 0.0 collective-permute-done.1.refs_1_
  15.1 0.0 collective-permute-done.2.refs_2_
  15.1 0.0 collective-permute-done.3.refs_3_
  15.1 0.0 copy-done.4
  15.1 0.1 gather.1
  15.3 0.5 %collective-permute-done.refs_0_ = bf16[2,1,144,768]{3,2,1,0:T(8,128)(2,1)S(1)} collective-permute-done((bf16[2,1,144,768]{3,2,1,0:T(8,128)(2,1)}, bf16[2,1,144,768]{3,2,1,0:T(8,128)(2,1)S(1)}, u32[]{:S(2)}, u32[]{:S(2)}) %collective-permute-start) | collective-permute-done | bytes 442400 | tf_op jit(solution)/shard_map/ppermute | solution.py:276
  15.8 0.0 copy-done.7
  15.8 0.1 select_bitcast_fusion.1
  15.9 2.6 %collective-permute-start.4 = (bf16[1,144,1152]{2,1,0:T(8,128)(2,1)S(1)}, bf16[1,144,1152]{2,1,0:T(8,128)(2,1)S(1)}, u32[]{:S(2)}, u32[]{:S(2)}) collective-permute-start(bf16[1,144,1152]{2,1,0:T(8,128)(2,1)S(1)} %pad_maximum_fusion), channel_id=1, source_target_pairs={{0,4},{4,8},{8,12},{1,5},{5,9},{9,13},{2,6},{6,10},{10,14},{3,7},{... | collective-permute-start | bytes 995336 | tf_op jit(solution)/shard_map/ppermute | solution.py:31
  18.5 1.9 %collective-permute-start.6 = (bf16[1,144,384]{2,1,0:T(8,128)(2,1)S(1)}, bf16[1,144,384]{2,1,0:T(8,128)(2,1)S(1)}, u32[]{:S(2)}, u32[]{:S(2)}) collective-permute-start(bf16[1,144,384]{2,1,0:T(8,128)(2,1)S(1)} %get-tuple-element.54), channel_id=1, source_target_pairs={{0,4},{4,8},{8,12},{1,5},{5,9},{9,13},{2,6},{6,10},{10,14},{3,7},{... | collective-permute-start | bytes 331784 | tf_op jit(solution)/shard_map/ppermute | solution.py:31
  21.1 1.9 %collective-permute-start.10 = (bf16[24,512]{1,0:T(8,128)(2,1)S(1)}, bf16[24,512]{1,0:T(8,128)(2,1)S(1)}, u32[]{:S(2)}, u32[]{:S(2)}) collective-permute-start(bf16[24,512]{1,0:T(8,128)(2,1)S(1)} %get-tuple-element.51), channel_id=1, source_target_pairs={{0,4},{4,8},{8,12},{1,5},{5,9},{9,13},{2,6},{6,10},{10,14},{3,7},{... | collective-permute-start | bytes 73736 | tf_op jit(solution)/shard_map/ppermute | solution.py:31
  23.0 0.0 copy-done.1
  23.0 0.0 copy-done.6
  23.0 2.7 %middle.2 = (f32[6,128,576]{2,1,0:T(8,128)S(1)}, f32[6,576]{1,0:T(8,128)S(1)}, f32[6,576]{1,0:T(8,128)S(1)}) custom-call(s32[4,4]{1,0:T(4,128)S(1)} %copy-done.5, s32[4,4]{1,0:T(4,128)S(1)} %copy-done.6, bf16[4,1,144,768]{3,2,1,0:T(8,128)(2,1)S(1)} %copy-done.1, bf16[2,1,144,768]{3,2,1,0:T(8,128)(2,1)S(1)} %collective-permute-done.refs_0_, ...), custom_call_target="tpu_custom_call" | custom-call | flops 254803968 | bytes 3124352 | tf_op jit(solution)/shard_map/middle/pallas_call | solution.py:287
  25.8 0.0 collective-permute-done.5.refs_0_
  25.8 0.7 %middle.3 = (f32[6,128,576]{2,1,0:T(8,128)S(1)}, f32[6,576]{1,0:T(8,128)S(1)}, f32[6,576]{1,0:T(8,128)S(1)}) custom-call(s32[4,4]{1,0:T(4,128)S(1)} %copy-done.5, s32[4,4]{1,0:T(4,128)S(1)} %copy-done.6, bf16[4,1,144,768]{3,2,1,0:T(8,128)(2,1)S(1)} %copy-done.1, bf16[2,1,144,768]{3,2,1,0:T(8,128)(2,1)S(1)} %collective-permute-done.5.refs_0_, ...), custom_call_target="tpu_custom_call" | custom-call | flops 254803968 | bytes 3124352 | tf_op jit(solution)/shard_map/middle/pallas_call | solution.py:287
  26.5 5.8 %collective-permute-done.4.refs_0_.value_ref = bf16[1,144,1152]{2,1,0:T(8,128)(2,1)S(1)} collective-permute-done((bf16[1,144,1152]{2,1,0:T(8,128)(2,1)S(1)}, bf16[1,144,1152]{2,1,0:T(8,128)(2,1)S(1)}, u32[]{:S(2)}, u32[]{:S(2)}) %collective-permute-start.4) | collective-permute-done | bytes 331808 | tf_op jit(solution)/shard_map/ppermute | solution.py:31
  32.4 0.8 %score.1 = (f32[6,128,576]{2,1,0:T(8,128)S(1)}, bf16[6,144,576]{2,1,0:T(8,128)(2,1)S(1)}) custom-call(s32[4,4]{1,0:T(4,128)S(1)} %copy-done.5, s32[4,4]{1,0:T(4,128)S(1)} %copy-done.6, bf16[4,1,144,768]{3,2,1,0:T(8,128)(2,1)S(1)} %copy-done.1, bf16[1,144,1152]{2,1,0:T(8,128)(2,1)S(1)} %collective-permute-done.4.refs_0_.value_ref, ...), custom_call_target="tpu_custom_call" | custom-call | flops 127401984 | bytes 3013760 | tf_op jit(solution)/shard_map/score/pallas_call | solution.py:287
  33.2 0.5 %average.1 = (f32[4,144,384]{2,1,0:T(8,128)S(1)}, f32[1,576]{1,0:T(1,128)S(1)}) custom-call(f32[6,128,576]{2,1,0:T(8,128)S(1)} %get-tuple-element.42.acc_ref, bf16[6,144,576]{2,1,0:T(8,128)(2,1)S(1)} %get-tuple-element.43.w_ref, bf16[1,144,1152]{2,1,0:T(8,128)(2,1)S(1)} %collective-permute-done.4.refs_0_.value_ref), custom_call_target="tpu_custom_call" | custom-call | flops 63700992 | bytes 3096576 | tf_op jit(solution)/shard_map/average/pallas_call | solution.py:287
  33.7 1.0 %collective-permute-done.6.value_ref = bf16[1,144,384]{2,1,0:T(8,128)(2,1)S(1)} collective-permute-done((bf16[1,144,384]{2,1,0:T(8,128)(2,1)S(1)}, bf16[1,144,384]{2,1,0:T(8,128)(2,1)S(1)}, u32[]{:S(2)}, u32[]{:S(2)}) %collective-permute-start.6) | collective-permute-done | bytes 110624 | tf_op jit(solution)/shard_map/ppermute | solution.py:31
  34.7 0.4 rest.1
  35.1 1.6 %collective-permute-start.7 = (f32[1,576]{1,0:T(1,128)S(1)}, f32[1,576]{1,0:T(1,128)S(1)}, u32[]{:S(2)}, u32[]{:S(2)}) collective-permute-start(f32[1,576]{1,0:T(1,128)S(1)} %get-tuple-element.47.square_in), channel_id=1, source_target_pairs={{0,2},{1,3},{2,0},{3,1},{4,6},{5,7},{6,4},{7,5},{8,10},{9,11},{10,... | collective-permute-start | bytes 6920 | tf_op jit(solution)/shard_map/ppermute | solution.py:40
  36.7 0.0 collective-permute-start.8
  36.7 0.3 turn.1
  37.0 0.7 %collective-permute-start.9 = (f32[1,576]{1,0:T(1,128)S(1)}, f32[1,576]{1,0:T(1,128)S(1)}, u32[]{:S(2)}, u32[]{:S(2)}) collective-permute-start(f32[1,576]{1,0:T(1,128)S(1)} %get-tuple-element.49.refs_0_), channel_id=1, source_target_pairs={{0,1},{1,0},{2,3},{3,2},{4,5},{5,4},{6,7},{7,6},{8,9},{9,8},{10,11... | collective-permute-start | bytes 6920 | tf_op jit(solution)/shard_map/ppermute | solution.py:40
  37.7 0.0 collective-permute-done.10.tail_ref
  37.7 0.0 copy-done.3
  37.7 1.4 %decode.1 = bf16[1,36,512]{2,1,0:T(8,128)(2,1)} custom-call(s32[1]{0:T(128)S(6)} %copy.11.fade_ref, bf16[36,512]{1,0:T(8,128)(2,1)S(1)} %get-tuple-element.50.hidden_ref, bf16[24,512]{1,0:T(8,128)(2,1)S(1)} %collective-permute-done.10.tail_ref, bf16[3,512,512]{2,1,0:T(8,128)(2,1)S(1)} %copy-done.3), custom_call_target="tpu_custom_call" | custom-call | flops 56623104 | bytes 1634308 | tf_op jit(solution)/shard_map/decode/pallas_call | solution.py:287
  39.1 0.0 collective-permute-done.9.refs_3_
  39.1 0.0 collective-permute-done.7.refs_1_
  39.2 0.5 %collective-permute-done.8.refs_2_ = f32[1,576]{1,0:T(1,128)S(1)} collective-permute-done((f32[1,576]{1,0:T(1,128)S(1)}, f32[1,576]{1,0:T(1,128)S(1)}, u32[]{:S(2)}, u32[]{:S(2)}) %collective-permute-start.8) | collective-permute-done | bytes 2336 | tf_op jit(solution)/shard_map/ppermute | solution.py:40
  39.7 1.1 %scale.1 = bf16[4,1,144,768]{3,2,1,0:T(8,128)(2,1)} custom-call(f32[4,144,384]{2,1,0:T(8,128)S(1)} %get-tuple-element.44.front_ref, f32[4,144,384]{2,1,0:T(8,128)S(1)} %get-tuple-element.48.back_ref, f32[1,576]{1,0:T(1,128)S(1)} %get-tuple-element.49.refs_0_, f32[1,576]{1,0:T(1,128)S(1)} %collective-permute-done.7.refs_1_, ...), custom_call_target="tpu_custom_call" | custom-call | flops 442368 | bytes 1778688 | tf_op jit(solution)/shard_map/scale/pallas_call | solution.py:287
  (4 shorter events, 0.1 us)
Async XLA Ops:
  0.6 15.2 %copy-start.7 = (bf16[2,1,144,768]{3,2,1,0:T(8,128)(2,1)S(1)}, bf16[2,1,144,768]{3,2,1,0:T(8,128)(2,1)}, u32[]{:S(2)}) copy-start(bf16[2,1,144,768]{3,2,1,0:T(8,128)(2,1)} %param.11) | copy-start | bytes 1327108
  0.6 15.1 %collective-permute-start = (bf16[2,1,144,768]{3,2,1,0:T(8,128)(2,1)}, bf16[2,1,144,768]{3,2,1,0:T(8,128)(2,1)S(1)}, u32[]{:S(2)}, u32[]{:S(2)}) collective-permute-start(bf16[2,1,144,768]{3,2,1,0:T(8,128)(2,1)} %param.11), channel_id=1, source_target_pairs={{0,8},{8,12},{1,9},{9,13},{2,10},{10,14},{3,11},{11,15},{16,24},{2... | collective-permute-start | bytes 1327112 | tf_op jit(solution)/shard_map/ppermute | solution.py:276
  6.6 8.5 %collective-permute-start.1 = (bf16[36,512]{1,0:T(8,128)(2,1)}, bf16[36,512]{1,0:T(8,128)(2,1)S(1)}, u32[]{:S(2)}, u32[]{:S(2)}) collective-permute-start(bf16[36,512]{1,0:T(8,128)(2,1)} %get-tuple-element.29), channel_id=1, source_target_pairs={{0,1},{1,0},{2,3},{3,2},{4,5},{5,4},{6,7},{7,6},{8,9},{9,8},{10,11... | collective-permute-start | bytes 110600 | tf_op jit(solution)/shard_map/ppermute | solution.py:40
  6.6 8.5 %collective-permute-start.2 = (bf16[36,512]{1,0:T(8,128)(2,1)}, bf16[36,512]{1,0:T(8,128)(2,1)S(1)}, u32[]{:S(2)}, u32[]{:S(2)}) collective-permute-start(bf16[36,512]{1,0:T(8,128)(2,1)} %get-tuple-element.30), channel_id=1, source_target_pairs={{0,2},{1,3},{2,0},{3,1},{4,6},{5,7},{6,4},{7,5},{8,10},{9,11},{10,... | collective-permute-start | bytes 110600 | tf_op jit(solution)/shard_map/ppermute | solution.py:40
  8.2 6.9 %collective-permute-start.3 = (bf16[36,512]{1,0:T(8,128)(2,1)}, bf16[36,512]{1,0:T(8,128)(2,1)S(1)}, u32[]{:S(2)}, u32[]{:S(2)}) collective-permute-start(bf16[36,512]{1,0:T(8,128)(2,1)} %get-tuple-element.31), channel_id=1, source_target_pairs={{0,3},{1,2},{2,1},{3,0},{4,7},{5,6},{6,5},{7,4},{8,11},{9,10},{10,... | collective-permute-start | bytes 110600 | tf_op jit(solution)/shard_map/ppermute | solution.py:40
  8.5 17.3 %collective-permute-start.5 = (bf16[2,1,144,768]{3,2,1,0:T(8,128)(2,1)}, bf16[2,1,144,768]{3,2,1,0:T(8,128)(2,1)S(1)}, u32[]{:S(2)}, u32[]{:S(2)}) collective-permute-start(bf16[2,1,144,768]{3,2,1,0:T(8,128)(2,1)} %param.11), channel_id=1, source_target_pairs={{4,12},{5,13},{6,14},{7,15},{20,28},{21,29},{22,30},{23,31}} | collective-permute-start | bytes 1327112 | tf_op jit(solution)/shard_map/ppermute | solution.py:276
  9.2 1.2 %copy-start = (bf16[4,1,144,768]{3,2,1,0:T(8,128)(2,1)S(1)}, bf16[4,1,144,768]{3,2,1,0:T(8,128)(2,1)}, u32[]{:S(2)}) copy-start(bf16[4,1,144,768]{3,2,1,0:T(8,128)(2,1)} %q_ref.7) | copy-start | bytes 2654212
  10.4 1.5 %copy-start.2 = (bf16[4,2,1,144,768]{4,3,2,1,0:T(8,128)(2,1)S(1)}, bf16[4,2,1,144,768]{4,3,2,1,0:T(8,128)(2,1)}, u32[]{:S(2)}) copy-start(bf16[4,2,1,144,768]{4,3,2,1,0:T(8,128)(2,1)} %kv_ref.1) | copy-start | bytes 5308420
  11.8 0.7 %copy-start.5 = (s32[4,4]{1,0:T(4,128)S(1)}, s32[4,4]{1,0:T(4,128)}, u32[]{:S(2)}) copy-start(s32[4,4]{1,0:T(4,128)} %step_ref.7) | copy-start | bytes 196
  12.5 2.6 %copy-start.4 = (bf16[36,512]{1,0:T(8,128)(2,1)S(1)}, bf16[36,512]{1,0:T(8,128)(2,1)}, u32[]{:S(2)}) copy-start(bf16[36,512]{1,0:T(8,128)(2,1)} %get-tuple-element.28.refs_0_) | copy-start | bytes 110596
  15.1 7.9 %copy-start.1 = (bf16[4,1,144,768]{3,2,1,0:T(8,128)(2,1)S(1)}, bf16[4,1,144,768]{3,2,1,0:T(8,128)(2,1)}, u32[]{:S(2)}) copy-start(bf16[4,1,144,768]{3,2,1,0:T(8,128)(2,1)} %q_ref.7) | copy-start | bytes 2654212
  15.1 7.9 %copy-start.6 = (s32[4,4]{1,0:T(4,128)S(1)}, s32[4,4]{1,0:T(4,128)}, u32[]{:S(2)}) copy-start(s32[4,4]{1,0:T(4,128)} %mask_ref.5) | copy-start | bytes 196
  15.9 16.5 %collective-permute-start.4 = (bf16[1,144,1152]{2,1,0:T(8,128)(2,1)S(1)}, bf16[1,144,1152]{2,1,0:T(8,128)(2,1)S(1)}, u32[]{:S(2)}, u32[]{:S(2)}) collective-permute-start(bf16[1,144,1152]{2,1,0:T(8,128)(2,1)S(1)} %pad_maximum_fusion), channel_id=1, source_target_pairs={{0,4},{4,8},{8,12},{1,5},{5,9},{9,13},{2,6},{6,10},{10,14},{3,7},{... | collective-permute-start | bytes 995336 | tf_op jit(solution)/shard_map/ppermute | solution.py:31
  18.5 16.2 %collective-permute-start.6 = (bf16[1,144,384]{2,1,0:T(8,128)(2,1)S(1)}, bf16[1,144,384]{2,1,0:T(8,128)(2,1)S(1)}, u32[]{:S(2)}, u32[]{:S(2)}) collective-permute-start(bf16[1,144,384]{2,1,0:T(8,128)(2,1)S(1)} %get-tuple-element.54), channel_id=1, source_target_pairs={{0,4},{4,8},{8,12},{1,5},{5,9},{9,13},{2,6},{6,10},{10,14},{3,7},{... | collective-permute-start | bytes 331784 | tf_op jit(solution)/shard_map/ppermute | solution.py:31
  21.1 16.6 %collective-permute-start.10 = (bf16[24,512]{1,0:T(8,128)(2,1)S(1)}, bf16[24,512]{1,0:T(8,128)(2,1)S(1)}, u32[]{:S(2)}, u32[]{:S(2)}) collective-permute-start(bf16[24,512]{1,0:T(8,128)(2,1)S(1)} %get-tuple-element.51), channel_id=1, source_target_pairs={{0,4},{4,8},{8,12},{1,5},{5,9},{9,13},{2,6},{6,10},{10,14},{3,7},{... | collective-permute-start | bytes 73736 | tf_op jit(solution)/shard_map/ppermute | solution.py:31
  34.7 3.0 %copy-start.3 = (bf16[3,512,512]{2,1,0:T(8,128)(2,1)S(1)}, bf16[3,512,512]{2,1,0:T(8,128)(2,1)}, u32[]{:S(2)}) copy-start(bf16[3,512,512]{2,1,0:T(8,128)(2,1)} %conv_ref.1) | copy-start | bytes 4718596
  35.1 4.0 %collective-permute-start.7 = (f32[1,576]{1,0:T(1,128)S(1)}, f32[1,576]{1,0:T(1,128)S(1)}, u32[]{:S(2)}, u32[]{:S(2)}) collective-permute-start(f32[1,576]{1,0:T(1,128)S(1)} %get-tuple-element.47.square_in), channel_id=1, source_target_pairs={{0,2},{1,3},{2,0},{3,1},{4,6},{5,7},{6,4},{7,5},{8,10},{9,11},{10,... | collective-permute-start | bytes 6920 | tf_op jit(solution)/shard_map/ppermute | solution.py:40
  36.7 3.0 %collective-permute-start.8 = (f32[1,576]{1,0:T(1,128)S(1)}, f32[1,576]{1,0:T(1,128)S(1)}, u32[]{:S(2)}, u32[]{:S(2)}) collective-permute-start(f32[1,576]{1,0:T(1,128)S(1)} %get-tuple-element.47.square_in), channel_id=1, source_target_pairs={{0,3},{1,2},{2,1},{3,0},{4,7},{5,6},{6,5},{7,4},{8,11},{9,10},{10,... | collective-permute-start | bytes 6920 | tf_op jit(solution)/shard_map/ppermute | solution.py:40
  37.0 2.2 %collective-permute-start.9 = (f32[1,576]{1,0:T(1,128)S(1)}, f32[1,576]{1,0:T(1,128)S(1)}, u32[]{:S(2)}, u32[]{:S(2)}) collective-permute-start(f32[1,576]{1,0:T(1,128)S(1)} %get-tuple-element.49.refs_0_), channel_id=1, source_target_pairs={{0,1},{1,0},{2,3},{3,2},{4,5},{5,4},{6,7},{7,6},{8,9},{9,8},{10,11... | collective-permute-start | bytes 6920 | tf_op jit(solution)/shard_map/ppermute | solution.py:40

commit v12 on v11

--- a/solution.py
+++ b/solution.py
@@ -256,10 +256,10 @@
         total = total + ref[...]
     inverse = lax.rsqrt(total / width + 1e-06)
     steps, rows, columns = out_ref.shape
-    spread = jnp.broadcast_to(inverse, (HD, steps * rows)).T
     copies = []
     for step in range(steps):
-        factor = spread[step * rows : (step + 1) * rows]
+        own = inverse[:, step * rows : (step + 1) * rows]
+        factor = jnp.broadcast_to(own, (HD, rows)).T
         place = 0
         for ref in (front_ref, back_ref):
             for first in range(0, ref.shape[2], HD):

time: 41.1 us -> 41.1 us (level)
  Pallas kernels: 13 us -> 11 us
  waiting for transfers between devices: 7.91 us -> 9.91 us
    ppermute x3, waiting for transfers between devices: 6.86 us -> 8.86 us  [hop(): lax.ppermute(value, axis, [(source, source + steps) for source in range(c...]
    pallas_call x11, Pallas kernels: 13 us -> 11 us  [plain_call(): pl.pallas_call(kernel, in_specs=list(in_specs) + [VMEM_SPEC] * (len(opera...]
  transfers between devices with their start and end apart: 11 -> 11, of which waited for: 4 -> 4; matrix products, arithmetic and copies ran while one was open for 0% -> 0% of each run, Pallas kernels for 29% -> 24%
where the time goes in v12:
time: 41.1 us; the launch traced here: 40.8 us
  starting transfers between devices  14.9 us (36%)
  Pallas kernels  11 us (27%)
  waiting for transfers between devices  9.91 us (24%)
  local copies, waits for them, and re-layouts  3.37 us (8%)
  between operations  1.49 us (4%)
    pallas_call x11, Pallas kernels, plain_call(): pl.pallas_call(kernel, in_specs=list(in_specs) + [VMEM_SPEC] * (len(opera...  11 us
    ppermute x3, waiting for transfers between devices, hop(): lax.ppermute(value, axis, [(source, source + steps) for source in range(c...  8.86 us
    ppermute x3, starting transfers between devices, hop(): lax.ppermute(value, axis, [(source, source + steps) for source in range(c...  6.43 us
    ppermute x2, starting transfers between devices, send(): return lax.ppermute(value, 'span', pairs)  4.3 us
    ppermute x6, starting transfers between devices, swap(): return lax.ppermute(value, axes, pairs)  4.2 us
    unnamed x16, local copies, waits for them, and re-layouts  3.35 us
  transfers between devices with their start and end apart: 11, of which 4 were waited for; matrix products, arithmetic and copies ran while one was open for 0% of the time, Pallas kernels for 24%

profile of v12, /device:TPU:20, one launch (start us, length us, event | category | flops | bytes accessed | tf_op | source)
XLA Modules:
  0.0 40.8 jit_solution(2508516195270563301)
XLA Ops:
  0.6 0.0 copy-start.7
  0.6 3.6 %collective-permute-start = (bf16[2,1,144,768]{3,2,1,0:T(8,128)(2,1)}, bf16[2,1,144,768]{3,2,1,0:T(8,128)(2,1)S(1)}, u32[]{:S(2)}, u32[]{:S(2)}) collective-permute-start(bf16[2,1,144,768]{3,2,1,0:T(8,128)(2,1)} %param.11), channel_id=1, source_target_pairs={{0,8},{8,12},{1,9},{9,13},{2,10},{10,14},{3,11},{11,15},{16,24},{2... | collective-permute-start | bytes 1327112 | tf_op jit(solution)/shard_map/ppermute | solution.py:276
  4.3 2.3 %project.1 = (bf16[36,512]{1,0:T(8,128)(2,1)}, bf16[36,512]{1,0:T(8,128)(2,1)}, bf16[36,512]{1,0:T(8,128)(2,1)}, bf16[36,512]{1,0:T(8,128)(2,1)}) custom-call(bf16[1,144,768]{2,1,0:T(8,128)(2,1)} %x_hbm.1, bf16[768,512]{1,0:T(8,128)(2,1)} %w_hbm.1), custom_call_target="tpu_custom_call" | custom-call | flops 113246208 | bytes 1007616 | tf_op jit(solution)/shard_map/project/pallas_call | solution.py:287
  6.6 0.1 collective-permute-start.1
  6.6 1.6 %collective-permute-start.2 = (bf16[36,512]{1,0:T(8,128)(2,1)}, bf16[36,512]{1,0:T(8,128)(2,1)S(1)}, u32[]{:S(2)}, u32[]{:S(2)}) collective-permute-start(bf16[36,512]{1,0:T(8,128)(2,1)} %get-tuple-element.30), channel_id=1, source_target_pairs={{0,2},{1,3},{2,0},{3,1},{4,6},{5,7},{6,4},{7,5},{8,10},{9,11},{10,... | collective-permute-start | bytes 110600 | tf_op jit(solution)/shard_map/ppermute | solution.py:40
  8.2 0.3 collective-permute-start.3
  8.5 0.7 %collective-permute-start.5 = (bf16[2,1,144,768]{3,2,1,0:T(8,128)(2,1)}, bf16[2,1,144,768]{3,2,1,0:T(8,128)(2,1)S(1)}, u32[]{:S(2)}, u32[]{:S(2)}) collective-permute-start(bf16[2,1,144,768]{3,2,1,0:T(8,128)(2,1)} %param.11), channel_id=1, source_target_pairs={{4,12},{5,13},{6,14},{7,15},{20,28},{21,29},{22,30},{23,31}} | collective-permute-start | bytes 1327112 | tf_op jit(solution)/shard_map/ppermute | solution.py:276
  9.2 0.0 copy-start
  9.2 1.2 %copy-done = bf16[4,1,144,768]{3,2,1,0:T(8,128)(2,1)S(1)} copy-done((bf16[4,1,144,768]{3,2,1,0:T(8,128)(2,1)S(1)}, bf16[4,1,144,768]{3,2,1,0:T(8,128)(2,1)}, u32[]{:S(2)}) %copy-start) | copy-done | bytes 884760
  10.4 0.0 copy-start.2
  10.4 1.5 %copy-done.2 = bf16[4,2,1,144,768]{4,3,2,1,0:T(8,128)(2,1)S(1)} copy-done((bf16[4,2,1,144,768]{4,3,2,1,0:T(8,128)(2,1)S(1)}, bf16[4,2,1,144,768]{4,3,2,1,0:T(8,128)(2,1)}, u32[]{:S(2)}) %copy-start.2) | copy-done | bytes 1769496
  11.8 0.0 copy-start.5
  11.8 0.7 %copy-done.5 = s32[4,4]{1,0:T(4,128)S(1)} copy-done((s32[4,4]{1,0:T(4,128)S(1)}, s32[4,4]{1,0:T(4,128)}, u32[]{:S(2)}) %copy-start.5) | copy-done | bytes 88
  12.5 2.5 %own.1 = (f32[6,128,576]{2,1,0:T(8,128)S(1)}, f32[6,576]{1,0:T(8,128)S(1)}, f32[6,576]{1,0:T(8,128)S(1)}) custom-call(s32[4,4]{1,0:T(4,128)S(1)} %copy-done.5, bf16[4,1,144,768]{3,2,1,0:T(8,128)(2,1)S(1)} %copy-done, bf16[4,2,1,144,768]{4,3,2,1,0:T(8,128)(2,1)S(1)} %copy-done.2), custom_call_target="tpu_custom_call" | custom-call | flops 254803968 | bytes 2654272 | tf_op jit(solution)/shard_map/own/pallas_call | solution.py:287
  15.1 0.0 copy-start.1
  15.1 0.0 copy-start.6
  15.1 0.0 collective-permute-done.1.refs_1_
  15.1 0.0 collective-permute-done.2.refs_2_
  15.1 0.0 collective-permute-done.3.refs_3_
  15.1 0.0 copy-done.4
  15.1 0.1 gather.1
  15.3 0.5 %collective-permute-done.refs_0_ = bf16[2,1,144,768]{3,2,1,0:T(8,128)(2,1)S(1)} collective-permute-done((bf16[2,1,144,768]{3,2,1,0:T(8,128)(2,1)}, bf16[2,1,144,768]{3,2,1,0:T(8,128)(2,1)S(1)}, u32[]{:S(2)}, u32[]{:S(2)}) %collective-permute-start) | collective-permute-done | bytes 442400 | tf_op jit(solution)/shard_map/ppermute | solution.py:276
  15.8 0.0 copy-done.7
  15.8 0.1 select_bitcast_fusion.1
  15.9 2.6 %collective-permute-start.4 = (bf16[1,144,1152]{2,1,0:T(8,128)(2,1)S(1)}, bf16[1,144,1152]{2,1,0:T(8,128)(2,1)S(1)}, u32[]{:S(2)}, u32[]{:S(2)}) collective-permute-start(bf16[1,144,1152]{2,1,0:T(8,128)(2,1)S(1)} %pad_maximum_fusion), channel_id=1, source_target_pairs={{0,4},{4,8},{8,12},{1,5},{5,9},{9,13},{2,6},{6,10},{10,14},{3,7},{... | collective-permute-start | bytes 995336 | tf_op jit(solution)/shard_map/ppermute | solution.py:31
  18.5 1.9 %collective-permute-start.6 = (bf16[1,144,384]{2,1,0:T(8,128)(2,1)S(1)}, bf16[1,144,384]{2,1,0:T(8,128)(2,1)S(1)}, u32[]{:S(2)}, u32[]{:S(2)}) collective-permute-start(bf16[1,144,384]{2,1,0:T(8,128)(2,1)S(1)} %get-tuple-element.54), channel_id=1, source_target_pairs={{0,4},{4,8},{8,12},{1,5},{5,9},{9,13},{2,6},{6,10},{10,14},{3,7},{... | collective-permute-start | bytes 331784 | tf_op jit(solution)/shard_map/ppermute | solution.py:31
  21.1 1.9 %collective-permute-start.10 = (bf16[24,512]{1,0:T(8,128)(2,1)S(1)}, bf16[24,512]{1,0:T(8,128)(2,1)S(1)}, u32[]{:S(2)}, u32[]{:S(2)}) collective-permute-start(bf16[24,512]{1,0:T(8,128)(2,1)S(1)} %get-tuple-element.51), channel_id=1, source_target_pairs={{0,4},{4,8},{8,12},{1,5},{5,9},{9,13},{2,6},{6,10},{10,14},{3,7},{... | collective-permute-start | bytes 73736 | tf_op jit(solution)/shard_map/ppermute | solution.py:31
  23.0 0.0 copy-done.1
  23.0 0.0 copy-done.6
  23.0 0.7 %middle.2 = (f32[6,128,576]{2,1,0:T(8,128)S(1)}, f32[6,576]{1,0:T(8,128)S(1)}, f32[6,576]{1,0:T(8,128)S(1)}) custom-call(s32[4,4]{1,0:T(4,128)S(1)} %copy-done.5, s32[4,4]{1,0:T(4,128)S(1)} %copy-done.6, bf16[4,1,144,768]{3,2,1,0:T(8,128)(2,1)S(1)} %copy-done.1, bf16[2,1,144,768]{3,2,1,0:T(8,128)(2,1)S(1)} %collective-permute-done.refs_0_, ...), custom_call_target="tpu_custom_call" | custom-call | flops 254803968 | bytes 3124352 | tf_op jit(solution)/shard_map/middle/pallas_call | solution.py:287
  23.8 0.0 collective-permute-done.5.refs_0_
  23.8 0.7 %middle.3 = (f32[6,128,576]{2,1,0:T(8,128)S(1)}, f32[6,576]{1,0:T(8,128)S(1)}, f32[6,576]{1,0:T(8,128)S(1)}) custom-call(s32[4,4]{1,0:T(4,128)S(1)} %copy-done.5, s32[4,4]{1,0:T(4,128)S(1)} %copy-done.6, bf16[4,1,144,768]{3,2,1,0:T(8,128)(2,1)S(1)} %copy-done.1, bf16[2,1,144,768]{3,2,1,0:T(8,128)(2,1)S(1)} %collective-permute-done.5.refs_0_, ...), custom_call_target="tpu_custom_call" | custom-call | flops 254803968 | bytes 3124352 | tf_op jit(solution)/shard_map/middle/pallas_call | solution.py:287
  24.5 7.8 %collective-permute-done.4.refs_0_.value_ref = bf16[1,144,1152]{2,1,0:T(8,128)(2,1)S(1)} collective-permute-done((bf16[1,144,1152]{2,1,0:T(8,128)(2,1)S(1)}, bf16[1,144,1152]{2,1,0:T(8,128)(2,1)S(1)}, u32[]{:S(2)}, u32[]{:S(2)}) %collective-permute-start.4) | collective-permute-done | bytes 331808 | tf_op jit(solution)/shard_map/ppermute | solution.py:31
  32.4 0.8 %score.1 = (f32[6,128,576]{2,1,0:T(8,128)S(1)}, bf16[6,144,576]{2,1,0:T(8,128)(2,1)S(1)}) custom-call(s32[4,4]{1,0:T(4,128)S(1)} %copy-done.5, s32[4,4]{1,0:T(4,128)S(1)} %copy-done.6, bf16[4,1,144,768]{3,2,1,0:T(8,128)(2,1)S(1)} %copy-done.1, bf16[1,144,1152]{2,1,0:T(8,128)(2,1)S(1)} %collective-permute-done.4.refs_0_.value_ref, ...), custom_call_target="tpu_custom_call" | custom-call | flops 127401984 | bytes 3013760 | tf_op jit(solution)/shard_map/score/pallas_call | solution.py:287
  33.2 0.5 %average.1 = (f32[4,144,384]{2,1,0:T(8,128)S(1)}, f32[1,576]{1,0:T(1,128)S(1)}) custom-call(f32[6,128,576]{2,1,0:T(8,128)S(1)} %get-tuple-element.42.acc_ref, bf16[6,144,576]{2,1,0:T(8,128)(2,1)S(1)} %get-tuple-element.43.w_ref, bf16[1,144,1152]{2,1,0:T(8,128)(2,1)S(1)} %collective-permute-done.4.refs_0_.value_ref), custom_call_target="tpu_custom_call" | custom-call | flops 63700992 | bytes 3096576 | tf_op jit(solution)/shard_map/average/pallas_call | solution.py:287
  33.7 1.0 %collective-permute-done.6.value_ref = bf16[1,144,384]{2,1,0:T(8,128)(2,1)S(1)} collective-permute-done((bf16[1,144,384]{2,1,0:T(8,128)(2,1)S(1)}, bf16[1,144,384]{2,1,0:T(8,128)(2,1)S(1)}, u32[]{:S(2)}, u32[]{:S(2)}) %collective-permute-start.6) | collective-permute-done | bytes 110624 | tf_op jit(solution)/shard_map/ppermute | solution.py:31
  34.7 0.4 rest.1
  35.1 1.6 %collective-permute-start.7 = (f32[1,576]{1,0:T(1,128)S(1)}, f32[1,576]{1,0:T(1,128)S(1)}, u32[]{:S(2)}, u32[]{:S(2)}) collective-permute-start(f32[1,576]{1,0:T(1,128)S(1)} %get-tuple-element.47.square_in), channel_id=1, source_target_pairs={{0,2},{1,3},{2,0},{3,1},{4,6},{5,7},{6,4},{7,5},{8,10},{9,11},{10,... | collective-permute-start | bytes 6920 | tf_op jit(solution)/shard_map/ppermute | solution.py:40
  36.7 0.0 collective-permute-start.8
  36.7 0.3 turn.1
  37.0 0.7 %collective-permute-start.9 = (f32[1,576]{1,0:T(1,128)S(1)}, f32[1,576]{1,0:T(1,128)S(1)}, u32[]{:S(2)}, u32[]{:S(2)}) collective-permute-start(f32[1,576]{1,0:T(1,128)S(1)} %get-tuple-element.49.refs_0_), channel_id=1, source_target_pairs={{0,1},{1,0},{2,3},{3,2},{4,5},{5,4},{6,7},{7,6},{8,9},{9,8},{10,11... | collective-permute-start | bytes 6920 | tf_op jit(solution)/shard_map/ppermute | solution.py:40
  37.7 0.0 collective-permute-done.10.tail_ref
  37.7 0.0 copy-done.3
  37.7 1.4 %decode.1 = bf16[1,36,512]{2,1,0:T(8,128)(2,1)} custom-call(s32[1]{0:T(128)S(6)} %copy.11.fade_ref, bf16[36,512]{1,0:T(8,128)(2,1)S(1)} %get-tuple-element.50.hidden_ref, bf16[24,512]{1,0:T(8,128)(2,1)S(1)} %collective-permute-done.10.tail_ref, bf16[3,512,512]{2,1,0:T(8,128)(2,1)S(1)} %copy-done.3), custom_call_target="tpu_custom_call" | custom-call | flops 56623104 | bytes 1634308 | tf_op jit(solution)/shard_map/decode/pallas_call | solution.py:287
  39.1 0.0 collective-permute-done.9.refs_3_
  39.1 0.0 collective-permute-done.7.refs_1_
  39.2 0.5 %collective-permute-done.8.refs_2_ = f32[1,576]{1,0:T(1,128)S(1)} collective-permute-done((f32[1,576]{1,0:T(1,128)S(1)}, f32[1,576]{1,0:T(1,128)S(1)}, u32[]{:S(2)}, u32[]{:S(2)}) %collective-permute-start.8) | collective-permute-done | bytes 2336 | tf_op jit(solution)/shard_map/ppermute | solution.py:40
  39.7 1.1 %scale.1 = bf16[4,1,144,768]{3,2,1,0:T(8,128)(2,1)} custom-call(f32[4,144,384]{2,1,0:T(8,128)S(1)} %get-tuple-element.44.front_ref, f32[4,144,384]{2,1,0:T(8,128)S(1)} %get-tuple-element.48.back_ref, f32[1,576]{1,0:T(1,128)S(1)} %get-tuple-element.49.refs_0_, f32[1,576]{1,0:T(1,128)S(1)} %collective-permute-done.7.refs_1_, ...), custom_call_target="tpu_custom_call" | custom-call | flops 442368 | bytes 1778688 | tf_op jit(solution)/shard_map/scale/pallas_call | solution.py:287
  (4 shorter events, 0.1 us)
Async XLA Ops:
  0.6 15.2 %copy-start.7 = (bf16[2,1,144,768]{3,2,1,0:T(8,128)(2,1)S(1)}, bf16[2,1,144,768]{3,2,1,0:T(8,128)(2,1)}, u32[]{:S(2)}) copy-start(bf16[2,1,144,768]{3,2,1,0:T(8,128)(2,1)} %param.11) | copy-start | bytes 1327108
  0.6 15.1 %collective-permute-start = (bf16[2,1,144,768]{3,2,1,0:T(8,128)(2,1)}, bf16[2,1,144,768]{3,2,1,0:T(8,128)(2,1)S(1)}, u32[]{:S(2)}, u32[]{:S(2)}) collective-permute-start(bf16[2,1,144,768]{3,2,1,0:T(8,128)(2,1)} %param.11), channel_id=1, source_target_pairs={{0,8},{8,12},{1,9},{9,13},{2,10},{10,14},{3,11},{11,15},{16,24},{2... | collective-permute-start | bytes 1327112 | tf_op jit(solution)/shard_map/ppermute | solution.py:276
  6.6 8.5 %collective-permute-start.1 = (bf16[36,512]{1,0:T(8,128)(2,1)}, bf16[36,512]{1,0:T(8,128)(2,1)S(1)}, u32[]{:S(2)}, u32[]{:S(2)}) collective-permute-start(bf16[36,512]{1,0:T(8,128)(2,1)} %get-tuple-element.29), channel_id=1, source_target_pairs={{0,1},{1,0},{2,3},{3,2},{4,5},{5,4},{6,7},{7,6},{8,9},{9,8},{10,11... | collective-permute-start | bytes 110600 | tf_op jit(solution)/shard_map/ppermute | solution.py:40
  6.6 8.5 %collective-permute-start.2 = (bf16[36,512]{1,0:T(8,128)(2,1)}, bf16[36,512]{1,0:T(8,128)(2,1)S(1)}, u32[]{:S(2)}, u32[]{:S(2)}) collective-permute-start(bf16[36,512]{1,0:T(8,128)(2,1)} %get-tuple-element.30), channel_id=1, source_target_pairs={{0,2},{1,3},{2,0},{3,1},{4,6},{5,7},{6,4},{7,5},{8,10},{9,11},{10,... | collective-permute-start | bytes 110600 | tf_op jit(solution)/shard_map/ppermute | solution.py:40
  8.2 6.9 %collective-permute-start.3 = (bf16[36,512]{1,0:T(8,128)(2,1)}, bf16[36,512]{1,0:T(8,128)(2,1)S(1)}, u32[]{:S(2)}, u32[]{:S(2)}) collective-permute-start(bf16[36,512]{1,0:T(8,128)(2,1)} %get-tuple-element.31), channel_id=1, source_target_pairs={{0,3},{1,2},{2,1},{3,0},{4,7},{5,6},{6,5},{7,4},{8,11},{9,10},{10,... | collective-permute-start | bytes 110600 | tf_op jit(solution)/shard_map/ppermute | solution.py:40
  8.5 15.3 %collective-permute-start.5 = (bf16[2,1,144,768]{3,2,1,0:T(8,128)(2,1)}, bf16[2,1,144,768]{3,2,1,0:T(8,128)(2,1)S(1)}, u32[]{:S(2)}, u32[]{:S(2)}) collective-permute-start(bf16[2,1,144,768]{3,2,1,0:T(8,128)(2,1)} %param.11), channel_id=1, source_target_pairs={{4,12},{5,13},{6,14},{7,15},{20,28},{21,29},{22,30},{23,31}} | collective-permute-start | bytes 1327112 | tf_op jit(solution)/shard_map/ppermute | solution.py:276
  9.2 1.2 %copy-start = (bf16[4,1,144,768]{3,2,1,0:T(8,128)(2,1)S(1)}, bf16[4,1,144,768]{3,2,1,0:T(8,128)(2,1)}, u32[]{:S(2)}) copy-start(bf16[4,1,144,768]{3,2,1,0:T(8,128)(2,1)} %q_ref.7) | copy-start | bytes 2654212
  10.4 1.5 %copy-start.2 = (bf16[4,2,1,144,768]{4,3,2,1,0:T(8,128)(2,1)S(1)}, bf16[4,2,1,144,768]{4,3,2,1,0:T(8,128)(2,1)}, u32[]{:S(2)}) copy-start(bf16[4,2,1,144,768]{4,3,2,1,0:T(8,128)(2,1)} %kv_ref.1) | copy-start | bytes 5308420
  11.8 0.7 %copy-start.5 = (s32[4,4]{1,0:T(4,128)S(1)}, s32[4,4]{1,0:T(4,128)}, u32[]{:S(2)}) copy-start(s32[4,4]{1,0:T(4,128)} %step_ref.7) | copy-start | bytes 196
  12.5 2.6 %copy-start.4 = (bf16[36,512]{1,0:T(8,128)(2,1)S(1)}, bf16[36,512]{1,0:T(8,128)(2,1)}, u32[]{:S(2)}) copy-start(bf16[36,512]{1,0:T(8,128)(2,1)} %get-tuple-element.28.refs_0_) | copy-start | bytes 110596
  15.1 7.9 %copy-start.1 = (bf16[4,1,144,768]{3,2,1,0:T(8,128)(2,1)S(1)}, bf16[4,1,144,768]{3,2,1,0:T(8,128)(2,1)}, u32[]{:S(2)}) copy-start(bf16[4,1,144,768]{3,2,1,0:T(8,128)(2,1)} %q_ref.7) | copy-start | bytes 2654212
  15.1 7.9 %copy-start.6 = (s32[4,4]{1,0:T(4,128)S(1)}, s32[4,4]{1,0:T(4,128)}, u32[]{:S(2)}) copy-start(s32[4,4]{1,0:T(4,128)} %mask_ref.5) | copy-start | bytes 196
  15.9 16.5 %collective-permute-start.4 = (bf16[1,144,1152]{2,1,0:T(8,128)(2,1)S(1)}, bf16[1,144,1152]{2,1,0:T(8,128)(2,1)S(1)}, u32[]{:S(2)}, u32[]{:S(2)}) collective-permute-start(bf16[1,144,1152]{2,1,0:T(8,128)(2,1)S(1)} %pad_maximum_fusion), channel_id=1, source_target_pairs={{0,4},{4,8},{8,12},{1,5},{5,9},{9,13},{2,6},{6,10},{10,14},{3,7},{... | collective-permute-start | bytes 995336 | tf_op jit(solution)/shard_map/ppermute | solution.py:31
  18.5 16.2 %collective-permute-start.6 = (bf16[1,144,384]{2,1,0:T(8,128)(2,1)S(1)}, bf16[1,144,384]{2,1,0:T(8,128)(2,1)S(1)}, u32[]{:S(2)}, u32[]{:S(2)}) collective-permute-start(bf16[1,144,384]{2,1,0:T(8,128)(2,1)S(1)} %get-tuple-element.54), channel_id=1, source_target_pairs={{0,4},{4,8},{8,12},{1,5},{5,9},{9,13},{2,6},{6,10},{10,14},{3,7},{... | collective-permute-start | bytes 331784 | tf_op jit(solution)/shard_map/ppermute | solution.py:31
  21.1 16.6 %collective-permute-start.10 = (bf16[24,512]{1,0:T(8,128)(2,1)S(1)}, bf16[24,512]{1,0:T(8,128)(2,1)S(1)}, u32[]{:S(2)}, u32[]{:S(2)}) collective-permute-start(bf16[24,512]{1,0:T(8,128)(2,1)S(1)} %get-tuple-element.51), channel_id=1, source_target_pairs={{0,4},{4,8},{8,12},{1,5},{5,9},{9,13},{2,6},{6,10},{10,14},{3,7},{... | collective-permute-start | bytes 73736 | tf_op jit(solution)/shard_map/ppermute | solution.py:31
  34.7 3.0 %copy-start.3 = (bf16[3,512,512]{2,1,0:T(8,128)(2,1)S(1)}, bf16[3,512,512]{2,1,0:T(8,128)(2,1)}, u32[]{:S(2)}) copy-start(bf16[3,512,512]{2,1,0:T(8,128)(2,1)} %conv_ref.1) | copy-start | bytes 4718596
  35.1 4.0 %collective-permute-start.7 = (f32[1,576]{1,0:T(1,128)S(1)}, f32[1,576]{1,0:T(1,128)S(1)}, u32[]{:S(2)}, u32[]{:S(2)}) collective-permute-start(f32[1,576]{1,0:T(1,128)S(1)} %get-tuple-element.47.square_in), channel_id=1, source_target_pairs={{0,2},{1,3},{2,0},{3,1},{4,6},{5,7},{6,4},{7,5},{8,10},{9,11},{10,... | collective-permute-start | bytes 6920 | tf_op jit(solution)/shard_map/ppermute | solution.py:40
  36.7 3.0 %collective-permute-start.8 = (f32[1,576]{1,0:T(1,128)S(1)}, f32[1,576]{1,0:T(1,128)S(1)}, u32[]{:S(2)}, u32[]{:S(2)}) collective-permute-start(f32[1,576]{1,0:T(1,128)S(1)} %get-tuple-element.47.square_in), channel_id=1, source_target_pairs={{0,3},{1,2},{2,1},{3,0},{4,7},{5,6},{6,5},{7,4},{8,11},{9,10},{10,... | collective-permute-start | bytes 6920 | tf_op jit(solution)/shard_map/ppermute | solution.py:40
  37.0 2.2 %collective-permute-start.9 = (f32[1,576]{1,0:T(1,128)S(1)}, f32[1,576]{1,0:T(1,128)S(1)}, u32[]{:S(2)}, u32[]{:S(2)}) collective-permute-start(f32[1,576]{1,0:T(1,128)S(1)} %get-tuple-element.49.refs_0_), channel_id=1, source_target_pairs={{0,1},{1,0},{2,3},{3,2},{4,5},{5,4},{6,7},{7,6},{8,9},{9,8},{10,11... | collective-permute-start | bytes 6920 | tf_op jit(solution)/shard_map/ppermute | solution.py:40

commit v13 on v11

--- a/solution.py
+++ b/solution.py
@@ -444,7 +444,7 @@
         own_kernel,
         "own",
         [acc_shape, stat_shape, stat_shape],
-        pair_flops,
+        3 * pair_flops,
         (step_index, query, noisy_kv),
         [SMEM_SPEC],
     )

time: 41.1 us -> 41.1 us (level)
  no operation moved by 1% of the time
where the time goes in v13:
time: 41.1 us; the launch traced here: 40.8 us
  starting transfers between devices  14.9 us (36%)
  Pallas kernels  13 us (32%)
  waiting for transfers between devices  7.94 us (19%)
  local copies, waits for them, and re-layouts  3.37 us (8%)
  between operations  1.48 us (4%)
    pallas_call x11, Pallas kernels, plain_call(): pl.pallas_call(kernel, in_specs=list(in_specs) + [VMEM_SPEC] * (len(opera...  13 us
    ppermute x3, waiting for transfers between devices, hop(): lax.ppermute(value, axis, [(source, source + steps) for source in range(c...  6.91 us
    ppermute x3, starting transfers between devices, hop(): lax.ppermute(value, axis, [(source, source + steps) for source in range(c...  6.43 us
    ppermute x2, starting transfers between devices, send(): return lax.ppermute(value, 'span', pairs)  4.3 us
    ppermute x6, starting transfers between devices, swap(): return lax.ppermute(value, axes, pairs)  4.2 us
    unnamed x16, local copies, waits for them, and re-layouts  3.35 us
  transfers between devices with their start and end apart: 11, of which 4 were waited for; matrix products, arithmetic and copies ran while one was open for 0% of the time, Pallas kernels for 29%

profile of v13, /device:TPU:20, one launch (start us, length us, event | category | flops | bytes accessed | tf_op | source)
XLA Modules:
  0.0 40.8 jit_solution(7772732479718420770)
XLA Ops:
  0.6 0.0 copy-start.7
  0.6 3.6 %collective-permute-start = (bf16[2,1,144,768]{3,2,1,0:T(8,128)(2,1)}, bf16[2,1,144,768]{3,2,1,0:T(8,128)(2,1)S(1)}, u32[]{:S(2)}, u32[]{:S(2)}) collective-permute-start(bf16[2,1,144,768]{3,2,1,0:T(8,128)(2,1)} %param.11), channel_id=1, source_target_pairs={{0,8},{8,12},{1,9},{9,13},{2,10},{10,14},{3,11},{11,15},{16,24},{2... | collective-permute-start | bytes 1327112 | tf_op jit(solution)/shard_map/ppermute | solution.py:276
  4.3 0.7 %collective-permute-start.5 = (bf16[2,1,144,768]{3,2,1,0:T(8,128)(2,1)}, bf16[2,1,144,768]{3,2,1,0:T(8,128)(2,1)S(1)}, u32[]{:S(2)}, u32[]{:S(2)}) collective-permute-start(bf16[2,1,144,768]{3,2,1,0:T(8,128)(2,1)} %param.11), channel_id=1, source_target_pairs={{4,12},{5,13},{6,14},{7,15},{20,28},{21,29},{22,30},{23,31}} | collective-permute-start | bytes 1327112 | tf_op jit(solution)/shard_map/ppermute | solution.py:276
  5.0 2.3 %project.1 = (bf16[36,512]{1,0:T(8,128)(2,1)}, bf16[36,512]{1,0:T(8,128)(2,1)}, bf16[36,512]{1,0:T(8,128)(2,1)}, bf16[36,512]{1,0:T(8,128)(2,1)}) custom-call(bf16[1,144,768]{2,1,0:T(8,128)(2,1)} %x_hbm.1, bf16[768,512]{1,0:T(8,128)(2,1)} %w_hbm.1), custom_call_target="tpu_custom_call" | custom-call | flops 113246208 | bytes 1007616 | tf_op jit(solution)/shard_map/project/pallas_call | solution.py:287
  7.3 0.1 collective-permute-start.1
  7.3 1.6 %collective-permute-start.2 = (bf16[36,512]{1,0:T(8,128)(2,1)}, bf16[36,512]{1,0:T(8,128)(2,1)S(1)}, u32[]{:S(2)}, u32[]{:S(2)}) collective-permute-start(bf16[36,512]{1,0:T(8,128)(2,1)} %get-tuple-element.30), channel_id=1, source_target_pairs={{0,2},{1,3},{2,0},{3,1},{4,6},{5,7},{6,4},{7,5},{8,10},{9,11},{10,... | collective-permute-start | bytes 110600 | tf_op jit(solution)/shard_map/ppermute | solution.py:40
  8.9 0.3 collective-permute-start.3
  9.2 0.0 copy-start
  9.2 1.2 %copy-done = bf16[4,1,144,768]{3,2,1,0:T(8,128)(2,1)S(1)} copy-done((bf16[4,1,144,768]{3,2,1,0:T(8,128)(2,1)S(1)}, bf16[4,1,144,768]{3,2,1,0:T(8,128)(2,1)}, u32[]{:S(2)}) %copy-start) | copy-done | bytes 884760
  10.4 0.0 copy-start.4
  10.4 0.7 %copy-done.4 = s32[4,4]{1,0:T(4,128)S(1)} copy-done((s32[4,4]{1,0:T(4,128)S(1)}, s32[4,4]{1,0:T(4,128)}, u32[]{:S(2)}) %copy-start.4) | copy-done | bytes 88
  11.0 0.0 copy-start.6
  11.1 1.5 %copy-done.6 = bf16[4,2,1,144,768]{4,3,2,1,0:T(8,128)(2,1)S(1)} copy-done((bf16[4,2,1,144,768]{4,3,2,1,0:T(8,128)(2,1)S(1)}, bf16[4,2,1,144,768]{4,3,2,1,0:T(8,128)(2,1)}, u32[]{:S(2)}) %copy-start.6) | copy-done | bytes 1769496
  12.5 2.5 %own.1 = (f32[6,128,576]{2,1,0:T(8,128)S(1)}, f32[6,576]{1,0:T(8,128)S(1)}, f32[6,576]{1,0:T(8,128)S(1)}) custom-call(s32[4,4]{1,0:T(4,128)S(1)} %copy-done.4, bf16[4,1,144,768]{3,2,1,0:T(8,128)(2,1)S(1)} %copy-done, bf16[4,2,1,144,768]{4,3,2,1,0:T(8,128)(2,1)S(1)} %copy-done.6), custom_call_target="tpu_custom_call" | custom-call | flops 764411904 | bytes 2654272 | tf_op jit(solution)/shard_map/own/pallas_call | solution.py:287
  15.1 0.0 copy-start.1
  15.1 0.0 copy-start.5
  15.1 0.0 collective-permute-done.1.refs_1_
  15.1 0.0 collective-permute-done.2.refs_2_
  15.1 0.0 collective-permute-done.3.refs_3_
  15.1 0.0 copy-done.3
  15.1 0.1 gather.1
  15.3 0.5 %collective-permute-done.refs_0_ = bf16[2,1,144,768]{3,2,1,0:T(8,128)(2,1)S(1)} collective-permute-done((bf16[2,1,144,768]{3,2,1,0:T(8,128)(2,1)}, bf16[2,1,144,768]{3,2,1,0:T(8,128)(2,1)S(1)}, u32[]{:S(2)}, u32[]{:S(2)}) %collective-permute-start) | collective-permute-done | bytes 442400 | tf_op jit(solution)/shard_map/ppermute | solution.py:276
  15.8 0.0 copy-done.7
  15.8 0.1 select_bitcast_fusion.1
  15.9 2.6 %collective-permute-start.4 = (bf16[1,144,1152]{2,1,0:T(8,128)(2,1)S(1)}, bf16[1,144,1152]{2,1,0:T(8,128)(2,1)S(1)}, u32[]{:S(2)}, u32[]{:S(2)}) collective-permute-start(bf16[1,144,1152]{2,1,0:T(8,128)(2,1)S(1)} %pad_maximum_fusion), channel_id=1, source_target_pairs={{0,4},{4,8},{8,12},{1,5},{5,9},{9,13},{2,6},{6,10},{10,14},{3,7},{... | collective-permute-start | bytes 995336 | tf_op jit(solution)/shard_map/ppermute | solution.py:31
  18.5 1.9 %collective-permute-start.6 = (bf16[1,144,384]{2,1,0:T(8,128)(2,1)S(1)}, bf16[1,144,384]{2,1,0:T(8,128)(2,1)S(1)}, u32[]{:S(2)}, u32[]{:S(2)}) collective-permute-start(bf16[1,144,384]{2,1,0:T(8,128)(2,1)S(1)} %get-tuple-element.54), channel_id=1, source_target_pairs={{0,4},{4,8},{8,12},{1,5},{5,9},{9,13},{2,6},{6,10},{10,14},{3,7},{... | collective-permute-start | bytes 331784 | tf_op jit(solution)/shard_map/ppermute | solution.py:31
  21.1 1.9 %collective-permute-start.10 = (bf16[24,512]{1,0:T(8,128)(2,1)S(1)}, bf16[24,512]{1,0:T(8,128)(2,1)S(1)}, u32[]{:S(2)}, u32[]{:S(2)}) collective-permute-start(bf16[24,512]{1,0:T(8,128)(2,1)S(1)} %get-tuple-element.51), channel_id=1, source_target_pairs={{0,4},{4,8},{8,12},{1,5},{5,9},{9,13},{2,6},{6,10},{10,14},{3,7},{... | collective-permute-start | bytes 73736 | tf_op jit(solution)/shard_map/ppermute | solution.py:31
  23.0 0.0 copy-done.1
  23.0 0.0 copy-done.5
  23.0 2.7 %middle.2 = (f32[6,128,576]{2,1,0:T(8,128)S(1)}, f32[6,576]{1,0:T(8,128)S(1)}, f32[6,576]{1,0:T(8,128)S(1)}) custom-call(s32[4,4]{1,0:T(4,128)S(1)} %copy-done.4, s32[4,4]{1,0:T(4,128)S(1)} %copy-done.5, bf16[4,1,144,768]{3,2,1,0:T(8,128)(2,1)S(1)} %copy-done.1, bf16[2,1,144,768]{3,2,1,0:T(8,128)(2,1)S(1)} %collective-permute-done.refs_0_, ...), custom_call_target="tpu_custom_call" | custom-call | flops 254803968 | bytes 3124352 | tf_op jit(solution)/shard_map/middle/pallas_call | solution.py:287
  25.8 0.0 collective-permute-done.5.refs_0_
  25.8 0.7 %middle.3 = (f32[6,128,576]{2,1,0:T(8,128)S(1)}, f32[6,576]{1,0:T(8,128)S(1)}, f32[6,576]{1,0:T(8,128)S(1)}) custom-call(s32[4,4]{1,0:T(4,128)S(1)} %copy-done.4, s32[4,4]{1,0:T(4,128)S(1)} %copy-done.5, bf16[4,1,144,768]{3,2,1,0:T(8,128)(2,1)S(1)} %copy-done.1, bf16[2,1,144,768]{3,2,1,0:T(8,128)(2,1)S(1)} %collective-permute-done.5.refs_0_, ...), custom_call_target="tpu_custom_call" | custom-call | flops 254803968 | bytes 3124352 | tf_op jit(solution)/shard_map/middle/pallas_call | solution.py:287
  26.5 5.9 %collective-permute-done.4.refs_0_.value_ref = bf16[1,144,1152]{2,1,0:T(8,128)(2,1)S(1)} collective-permute-done((bf16[1,144,1152]{2,1,0:T(8,128)(2,1)S(1)}, bf16[1,144,1152]{2,1,0:T(8,128)(2,1)S(1)}, u32[]{:S(2)}, u32[]{:S(2)}) %collective-permute-start.4) | collective-permute-done | bytes 331808 | tf_op jit(solution)/shard_map/ppermute | solution.py:31
  32.4 0.8 %score.1 = (f32[6,128,576]{2,1,0:T(8,128)S(1)}, bf16[6,144,576]{2,1,0:T(8,128)(2,1)S(1)}) custom-call(s32[4,4]{1,0:T(4,128)S(1)} %copy-done.4, s32[4,4]{1,0:T(4,128)S(1)} %copy-done.5, bf16[4,1,144,768]{3,2,1,0:T(8,128)(2,1)S(1)} %copy-done.1, bf16[1,144,1152]{2,1,0:T(8,128)(2,1)S(1)} %collective-permute-done.4.refs_0_.value_ref, ...), custom_call_target="tpu_custom_call" | custom-call | flops 127401984 | bytes 3013760 | tf_op jit(solution)/shard_map/score/pallas_call | solution.py:287
  33.2 0.5 %average.1 = (f32[4,144,384]{2,1,0:T(8,128)S(1)}, f32[1,576]{1,0:T(1,128)S(1)}) custom-call(f32[6,128,576]{2,1,0:T(8,128)S(1)} %get-tuple-element.42.acc_ref, bf16[6,144,576]{2,1,0:T(8,128)(2,1)S(1)} %get-tuple-element.43.w_ref, bf16[1,144,1152]{2,1,0:T(8,128)(2,1)S(1)} %collective-permute-done.4.refs_0_.value_ref), custom_call_target="tpu_custom_call" | custom-call | flops 63700992 | bytes 3096576 | tf_op jit(solution)/shard_map/average/pallas_call | solution.py:287
  33.8 1.0 %collective-permute-done.6.value_ref = bf16[1,144,384]{2,1,0:T(8,128)(2,1)S(1)} collective-permute-done((bf16[1,144,384]{2,1,0:T(8,128)(2,1)S(1)}, bf16[1,144,384]{2,1,0:T(8,128)(2,1)S(1)}, u32[]{:S(2)}, u32[]{:S(2)}) %collective-permute-start.6) | collective-permute-done | bytes 110624 | tf_op jit(solution)/shard_map/ppermute | solution.py:31
  34.8 0.4 rest.1
  35.2 1.5 %collective-permute-start.7 = (f32[1,576]{1,0:T(1,128)S(1)}, f32[1,576]{1,0:T(1,128)S(1)}, u32[]{:S(2)}, u32[]{:S(2)}) collective-permute-start(f32[1,576]{1,0:T(1,128)S(1)} %get-tuple-element.47.square_in), channel_id=1, source_target_pairs={{0,2},{1,3},{2,0},{3,1},{4,6},{5,7},{6,4},{7,5},{8,10},{9,11},{10,... | collective-permute-start | bytes 6920 | tf_op jit(solution)/shard_map/ppermute | solution.py:40
  36.7 0.0 collective-permute-start.8
  36.7 0.3 turn.1
  37.0 0.7 %collective-permute-start.9 = (f32[1,576]{1,0:T(1,128)S(1)}, f32[1,576]{1,0:T(1,128)S(1)}, u32[]{:S(2)}, u32[]{:S(2)}) collective-permute-start(f32[1,576]{1,0:T(1,128)S(1)} %get-tuple-element.49.refs_0_), channel_id=1, source_target_pairs={{0,1},{1,0},{2,3},{3,2},{4,5},{5,4},{6,7},{7,6},{8,9},{9,8},{10,11... | collective-permute-start | bytes 6920 | tf_op jit(solution)/shard_map/ppermute | solution.py:40
  37.8 0.0 collective-permute-done.10.tail_ref
  37.8 0.0 copy-done.2
  37.8 1.4 %decode.1 = bf16[1,36,512]{2,1,0:T(8,128)(2,1)} custom-call(s32[1]{0:T(128)S(6)} %copy.11.fade_ref, bf16[36,512]{1,0:T(8,128)(2,1)S(1)} %get-tuple-element.50.hidden_ref, bf16[24,512]{1,0:T(8,128)(2,1)S(1)} %collective-permute-done.10.tail_ref, bf16[3,512,512]{2,1,0:T(8,128)(2,1)S(1)} %copy-done.2), custom_call_target="tpu_custom_call" | custom-call | flops 56623104 | bytes 1634308 | tf_op jit(solution)/shard_map/decode/pallas_call | solution.py:287
  39.2 0.0 collective-permute-done.9.refs_3_
  39.2 0.0 collective-permute-done.7.refs_1_
  39.2 0.5 %collective-permute-done.8.refs_2_ = f32[1,576]{1,0:T(1,128)S(1)} collective-permute-done((f32[1,576]{1,0:T(1,128)S(1)}, f32[1,576]{1,0:T(1,128)S(1)}, u32[]{:S(2)}, u32[]{:S(2)}) %collective-permute-start.8) | collective-permute-done | bytes 2336 | tf_op jit(solution)/shard_map/ppermute | solution.py:40
  39.7 1.1 %scale.1 = bf16[4,1,144,768]{3,2,1,0:T(8,128)(2,1)} custom-call(f32[4,144,384]{2,1,0:T(8,128)S(1)} %get-tuple-element.44.front_ref, f32[4,144,384]{2,1,0:T(8,128)S(1)} %get-tuple-element.48.back_ref, f32[1,576]{1,0:T(1,128)S(1)} %get-tuple-element.49.refs_0_, f32[1,576]{1,0:T(1,128)S(1)} %collective-permute-done.7.refs_1_, ...), custom_call_target="tpu_custom_call" | custom-call | flops 442368 | bytes 1778688 | tf_op jit(solution)/shard_map/scale/pallas_call | solution.py:287
  (4 shorter events, 0.1 us)
Async XLA Ops:
  0.6 15.2 %copy-start.7 = (bf16[2,1,144,768]{3,2,1,0:T(8,128)(2,1)S(1)}, bf16[2,1,144,768]{3,2,1,0:T(8,128)(2,1)}, u32[]{:S(2)}) copy-start(bf16[2,1,144,768]{3,2,1,0:T(8,128)(2,1)} %param.11) | copy-start | bytes 1327108
  0.6 15.1 %collective-permute-start = (bf16[2,1,144,768]{3,2,1,0:T(8,128)(2,1)}, bf16[2,1,144,768]{3,2,1,0:T(8,128)(2,1)S(1)}, u32[]{:S(2)}, u32[]{:S(2)}) collective-permute-start(bf16[2,1,144,768]{3,2,1,0:T(8,128)(2,1)} %param.11), channel_id=1, source_target_pairs={{0,8},{8,12},{1,9},{9,13},{2,10},{10,14},{3,11},{11,15},{16,24},{2... | collective-permute-start | bytes 1327112 | tf_op jit(solution)/shard_map/ppermute | solution.py:276
  4.3 21.5 %collective-permute-start.5 = (bf16[2,1,144,768]{3,2,1,0:T(8,128)(2,1)}, bf16[2,1,144,768]{3,2,1,0:T(8,128)(2,1)S(1)}, u32[]{:S(2)}, u32[]{:S(2)}) collective-permute-start(bf16[2,1,144,768]{3,2,1,0:T(8,128)(2,1)} %param.11), channel_id=1, source_target_pairs={{4,12},{5,13},{6,14},{7,15},{20,28},{21,29},{22,30},{23,31}} | collective-permute-start | bytes 1327112 | tf_op jit(solution)/shard_map/ppermute | solution.py:276
  7.3 7.8 %collective-permute-start.1 = (bf16[36,512]{1,0:T(8,128)(2,1)}, bf16[36,512]{1,0:T(8,128)(2,1)S(1)}, u32[]{:S(2)}, u32[]{:S(2)}) collective-permute-start(bf16[36,512]{1,0:T(8,128)(2,1)} %get-tuple-element.29), channel_id=1, source_target_pairs={{0,1},{1,0},{2,3},{3,2},{4,5},{5,4},{6,7},{7,6},{8,9},{9,8},{10,11... | collective-permute-start | bytes 110600 | tf_op jit(solution)/shard_map/ppermute | solution.py:40
  7.3 7.8 %collective-permute-start.2 = (bf16[36,512]{1,0:T(8,128)(2,1)}, bf16[36,512]{1,0:T(8,128)(2,1)S(1)}, u32[]{:S(2)}, u32[]{:S(2)}) collective-permute-start(bf16[36,512]{1,0:T(8,128)(2,1)} %get-tuple-element.30), channel_id=1, source_target_pairs={{0,2},{1,3},{2,0},{3,1},{4,6},{5,7},{6,4},{7,5},{8,10},{9,11},{10,... | collective-permute-start | bytes 110600 | tf_op jit(solution)/shard_map/ppermute | solution.py:40
  8.9 6.2 %collective-permute-start.3 = (bf16[36,512]{1,0:T(8,128)(2,1)}, bf16[36,512]{1,0:T(8,128)(2,1)S(1)}, u32[]{:S(2)}, u32[]{:S(2)}) collective-permute-start(bf16[36,512]{1,0:T(8,128)(2,1)} %get-tuple-element.31), channel_id=1, source_target_pairs={{0,3},{1,2},{2,1},{3,0},{4,7},{5,6},{6,5},{7,4},{8,11},{9,10},{10,... | collective-permute-start | bytes 110600 | tf_op jit(solution)/shard_map/ppermute | solution.py:40
  9.2 1.2 %copy-start = (bf16[4,1,144,768]{3,2,1,0:T(8,128)(2,1)S(1)}, bf16[4,1,144,768]{3,2,1,0:T(8,128)(2,1)}, u32[]{:S(2)}) copy-start(bf16[4,1,144,768]{3,2,1,0:T(8,128)(2,1)} %q_ref.7) | copy-start | bytes 2654212
  10.4 0.7 %copy-start.4 = (s32[4,4]{1,0:T(4,128)S(1)}, s32[4,4]{1,0:T(4,128)}, u32[]{:S(2)}) copy-start(s32[4,4]{1,0:T(4,128)} %step_ref.7) | copy-start | bytes 196
  11.0 1.5 %copy-start.6 = (bf16[4,2,1,144,768]{4,3,2,1,0:T(8,128)(2,1)S(1)}, bf16[4,2,1,144,768]{4,3,2,1,0:T(8,128)(2,1)}, u32[]{:S(2)}) copy-start(bf16[4,2,1,144,768]{4,3,2,1,0:T(8,128)(2,1)} %kv_ref.1) | copy-start | bytes 5308420
  12.5 2.6 %copy-start.3 = (bf16[36,512]{1,0:T(8,128)(2,1)S(1)}, bf16[36,512]{1,0:T(8,128)(2,1)}, u32[]{:S(2)}) copy-start(bf16[36,512]{1,0:T(8,128)(2,1)} %get-tuple-element.28.refs_0_) | copy-start | bytes 110596
  15.1 7.9 %copy-start.1 = (bf16[4,1,144,768]{3,2,1,0:T(8,128)(2,1)S(1)}, bf16[4,1,144,768]{3,2,1,0:T(8,128)(2,1)}, u32[]{:S(2)}) copy-start(bf16[4,1,144,768]{3,2,1,0:T(8,128)(2,1)} %q_ref.7) | copy-start | bytes 2654212
  15.1 7.9 %copy-start.5 = (s32[4,4]{1,0:T(4,128)S(1)}, s32[4,4]{1,0:T(4,128)}, u32[]{:S(2)}) copy-start(s32[4,4]{1,0:T(4,128)} %mask_ref.5) | copy-start | bytes 196
  15.9 16.5 %collective-permute-start.4 = (bf16[1,144,1152]{2,1,0:T(8,128)(2,1)S(1)}, bf16[1,144,1152]{2,1,0:T(8,128)(2,1)S(1)}, u32[]{:S(2)}, u32[]{:S(2)}) collective-permute-start(bf16[1,144,1152]{2,1,0:T(8,128)(2,1)S(1)} %pad_maximum_fusion), channel_id=1, source_target_pairs={{0,4},{4,8},{8,12},{1,5},{5,9},{9,13},{2,6},{6,10},{10,14},{3,7},{... | collective-permute-start | bytes 995336 | tf_op jit(solution)/shard_map/ppermute | solution.py:31
  18.5 16.3 %collective-permute-start.6 = (bf16[1,144,384]{2,1,0:T(8,128)(2,1)S(1)}, bf16[1,144,384]{2,1,0:T(8,128)(2,1)S(1)}, u32[]{:S(2)}, u32[]{:S(2)}) collective-permute-start(bf16[1,144,384]{2,1,0:T(8,128)(2,1)S(1)} %get-tuple-element.54), channel_id=1, source_target_pairs={{0,4},{4,8},{8,12},{1,5},{5,9},{9,13},{2,6},{6,10},{10,14},{3,7},{... | collective-permute-start | bytes 331784 | tf_op jit(solution)/shard_map/ppermute | solution.py:31
  21.1 16.7 %collective-permute-start.10 = (bf16[24,512]{1,0:T(8,128)(2,1)S(1)}, bf16[24,512]{1,0:T(8,128)(2,1)S(1)}, u32[]{:S(2)}, u32[]{:S(2)}) collective-permute-start(bf16[24,512]{1,0:T(8,128)(2,1)S(1)} %get-tuple-element.51), channel_id=1, source_target_pairs={{0,4},{4,8},{8,12},{1,5},{5,9},{9,13},{2,6},{6,10},{10,14},{3,7},{... | collective-permute-start | bytes 73736 | tf_op jit(solution)/shard_map/ppermute | solution.py:31
  34.8 3.0 %copy-start.2 = (bf16[3,512,512]{2,1,0:T(8,128)(2,1)S(1)}, bf16[3,512,512]{2,1,0:T(8,128)(2,1)}, u32[]{:S(2)}) copy-start(bf16[3,512,512]{2,1,0:T(8,128)(2,1)} %conv_ref.1) | copy-start | bytes 4718596
  35.2 4.0 %collective-permute-start.7 = (f32[1,576]{1,0:T(1,128)S(1)}, f32[1,576]{1,0:T(1,128)S(1)}, u32[]{:S(2)}, u32[]{:S(2)}) collective-permute-start(f32[1,576]{1,0:T(1,128)S(1)} %get-tuple-element.47.square_in), channel_id=1, source_target_pairs={{0,2},{1,3},{2,0},{3,1},{4,6},{5,7},{6,4},{7,5},{8,10},{9,11},{10,... | collective-permute-start | bytes 6920 | tf_op jit(solution)/shard_map/ppermute | solution.py:40
  36.7 3.0 %collective-permute-start.8 = (f32[1,576]{1,0:T(1,128)S(1)}, f32[1,576]{1,0:T(1,128)S(1)}, u32[]{:S(2)}, u32[]{:S(2)}) collective-permute-start(f32[1,576]{1,0:T(1,128)S(1)} %get-tuple-element.47.square_in), channel_id=1, source_target_pairs={{0,3},{1,2},{2,1},{3,0},{4,7},{5,6},{6,5},{7,4},{8,11},{9,10},{10,... | collective-permute-start | bytes 6920 | tf_op jit(solution)/shard_map/ppermute | solution.py:40
  37.0 2.2 %collective-permute-start.9 = (f32[1,576]{1,0:T(1,128)S(1)}, f32[1,576]{1,0:T(1,128)S(1)}, u32[]{:S(2)}, u32[]{:S(2)}) collective-permute-start(f32[1,576]{1,0:T(1,128)S(1)} %get-tuple-element.49.refs_0_), channel_id=1, source_target_pairs={{0,1},{1,0},{2,3},{3,2},{4,5},{5,4},{6,7},{7,6},{8,9},{9,8},{10,11... | collective-permute-start | bytes 6920 | tf_op jit(solution)/shard_map/ppermute | solution.py:40
